TPU v7x, 256 devices: a whole 4x4x8 slice. The times are simulated.
256 devices in a mesh: dp: 4 (over y), gx: 16 (over z, x_hi), gy: 4 (over x_lo, core).
Axes of the slice: x: 4 (x_hi: 2, x_lo: 2; x = x_hi * 2 + x_lo), y: 4, z: 8, core: 2. Of those that a mesh axis runs over, the one named last changes fastest.
Arguments:
- tokens: bfloat16 [4, 32, 32, 32, 256], P('dp', 'gx', 'gy'), may hold values from -120 to 120
- attn: bfloat16 [4, 32, 32, 32, 256], P('dp', 'gx', 'gy'), may hold values from -6 to 6
- cotangent: bfloat16 [4, 32, 32, 32, 256], P('dp', 'gx', 'gy'), may hold values from -6 to 6
- gain: float32 [256], replicated, may hold values from 0.25 to 1.75
- w_qkv: bfloat16 [256, 768], replicated, may hold values from -0.26796875 to 0.26796875
- w_out: bfloat16 [256, 256], replicated, may hold values from -0.375 to 0.375
Outputs:
- d_tokens: bfloat16 [4, 32, 32, 32, 256], P('dp', 'gx', 'gy')
- d_w_qkv: float32 [256, 768], replicated
- d_w_out: float32 [256, 256], replicated
- d_gain: float32 [256], replicated
All inputs are finite; a program needn't handle non-finite values.
Results may differ from a plain program's by a relative error of at most 0.012.
The roundings to bfloat16 on the way count: a program that leaves them out, or rounds other values in their place, can miss the bound.
Values may be sent and summed in bfloat16 or wider, within the bound.
No kernel may reach another device: no remote copies, remote signals or barrier semaphores. Data moves between devices by JAX's collectives and lax.ppermute only.
A program may use at most 64 MiB of HBM per device.

v0:
```python
import math

import jax
import jax.numpy as jnp
from jax import lax
from jax.sharding import PartitionSpec as P

HEADS = 8


EPSILON = 1e-06


def pencil_grads(linear, grad_attn):
    batch, length, width = grad_attn.shape
    head_size = width // HEADS
    factor = 1.0 / math.sqrt(head_size)
    query = linear[..., :width].reshape(batch, length, HEADS, head_size)
    keys_h = linear[..., width : 2 * width].reshape(batch, length, HEADS, head_size)
    values_h = linear[..., 2 * width :].reshape(batch, length, HEADS, head_size)
    grad_h = grad_attn.reshape(batch, length, HEADS, head_size)
    scores = (
        jnp.einsum("blhd,bmhd->bhlm", query, keys_h, preferred_element_type=jnp.float32) * factor
    )
    probs = jax.nn.softmax(scores, axis=-1)
    probs_low = probs.astype(jnp.bfloat16)
    grad_values = jnp.einsum(
        "bhlm,blhd->bmhd", probs_low, grad_h, preferred_element_type=jnp.float32
    )
    grad_probs = jnp.einsum("blhd,bmhd->bhlm", grad_h, values_h, preferred_element_type=jnp.float32)
    grad_scores = probs * (grad_probs - jnp.sum(probs * grad_probs, axis=-1, keepdims=True))
    scores_low = grad_scores.astype(jnp.bfloat16)
    grad_query = (
        jnp.einsum("bhlm,bmhd->blhd", scores_low, keys_h, preferred_element_type=jnp.float32)
        * factor
    )
    grad_keys = (
        jnp.einsum("bhlm,blhd->bmhd", scores_low, query, preferred_element_type=jnp.float32)
        * factor
    )
    joined = jnp.concatenate(
        [
            grad_query.reshape(batch, length, width),
            grad_keys.reshape(batch, length, width),
            grad_values.reshape(batch, length, width),
        ],
        axis=-1,
    )
    return joined.astype(jnp.bfloat16)


def first_grads(linear, grads):
    length, items, slab, triple = linear.shape
    width = grads.shape[-1]
    lined = linear.transpose(1, 2, 0, 3).reshape(items * slab, length, triple)
    lined_grad = grads.transpose(1, 2, 0, 3).reshape(items * slab, length, width)
    return (
        pencil_grads(lined, lined_grad).reshape(items, slab, length, triple).transpose(2, 0, 1, 3)
    )


def second_grads(linear, grads):
    items, length, slab, triple = linear.shape
    width = grads.shape[-1]
    lined = linear.transpose(0, 2, 1, 3).reshape(items * slab, length, triple)
    lined_grad = grads.transpose(0, 2, 1, 3).reshape(items * slab, length, width)
    return (
        pencil_grads(lined, lined_grad).reshape(items, slab, length, triple).transpose(0, 2, 1, 3)
    )


def weight_part(normed_rows, grad_rows):
    flat_normed = normed_rows.reshape(-1, normed_rows.shape[-1])
    flat_grad = grad_rows.reshape(-1, grad_rows.shape[-1])
    return lax.dot_general(
        flat_normed, flat_grad, (((0,), (0,)), ((), ())), preferred_element_type=jnp.float32
    )


def input_part(grad_rows, w_qkv):
    flat_grad = grad_rows.reshape(-1, grad_rows.shape[-1])
    result = lax.dot_general(
        flat_grad, w_qkv, (((1,), (1,)), ((), ())), preferred_element_type=jnp.float32
    )
    return result.reshape(grad_rows.shape[:-1] + (w_qkv.shape[0],))


def on_device(tokens, attn, cotangent, gain, w_qkv, w_out):
    volume = tokens[0]
    depth_x, depth_y, depth_z, width = volume.shape
    tokens_f = volume.astype(jnp.float32)
    root = jnp.sqrt(jnp.mean(tokens_f * tokens_f, axis=-1, keepdims=True) + EPSILON)
    normed = (tokens_f / root * gain).astype(jnp.bfloat16)
    upstream = cotangent[0]
    grad_attn = jnp.einsum(
        "abzd,cd->abzc", upstream, w_out, preferred_element_type=jnp.float32
    ).astype(jnp.bfloat16)
    qkv = jnp.einsum("abzc,ce->abze", normed, w_qkv, preferred_element_type=jnp.float32).astype(
        jnp.bfloat16
    )
    grad_third = pencil_grads(
        qkv.reshape(depth_x * depth_y, depth_z, 3 * width),
        grad_attn.reshape(depth_x * depth_y, depth_z, width),
    ).reshape(depth_x, depth_y, depth_z, 3 * width)
    part_qkv = weight_part(normed, grad_third)
    grad_normed = input_part(grad_third, w_qkv)
    grad_first = (
        lambda pieces: lax.all_to_all(
            first_grads(pieces[0], pieces[1]), "gx", split_axis=0, concat_axis=2, tiled=True
        )
    )(
        (
            lax.all_to_all(qkv, "gx", split_axis=2, concat_axis=0, tiled=True),
            lax.all_to_all(grad_attn, "gx", split_axis=2, concat_axis=0, tiled=True),
        )
    )
    grad_second = (
        lambda pieces: lax.all_to_all(
            second_grads(pieces[0], pieces[1]), "gy", split_axis=1, concat_axis=2, tiled=True
        )
    )(
        (
            lax.all_to_all(qkv, "gy", split_axis=2, concat_axis=1, tiled=True),
            lax.all_to_all(grad_attn, "gy", split_axis=2, concat_axis=1, tiled=True),
        )
    )
    stacked = jnp.concatenate(
        [grad_first.reshape(-1, 3 * width), grad_second.reshape(-1, 3 * width)], axis=0
    )
    doubled = jnp.concatenate([normed.reshape(-1, width), normed.reshape(-1, width)], axis=0)
    part_qkv = part_qkv + weight_part(doubled, stacked)
    grad_normed = grad_normed + input_part(grad_first, w_qkv) + input_part(grad_second, w_qkv)
    count = (
        depth_x
        * depth_y
        * depth_z
        * lax.axis_size("dp")
        * lax.axis_size("gx")
        * lax.axis_size("gy")
    )
    scale = 1.0 / math.sqrt(count)
    part_qkv = part_qkv * scale
    part_out = weight_part(attn[0], upstream) * scale
    flat_normed_grad = grad_normed.reshape(-1, width)
    flat_tokens = tokens_f.reshape(-1, width)
    flat_root = root.reshape(-1, 1)
    part_gain = jnp.sum(flat_normed_grad * flat_tokens / flat_root, axis=0) * scale
    gained = gain * flat_normed_grad
    inner = jnp.sum(gained * flat_tokens, axis=-1, keepdims=True)
    result = gained / flat_root - flat_tokens * inner / (width * flat_root**3)
    d_tokens = result.astype(jnp.bfloat16).reshape(1, depth_x, depth_y, depth_z, width)
    d_w_qkv, d_w_out, d_gain = lax.psum((part_qkv, part_out, part_gain), ("dp", "gx", "gy"))
    return (d_tokens, d_w_qkv, d_w_out, d_gain)


def solution(mesh):
    return jax.shard_map(
        on_device,
        mesh=mesh,
        in_specs=(
            P("dp", "gx", "gy", None, None),
            P("dp", "gx", "gy", None, None),
            P("dp", "gx", "gy", None, None),
            P(),
            P(),
            P(),
        ),
        out_specs=(P("dp", "gx", "gy", None, None), P(), P(), P()),
        check_vma=False,
    )
```

profile of v0, /device:TPU:1, one launch (start us, length us, event | category | flops | bytes accessed | tf_op | source)
XLA Modules:
  0.0 443.0 jit_solution(16454929206338457476)
XLA Ops:
  9.3 7.2 %all-to-all-start.4 = ((bf16[2,8,32,256]{3,1,0,2:T(8,128)(2,1)}), bf16[2,8,32,256]{3,1,0,2:T(8,128)(2,1)}, u32[]{:S(2)}, u32[]{:S(2)}) async-start(bf16[2,8,32,256]{3,1,0,2:T(8,128)(2,1)} %copy.244), calls=%async_computation.4 | async-start | bytes 524288 | tf_op jit(solution)/shard_map/all_to_all | solution.py:124
  20.5 1.4 copy.319
  21.9 9.1 %all-to-all-start.1 = ((bf16[2,8,32,256]{3,1,0,2:T(8,128)(2,1)}), bf16[2,8,32,256]{3,1,0,2:T(8,128)(2,1)}, u32[]{:S(2)}, u32[]{:S(2)}) async-start(bf16[2,8,32,256]{3,1,0,2:T(8,128)(2,1)} %copy.244), calls=%async_computation.1 | async-start | bytes 524288 | tf_op jit(solution)/shard_map/all_to_all | solution.py:114
  31.0 3.0 fusion.89
  36.6 1.7 reshape.216
  38.3 4.3 multiply_reduce_fusion.2
  42.7 7.1 %all-to-all-start.3 = ((bf16[2,8,32,768]{3,1,0,2:T(8,128)(2,1)}), bf16[2,8,32,768]{3,1,0,2:T(8,128)(2,1)}, u32[]{:S(2)}, u32[]{:S(2)}) async-start(bf16[2,8,32,768]{3,1,0,2:T(8,128)(2,1)} %copy.238), calls=%async_computation.3 | async-start | bytes 1572864 | tf_op jit(solution)/shard_map/all_to_all | solution.py:123
  49.8 2.9 multiply_convert_fusion.8
  52.7 1.7 fusion.11
  55.4 1.4 copy.328
  59.2 1.5 all-to-all-done.3
  60.7 7.9 %all-to-all-start = ((bf16[2,8,32,768]{3,1,0,2:T(8,128)(2,1)}), bf16[2,8,32,768]{3,1,0,2:T(8,128)(2,1)}, u32[]{:S(2)}, u32[]{:S(2)}) async-start(bf16[2,8,32,768]{3,1,0,2:T(8,128)(2,1)} %copy.238), calls=%async_computation | async-start | bytes 1572864 | tf_op jit(solution)/shard_map/all_to_all | solution.py:113
  72.3 1.4 copy.326
  73.7 4.6 %fusion.91 = (f32[16,8,32]{2,1,0:T(8,128)}, f32[16,8,32,32]{2,3,1,0:T(8,128)}) fusion(bf16[16,32,8,32]{1,3,2,0:T(8,128)(2,1)} %bitcast.187, bf16[16,32,8,32]{1,3,2,0:T(8,128)(2,1)S(1)} %bitcast.183), kind=kOutput, calls=%fused_computation.124 | convolution fusion | flops 8781855 | bytes 1064960 | tf_op jit(solution)/shard_map/sub | solution.py:25
  78.3 3.5 convolution_convert_fusion
  81.8 2.3 copy.286
  84.2 2.4 reshape.224
  86.6 2.7 multiply_reduce_fusion
  92.7 2.6 concatenate.58
  95.3 1.9 fusion.14
  97.7 1.4 concatenate.57
  101.6 5.5 %all-to-all-start.5 = ((bf16[2,32,8,768]{3,2,0,1:T(8,128)(2,1)}), bf16[2,32,8,768]{3,2,0,1:T(8,128)(2,1)}, u32[]{:S(2)}, u32[]{:S(2)}) async-start(bf16[2,32,8,768]{3,2,0,1:T(8,128)(2,1)} %copy.287), calls=%async_computation.5 | async-start | bytes 1572864 | tf_op jit(solution)/shard_map/all_to_all | solution.py:118
  110.9 1.4 copy.322
  112.3 4.6 %fusion.90 = (f32[16,8,32]{2,1,0:T(8,128)}, f32[16,8,32,32]{2,3,1,0:T(8,128)}) fusion(bf16[16,32,8,32]{1,3,2,0:T(8,128)(2,1)} %bitcast.189, bf16[16,32,8,32]{1,3,2,0:T(8,128)(2,1)S(1)} %bitcast.185), kind=kOutput, calls=%fused_computation.123 | convolution fusion | flops 8781855 | bytes 1064960 | tf_op jit(solution)/shard_map/sub | solution.py:25
  116.9 3.5 convolution_convert_fusion.1
  120.4 2.3 copy.260
  122.7 2.4 reshape.220
  125.2 2.7 multiply_reduce_fusion.1
  129.8 1.4 copy.257
  131.2 2.6 concatenate.54
  133.9 1.9 fusion.12
  136.3 1.4 concatenate.53
  138.9 1.7 copy.261
  140.6 9.6 %all-to-all-start.2 = ((bf16[32,8,2,768]{3,2,1,0:T(2,128)(2,1)}), bf16[32,8,2,768]{3,2,1,0:T(2,128)(2,1)}, u32[]{:S(2)}, u32[]{:S(2)}) async-start(bf16[32,8,2,768]{3,2,1,0:T(2,128)(2,1)} %copy.261), calls=%async_computation.2 | async-start | bytes 1572864 | tf_op jit(solution)/shard_map/all_to_all | solution.py:108
  150.4 1.7 fusion.10
  153.2 1.4 concatenate.50
  156.5 1.4 concatenate.49
  158.0 1.4 concatenate.61
  159.4 1.9 convolution_convert_fusion.2
  163.4 2.0 fusion.22
  169.2 3.5 all-to-all-done.2
  176.1 1.6 convolution_add_fusion.1
  177.7 1.5 fusion.19
  179.3 1.7 fusion.60
  180.9 77.2 %psum.23 = f32[256]{0:T(256)} all-reduce(f32[256]{0:T(256)S(1)} %broadcast_multiply_fusion), channel_id=1, replica_groups=mesh['dp'=4,'gx'=16,'gy'=4] {'dp','gx','gy'}, use_global_device_ids=true, to_apply=%region_14.0 | all-reduce | flops 256 | bytes 2048 | tf_op jit(solution)/shard_map/psum | solution.py:152
  259.1 173.1 %all-reduce.3.cloned.1.call-done = (f32[256,768]{1,0:T(8,128)}, f32[256,256]{1,0:T(8,128)}) async-done(((f32[256,768]{1,0:T(8,128)}, f32[256,256]{1,0:T(8,128)}), (f32[256,768]{1,0:T(8,128)}, f32[256,256]{1,0:T(8,128)})) %all-reduce.3.cloned.1.call-update) | async-done | bytes 1048592 | tf_op jit(solution)/shard_map/psum | solution.py:152
  432.2 2.1 copy.350
  434.3 1.7 copy.351
  (107 shorter events, 42.7 us)
Async XLA Ops:
  7.2 10.5 %copy-start = (bf16[256,768]{1,0:T(8,128)(2,1)S(1)}, bf16[256,768]{1,0:T(8,128)(2,1)}, u32[]{:S(2)}) copy-start(bf16[256,768]{1,0:T(8,128)(2,1)} %param.10) | copy-start | bytes 1179652
  9.3 12.6 %all-to-all-start.4 = ((bf16[2,8,32,256]{3,1,0,2:T(8,128)(2,1)}), bf16[2,8,32,256]{3,1,0,2:T(8,128)(2,1)}, u32[]{:S(2)}, u32[]{:S(2)}) async-start(bf16[2,8,32,256]{3,1,0,2:T(8,128)(2,1)} %copy.244), calls=%async_computation.4 | async-start | bytes 524288 | tf_op jit(solution)/shard_map/all_to_all | solution.py:124
  21.9 20.8 %all-to-all-start.1 = ((bf16[2,8,32,256]{3,1,0,2:T(8,128)(2,1)}), bf16[2,8,32,256]{3,1,0,2:T(8,128)(2,1)}, u32[]{:S(2)}, u32[]{:S(2)}) async-start(bf16[2,8,32,256]{3,1,0,2:T(8,128)(2,1)} %copy.244), calls=%async_computation.1 | async-start | bytes 524288 | tf_op jit(solution)/shard_map/all_to_all | solution.py:114
  42.7 18.0 %all-to-all-start.3 = ((bf16[2,8,32,768]{3,1,0,2:T(8,128)(2,1)}), bf16[2,8,32,768]{3,1,0,2:T(8,128)(2,1)}, u32[]{:S(2)}, u32[]{:S(2)}) async-start(bf16[2,8,32,768]{3,1,0,2:T(8,128)(2,1)} %copy.238), calls=%async_computation.3 | async-start | bytes 1572864 | tf_op jit(solution)/shard_map/all_to_all | solution.py:123
  60.7 40.9 %all-to-all-start = ((bf16[2,8,32,768]{3,1,0,2:T(8,128)(2,1)}), bf16[2,8,32,768]{3,1,0,2:T(8,128)(2,1)}, u32[]{:S(2)}, u32[]{:S(2)}) async-start(bf16[2,8,32,768]{3,1,0,2:T(8,128)(2,1)} %copy.238), calls=%async_computation | async-start | bytes 1572864 | tf_op jit(solution)/shard_map/all_to_all | solution.py:113
  73.7 4.6 %copy-start.1 = (bf16[16,32,256]{1,2,0:T(8,128)(2,1)}, bf16[16,32,256]{1,2,0:T(8,128)(2,1)S(1)}, u32[]{:S(2)}) copy-start(bf16[16,32,256]{1,2,0:T(8,128)(2,1)S(1)} %copy.326) | copy-start | bytes 786436
  81.8 4.8 %copy-start.12 = (bf16[2,8,32,256]{2,3,1,0:T(8,128)(2,1)S(1)}, bf16[2,8,32,256]{2,3,1,0:T(8,128)(2,1)}, u32[]{:S(2)}) copy-start(bf16[2,8,32,256]{2,3,1,0:T(8,128)(2,1)} %copy.328) | copy-start | bytes 786436
  86.6 2.7 copy-start.9
  86.6 2.7 copy-start.21
  89.3 1.2 copy-start.3
  101.6 38.9 %all-to-all-start.5 = ((bf16[2,32,8,768]{3,2,0,1:T(8,128)(2,1)}), bf16[2,32,8,768]{3,2,0,1:T(8,128)(2,1)}, u32[]{:S(2)}, u32[]{:S(2)}) async-start(bf16[2,32,8,768]{3,2,0,1:T(8,128)(2,1)} %copy.287), calls=%async_computation.5 | async-start | bytes 1572864 | tf_op jit(solution)/shard_map/all_to_all | solution.py:118
  112.3 4.6 %copy-start.2 = (bf16[16,32,256]{1,2,0:T(8,128)(2,1)}, bf16[16,32,256]{1,2,0:T(8,128)(2,1)S(1)}, u32[]{:S(2)}) copy-start(bf16[16,32,256]{1,2,0:T(8,128)(2,1)S(1)} %copy.322) | copy-start | bytes 786436
  120.4 4.8 %copy-start.11 = (bf16[8,2,32,256]{2,3,1,0:T(8,128)(2,1)S(1)}, bf16[8,2,32,256]{2,3,1,0:T(8,128)(2,1)}, u32[]{:S(2)}) copy-start(bf16[8,2,32,256]{2,3,1,0:T(8,128)(2,1)} %copy.324) | copy-start | bytes 786436
  125.2 2.7 copy-start.10
  125.2 2.7 copy-start.22
  127.9 1.2 copy-start.4
  140.6 12.2 %copy-start.5 = (bf16[16,32,8,32]{3,1,2,0:T(8,128)(2,1)S(1)}, bf16[16,32,8,32]{3,1,2,0:T(8,128)(2,1)}, u32[]{:S(2)}) copy-start(bf16[16,32,8,32]{3,1,2,0:T(8,128)(2,1)} %fusion.11) | copy-start | bytes 786436
  140.6 32.1 %all-to-all-start.2 = ((bf16[32,8,2,768]{3,2,1,0:T(2,128)(2,1)}), bf16[32,8,2,768]{3,2,1,0:T(2,128)(2,1)}, u32[]{:S(2)}, u32[]{:S(2)}) async-start(bf16[32,8,2,768]{3,2,1,0:T(2,128)(2,1)} %copy.261), calls=%async_computation.2 | async-start | bytes 1572864 | tf_op jit(solution)/shard_map/all_to_all | solution.py:108
  150.2 282.1 %all-reduce.3.cloned.1.call-start = ((), (), s32[]{:S(2)}) async-start(), calls=%async_computation.6 | async-start | bytes 2097152 | tf_op jit(solution)/shard_map/psum | solution.py:152
  152.8 3.3 copy-start.6
  156.5 2.9 copy-start.8
  161.3 1.9 copy-start.7
  161.3 1.9 copy-start.23
  161.3 1.9 copy-start.24
  161.6 1.7 copy-start.18
  162.4 3.0 copy-start.15
  162.5 3.0 copy-start.17
  163.4 3.3 copy-start.19
  163.4 3.3 copy-start.14
  163.4 3.3 copy-start.16
  176.1 1.6 copy-start.13
  176.1 1.6 copy-start.20
  176.1 1.6 copy-start.26
  177.7 1.5 copy-start.25
Sparse Core Ops, SparseCore 0:
  179.4 252.8 all-reduce.2
where the time goes:
time: 451 us; the launch traced here: 443 us
  waiting for transfers between devices  178 us (39%)
  blocking collectives  77.2 us (17%)
  local copies, waits for them, and re-layouts  66.1 us (15%)
  matrix products  51.3 us (11%)
  starting transfers between devices  46.6 us (10%)
  between operations  14.8 us (3%)
  other arithmetic  8.83 us (2%)
    psum x1, waiting for transfers between devices, on_device(): lax.psum((part_qkv, part_out, part_gain), ('dp', 'gx', 'gy'))  173 us
    psum x1, blocking collectives, on_device(): lax.psum((part_qkv, part_out, part_gain), ('dp', 'gx', 'gy'))  77.2 us
    concatenate x12, local copies, waits for them, and re-layouts, pencil_grads(): jnp.concatenate([grad_query.reshape(batch, length, width), grad_keys.resh...  19.5 us
    sub x3, matrix products, pencil_grads(): probs = jax.nn.softmax(scores, axis=-1)  12.2 us
    dot_general x3, matrix products, pencil_grads(): jnp.einsum('blhd,bmhd->bhlm', grad_h, values_h, preferred_element_type=jn...  9.71 us
    all_to_all x1, starting transfers between devices, on_device(): lax.all_to_all(first_grads(pieces[0], pieces[1]), 'gx', split_axis=0, con...  9.61 us
    all_to_all x1, starting transfers between devices, on_device(): lax.all_to_all(grad_attn, 'gx', split_axis=2, concat_axis=0, tiled=True)  9.09 us
  transfers between devices with their start and end apart: 7, of which 4 were waited for; matrix products, arithmetic and copies ran while one was open for 25% of the time, Pallas kernels for 0%

commit v1 on v0

v1 whole, which is shorter than its diff:
```python
import functools
import math

import jax
import jax.numpy as jnp
from jax import lax
from jax.experimental import pallas as pl
from jax.experimental.pallas import tpu as pltpu
from jax.sharding import Mesh
from jax.sharding import PartitionSpec as P

HEADS = 8
HEAD = 32
WIDTH = 256
TRIPLE = 3 * WIDTH
EPSILON = 1e-06
FACTOR = 1.0 / math.sqrt(HEAD)
TOKENS = 512
LENGTH = 32
PENCILS = 16
ROWS = 16
LANES = 128
TILES = 64
BF16 = jnp.bfloat16
F32 = jnp.float32
VMEM = pl.BlockSpec(memory_space=pltpu.VMEM)
SMEM = pl.BlockSpec(memory_space=pltpu.SMEM)
PLANE = ("y", "xh", "xl")
FIRST = ("z", "xh")
SECOND = ("xl", "c")


def params():
    return pltpu.CompilerParams(vmem_limit_bytes=48 * 2**20)


def cost(us):
    return pl.CostEstimate(
        flops=int(us * 8e8), bytes_accessed=int(us * 2e6), transcendentals=0
    )


def dot(left, right, left_dim, right_dim):
    return lax.dot_general(
        left, right, (((left_dim,), (right_dim,)), ((), ())), preferred_element_type=F32
    )


def wide(ref, first, rows):
    return jnp.concatenate([ref[first, rows, :], ref[first + 1, rows, :]], axis=1).astype(BF16)


def attention(proj, grads, rows_of, block, lane):
    q = [wide(proj, 0, rows) for rows in rows_of]
    k = [wide(proj, 2, rows) for rows in rows_of]
    v = [wide(proj, 4, rows) for rows in rows_of]
    g = [wide(proj, 6, rows) for rows in rows_of]
    lows = []
    for i, rows in enumerate(rows_of):
        q_block = jnp.concatenate([q[i]] * HEADS, axis=0) * block
        g_block = jnp.concatenate([g[i]] * HEADS, axis=0) * block
        scores = dot(k[i], q_block, 1, 1)
        grad_probs = dot(v[i], g_block, 1, 1)
        top = jnp.max(scores, axis=0, keepdims=True)
        powers = jnp.exp((scores - top) * FACTOR)
        probs = powers * (1.0 / jnp.sum(powers, axis=0, keepdims=True))
        inner = jnp.sum(probs * grad_probs, axis=0, keepdims=True)
        low = (probs * (grad_probs - inner)).astype(BF16)
        grad_v = dot(probs.astype(BF16), g_block, 1, 0)
        grad_k = dot(low, q_block, 1, 0) * FACTOR
        for half in range(2):
            cols = slice(half * LANES, (half + 1) * LANES)
            grads[2 + half, rows, :] = grad_k[:, cols]
            grads[4 + half, rows, :] = grad_v[:, cols]
        lows.append(low)
    stacked = jnp.concatenate(lows, axis=0)
    for half in range(2):
        cols = slice(half * LANES, (half + 1) * LANES)
        turned = stacked[:, cols].T
        for i, rows in enumerate(rows_of):
            every = dot(turned[:, i * LENGTH : (i + 1) * LENGTH], k[i][:, cols], 1, 0)
            picked = every[96:128]
            for head in (2, 1, 0):
                picked = jnp.where(
                    lane < HEAD * (head + 1), every[head * 32 : head * 32 + 32], picked
                )
            grads[half, rows, :] = picked * FACTOR


def axis_grads(tokens, cotangent, gain, w_qkv, w_out, proj, grads, strided):
    tokens_f = tokens.astype(F32)
    root = jnp.sqrt(jnp.mean(tokens_f * tokens_f, axis=-1, keepdims=True) + EPSILON)
    unit = tokens_f / root
    normed = (unit * gain).astype(BF16)
    qkv = dot(normed, w_qkv, 1, 0)
    for col in range(6):
        proj[col] = qkv[:, col * LANES : (col + 1) * LANES]
    grad_attn = dot(cotangent, w_out, 1, 1)
    for col in range(2):
        proj[6 + col] = grad_attn[:, col * LANES : (col + 1) * LANES]
    shape = (WIDTH, WIDTH)
    block = (
        lax.broadcasted_iota(jnp.int32, shape, 0) // HEAD
        == lax.broadcasted_iota(jnp.int32, shape, 1) // HEAD
    )
    block = block.astype(F32).astype(BF16)
    lane = lax.broadcasted_iota(jnp.int32, (LENGTH, LANES), 1)
    for base in range(0, PENCILS, 4):
        if strided:
            rows_of = [pl.ds(base + i, LENGTH, stride=PENCILS) for i in range(4)]
        else:
            rows_of = [pl.ds((base + i) * LENGTH, LENGTH) for i in range(4)]
        attention(proj, grads, rows_of, block, lane)
    joined = jnp.concatenate([grads[col].astype(BF16) for col in range(6)], axis=1)
    grad_normed = dot(joined, w_qkv, 1, 1)
    part_qkv = dot(normed, joined, 0, 0)
    part_gain = jnp.sum(grad_normed * unit, axis=0, keepdims=True)
    return grad_normed, part_qkv, part_gain


SCRATCH = [
    pltpu.VMEM((8, TOKENS, LANES), F32),
    pltpu.VMEM((6, TOKENS, LANES), F32),
]


def prepare_kernel(tokens, cotangent, to_first, to_second):
    for kind, ref in enumerate((tokens, cotangent)):
        for x in range(2):
            for y in range(8):
                for z in range(2):
                    rows = ref[x, y, z * ROWS : (z + 1) * ROWS, :]
                    to_first[y * 2 + z, kind, x] = rows
                    to_second[x * 2 + z, kind, y] = rows


def third_kernel(
    tokens, cotangent, attn, gain, w_qkv, w_out, normed_out, qkv_out, out_out, gain_out, proj, grads
):
    cot = cotangent[...]
    grad_normed, part_qkv, part_gain = axis_grads(
        tokens[...], cot, gain[...], w_qkv[...], w_out[...], proj, grads, False
    )
    normed_out[...] = grad_normed
    qkv_out[...] = part_qkv
    gain_out[...] = part_gain
    out_out[...] = dot(attn[...], cot, 0, 0)


def second_kernel(
    pieces, gain, w_qkv, w_out, qkv_in, gain_in, back, qkv_out, gain_out, proj, grads
):
    tokens = pieces[:, 0].reshape(TOKENS, WIDTH)
    cot = pieces[:, 1].reshape(TOKENS, WIDTH)
    grad_normed, part_qkv, part_gain = axis_grads(
        tokens, cot, gain[...], w_qkv[...], w_out[...], proj, grads, True
    )
    back[...] = grad_normed.astype(BF16).reshape(back.shape)
    qkv_out[...] = qkv_in[...] + part_qkv
    gain_out[...] = gain_in[...] + part_gain


def first_kernel(
    core,
    pieces,
    gain,
    w_qkv,
    w_out,
    qkv_in,
    out_in,
    gain_in,
    back,
    own,
    other,
    proj,
    grads,
    halves,
):
    tokens = pieces[:, 0].reshape(TOKENS, WIDTH)
    cot = pieces[:, 1].reshape(TOKENS, WIDTH)
    grad_normed, part_qkv, part_gain = axis_grads(
        tokens, cot, gain[...], w_qkv[...], w_out[...], proj, grads, True
    )
    back[...] = grad_normed.astype(BF16).reshape(back.shape)
    total = qkv_in[...] + part_qkv
    for at in range(2 * TILES):
        half, tile = divmod(at, TILES)
        if at < 96:
            row, col = divmod(at, 6)
            halves[half, tile] = total[row * 16 : row * 16 + 16, col * LANES : (col + 1) * LANES]
        else:
            row, col = divmod(at - 96, 2)
            halves[half, tile] = out_in[row * 16 : row * 16 + 16, col * LANES : (col + 1) * LANES]
    mine = core[0]
    own[0:TILES] = halves[mine]
    other[0:TILES] = halves[1 - mine]
    part_gain = gain_in[...] + part_gain
    gains = jnp.concatenate(
        [part_gain[:, :LANES], part_gain[:, LANES:], jnp.zeros((14, LANES), F32)], axis=0
    )
    own[TILES] = gains
    other[TILES] = gains


def pair_kernel(own, received, pieces):
    for peer in range(16):
        tiles = slice(peer * 4, peer * 4 + 4)
        pieces[peer, 0:4] = (own[tiles] + received[tiles]).astype(BF16)
    gains = (own[TILES] + received[TILES]).astype(BF16)
    for peer in range(16):
        pieces[peer, 4] = gains


def plane_kernel(received, pieces):
    total = jnp.sum(received[...].astype(F32), axis=0).astype(BF16)
    for peer in range(8):
        pieces[peer] = total


def line_kernel(scale, received, pieces, gain_out):
    total = jnp.sum(received[...].astype(F32), axis=0) * scale
    low = total[0:4].astype(BF16)
    for peer in range(16):
        pieces[peer] = low
    gain_out[...] = jnp.concatenate([total[4, 0:1], total[4, 1:2]], axis=1)


def assemble_kernel(core, mine, theirs, w_qkv_out, w_out_out, halves):
    at_core = core[0]
    halves[at_core] = mine[...]
    halves[1 - at_core] = theirs[...]
    for at in range(2 * TILES):
        half, tile = divmod(at, TILES)
        rows = halves[half, tile].astype(F32)
        if at < 96:
            row, col = divmod(at, 6)
            w_qkv_out[row * 16 : row * 16 + 16, col * LANES : (col + 1) * LANES] = rows
        else:
            row, col = divmod(at - 96, 2)
            w_out_out[row * 16 : row * 16 + 16, col * LANES : (col + 1) * LANES] = rows


def tokens_kernel(tokens, gain, third, from_first, from_second, out):
    for x in range(2):
        for y in range(8):
            tokens_f = tokens[x, y].astype(F32)
            first = jnp.concatenate([from_first[y * 2, x], from_first[y * 2 + 1, x]], axis=0)
            second = jnp.concatenate([from_second[x * 2, y], from_second[x * 2 + 1, y]], axis=0)
            grad_normed = third[x, y] + first.astype(F32) + second.astype(F32)
            square = jnp.mean(tokens_f * tokens_f, axis=-1, keepdims=True) + EPSILON
            root = jnp.sqrt(square)
            gained = gain[...] * grad_normed
            inner = jnp.sum(gained * tokens_f, axis=-1, keepdims=True)
            result = gained / root - tokens_f * (inner / (WIDTH * root * square))
            out[x, y] = result.astype(BF16)


def shape(dims, dtype):
    return jax.ShapeDtypeStruct(dims, dtype)


def kernel_call(body, outs, operands, us, scratch=(), scalars=0):
    return pl.pallas_call(
        body,
        out_shape=outs,
        in_specs=[SMEM] * scalars + [VMEM] * (len(operands) - scalars),
        out_specs=jax.tree.map(lambda _: VMEM, outs),
        scratch_shapes=list(scratch),
        compiler_params=params(),
        cost_estimate=cost(us),
    )(*operands)


def exchange(pieces, axes):
    return lax.all_to_all(pieces, axes, split_axis=0, concat_axis=0, tiled=True)


def on_device(count, tokens, attn, cotangent, gain, w_qkv, w_out):
    core = lax.axis_index("c").astype(jnp.int32).reshape(1)
    gain_row = gain.reshape(1, WIDTH)
    local = tokens[0]
    upstream = cotangent[0]
    to_first, to_second = kernel_call(
        prepare_kernel,
        (shape((16, 2, 2, ROWS, WIDTH), BF16), shape((4, 2, 8, ROWS, WIDTH), BF16)),
        (local, upstream),
        2,
    )
    at_first = exchange(to_first, FIRST)
    at_second = exchange(to_second, SECOND)
    flat = (TOKENS, WIDTH)
    third, part_qkv, part_out, part_gain = kernel_call(
        third_kernel,
        (
            shape(flat, F32),
            shape((WIDTH, TRIPLE), F32),
            shape((WIDTH, WIDTH), F32),
            shape((1, WIDTH), F32),
        ),
        (local.reshape(flat), upstream.reshape(flat), attn.reshape(flat), gain_row, w_qkv, w_out),
        7,
        SCRATCH,
    )
    back_second, part_qkv, part_gain = kernel_call(
        second_kernel,
        (
            shape((4, 8, ROWS, WIDTH), BF16),
            shape((WIDTH, TRIPLE), F32),
            shape((1, WIDTH), F32),
        ),
        (at_second, gain_row, w_qkv, w_out, part_qkv, part_gain),
        7,
        SCRATCH,
    )
    from_second = exchange(back_second, SECOND)
    tile = (16, LANES)
    back_first, own, other = kernel_call(
        first_kernel,
        (
            shape((16, 2, ROWS, WIDTH), BF16),
            shape((TILES + 1, *tile), F32),
            shape((TILES + 1, *tile), F32),
        ),
        (core, at_first, gain_row, w_qkv, w_out, part_qkv, part_out, part_gain),
        7,
        SCRATCH + [pltpu.VMEM((2, TILES, *tile), F32)],
        1,
    )
    swap = [(0, 1), (1, 0)]
    received = lax.ppermute(other, "c", swap)
    pieces = kernel_call(pair_kernel, shape((16, 5, *tile), BF16), (own, received), 1)
    summed = exchange(pieces, PLANE)
    from_first = exchange(back_first, FIRST)
    pieces = kernel_call(plane_kernel, shape((8, 5, *tile), BF16), (summed,), 1)
    summed = exchange(pieces, "z")
    pieces, d_gain = kernel_call(
        functools.partial(line_kernel, 1.0 / math.sqrt(count)),
        (shape((16, 4, *tile), BF16), shape((1, WIDTH), F32)),
        (summed,),
        1,
    )
    mine = exchange(pieces, PLANE).reshape(TILES, *tile)
    theirs = lax.ppermute(mine, "c", swap)
    d_w_qkv, d_w_out = kernel_call(
        assemble_kernel,
        (shape((WIDTH, TRIPLE), F32), shape((WIDTH, WIDTH), F32)),
        (core, mine, theirs),
        1,
        [pltpu.VMEM((2, TILES, *tile), BF16)],
        1,
    )
    d_tokens = kernel_call(
        tokens_kernel,
        shape(local.shape, BF16),
        (local, gain_row, third.reshape(local.shape), from_first, from_second),
        2,
    )
    return (d_tokens[None], d_w_qkv, d_w_out, d_gain.reshape(WIDTH))


def solution(mesh):
    fine = Mesh(mesh.devices.reshape(4, 8, 2, 2, 2), ("y", "z", "xh", "xl", "c"))
    split = P("y", FIRST, SECOND, None, None)
    count = 4 * 32 * 32 * 32
    return jax.shard_map(
        functools.partial(on_device, count),
        mesh=fine,
        in_specs=(split, split, split, P(), P(), P()),
        out_specs=(split, P(), P(), P()),
        check_vma=False,
    )
```

time: 451 us -> 122 us (0.27); the launches traced: 443 us -> 120 us
  waiting for transfers between devices: 178 us -> 26.4 us
  local copies, waits for them, and re-layouts: 66.1 us -> 4.55 us
  matrix products: 51.3 us -> 0 us
  blocking collectives: 77.2 us -> 35.5 us
  Pallas kernels: 0 us -> 22.4 us
  starting transfers between devices: 46.6 us -> 30.6 us
  between operations: 14.8 us -> 0.73 us
  other arithmetic: 8.83 us -> 0 us
    psum x1 -> x0, waiting for transfers between devices: 173 us -> none  [on_device(): lax.psum((part_qkv, part_out, part_gain), ('dp', 'gx', 'gy'))]
    psum x1 -> x0, blocking collectives: 77.2 us -> none  [on_device(): lax.psum((part_qkv, part_out, part_gain), ('dp', 'gx', 'gy'))]
    dot_general x20 -> x0, matrix products: 39.1 us -> none  [the longest x3 9.71 us: pencil_grads(): jnp.einsum('blhd,bmhd->bhlm', grad_h, values_h, preferred_element_type=jn...]
    all_to_all x0 -> x3, blocking collectives: none -> 35.5 us  [exchange(): return lax.all_to_all(pieces, axes, split_axis=0, concat_axis=0, tiled=True)]
    pallas_call x0 -> x9, Pallas kernels: none -> 22.4 us  [kernel_call(): pl.pallas_call(body, out_shape=outs, in_specs=[SMEM] * scalars + [VMEM] *...]
    all_to_all x6 -> x4, starting transfers between devices: 46.4 us -> 25.8 us  [exchange(): return lax.all_to_all(pieces, axes, split_axis=0, concat_axis=0, tiled=True)]
    all_to_all x6 -> x4, waiting for transfers between devices: 5.02 us -> 24.9 us  [exchange(): return lax.all_to_all(pieces, axes, split_axis=0, concat_axis=0, tiled=True)]
    concatenate x12 -> x0, local copies, waits for them, and re-layouts: 19.5 us -> none  [pencil_grads(): jnp.concatenate([grad_query.reshape(batch, length, width), grad_keys.resh...]
  transfers between devices with their start and end apart: 7 -> 6, of which waited for: 4 -> 5; matrix products, arithmetic and copies ran while one was open for 25% -> 0% of each run, Pallas kernels for 0% -> 11%
where the time goes in v1:
time: 122 us; the launch traced here: 120 us
  blocking collectives  35.5 us (29%)
  starting transfers between devices  30.6 us (25%)
  waiting for transfers between devices  26.4 us (22%)
  Pallas kernels  22.4 us (18%)
  local copies, waits for them, and re-layouts  4.55 us (4%)
    all_to_all x3, blocking collectives, exchange(): return lax.all_to_all(pieces, axes, split_axis=0, concat_axis=0, tiled=True)  35.5 us
    all_to_all x4, starting transfers between devices, exchange(): return lax.all_to_all(pieces, axes, split_axis=0, concat_axis=0, tiled=True)  25.8 us
    all_to_all x4, waiting for transfers between devices, exchange(): return lax.all_to_all(pieces, axes, split_axis=0, concat_axis=0, tiled=True)  24.9 us
    pallas_call x9, Pallas kernels, kernel_call(): pl.pallas_call(body, out_shape=outs, in_specs=[SMEM] * scalars + [VMEM] *...  22.4 us
    unnamed x20, local copies, waits for them, and re-layouts  4.55 us
    ppermute x1, starting transfers between devices, on_device(): received = lax.ppermute(other, 'c', swap)  2.45 us
  transfers between devices with their start and end apart: 6, of which 5 were waited for; matrix products, arithmetic and copies ran while one was open for 0% of the time, Pallas kernels for 11%

profile of v1, /device:TPU:1, one launch (start us, length us, event | category | flops | bytes accessed | tf_op | source)
XLA Modules:
  0.0 120.2 jit_solution(3041792947603065628)
XLA Ops:
  0.6 0.0 copy-start.1
  0.6 0.9 copy-done.1
  1.6 0.0 copy-start.4
  1.6 0.9 copy-done.4
  2.5 1.0 shard_map.94
  3.6 0.0 copy-start.5
  3.6 6.8 %all-to-all-start.1 = ((bf16[4,2,8,16,256]{4,3,2,1,0:T(8,128)(2,1)}), bf16[4,2,8,16,256]{4,3,2,1,0:T(8,128)(2,1)S(1)}, u32[]{:S(2)}, u32[]{:S(2)}) async-start(bf16[4,2,8,16,256]{4,3,2,1,0:T(8,128)(2,1)} %get-tuple-element.22), calls=%async_computation.1 | async-start | bytes 1048576 | tf_op jit(solution)/shard_map/all_to_all | solution.py:275
  10.4 8.0 %all-to-all-done.1.pieces = bf16[4,2,8,16,256]{4,3,2,1,0:T(8,128)(2,1)S(1)} async-done(((bf16[4,2,8,16,256]{4,3,2,1,0:T(8,128)(2,1)}), bf16[4,2,8,16,256]{4,3,2,1,0:T(8,128)(2,1)S(1)}, u32[]{:S(2)}, u32[]{:S(2)}) %all-to-all-start.1) | async-done | bytes 524320 | tf_op jit(solution)/shard_map/all_to_all | solution.py:275
  18.4 0.0 copy-start
  18.4 0.0 copy-start.2
  18.4 0.0 copy-start.3
  18.4 0.0 copy-start.6
  18.4 9.2 %all-to-all-start = ((bf16[16,2,2,16,256]{4,3,2,1,0:T(8,128)(2,1)}), bf16[16,2,2,16,256]{4,3,2,1,0:T(8,128)(2,1)S(1)}, u32[]{:S(2)}, u32[]{:S(2)}) async-start(bf16[16,2,2,16,256]{4,3,2,1,0:T(8,128)(2,1)} %get-tuple-element.21), calls=%async_computation | async-start | bytes 1048576 | tf_op jit(solution)/shard_map/all_to_all | solution.py:275
  27.5 0.0 copy-start.7
  27.5 0.0 copy-done.5
  27.6 0.0 copy-done
  27.6 0.0 copy-done.2
  27.6 0.0 copy-done.3
  27.6 0.0 copy-done.6
  27.6 0.6 copy-done.7
  28.2 5.6 %shard_map.93 = (f32[512,256]{1,0:T(8,128)S(1)}, f32[256,768]{1,0:T(8,128)S(1)}, f32[256,256]{1,0:T(8,128)S(1)}, f32[1,256]{1,0:T(1,128)S(1)}) custom-call(bf16[512,256]{1,0:T(8,128)(2,1)S(1)} %bitcast.17, bf16[512,256]{1,0:T(8,128)(2,1)S(1)} %bitcast.14, bf16[512,256]{1,0:T(8,128)(2,1)S(1)} %bitcast.15, f32[1,256]{1,0:T(1,128)S(1)} %bitcast.19, ...), custom_call_target="tpu_custom_call" | custom-call | flops 5600000000 | bytes 14000000 | tf_op jit(solution)/shard_map/pallas_call | solution.py:263
  33.8 6.5 %shard_map.95 = (bf16[4,8,16,256]{3,2,1,0:T(8,128)(2,1)}, f32[256,768]{1,0:T(8,128)S(1)}, f32[1,256]{1,0:T(1,128)S(1)}) custom-call(bf16[4,2,8,16,256]{4,3,2,1,0:T(8,128)(2,1)S(1)} %all-to-all-done.1.pieces, f32[1,256]{1,0:T(1,128)S(1)} %bitcast.20, bf16[256,768]{1,0:T(8,128)(2,1)S(1)} %copy-done, bf16[256,256]{1,0:T(8,128)(2,1)S(1)} %copy-done.6, ...), custom_call_target="tpu_custom_call" | custom-call | flops 5600000000 | bytes 14000000 | tf_op jit(solution)/shard_map/pallas_call | solution.py:263
  40.3 0.0 copy-start.8
  40.3 0.9 copy-done.8
  41.1 3.6 %all-to-all-done.pieces = bf16[16,2,2,16,256]{4,3,2,1,0:T(8,128)(2,1)S(1)} async-done(((bf16[16,2,2,16,256]{4,3,2,1,0:T(8,128)(2,1)}), bf16[16,2,2,16,256]{4,3,2,1,0:T(8,128)(2,1)S(1)}, u32[]{:S(2)}, u32[]{:S(2)}) %all-to-all-start) | async-done | bytes 524320 | tf_op jit(solution)/shard_map/all_to_all | solution.py:275
  44.7 0.0 copy-start.9
  44.7 1.1 copy-done.9
  45.9 6.5 %shard_map.96 = (bf16[16,2,16,256]{3,2,1,0:T(8,128)(2,1)}, f32[65,16,128]{2,1,0:T(8,128)S(1)}, f32[65,16,128]{2,1,0:T(8,128)S(1)}) custom-call(s32[1]{0:T(128)} %bitcast.6.core, bf16[16,2,2,16,256]{4,3,2,1,0:T(8,128)(2,1)S(1)} %all-to-all-done.pieces, f32[1,256]{1,0:T(1,128)S(1)} %bitcast.21, bf16[256,768]{1,0:T(8,128)(2,1)S(1)} %copy-done, ...), custom_call_target="tpu_custom_call" | custom-call | flops 5600000000 | bytes 14000000 | tf_op jit(solution)/shard_map/pallas_call | solution.py:263
  52.3 2.5 %collective-permute-start = (f32[65,16,128]{2,1,0:T(8,128)S(1)}, f32[65,16,128]{2,1,0:T(8,128)S(1)}, u32[]{:S(2)}, u32[]{:S(2)}) collective-permute-start(f32[65,16,128]{2,1,0:T(8,128)S(1)} %get-tuple-element.31), channel_id=1, source_target_pairs={{0,1},{1,0},{2,3},{3,2},{4,5},{5,4},{6,7},{7,6},{8,9},{9,8},{10,11... | collective-permute-start | bytes 1597448 | tf_op jit(solution)/shard_map/ppermute | solution.py:330
  54.8 1.5 %collective-permute-done.received = f32[65,16,128]{2,1,0:T(8,128)S(1)} collective-permute-done((f32[65,16,128]{2,1,0:T(8,128)S(1)}, f32[65,16,128]{2,1,0:T(8,128)S(1)}, u32[]{:S(2)}, u32[]{:S(2)}) %collective-permute-start) | collective-permute-done | bytes 532512 | tf_op jit(solution)/shard_map/ppermute | solution.py:330
  56.3 0.1 shard_map.98
  56.4 12.9 %all_to_all.35.received = bf16[16,5,16,128]{3,2,1,0:T(8,128)(2,1)S(1)} all-to-all(bf16[16,5,16,128]{3,2,1,0:T(8,128)(2,1)S(1)} %shard_map.98), channel_id=1, replica_groups=mesh['y'=4,'z'=8,'xh'=2,'xl'=2,'c'=2] {'y','xh','xl'}, dimensions={0} | all-to-all | bytes 655360 | tf_op jit(solution)/shard_map/all_to_all | solution.py:275
  69.3 0.1 shard_map.99
  69.4 12.5 %all_to_all.36.received = bf16[8,5,16,128]{3,2,1,0:T(8,128)(2,1)S(1)} all-to-all(bf16[8,5,16,128]{3,2,1,0:T(8,128)(2,1)S(1)} %shard_map.99), channel_id=1, replica_groups=mesh['y'=4,'z'=8,'xh'=2,'xl'=2,'c'=2] {'z'}, dimensions={0} | all-to-all | bytes 327680 | tf_op jit(solution)/shard_map/all_to_all | solution.py:275
  81.9 6.3 %all-to-all-start.3 = ((bf16[4,8,16,256]{3,2,1,0:T(8,128)(2,1)}), bf16[4,8,16,256]{3,2,1,0:T(8,128)(2,1)S(1)}, u32[]{:S(2)}, u32[]{:S(2)}) async-start(bf16[4,8,16,256]{3,2,1,0:T(8,128)(2,1)} %get-tuple-element.29), calls=%async_computation.3 | async-start | bytes 524288 | tf_op jit(solution)/shard_map/all_to_all | solution.py:275
  88.2 0.6 shard_map.100
  88.7 4.6 %all-to-all-done.3.from_second = bf16[4,8,16,256]{3,2,1,0:T(8,128)(2,1)S(1)} async-done(((bf16[4,8,16,256]{3,2,1,0:T(8,128)(2,1)}), bf16[4,8,16,256]{3,2,1,0:T(8,128)(2,1)S(1)}, u32[]{:S(2)}, u32[]{:S(2)}) %all-to-all-start.3) | async-done | bytes 262176 | tf_op jit(solution)/shard_map/all_to_all | solution.py:275
  93.3 10.2 %all_to_all.37 = bf16[16,4,16,128]{3,2,1,0:T(8,128)(2,1)S(1)} all-to-all(bf16[16,4,16,128]{3,2,1,0:T(8,128)(2,1)S(1)} %get-tuple-element.32), channel_id=1, replica_groups=mesh['y'=4,'z'=8,'xh'=2,'xl'=2,'c'=2] {'y','xh','xl'}, dimensions={0} | all-to-all | bytes 524288 | tf_op jit(solution)/shard_map/all_to_all | solution.py:275
  103.5 3.5 %all-to-all-start.2 = ((bf16[16,2,16,256]{3,2,1,0:T(8,128)(2,1)}), bf16[16,2,16,256]{3,2,1,0:T(8,128)(2,1)S(1)}, u32[]{:S(2)}, u32[]{:S(2)}) async-start(bf16[16,2,16,256]{3,2,1,0:T(8,128)(2,1)} %get-tuple-element.28), calls=%async_computation.2 | async-start | bytes 524288 | tf_op jit(solution)/shard_map/all_to_all | solution.py:275
  107.0 2.3 %collective-permute-start.1 = (bf16[64,16,128]{2,1,0:T(8,128)(2,1)S(1)}, bf16[64,16,128]{2,1,0:T(8,128)(2,1)S(1)}, u32[]{:S(2)}, u32[]{:S(2)}) collective-permute-start(bf16[64,16,128]{2,1,0:T(8,128)(2,1)S(1)} %bitcast.11), channel_id=1, source_target_pairs={{0,1},{1,0},{2,3},{3,2},{4,5},{5,4},{6,7},{7,6},{8,9},{9,8},{10,11... | collective-permute-start | bytes 786440 | tf_op jit(solution)/shard_map/ppermute | solution.py:343
  109.4 8.7 %all-to-all-done.2.from_first = bf16[16,2,16,256]{3,2,1,0:T(8,128)(2,1)S(1)} async-done(((bf16[16,2,16,256]{3,2,1,0:T(8,128)(2,1)}), bf16[16,2,16,256]{3,2,1,0:T(8,128)(2,1)S(1)}, u32[]{:S(2)}, u32[]{:S(2)}) %all-to-all-start.2) | async-done | bytes 262176 | tf_op jit(solution)/shard_map/all_to_all | solution.py:275
  118.1 1.1 shard_map.97
  119.1 0.0 collective-permute-done.1.theirs
  119.1 1.0 shard_map.101
Async XLA Ops:
  0.6 1.0 copy-start.1
  1.6 0.9 copy-start.4
  3.6 24.0 %copy-start.5 = (bf16[1,2,8,32,256]{4,3,2,1,0:T(8,128)(2,1)S(1)}, bf16[1,2,8,32,256]{4,3,2,1,0:T(8,128)(2,1)}, u32[]{:S(2)}) copy-start(bf16[1,2,8,32,256]{4,3,2,1,0:T(8,128)(2,1)} %param.6) | copy-start | bytes 786436
  3.6 14.8 %all-to-all-start.1 = ((bf16[4,2,8,16,256]{4,3,2,1,0:T(8,128)(2,1)}), bf16[4,2,8,16,256]{4,3,2,1,0:T(8,128)(2,1)S(1)}, u32[]{:S(2)}, u32[]{:S(2)}) async-start(bf16[4,2,8,16,256]{4,3,2,1,0:T(8,128)(2,1)} %get-tuple-element.22), calls=%async_computation.1 | async-start | bytes 1048576 | tf_op jit(solution)/shard_map/all_to_all | solution.py:275
  18.4 9.2 %copy-start = (bf16[256,768]{1,0:T(8,128)(2,1)S(1)}, bf16[256,768]{1,0:T(8,128)(2,1)}, u32[]{:S(2)}) copy-start(bf16[256,768]{1,0:T(8,128)(2,1)} %w_qkv.5) | copy-start | bytes 1179652
  18.4 9.2 %copy-start.2 = (bf16[1,2,8,32,256]{4,3,2,1,0:T(8,128)(2,1)S(1)}, bf16[1,2,8,32,256]{4,3,2,1,0:T(8,128)(2,1)}, u32[]{:S(2)}) copy-start(bf16[1,2,8,32,256]{4,3,2,1,0:T(8,128)(2,1)} %param.8) | copy-start | bytes 786436
  18.4 9.2 %copy-start.3 = (bf16[1,2,8,32,256]{4,3,2,1,0:T(8,128)(2,1)S(1)}, bf16[1,2,8,32,256]{4,3,2,1,0:T(8,128)(2,1)}, u32[]{:S(2)}) copy-start(bf16[1,2,8,32,256]{4,3,2,1,0:T(8,128)(2,1)} %param.7) | copy-start | bytes 786436
  18.4 9.2 %copy-start.6 = (bf16[256,256]{1,0:T(8,128)(2,1)S(1)}, bf16[256,256]{1,0:T(8,128)(2,1)}, u32[]{:S(2)}) copy-start(bf16[256,256]{1,0:T(8,128)(2,1)} %w_out.5) | copy-start | bytes 393220
  18.4 26.4 %all-to-all-start = ((bf16[16,2,2,16,256]{4,3,2,1,0:T(8,128)(2,1)}), bf16[16,2,2,16,256]{4,3,2,1,0:T(8,128)(2,1)S(1)}, u32[]{:S(2)}, u32[]{:S(2)}) async-start(bf16[16,2,2,16,256]{4,3,2,1,0:T(8,128)(2,1)} %get-tuple-element.21), calls=%async_computation | async-start | bytes 1048576 | tf_op jit(solution)/shard_map/all_to_all | solution.py:275
  27.5 0.7 copy-start.7
  40.3 0.9 copy-start.8
  44.7 1.1 copy-start.9
  52.3 4.0 %collective-permute-start = (f32[65,16,128]{2,1,0:T(8,128)S(1)}, f32[65,16,128]{2,1,0:T(8,128)S(1)}, u32[]{:S(2)}, u32[]{:S(2)}) collective-permute-start(f32[65,16,128]{2,1,0:T(8,128)S(1)} %get-tuple-element.31), channel_id=1, source_target_pairs={{0,1},{1,0},{2,3},{3,2},{4,5},{5,4},{6,7},{7,6},{8,9},{9,8},{10,11... | collective-permute-start | bytes 1597448 | tf_op jit(solution)/shard_map/ppermute | solution.py:330
  81.9 11.5 %all-to-all-start.3 = ((bf16[4,8,16,256]{3,2,1,0:T(8,128)(2,1)}), bf16[4,8,16,256]{3,2,1,0:T(8,128)(2,1)S(1)}, u32[]{:S(2)}, u32[]{:S(2)}) async-start(bf16[4,8,16,256]{3,2,1,0:T(8,128)(2,1)} %get-tuple-element.29), calls=%async_computation.3 | async-start | bytes 524288 | tf_op jit(solution)/shard_map/all_to_all | solution.py:275
  103.5 14.6 %all-to-all-start.2 = ((bf16[16,2,16,256]{3,2,1,0:T(8,128)(2,1)}), bf16[16,2,16,256]{3,2,1,0:T(8,128)(2,1)S(1)}, u32[]{:S(2)}, u32[]{:S(2)}) async-start(bf16[16,2,16,256]{3,2,1,0:T(8,128)(2,1)} %get-tuple-element.28), calls=%async_computation.2 | async-start | bytes 524288 | tf_op jit(solution)/shard_map/all_to_all | solution.py:275
  107.0 12.1 %collective-permute-start.1 = (bf16[64,16,128]{2,1,0:T(8,128)(2,1)S(1)}, bf16[64,16,128]{2,1,0:T(8,128)(2,1)S(1)}, u32[]{:S(2)}, u32[]{:S(2)}) collective-permute-start(bf16[64,16,128]{2,1,0:T(8,128)(2,1)S(1)} %bitcast.11), channel_id=1, source_target_pairs={{0,1},{1,0},{2,3},{3,2},{4,5},{5,4},{6,7},{7,6},{8,9},{9,8},{10,11... | collective-permute-start | bytes 786440 | tf_op jit(solution)/shard_map/ppermute | solution.py:343

commit v2 on v1

--- a/solution.py
+++ b/solution.py
@@ -24,6 +24,7 @@
 BF16 = jnp.bfloat16
 F32 = jnp.float32
 VMEM = pl.BlockSpec(memory_space=pltpu.VMEM)
+ANY = pl.BlockSpec(memory_space=pl.ANY)
 SMEM = pl.BlockSpec(memory_space=pltpu.SMEM)
 PLANE = ("y", "xh", "xl")
 FIRST = ("z", "xh")
@@ -118,20 +119,66 @@
     return grad_normed, part_qkv, part_gain
 
 
+BITS = (2, 8, 1, 4)
+SWAPS = (("z", 1, 8), ("z", 4, 8), ("xh", 1, 2), ("z", 2, 8))
+
+
+def sources_before(stage):
+    masks = [0]
+    for bit in BITS[:stage]:
+        masks += [mask ^ bit for mask in masks]
+    return masks
+
+
+def span_masks(count):
+    masks = [0]
+    for bit in reversed(BITS[4 - count :]):
+        masks += [mask ^ bit for mask in masks]
+    return masks
+
+
+SPANS = [span_masks(count) for count in range(4)]
+
 SCRATCH = [
     pltpu.VMEM((8, TOKENS, LANES), F32),
     pltpu.VMEM((6, TOKENS, LANES), F32),
 ]
 
 
-def prepare_kernel(tokens, cotangent, to_first, to_second):
+def first_pieces_kernel(tokens, cotangent, pieces, sem):
+    copies = []
     for kind, ref in enumerate((tokens, cotangent)):
         for x in range(2):
-            for y in range(8):
-                for z in range(2):
-                    rows = ref[x, y, z * ROWS : (z + 1) * ROWS, :]
-                    to_first[y * 2 + z, kind, x] = rows
-                    to_second[x * 2 + z, kind, y] = rows
+            for z in range(2):
+                copies.append(
+                    pltpu.make_async_copy(
+                        ref.at[x, :, pl.ds(z * ROWS, ROWS), :],
+                        pieces.at[:, z, kind, x],
+                        sem.at[len(copies)],
+                    )
+                )
+    for copy in copies:
+        copy.start()
+    for copy in copies:
+        copy.wait()
+
+
+def second_pieces_kernel(place, tokens, cotangent, *rest):
+    pieces, sem = rest[:4], rest[4]
+    copies = []
+    for mask, out in enumerate(pieces):
+        peer = place[1] ^ mask
+        rows = pl.ds(pl.multiple_of((peer & 1) * ROWS, ROWS), ROWS)
+        for kind, ref in enumerate((tokens, cotangent)):
+            copies.append(
+                pltpu.make_async_copy(
+                    ref.at[peer >> 1, :, rows, :], out.at[kind], sem.at[len(copies)]
+                )
+            )
+    for copy in copies:
+        copy.start()
+    for copy in copies:
+        copy.wait()
 
 
 def third_kernel(
@@ -147,21 +194,24 @@
     out_out[...] = dot(attn[...], cot, 0, 0)
 
 
-def second_kernel(
-    pieces, gain, w_qkv, w_out, qkv_in, gain_in, back, qkv_out, gain_out, proj, grads
-):
-    tokens = pieces[:, 0].reshape(TOKENS, WIDTH)
-    cot = pieces[:, 1].reshape(TOKENS, WIDTH)
+def second_kernel(*refs):
+    pieces, (gain, w_qkv, w_out, qkv_in, gain_in) = refs[:4], refs[4:9]
+    back, (qkv_out, gain_out, proj, grads) = refs[9:13], refs[13:]
+    tokens = jnp.concatenate([piece[0].reshape(-1, WIDTH) for piece in pieces], axis=0)
+    cot = jnp.concatenate([piece[1].reshape(-1, WIDTH) for piece in pieces], axis=0)
     grad_normed, part_qkv, part_gain = axis_grads(
         tokens, cot, gain[...], w_qkv[...], w_out[...], proj, grads, True
     )
-    back[...] = grad_normed.astype(BF16).reshape(back.shape)
+    returned = grad_normed.astype(BF16)
+    rows = TOKENS // 4
+    for mask, out in enumerate(back):
+        out[...] = returned[mask * rows : (mask + 1) * rows].reshape(out.shape)
     qkv_out[...] = qkv_in[...] + part_qkv
     gain_out[...] = gain_in[...] + part_gain
 
 
 def first_kernel(
-    core,
+    place,
     pieces,
     gain,
     w_qkv,
@@ -169,19 +219,25 @@
     qkv_in,
     out_in,
     gain_in,
-    back,
+    stay,
+    leave,
     own,
     other,
     proj,
     grads,
     halves,
+    returned,
 ):
     tokens = pieces[:, 0].reshape(TOKENS, WIDTH)
     cot = pieces[:, 1].reshape(TOKENS, WIDTH)
     grad_normed, part_qkv, part_gain = axis_grads(
         tokens, cot, gain[...], w_qkv[...], w_out[...], proj, grads, True
     )
-    back[...] = grad_normed.astype(BF16).reshape(back.shape)
+    returned[...] = grad_normed.astype(BF16).reshape(returned.shape)
+    here = place[2]
+    for at, mask in enumerate(SPANS[3]):
+        stay[at] = returned[here ^ mask]
+        leave[at] = returned[here ^ mask ^ BITS[0]]
     total = qkv_in[...] + part_qkv
     for at in range(2 * TILES):
         half, tile = divmod(at, TILES)
@@ -191,7 +247,7 @@
         else:
             row, col = divmod(at - 96, 2)
             halves[half, tile] = out_in[row * 16 : row * 16 + 16, col * LANES : (col + 1) * LANES]
-    mine = core[0]
+    mine = place[0]
     own[0:TILES] = halves[mine]
     other[0:TILES] = halves[1 - mine]
     part_gain = gain_in[...] + part_gain
@@ -200,6 +256,18 @@
     )
     own[TILES] = gains
     other[TILES] = gains
+
+
+def stage_kernel(*refs):
+    groups, out = refs[:-1], refs[-1]
+    left = 16 >> (len(groups) - 1)
+    at = 0
+    for order, ref in enumerate(groups):
+        span = 8 >> max(order - 1, 0)
+        for base in range(0, 8, span):
+            for block in range(left // 2, left):
+                out[at] = ref[base + block]
+                at += 1
 
 
 def pair_kernel(own, received, pieces):
@@ -225,8 +293,8 @@
     gain_out[...] = jnp.concatenate([total[4, 0:1], total[4, 1:2]], axis=1)
 
 
-def assemble_kernel(core, mine, theirs, w_qkv_out, w_out_out, halves):
-    at_core = core[0]
+def assemble_kernel(place, mine, theirs, w_qkv_out, w_out_out, halves):
+    at_core = place[0]
     halves[at_core] = mine[...]
     halves[1 - at_core] = theirs[...]
     for at in range(2 * TILES):
@@ -240,7 +308,17 @@
             w_out_out[row * 16 : row * 16 + 16, col * LANES : (col + 1) * LANES] = rows
 
 
-def tokens_kernel(tokens, gain, third, from_first, from_second, out):
+def tokens_kernel(place, tokens, gain, third, *rest):
+    groups, seconds = rest[:5], rest[5:9]
+    out, from_first, from_second = rest[9:]
+    here = place[2]
+    from_first[here] = groups[0][0]
+    for stage in range(4):
+        span = 8 >> stage
+        for at, mask in enumerate(sources_before(stage)):
+            from_first[here ^ (mask ^ BITS[stage])] = groups[stage + 1][at * span]
+    for mask, ref in enumerate(seconds):
+        from_second[place[1] ^ mask] = ref[...]
     for x in range(2):
         for y in range(8):
             tokens_f = tokens[x, y].astype(F32)
@@ -259,36 +337,55 @@
     return jax.ShapeDtypeStruct(dims, dtype)
 
 
-def kernel_call(body, outs, operands, us, scratch=(), scalars=0):
+def kernel_call(body, outs, operands, us, scratch=(), scalars=0, space=VMEM):
     return pl.pallas_call(
         body,
         out_shape=outs,
-        in_specs=[SMEM] * scalars + [VMEM] * (len(operands) - scalars),
-        out_specs=jax.tree.map(lambda _: VMEM, outs),
+        in_specs=[SMEM] * scalars + [space] * (len(operands) - scalars),
+        out_specs=jax.tree.map(lambda _: space, outs),
         scratch_shapes=list(scratch),
         compiler_params=params(),
         cost_estimate=cost(us),
     )(*operands)
 
 
+def swap(array, axis, mask, size):
+    return lax.ppermute(array, axis, [(i, i ^ mask) for i in range(size)])
+
+
 def exchange(pieces, axes):
     return lax.all_to_all(pieces, axes, split_axis=0, concat_axis=0, tiled=True)
 
 
 def on_device(count, tokens, attn, cotangent, gain, w_qkv, w_out):
-    core = lax.axis_index("c").astype(jnp.int32).reshape(1)
+    core = lax.axis_index("c")
+    along_second = lax.axis_index("xl") * 2 + core
+    along_first = lax.axis_index("z") * 2 + lax.axis_index("xh")
+    place = jnp.stack([core, along_second, along_first]).astype(jnp.int32)
     gain_row = gain.reshape(1, WIDTH)
     local = tokens[0]
     upstream = cotangent[0]
-    to_first, to_second = kernel_call(
-        prepare_kernel,
-        (shape((16, 2, 2, ROWS, WIDTH), BF16), shape((4, 2, 8, ROWS, WIDTH), BF16)),
+    flat = (TOKENS, WIDTH)
+    tile = (16, LANES)
+    to_first = kernel_call(
+        first_pieces_kernel,
+        shape((8, 2, 2, 2, ROWS, WIDTH), BF16),
         (local, upstream),
         2,
-    )
-    at_first = exchange(to_first, FIRST)
-    at_second = exchange(to_second, SECOND)
-    flat = (TOKENS, WIDTH)
+        [pltpu.SemaphoreType.DMA((8,))],
+        space=ANY,
+    )
+    at_first = exchange(to_first.reshape(16, 2, 2, ROWS, WIDTH), FIRST)
+    to_second = kernel_call(
+        second_pieces_kernel,
+        (shape((2, 8, ROWS, WIDTH), BF16),) * 4,
+        (place, local, upstream),
+        2,
+        [pltpu.SemaphoreType.DMA((8,))],
+        1,
+        ANY,
+    )
+    at_second = [to_second[0]] + [swap(to_second[m], SECOND, m, 4) for m in (1, 2, 3)]
     third, part_qkv, part_out, part_gain = kernel_call(
         third_kernel,
         (
@@ -301,36 +398,36 @@
         7,
         SCRATCH,
     )
-    back_second, part_qkv, part_gain = kernel_call(
+    *back, part_qkv, part_gain = kernel_call(
         second_kernel,
-        (
-            shape((4, 8, ROWS, WIDTH), BF16),
-            shape((WIDTH, TRIPLE), F32),
-            shape((1, WIDTH), F32),
-        ),
-        (at_second, gain_row, w_qkv, w_out, part_qkv, part_gain),
+        (shape((8, ROWS, WIDTH), BF16),) * 4
+        + (shape((WIDTH, TRIPLE), F32), shape((1, WIDTH), F32)),
+        (*at_second, gain_row, w_qkv, w_out, part_qkv, part_gain),
         7,
         SCRATCH,
     )
-    from_second = exchange(back_second, SECOND)
-    tile = (16, LANES)
-    back_first, own, other = kernel_call(
+    from_second = [back[0]] + [swap(back[m], SECOND, m, 4) for m in (1, 2, 3)]
+    block = (2, ROWS, WIDTH)
+    stay, leave, own, other = kernel_call(
         first_kernel,
         (
-            shape((16, 2, ROWS, WIDTH), BF16),
+            shape((8, *block), BF16),
+            shape((8, *block), BF16),
             shape((TILES + 1, *tile), F32),
             shape((TILES + 1, *tile), F32),
         ),
-        (core, at_first, gain_row, w_qkv, w_out, part_qkv, part_out, part_gain),
+        (place, at_first, gain_row, w_qkv, w_out, part_qkv, part_out, part_gain),
         7,
-        SCRATCH + [pltpu.VMEM((2, TILES, *tile), F32)],
-        1,
-    )
-    swap = [(0, 1), (1, 0)]
-    received = lax.ppermute(other, "c", swap)
+        SCRATCH + [pltpu.VMEM((2, TILES, *tile), F32), pltpu.VMEM((16, *block), BF16)],
+        1,
+    )
+    received = swap(other, "c", 1, 2)
+    groups = [stay, swap(leave, *SWAPS[0])]
     pieces = kernel_call(pair_kernel, shape((16, 5, *tile), BF16), (own, received), 1)
     summed = exchange(pieces, PLANE)
-    from_first = exchange(back_first, FIRST)
+    for stage in (1, 2, 3):
+        leave = kernel_call(stage_kernel, shape((8, *block), BF16), groups, 1)
+        groups.append(swap(leave, *SWAPS[stage]))
     pieces = kernel_call(plane_kernel, shape((8, 5, *tile), BF16), (summed,), 1)
     summed = exchange(pieces, "z")
     pieces, d_gain = kernel_call(
@@ -340,11 +437,11 @@
         1,
     )
     mine = exchange(pieces, PLANE).reshape(TILES, *tile)
-    theirs = lax.ppermute(mine, "c", swap)
+    theirs = swap(mine, "c", 1, 2)
     d_w_qkv, d_w_out = kernel_call(
         assemble_kernel,
         (shape((WIDTH, TRIPLE), F32), shape((WIDTH, WIDTH), F32)),
-        (core, mine, theirs),
+        (place, mine, theirs),
         1,
         [pltpu.VMEM((2, TILES, *tile), BF16)],
         1,
@@ -352,8 +449,10 @@
     d_tokens = kernel_call(
         tokens_kernel,
         shape(local.shape, BF16),
-        (local, gain_row, third.reshape(local.shape), from_first, from_second),
+        (place, local, gain_row, third.reshape(local.shape), *groups, *from_second),
         2,
+        [pltpu.VMEM((16, *block), BF16), pltpu.VMEM((4, 8, ROWS, WIDTH), BF16)],
+        1,
     )
     return (d_tokens[None], d_w_qkv, d_w_out, d_gain.reshape(WIDTH))
 

time: 122 us -> 104 us (0.85); the launches traced: 120 us -> 104 us
  blocking collectives: 35.5 us -> 16.1 us
  starting transfers between devices: 30.6 us -> 40 us
  waiting for transfers between devices: 26.4 us -> 20.1 us
  local copies, waits for them, and re-layouts: 4.55 us -> 2.59 us
  Pallas kernels: 22.4 us -> 24.2 us
    all_to_all x4 -> x3, waiting for transfers between devices: 24.9 us -> 0.16 us  [exchange(): return lax.all_to_all(pieces, axes, split_axis=0, concat_axis=0, tiled=True)]
    all_to_all x3 -> x1, blocking collectives: 35.5 us -> 16.1 us  [exchange(): return lax.all_to_all(pieces, axes, split_axis=0, concat_axis=0, tiled=True)]
    ppermute x2 -> x12, waiting for transfers between devices: 1.55 us -> 19.9 us  [swap(): return lax.ppermute(array, axis, [(i, i ^ mask) for i in range(size)])]
    ppermute x2 -> x12, starting transfers between devices: 4.79 us -> 18.2 us  [swap(): return lax.ppermute(array, axis, [(i, i ^ mask) for i in range(size)])]
    all_to_all x4 -> x3, starting transfers between devices: 25.8 us -> 21.8 us  [exchange(): return lax.all_to_all(pieces, axes, split_axis=0, concat_axis=0, tiled=True)]
    unnamed x20 -> x16, local copies, waits for them, and re-layouts: 4.55 us -> 2.59 us
    pallas_call x9 -> x13, Pallas kernels: 22.4 us -> 24.2 us  [kernel_call(): pl.pallas_call(body, out_shape=outs, in_specs=[SMEM] * scalars + [space]...]
  transfers between devices with their start and end apart: 6 -> 15, of which waited for: 5 -> 7; matrix products, arithmetic and copies ran while one was open for 0% -> 0% of each run, Pallas kernels for 11% -> 14%
where the time goes in v2:
time: 104 us
  starting transfers between devices  40 us (38%)
  Pallas kernels  24.2 us (23%)
  waiting for transfers between devices  20.1 us (19%)
  blocking collectives  16.1 us (15%)
  local copies, waits for them, and re-layouts  2.59 us (2%)
    pallas_call x13, Pallas kernels, kernel_call(): pl.pallas_call(body, out_shape=outs, in_specs=[SMEM] * scalars + [space]...  24.2 us
    all_to_all x3, starting transfers between devices, exchange(): return lax.all_to_all(pieces, axes, split_axis=0, concat_axis=0, tiled=True)  21.8 us
    ppermute x12, waiting for transfers between devices, swap(): return lax.ppermute(array, axis, [(i, i ^ mask) for i in range(size)])  19.9 us
    ppermute x12, starting transfers between devices, swap(): return lax.ppermute(array, axis, [(i, i ^ mask) for i in range(size)])  18.2 us
    all_to_all x1, blocking collectives, exchange(): return lax.all_to_all(pieces, axes, split_axis=0, concat_axis=0, tiled=True)  16.1 us
    unnamed x16, local copies, waits for them, and re-layouts  2.59 us
  transfers between devices with their start and end apart: 15, of which 7 were waited for; matrix products, arithmetic and copies ran while one was open for 0% of the time, Pallas kernels for 14%

profile of v2, /device:TPU:1, one launch (start us, length us, event | category | flops | bytes accessed | tf_op | source)
XLA Modules:
  0.0 103.9 jit_solution(4832970889014608459)
XLA Ops:
  0.6 0.0 copy-start.1
  0.6 0.9 copy-done.1
  1.6 0.9 copy-done.4
  2.5 0.8 shard_map.94
  3.4 0.0 copy-start.2
  3.4 0.0 copy-start.5
  3.4 11.7 %all-to-all-start = ((bf16[16,2,2,16,256]{4,3,2,1,0:T(8,128)(2,1)}), bf16[16,2,2,16,256]{4,3,2,1,0:T(8,128)(2,1)S(1)}, u32[]{:S(2)}, u32[]{:S(2)}) async-start(bf16[16,2,2,16,256]{4,3,2,1,0:T(8,128)(2,1)} %bitcast.10), calls=%async_computation | async-start | bytes 1048576 | tf_op jit(solution)/shard_map/all_to_all | solution.py:357
  15.2 0.1 pad_add_fusion.place
  15.2 0.0 copy-start.3
  15.3 0.0 copy-start.6
  15.3 0.7 shard_map.95
  16.0 1.0 %collective-permute-start = (bf16[2,8,16,256]{3,2,1,0:T(8,128)(2,1)S(1)}, bf16[2,8,16,256]{3,2,1,0:T(8,128)(2,1)S(1)}, u32[]{:S(2)}, u32[]{:S(2)}) collective-permute-start(bf16[2,8,16,256]{3,2,1,0:T(8,128)(2,1)S(1)} %get-tuple-element.28), channel_id=1, source_target_pairs={{0,1},{1,0},{2,3},{3,2},{4,5},{5,4},{6,7},{7,6},{8,9},{9,8},{10,11... | collective-permute-start | bytes 393224 | tf_op jit(solution)/shard_map/ppermute | solution.py:353
  17.1 0.3 collective-permute-start.1
  17.4 1.4 %collective-permute-start.2 = (bf16[2,8,16,256]{3,2,1,0:T(8,128)(2,1)S(1)}, bf16[2,8,16,256]{3,2,1,0:T(8,128)(2,1)S(1)}, u32[]{:S(2)}, u32[]{:S(2)}) collective-permute-start(bf16[2,8,16,256]{3,2,1,0:T(8,128)(2,1)S(1)} %get-tuple-element.30), channel_id=1, source_target_pairs={{0,3},{1,2},{2,1},{3,0},{4,7},{5,6},{6,5},{7,4},{8,11},{9,10},{10,... | collective-permute-start | bytes 393224 | tf_op jit(solution)/shard_map/ppermute | solution.py:353
  18.8 0.7 copy-done.7
  19.5 5.6 %shard_map.93 = (f32[512,256]{1,0:T(8,128)S(1)}, f32[256,768]{1,0:T(8,128)S(1)}, f32[256,256]{1,0:T(8,128)S(1)}, f32[1,256]{1,0:T(1,128)S(1)}) custom-call(bf16[512,256]{1,0:T(8,128)(2,1)S(1)} %bitcast.22, bf16[512,256]{1,0:T(8,128)(2,1)S(1)} %bitcast.18, bf16[512,256]{1,0:T(8,128)(2,1)S(1)} %bitcast.19, f32[1,256]{1,0:T(1,128)S(1)} %bitcast.24, ...), custom_call_target="tpu_custom_call" | custom-call | flops 5600000000 | bytes 14000000 | tf_op jit(solution)/shard_map/pallas_call | solution.py:341
  25.1 0.0 collective-permute-done.refs_1_
  25.1 0.0 collective-permute-done.1.refs_2_
  25.1 4.4 %collective-permute-done.2.refs_3_ = bf16[2,8,16,256]{3,2,1,0:T(8,128)(2,1)S(1)} collective-permute-done((bf16[2,8,16,256]{3,2,1,0:T(8,128)(2,1)S(1)}, bf16[2,8,16,256]{3,2,1,0:T(8,128)(2,1)S(1)}, u32[]{:S(2)}, u32[]{:S(2)}) %collective-permute-start.2) | collective-permute-done | bytes 131104 | tf_op jit(solution)/shard_map/ppermute | solution.py:353
  29.5 5.8 %shard_map.96 = (bf16[8,16,256]{2,1,0:T(8,128)(2,1)S(1)}, bf16[8,16,256]{2,1,0:T(8,128)(2,1)S(1)}, bf16[8,16,256]{2,1,0:T(8,128)(2,1)S(1)}, bf16[8,16,256]{2,1,0...) custom-call(bf16[2,8,16,256]{3,2,1,0:T(8,128)(2,1)S(1)} %get-tuple-element.27.refs_0_, ...), custom_call_target="tpu_custom_call" | custom-call | flops 5600000000 | bytes 14000000 | tf_op jit(solution)/shard_map/pallas_call | solution.py:341
  35.3 0.0 all-to-all-done.pieces
  35.3 6.4 %shard_map.97 = (bf16[8,2,16,256]{3,2,1,0:T(8,128)(2,1)S(1)}, bf16[8,2,16,256]{3,2,1,0:T(8,128)(2,1)S(1)}, f32[65,16,128]{2,1,0:T(8,128)S(1)}, f32[65,16,128]{2,1,0:T(8,128)S(1)}) custom-call(s32[3]{0:T(128)S(1)} %pad_add_fusion.place, bf16[16,2,2,16,256]{4,3,2,1,0:T(8,128)(2,1)S(1)} %all-to-all-done.pieces, f32[1,256]{1,0:T(1,128)S(1)} %bitcast.26, ...), custom_call_target="tpu_custom_call" | custom-call | flops 5600000000 | bytes 14000000 | tf_op jit(solution)/shard_map/pallas_call | solution.py:341
  41.7 0.3 collective-permute-start.10
  42.0 1.9 %collective-permute-done.10.received = f32[65,16,128]{2,1,0:T(8,128)S(1)} collective-permute-done((f32[65,16,128]{2,1,0:T(8,128)S(1)}, f32[65,16,128]{2,1,0:T(8,128)S(1)}, u32[]{:S(2)}, u32[]{:S(2)}) %collective-permute-start.10) | collective-permute-done | bytes 532512 | tf_op jit(solution)/shard_map/ppermute | solution.py:353
  43.9 0.1 shard_map.102
  44.0 16.1 %all_to_all.20.received = bf16[16,5,16,128]{3,2,1,0:T(8,128)(2,1)S(1)} all-to-all(bf16[16,5,16,128]{3,2,1,0:T(8,128)(2,1)S(1)} %shard_map.102), channel_id=1, replica_groups=mesh['y'=4,'z'=8,'xh'=2,'xl'=2,'c'=2] {'y','xh','xl'}, dimensions={0} | all-to-all | bytes 655360 | tf_op jit(solution)/shard_map/all_to_all | solution.py:357
  60.1 0.7 shard_map.103
  60.8 6.6 %all-to-all-start.2 = ((bf16[8,5,16,128]{3,2,1,0:T(8,128)(2,1)}), bf16[8,5,16,128]{3,2,1,0:T(8,128)(2,1)S(1)}, u32[]{:S(2)}, u32[]{:S(2)}) async-start(bf16[8,5,16,128]{3,2,1,0:T(8,128)(2,1)} %shard_map.103), calls=%async_computation.2 | async-start | bytes 327680 | tf_op jit(solution)/shard_map/all_to_all | solution.py:357
  67.3 1.5 %collective-permute-start.3 = (bf16[8,2,16,256]{3,2,1,0:T(8,128)(2,1)S(1)}, bf16[8,2,16,256]{3,2,1,0:T(8,128)(2,1)S(1)}, u32[]{:S(2)}, u32[]{:S(2)}) collective-permute-start(bf16[8,2,16,256]{3,2,1,0:T(8,128)(2,1)S(1)} %get-tuple-element.37), channel_id=1, source_target_pairs={{0,8},{8,0},{16,24},{24,16},{32,40},{40,32},{48,56},{56,48},{1,9},... | collective-permute-start | bytes 393224 | tf_op jit(solution)/shard_map/ppermute | solution.py:353
  68.8 5.5 %collective-permute-done.3.refs_1_.rest_1_ = bf16[8,2,16,256]{3,2,1,0:T(8,128)(2,1)S(1)} collective-permute-done((bf16[8,2,16,256]{3,2,1,0:T(8,128)(2,1)S(1)}, bf16[8,2,16,256]{3,2,1,0:T(8,128)(2,1)S(1)}, u32[]{:S(2)}, u32[]{:S(2)}) %collective-permute-start.3) | collective-permute-done | bytes 131104 | tf_op jit(solution)/shard_map/ppermute | solution.py:353
  74.3 5.2 %collective-permute-start.4 = (bf16[8,2,16,256]{3,2,1,0:T(8,128)(2,1)S(1)}, bf16[8,2,16,256]{3,2,1,0:T(8,128)(2,1)S(1)}, u32[]{:S(2)}, u32[]{:S(2)}) collective-permute-start(bf16[8,2,16,256]{3,2,1,0:T(8,128)(2,1)S(1)} %shard_map.98), channel_id=1, source_target_pairs={{0,32},{8,40},{16,48},{24,56},{32,0},{40,8},{48,16},{56,24},{1,33}... | collective-permute-start | bytes 393224 | tf_op jit(solution)/shard_map/ppermute | solution.py:353
  79.5 0.0 all-to-all-done.2.received
  79.5 0.7 shard_map.104
  80.2 3.5 %all-to-all-start.3 = ((bf16[16,4,16,128]{3,2,1,0:T(8,128)(2,1)}), bf16[16,4,16,128]{3,2,1,0:T(8,128)(2,1)S(1)}, u32[]{:S(2)}, u32[]{:S(2)}) async-start(bf16[16,4,16,128]{3,2,1,0:T(8,128)(2,1)} %get-tuple-element.44), calls=%async_computation.3 | async-start | bytes 524288 | tf_op jit(solution)/shard_map/all_to_all | solution.py:357
  83.8 0.0 collective-permute-done.4.refs_2_.rest_2_
  83.8 2.8 %collective-permute-start.5 = (bf16[8,2,16,256]{3,2,1,0:T(8,128)(2,1)S(1)}, bf16[8,2,16,256]{3,2,1,0:T(8,128)(2,1)S(1)}, u32[]{:S(2)}, u32[]{:S(2)}) collective-permute-start(bf16[8,2,16,256]{3,2,1,0:T(8,128)(2,1)S(1)} %shard_map.99), channel_id=1, source_target_pairs={{0,4},{4,0},{1,5},{5,1},{2,6},{6,2},{3,7},{7,3},{8,12},{12,8},{9,1... | collective-permute-start | bytes 393224 | tf_op jit(solution)/shard_map/ppermute | solution.py:353
  86.6 4.4 %collective-permute-done.5.refs_3_.rest_3_ = bf16[8,2,16,256]{3,2,1,0:T(8,128)(2,1)S(1)} collective-permute-done((bf16[8,2,16,256]{3,2,1,0:T(8,128)(2,1)S(1)}, bf16[8,2,16,256]{3,2,1,0:T(8,128)(2,1)S(1)}, u32[]{:S(2)}, u32[]{:S(2)}) %collective-permute-start.5) | collective-permute-done | bytes 131104 | tf_op jit(solution)/shard_map/ppermute | solution.py:353
  91.0 0.1 collective-permute-start.6
  91.1 0.2 all-to-all-done.3
  91.3 3.5 %collective-permute-start.11 = (bf16[64,16,128]{2,1,0:T(8,128)(2,1)S(1)}, bf16[64,16,128]{2,1,0:T(8,128)(2,1)S(1)}, u32[]{:S(2)}, u32[]{:S(2)}) collective-permute-start(bf16[64,16,128]{2,1,0:T(8,128)(2,1)S(1)} %bitcast.14), channel_id=1, source_target_pairs={{0,1},{1,0},{2,3},{3,2},{4,5},{5,4},{6,7},{7,6},{8,9},{9,8},{10,11... | collective-permute-start | bytes 786440 | tf_op jit(solution)/shard_map/ppermute | solution.py:353
  94.8 0.0 collective-permute-start.7
  94.8 1.3 %collective-permute-start.8 = (bf16[8,16,256]{2,1,0:T(8,128)(2,1)S(1)}, bf16[8,16,256]{2,1,0:T(8,128)(2,1)S(1)}, u32[]{:S(2)}, u32[]{:S(2)}) collective-permute-start(bf16[8,16,256]{2,1,0:T(8,128)(2,1)S(1)} %get-tuple-element.40), channel_id=1, source_target_pairs={{0,2},{1,3},{2,0},{3,1},{4,6},{5,7},{6,4},{7,5},{8,10},{9,11},{10,... | collective-permute-start | bytes 196616 | tf_op jit(solution)/shard_map/ppermute | solution.py:353
  96.1 0.8 collective-permute-start.9
  96.9 1.3 %collective-permute-done.8.rest_7_ = bf16[8,16,256]{2,1,0:T(8,128)(2,1)S(1)} collective-permute-done((bf16[8,16,256]{2,1,0:T(8,128)(2,1)S(1)}, bf16[8,16,256]{2,1,0:T(8,128)(2,1)S(1)}, u32[]{:S(2)}, u32[]{:S(2)}) %collective-permute-start.8) | collective-permute-done | bytes 65568 | tf_op jit(solution)/shard_map/ppermute | solution.py:353
  98.2 2.5 %collective-permute-done.9.rest_8_ = bf16[8,16,256]{2,1,0:T(8,128)(2,1)S(1)} collective-permute-done((bf16[8,16,256]{2,1,0:T(8,128)(2,1)S(1)}, bf16[8,16,256]{2,1,0:T(8,128)(2,1)S(1)}, u32[]{:S(2)}, u32[]{:S(2)}) %collective-permute-start.9) | collective-permute-done | bytes 65568 | tf_op jit(solution)/shard_map/ppermute | solution.py:353
  100.7 0.0 collective-permute-done.6.rest_4_
  100.7 1.6 %shard_map.101 = bf16[2,8,32,256]{3,2,1,0:T(8,128)(2,1)} custom-call(s32[3]{0:T(128)S(1)} %pad_add_fusion.place, bf16[2,8,32,256]{3,2,1,0:T(8,128)(2,1)S(1)} %bitcast.23, f32[1,256]{1,0:T(1,128)S(1)} %bitcast.27, f32[2,8,32,256]{3,2,1,0:T(8,128)S(1)} %bitcast.28, bf16[8,2,16,256]{3,2,1,0:T(8,128)(2,1)S(1)} %get-tuple-element.36.refs_0_.rest_0_, ...), custom_call_target="tpu_custom_call" | custom-call | flops 1600000000 | bytes 4000000 | tf_op jit(solution)/shard_map/pallas_call | solution.py:341
  102.3 1.6 %shard_map.105 = (f32[256,768]{1,0:T(8,128)}, f32[256,256]{1,0:T(8,128)}) custom-call(s32[3]{0:T(128)S(1)} %pad_add_fusion.place, bf16[64,16,128]{2,1,0:T(8,128)(2,1)S(1)} %bitcast.15, bf16[64,16,128]{2,1,0:T(8,128)(2,1)S(1)} %collective-permute-done.11.theirs), custom_call_target="tpu_custom_call" | custom-call | flops 800000000 | bytes 2000000 | tf_op jit(solution)/shard_map/pallas_call | solution.py:341
  (13 shorter events, 0.1 us)
Async XLA Ops:
  0.6 1.0 copy-start.1
  1.6 0.9 copy-start.4
  3.4 11.8 %copy-start.2 = (bf16[1,2,8,32,256]{4,3,2,1,0:T(8,128)(2,1)S(1)}, bf16[1,2,8,32,256]{4,3,2,1,0:T(8,128)(2,1)}, u32[]{:S(2)}) copy-start(bf16[1,2,8,32,256]{4,3,2,1,0:T(8,128)(2,1)} %param.8) | copy-start | bytes 786436
  3.4 11.8 %copy-start.5 = (bf16[1,2,8,32,256]{4,3,2,1,0:T(8,128)(2,1)S(1)}, bf16[1,2,8,32,256]{4,3,2,1,0:T(8,128)(2,1)}, u32[]{:S(2)}) copy-start(bf16[1,2,8,32,256]{4,3,2,1,0:T(8,128)(2,1)} %param.6) | copy-start | bytes 786436
  3.4 31.9 %all-to-all-start = ((bf16[16,2,2,16,256]{4,3,2,1,0:T(8,128)(2,1)}), bf16[16,2,2,16,256]{4,3,2,1,0:T(8,128)(2,1)S(1)}, u32[]{:S(2)}, u32[]{:S(2)}) async-start(bf16[16,2,2,16,256]{4,3,2,1,0:T(8,128)(2,1)} %bitcast.10), calls=%async_computation | async-start | bytes 1048576 | tf_op jit(solution)/shard_map/all_to_all | solution.py:357
  15.2 3.6 %copy-start = (bf16[256,768]{1,0:T(8,128)(2,1)S(1)}, bf16[256,768]{1,0:T(8,128)(2,1)}, u32[]{:S(2)}) copy-start(bf16[256,768]{1,0:T(8,128)(2,1)} %w_qkv.3) | copy-start | bytes 1179652
  15.2 3.6 %copy-start.3 = (bf16[1,2,8,32,256]{4,3,2,1,0:T(8,128)(2,1)S(1)}, bf16[1,2,8,32,256]{4,3,2,1,0:T(8,128)(2,1)}, u32[]{:S(2)}) copy-start(bf16[1,2,8,32,256]{4,3,2,1,0:T(8,128)(2,1)} %param.7) | copy-start | bytes 786436
  15.3 3.5 %copy-start.6 = (bf16[256,256]{1,0:T(8,128)(2,1)S(1)}, bf16[256,256]{1,0:T(8,128)(2,1)}, u32[]{:S(2)}) copy-start(bf16[256,256]{1,0:T(8,128)(2,1)} %w_out.3) | copy-start | bytes 393220
  16.0 9.1 %collective-permute-start = (bf16[2,8,16,256]{3,2,1,0:T(8,128)(2,1)S(1)}, bf16[2,8,16,256]{3,2,1,0:T(8,128)(2,1)S(1)}, u32[]{:S(2)}, u32[]{:S(2)}) collective-permute-start(bf16[2,8,16,256]{3,2,1,0:T(8,128)(2,1)S(1)} %get-tuple-element.28), channel_id=1, source_target_pairs={{0,1},{1,0},{2,3},{3,2},{4,5},{5,4},{6,7},{7,6},{8,9},{9,8},{10,11... | collective-permute-start | bytes 393224 | tf_op jit(solution)/shard_map/ppermute | solution.py:353
  17.1 8.0 %collective-permute-start.1 = (bf16[2,8,16,256]{3,2,1,0:T(8,128)(2,1)S(1)}, bf16[2,8,16,256]{3,2,1,0:T(8,128)(2,1)S(1)}, u32[]{:S(2)}, u32[]{:S(2)}) collective-permute-start(bf16[2,8,16,256]{3,2,1,0:T(8,128)(2,1)S(1)} %get-tuple-element.29), channel_id=1, source_target_pairs={{0,2},{1,3},{2,0},{3,1},{4,6},{5,7},{6,4},{7,5},{8,10},{9,11},{10,... | collective-permute-start | bytes 393224 | tf_op jit(solution)/shard_map/ppermute | solution.py:353
  17.4 12.1 %collective-permute-start.2 = (bf16[2,8,16,256]{3,2,1,0:T(8,128)(2,1)S(1)}, bf16[2,8,16,256]{3,2,1,0:T(8,128)(2,1)S(1)}, u32[]{:S(2)}, u32[]{:S(2)}) collective-permute-start(bf16[2,8,16,256]{3,2,1,0:T(8,128)(2,1)S(1)} %get-tuple-element.30), channel_id=1, source_target_pairs={{0,3},{1,2},{2,1},{3,0},{4,7},{5,6},{6,5},{7,4},{8,11},{9,10},{10,... | collective-permute-start | bytes 393224 | tf_op jit(solution)/shard_map/ppermute | solution.py:353
  18.8 0.7 copy-start.7
  41.7 2.2 %collective-permute-start.10 = (f32[65,16,128]{2,1,0:T(8,128)S(1)}, f32[65,16,128]{2,1,0:T(8,128)S(1)}, u32[]{:S(2)}, u32[]{:S(2)}) collective-permute-start(f32[65,16,128]{2,1,0:T(8,128)S(1)} %get-tuple-element.43), channel_id=1, source_target_pairs={{0,1},{1,0},{2,3},{3,2},{4,5},{5,4},{6,7},{7,6},{8,9},{9,8},{10,11... | collective-permute-start | bytes 1597448 | tf_op jit(solution)/shard_map/ppermute | solution.py:353
  60.8 18.7 %all-to-all-start.2 = ((bf16[8,5,16,128]{3,2,1,0:T(8,128)(2,1)}), bf16[8,5,16,128]{3,2,1,0:T(8,128)(2,1)S(1)}, u32[]{:S(2)}, u32[]{:S(2)}) async-start(bf16[8,5,16,128]{3,2,1,0:T(8,128)(2,1)} %shard_map.103), calls=%async_computation.2 | async-start | bytes 327680 | tf_op jit(solution)/shard_map/all_to_all | solution.py:357
  67.3 7.0 %collective-permute-start.3 = (bf16[8,2,16,256]{3,2,1,0:T(8,128)(2,1)S(1)}, bf16[8,2,16,256]{3,2,1,0:T(8,128)(2,1)S(1)}, u32[]{:S(2)}, u32[]{:S(2)}) collective-permute-start(bf16[8,2,16,256]{3,2,1,0:T(8,128)(2,1)S(1)} %get-tuple-element.37), channel_id=1, source_target_pairs={{0,8},{8,0},{16,24},{24,16},{32,40},{40,32},{48,56},{56,48},{1,9},... | collective-permute-start | bytes 393224 | tf_op jit(solution)/shard_map/ppermute | solution.py:353
  74.3 9.4 %collective-permute-start.4 = (bf16[8,2,16,256]{3,2,1,0:T(8,128)(2,1)S(1)}, bf16[8,2,16,256]{3,2,1,0:T(8,128)(2,1)S(1)}, u32[]{:S(2)}, u32[]{:S(2)}) collective-permute-start(bf16[8,2,16,256]{3,2,1,0:T(8,128)(2,1)S(1)} %shard_map.98), channel_id=1, source_target_pairs={{0,32},{8,40},{16,48},{24,56},{32,0},{40,8},{48,16},{56,24},{1,33}... | collective-permute-start | bytes 393224 | tf_op jit(solution)/shard_map/ppermute | solution.py:353
  80.2 11.0 %all-to-all-start.3 = ((bf16[16,4,16,128]{3,2,1,0:T(8,128)(2,1)}), bf16[16,4,16,128]{3,2,1,0:T(8,128)(2,1)S(1)}, u32[]{:S(2)}, u32[]{:S(2)}) async-start(bf16[16,4,16,128]{3,2,1,0:T(8,128)(2,1)} %get-tuple-element.44), calls=%async_computation.3 | async-start | bytes 524288 | tf_op jit(solution)/shard_map/all_to_all | solution.py:357
  83.8 7.2 %collective-permute-start.5 = (bf16[8,2,16,256]{3,2,1,0:T(8,128)(2,1)S(1)}, bf16[8,2,16,256]{3,2,1,0:T(8,128)(2,1)S(1)}, u32[]{:S(2)}, u32[]{:S(2)}) collective-permute-start(bf16[8,2,16,256]{3,2,1,0:T(8,128)(2,1)S(1)} %shard_map.99), channel_id=1, source_target_pairs={{0,4},{4,0},{1,5},{5,1},{2,6},{6,2},{3,7},{7,3},{8,12},{12,8},{9,1... | collective-permute-start | bytes 393224 | tf_op jit(solution)/shard_map/ppermute | solution.py:353
  91.0 9.7 %collective-permute-start.6 = (bf16[8,2,16,256]{3,2,1,0:T(8,128)(2,1)S(1)}, bf16[8,2,16,256]{3,2,1,0:T(8,128)(2,1)S(1)}, u32[]{:S(2)}, u32[]{:S(2)}) collective-permute-start(bf16[8,2,16,256]{3,2,1,0:T(8,128)(2,1)S(1)} %shard_map.100), channel_id=1, source_target_pairs={{0,16},{8,24},{16,0},{24,8},{32,48},{40,56},{48,32},{56,40},{1,17}... | collective-permute-start | bytes 393224 | tf_op jit(solution)/shard_map/ppermute | solution.py:353
  91.3 11.0 %collective-permute-start.11 = (bf16[64,16,128]{2,1,0:T(8,128)(2,1)S(1)}, bf16[64,16,128]{2,1,0:T(8,128)(2,1)S(1)}, u32[]{:S(2)}, u32[]{:S(2)}) collective-permute-start(bf16[64,16,128]{2,1,0:T(8,128)(2,1)S(1)} %bitcast.14), channel_id=1, source_target_pairs={{0,1},{1,0},{2,3},{3,2},{4,5},{5,4},{6,7},{7,6},{8,9},{9,8},{10,11... | collective-permute-start | bytes 786440 | tf_op jit(solution)/shard_map/ppermute | solution.py:353
  94.8 2.1 %collective-permute-start.7 = (bf16[8,16,256]{2,1,0:T(8,128)(2,1)S(1)}, bf16[8,16,256]{2,1,0:T(8,128)(2,1)S(1)}, u32[]{:S(2)}, u32[]{:S(2)}) collective-permute-start(bf16[8,16,256]{2,1,0:T(8,128)(2,1)S(1)} %get-tuple-element.39), channel_id=1, source_target_pairs={{0,1},{1,0},{2,3},{3,2},{4,5},{5,4},{6,7},{7,6},{8,9},{9,8},{10,11... | collective-permute-start | bytes 196616 | tf_op jit(solution)/shard_map/ppermute | solution.py:353
  94.8 3.4 %collective-permute-start.8 = (bf16[8,16,256]{2,1,0:T(8,128)(2,1)S(1)}, bf16[8,16,256]{2,1,0:T(8,128)(2,1)S(1)}, u32[]{:S(2)}, u32[]{:S(2)}) collective-permute-start(bf16[8,16,256]{2,1,0:T(8,128)(2,1)S(1)} %get-tuple-element.40), channel_id=1, source_target_pairs={{0,2},{1,3},{2,0},{3,1},{4,6},{5,7},{6,4},{7,5},{8,10},{9,11},{10,... | collective-permute-start | bytes 196616 | tf_op jit(solution)/shard_map/ppermute | solution.py:353
  96.1 4.6 %collective-permute-start.9 = (bf16[8,16,256]{2,1,0:T(8,128)(2,1)S(1)}, bf16[8,16,256]{2,1,0:T(8,128)(2,1)S(1)}, u32[]{:S(2)}, u32[]{:S(2)}) collective-permute-start(bf16[8,16,256]{2,1,0:T(8,128)(2,1)S(1)} %get-tuple-element.41), channel_id=1, source_target_pairs={{0,3},{1,2},{2,1},{3,0},{4,7},{5,6},{6,5},{7,4},{8,11},{9,10},{10,... | collective-permute-start | bytes 196616 | tf_op jit(solution)/shard_map/ppermute | solution.py:353

commit v3 on v2

--- a/solution.py
+++ b/solution.py
@@ -17,6 +17,7 @@
 FACTOR = 1.0 / math.sqrt(HEAD)
 TOKENS = 512
 LENGTH = 32
+GROUP = 8
 PENCILS = 16
 ROWS = 16
 LANES = 128
@@ -24,15 +25,15 @@
 BF16 = jnp.bfloat16
 F32 = jnp.float32
 VMEM = pl.BlockSpec(memory_space=pltpu.VMEM)
-ANY = pl.BlockSpec(memory_space=pl.ANY)
+HBM = pl.BlockSpec(memory_space=pltpu.HBM)
 SMEM = pl.BlockSpec(memory_space=pltpu.SMEM)
 PLANE = ("y", "xh", "xl")
 FIRST = ("z", "xh")
 SECOND = ("xl", "c")
 
 
-def params():
-    return pltpu.CompilerParams(vmem_limit_bytes=48 * 2**20)
+def params(mib):
+    return pltpu.CompilerParams(vmem_limit_bytes=mib * 2**20)
 
 
 def cost(us):
@@ -47,76 +48,98 @@
     )
 
 
-def wide(ref, first, rows):
-    return jnp.concatenate([ref[first, rows, :], ref[first + 1, rows, :]], axis=1).astype(BF16)
-
-
-def attention(proj, grads, rows_of, block, lane):
-    q = [wide(proj, 0, rows) for rows in rows_of]
-    k = [wide(proj, 2, rows) for rows in rows_of]
-    v = [wide(proj, 4, rows) for rows in rows_of]
-    g = [wide(proj, 6, rows) for rows in rows_of]
-    lows = []
-    for i, rows in enumerate(rows_of):
-        q_block = jnp.concatenate([q[i]] * HEADS, axis=0) * block
-        g_block = jnp.concatenate([g[i]] * HEADS, axis=0) * block
-        scores = dot(k[i], q_block, 1, 1)
-        grad_probs = dot(v[i], g_block, 1, 1)
-        top = jnp.max(scores, axis=0, keepdims=True)
-        powers = jnp.exp((scores - top) * FACTOR)
+def attention(qkv, grad_attn, block, lane, count):
+    spans = [slice(i * LENGTH, (i + 1) * LENGTH) for i in range(count)]
+    k = [qkv[span, WIDTH : 2 * WIDTH] for span in spans]
+    v = [qkv[span, 2 * WIDTH :] for span in spans]
+    q_block = [jnp.concatenate([qkv[span, :WIDTH]] * HEADS, axis=0) * block for span in spans]
+    g_block = [jnp.concatenate([grad_attn[span]] * HEADS, axis=0) * block for span in spans]
+    scores = [dot(k[i], q_block[i], 1, 1) for i in range(count)]
+    grad_probs = [dot(v[i], g_block[i], 1, 1) for i in range(count)]
+    probs_low = []
+    scores_low = []
+    for i in range(count):
+        top = jnp.max(scores[i], axis=0, keepdims=True)
+        powers = jnp.exp((scores[i] - top) * FACTOR)
         probs = powers * (1.0 / jnp.sum(powers, axis=0, keepdims=True))
-        inner = jnp.sum(probs * grad_probs, axis=0, keepdims=True)
-        low = (probs * (grad_probs - inner)).astype(BF16)
-        grad_v = dot(probs.astype(BF16), g_block, 1, 0)
-        grad_k = dot(low, q_block, 1, 0) * FACTOR
-        for half in range(2):
-            cols = slice(half * LANES, (half + 1) * LANES)
-            grads[2 + half, rows, :] = grad_k[:, cols]
-            grads[4 + half, rows, :] = grad_v[:, cols]
-        lows.append(low)
-    stacked = jnp.concatenate(lows, axis=0)
+        inner = jnp.sum(probs * grad_probs[i], axis=0, keepdims=True)
+        scores_low.append((probs * (grad_probs[i] - inner)).astype(BF16))
+        probs_low.append(probs.astype(BF16))
+    grad_v = [dot(probs_low[i], g_block[i], 1, 0) for i in range(count)]
+    grad_k = [dot(scores_low[i], q_block[i], 1, 0) * FACTOR for i in range(count)]
+    grad_q = [[] for _ in range(count)]
     for half in range(2):
         cols = slice(half * LANES, (half + 1) * LANES)
-        turned = stacked[:, cols].T
-        for i, rows in enumerate(rows_of):
-            every = dot(turned[:, i * LENGTH : (i + 1) * LENGTH], k[i][:, cols], 1, 0)
-            picked = every[96:128]
-            for head in (2, 1, 0):
-                picked = jnp.where(
-                    lane < HEAD * (head + 1), every[head * 32 : head * 32 + 32], picked
-                )
-            grads[half, rows, :] = picked * FACTOR
-
-
-def axis_grads(tokens, cotangent, gain, w_qkv, w_out, proj, grads, strided):
-    tokens_f = tokens.astype(F32)
-    root = jnp.sqrt(jnp.mean(tokens_f * tokens_f, axis=-1, keepdims=True) + EPSILON)
-    unit = tokens_f / root
-    normed = (unit * gain).astype(BF16)
-    qkv = dot(normed, w_qkv, 1, 0)
-    for col in range(6):
-        proj[col] = qkv[:, col * LANES : (col + 1) * LANES]
-    grad_attn = dot(cotangent, w_out, 1, 1)
-    for col in range(2):
-        proj[6 + col] = grad_attn[:, col * LANES : (col + 1) * LANES]
-    shape = (WIDTH, WIDTH)
+        for base in range(0, count, 4):
+            turned = jnp.concatenate([low[:, cols] for low in scores_low[base : base + 4]], axis=0)
+            turned = turned.T
+            for i in range(4):
+                every = dot(turned[:, spans[i]], k[base + i][:, cols], 1, 0)
+                picked = every[96:128]
+                for head in (2, 1, 0):
+                    picked = jnp.where(
+                        lane < HEAD * (head + 1), every[head * HEAD : (head + 1) * HEAD], picked
+                    )
+                grad_q[base + i].append(picked * FACTOR)
+    joined = [
+        jnp.concatenate([*grad_q[i], grad_k[i], grad_v[i]], axis=1).astype(BF16)
+        for i in range(count)
+    ]
+    return jnp.concatenate(joined, axis=0)
+
+
+def axis_grads(tokens, cotangent, gain, w_qkv, w_out, scratch, strided):
+    tokens_cols, cot_cols, grad_cols, joined_rows, normed_rows = scratch
+    if strided:
+        tokens_f, cot_f = tokens.astype(F32), cotangent.astype(F32)
+        for col in range(2):
+            tokens_cols[col] = tokens_f[:, col * LANES : (col + 1) * LANES]
+            cot_cols[col] = cot_f[:, col * LANES : (col + 1) * LANES]
+    dims = (WIDTH, WIDTH)
     block = (
-        lax.broadcasted_iota(jnp.int32, shape, 0) // HEAD
-        == lax.broadcasted_iota(jnp.int32, shape, 1) // HEAD
+        lax.broadcasted_iota(jnp.int32, dims, 0) // HEAD
+        == lax.broadcasted_iota(jnp.int32, dims, 1) // HEAD
     )
     block = block.astype(F32).astype(BF16)
     lane = lax.broadcasted_iota(jnp.int32, (LENGTH, LANES), 1)
-    for base in range(0, PENCILS, 4):
+    part_gain = jnp.zeros((1, WIDTH), F32)
+    for base in range(0, PENCILS, GROUP):
+        group = slice(base * LENGTH, (base + GROUP) * LENGTH)
         if strided:
-            rows_of = [pl.ds(base + i, LENGTH, stride=PENCILS) for i in range(4)]
+            rows_of = [pl.ds(base + i, LENGTH, stride=PENCILS) for i in range(GROUP)]
+
+            def gathered(ref):
+                cols = [
+                    jnp.concatenate([ref[col, rows, :] for rows in rows_of], axis=0)
+                    for col in range(2)
+                ]
+                return jnp.concatenate(cols, axis=1)
+
+            tokens_f = gathered(tokens_cols)
+            cot = gathered(cot_cols).astype(BF16)
         else:
-            rows_of = [pl.ds((base + i) * LENGTH, LENGTH) for i in range(4)]
-        attention(proj, grads, rows_of, block, lane)
-    joined = jnp.concatenate([grads[col].astype(BF16) for col in range(6)], axis=1)
-    grad_normed = dot(joined, w_qkv, 1, 1)
-    part_qkv = dot(normed, joined, 0, 0)
-    part_gain = jnp.sum(grad_normed * unit, axis=0, keepdims=True)
-    return grad_normed, part_qkv, part_gain
+            rows_of = [pl.ds((base + i) * LENGTH, LENGTH) for i in range(GROUP)]
+            tokens_f = tokens[group].astype(F32)
+            cot = cotangent[group]
+        square = jnp.mean(tokens_f * tokens_f, axis=-1, keepdims=True) + EPSILON
+        unit = tokens_f * lax.rsqrt(square)
+        normed = (unit * gain).astype(BF16)
+        normed_rows[group] = normed
+        qkv = dot(normed, w_qkv, 1, 0).astype(BF16)
+        grad_attn = dot(cot, w_out, 1, 1).astype(BF16)
+        joined = attention(qkv, grad_attn, block, lane, GROUP)
+        joined_rows[group] = joined
+        grad_normed = dot(joined, w_qkv, 1, 1)
+        part_gain = part_gain + jnp.sum(grad_normed * unit, axis=0, keepdims=True)
+        for i, rows in enumerate(rows_of):
+            for col in range(2):
+                grad_cols[col, rows, :] = grad_normed[spans_of(i), col * LANES : (col + 1) * LANES]
+    part_qkv = dot(normed_rows[...], joined_rows[...], 0, 0)
+    return jnp.concatenate([grad_cols[0], grad_cols[1]], axis=1), part_qkv, part_gain
+
+
+def spans_of(i):
+    return slice(i * LENGTH, (i + 1) * LENGTH)
 
 
 BITS = (2, 8, 1, 4)
@@ -139,9 +162,9 @@
 
 SPANS = [span_masks(count) for count in range(4)]
 
-SCRATCH = [
-    pltpu.VMEM((8, TOKENS, LANES), F32),
-    pltpu.VMEM((6, TOKENS, LANES), F32),
+SCRATCH = [pltpu.VMEM((2, TOKENS, LANES), F32)] * 3 + [
+    pltpu.VMEM((TOKENS, TRIPLE), BF16),
+    pltpu.VMEM((TOKENS, WIDTH), BF16),
 ]
 
 
@@ -182,11 +205,11 @@
 
 
 def third_kernel(
-    tokens, cotangent, attn, gain, w_qkv, w_out, normed_out, qkv_out, out_out, gain_out, proj, grads
+    tokens, cotangent, attn, gain, w_qkv, w_out, normed_out, qkv_out, out_out, gain_out, *scratch
 ):
     cot = cotangent[...]
     grad_normed, part_qkv, part_gain = axis_grads(
-        tokens[...], cot, gain[...], w_qkv[...], w_out[...], proj, grads, False
+        tokens[...], cot, gain[...], w_qkv[...], w_out[...], scratch, False
     )
     normed_out[...] = grad_normed
     qkv_out[...] = part_qkv
@@ -194,50 +217,36 @@
     out_out[...] = dot(attn[...], cot, 0, 0)
 
 
-def second_kernel(*refs):
-    pieces, (gain, w_qkv, w_out, qkv_in, gain_in) = refs[:4], refs[4:9]
-    back, (qkv_out, gain_out, proj, grads) = refs[9:13], refs[13:]
-    tokens = jnp.concatenate([piece[0].reshape(-1, WIDTH) for piece in pieces], axis=0)
-    cot = jnp.concatenate([piece[1].reshape(-1, WIDTH) for piece in pieces], axis=0)
-    grad_normed, part_qkv, part_gain = axis_grads(
-        tokens, cot, gain[...], w_qkv[...], w_out[...], proj, grads, True
-    )
-    returned = grad_normed.astype(BF16)
-    rows = TOKENS // 4
-    for mask, out in enumerate(back):
-        out[...] = returned[mask * rows : (mask + 1) * rows].reshape(out.shape)
-    qkv_out[...] = qkv_in[...] + part_qkv
-    gain_out[...] = gain_in[...] + part_gain
-
-
 def first_kernel(
-    place,
-    pieces,
-    gain,
-    w_qkv,
-    w_out,
-    qkv_in,
-    out_in,
-    gain_in,
-    stay,
-    leave,
-    own,
-    other,
-    proj,
-    grads,
-    halves,
-    returned,
+    place, pieces, gain, w_qkv, w_out, qkv_in, gain_in, stay, leave, qkv_out, gain_out, *scratch
 ):
+    returned = scratch[-1]
     tokens = pieces[:, 0].reshape(TOKENS, WIDTH)
     cot = pieces[:, 1].reshape(TOKENS, WIDTH)
     grad_normed, part_qkv, part_gain = axis_grads(
-        tokens, cot, gain[...], w_qkv[...], w_out[...], proj, grads, True
+        tokens, cot, gain[...], w_qkv[...], w_out[...], scratch[:-1], True
     )
     returned[...] = grad_normed.astype(BF16).reshape(returned.shape)
     here = place[2]
     for at, mask in enumerate(SPANS[3]):
         stay[at] = returned[here ^ mask]
         leave[at] = returned[here ^ mask ^ BITS[0]]
+    qkv_out[...] = qkv_in[...] + part_qkv
+    gain_out[...] = gain_in[...] + part_gain
+
+
+def second_kernel(place, *refs):
+    pieces, (gain, w_qkv, w_out, qkv_in, out_in, gain_in) = refs[:4], refs[4:10]
+    back, (own, other), scratch, halves = refs[10:14], refs[14:16], refs[16:-1], refs[-1]
+    tokens = jnp.concatenate([piece[0].reshape(-1, WIDTH) for piece in pieces], axis=0)
+    cot = jnp.concatenate([piece[1].reshape(-1, WIDTH) for piece in pieces], axis=0)
+    grad_normed, part_qkv, part_gain = axis_grads(
+        tokens, cot, gain[...], w_qkv[...], w_out[...], scratch, True
+    )
+    returned = grad_normed.astype(BF16)
+    rows = TOKENS // 4
+    for mask, out in enumerate(back):
+        out[...] = returned[mask * rows : (mask + 1) * rows].reshape(out.shape)
     total = qkv_in[...] + part_qkv
     for at in range(2 * TILES):
         half, tile = divmod(at, TILES)
@@ -344,7 +353,7 @@
         in_specs=[SMEM] * scalars + [space] * (len(operands) - scalars),
         out_specs=jax.tree.map(lambda _: space, outs),
         scratch_shapes=list(scratch),
-        compiler_params=params(),
+        compiler_params=params(62 if space is HBM else 48),
         cost_estimate=cost(us),
     )(*operands)
 
@@ -373,7 +382,7 @@
         (local, upstream),
         2,
         [pltpu.SemaphoreType.DMA((8,))],
-        space=ANY,
+        space=HBM,
     )
     at_first = exchange(to_first.reshape(16, 2, 2, ROWS, WIDTH), FIRST)
     to_second = kernel_call(
@@ -383,7 +392,7 @@
         2,
         [pltpu.SemaphoreType.DMA((8,))],
         1,
-        ANY,
+        HBM,
     )
     at_second = [to_second[0]] + [swap(to_second[m], SECOND, m, 4) for m in (1, 2, 3)]
     third, part_qkv, part_out, part_gain = kernel_call(
@@ -395,48 +404,58 @@
             shape((1, WIDTH), F32),
         ),
         (local.reshape(flat), upstream.reshape(flat), attn.reshape(flat), gain_row, w_qkv, w_out),
-        7,
+        5,
         SCRATCH,
     )
-    *back, part_qkv, part_gain = kernel_call(
-        second_kernel,
-        (shape((8, ROWS, WIDTH), BF16),) * 4
-        + (shape((WIDTH, TRIPLE), F32), shape((1, WIDTH), F32)),
-        (*at_second, gain_row, w_qkv, w_out, part_qkv, part_gain),
-        7,
-        SCRATCH,
-    )
-    from_second = [back[0]] + [swap(back[m], SECOND, m, 4) for m in (1, 2, 3)]
     block = (2, ROWS, WIDTH)
-    stay, leave, own, other = kernel_call(
+    stay, leave, part_qkv, part_gain = kernel_call(
         first_kernel,
         (
             shape((8, *block), BF16),
             shape((8, *block), BF16),
-            shape((TILES + 1, *tile), F32),
-            shape((TILES + 1, *tile), F32),
+            shape((WIDTH, TRIPLE), F32),
+            shape((1, WIDTH), F32),
         ),
-        (place, at_first, gain_row, w_qkv, w_out, part_qkv, part_out, part_gain),
-        7,
-        SCRATCH + [pltpu.VMEM((2, TILES, *tile), F32), pltpu.VMEM((16, *block), BF16)],
+        (place, at_first, gain_row, w_qkv, w_out, part_qkv, part_gain),
+        5,
+        SCRATCH + [pltpu.VMEM((16, *block), BF16)],
+        1,
+    )
+    groups = [stay, swap(leave, *SWAPS[0])]
+    *back, own, other = kernel_call(
+        second_kernel,
+        (shape((8, ROWS, WIDTH), BF16),) * 4 + (shape((TILES + 1, *tile), F32),) * 2,
+        (place, *at_second, gain_row, w_qkv, w_out, part_qkv, part_out, part_gain),
+        5,
+        SCRATCH + [pltpu.VMEM((2, TILES, *tile), F32)],
         1,
     )
     received = swap(other, "c", 1, 2)
-    groups = [stay, swap(leave, *SWAPS[0])]
     pieces = kernel_call(pair_kernel, shape((16, 5, *tile), BF16), (own, received), 1)
+    leave = kernel_call(stage_kernel, shape((8, *block), BF16), groups, 1)
+    pieces, leave, *back = lax.optimization_barrier((pieces, leave, *back))
     summed = exchange(pieces, PLANE)
-    for stage in (1, 2, 3):
-        leave = kernel_call(stage_kernel, shape((8, *block), BF16), groups, 1)
-        groups.append(swap(leave, *SWAPS[stage]))
+    from_second = [back[0]] + [swap(back[m], SECOND, m, 4) for m in (1, 2, 3)]
+    groups.append(swap(leave, *SWAPS[1]))
+    summed, groups, from_second = lax.optimization_barrier((summed, groups, from_second))
     pieces = kernel_call(plane_kernel, shape((8, 5, *tile), BF16), (summed,), 1)
+    leave = kernel_call(stage_kernel, shape((8, *block), BF16), groups, 1)
+    pieces, leave = lax.optimization_barrier((pieces, leave))
     summed = exchange(pieces, "z")
+    groups.append(swap(leave, *SWAPS[2]))
+    summed, groups = lax.optimization_barrier((summed, groups))
     pieces, d_gain = kernel_call(
         functools.partial(line_kernel, 1.0 / math.sqrt(count)),
         (shape((16, 4, *tile), BF16), shape((1, WIDTH), F32)),
         (summed,),
         1,
     )
-    mine = exchange(pieces, PLANE).reshape(TILES, *tile)
+    leave = kernel_call(stage_kernel, shape((8, *block), BF16), groups, 1)
+    pieces, leave = lax.optimization_barrier((pieces, leave))
+    mine = exchange(pieces, PLANE)
+    groups.append(swap(leave, *SWAPS[3]))
+    mine, groups = lax.optimization_barrier((mine, groups))
+    mine = mine.reshape(TILES, *tile)
     theirs = swap(mine, "c", 1, 2)
     d_w_qkv, d_w_out = kernel_call(
         assemble_kernel,

time: 104 us -> 128 us (1.23)
  Pallas kernels: 24.2 us -> 51.4 us
  blocking collectives: 16.1 us -> 0 us
  starting transfers between devices: 40 us -> 50.4 us
    pallas_call x13, Pallas kernels: 24.2 us -> 51.4 us  [kernel_call(): pl.pallas_call(body, out_shape=outs, in_specs=[SMEM] * scalars + [space]...]
    all_to_all x1 -> x0, blocking collectives: 16.1 us -> none  [exchange(): return lax.all_to_all(pieces, axes, split_axis=0, concat_axis=0, tiled=True)]
    all_to_all x3 -> x4, starting transfers between devices: 21.8 us -> 29.4 us  [exchange(): return lax.all_to_all(pieces, axes, split_axis=0, concat_axis=0, tiled=True)]
    all_to_all x3 -> x4, waiting for transfers between devices: 0.16 us -> 4.5 us  [exchange(): return lax.all_to_all(pieces, axes, split_axis=0, concat_axis=0, tiled=True)]
    ppermute x12, waiting for transfers between devices: 19.9 us -> 16.4 us  [swap(): return lax.ppermute(array, axis, [(i, i ^ mask) for i in range(size)])]
    ppermute x12, starting transfers between devices: 18.2 us -> 21 us  [swap(): return lax.ppermute(array, axis, [(i, i ^ mask) for i in range(size)])]
    unnamed x16 -> x24, local copies, waits for them, and re-layouts: 2.59 us -> 3.29 us
  transfers between devices with their start and end apart: 15 -> 16, of which waited for: 7 -> 7; matrix products, arithmetic and copies ran while one was open for 0% -> 0% of each run, Pallas kernels for 14% -> 21%
where the time goes in v3:
time: 128 us; the launch traced here: 127 us
  Pallas kernels  51.4 us (40%)
  starting transfers between devices  50.4 us (39%)
  waiting for transfers between devices  20.9 us (16%)
  local copies, waits for them, and re-layouts  3.29 us (3%)
    pallas_call x13, Pallas kernels, kernel_call(): pl.pallas_call(body, out_shape=outs, in_specs=[SMEM] * scalars + [space]...  51.4 us
    all_to_all x4, starting transfers between devices, exchange(): return lax.all_to_all(pieces, axes, split_axis=0, concat_axis=0, tiled=True)  29.4 us
    ppermute x12, starting transfers between devices, swap(): return lax.ppermute(array, axis, [(i, i ^ mask) for i in range(size)])  21 us
    ppermute x12, waiting for transfers between devices, swap(): return lax.ppermute(array, axis, [(i, i ^ mask) for i in range(size)])  16.4 us
    all_to_all x4, waiting for transfers between devices, exchange(): return lax.all_to_all(pieces, axes, split_axis=0, concat_axis=0, tiled=True)  4.5 us
    unnamed x24, local copies, waits for them, and re-layouts  3.29 us
  transfers between devices with their start and end apart: 16, of which 7 were waited for; matrix products, arithmetic and copies ran while one was open for 0% of the time, Pallas kernels for 21%

profile of v3, /device:TPU:1, one launch (start us, length us, event | category | flops | bytes accessed | tf_op | source)
XLA Modules:
  0.0 127.4 jit_solution(17024053546543915245)
XLA Ops:
  0.6 17.1 %shard_map.95 = bf16[8,2,2,2,16,256]{5,4,3,2,1,0:T(8,128)(2,1)} custom-call(bf16[2,8,32,256]{3,2,1,0:T(8,128)(2,1)} %bitcast.20, bf16[2,8,32,256]{3,2,1,0:T(8,128)(2,1)} %bitcast.16), custom_call_target="tpu_custom_call" | custom-call | flops 1600000000 | bytes 4000000 | tf_op jit(solution)/shard_map/pallas_call | solution.py:350
  17.7 11.6 %all-to-all-start = ((bf16[16,2,2,16,256]{4,3,2,1,0:T(8,128)(2,1)}), bf16[16,2,2,16,256]{4,3,2,1,0:T(8,128)(2,1)S(1)}, u32[]{:S(2)}, u32[]{:S(2)}) async-start(bf16[16,2,2,16,256]{4,3,2,1,0:T(8,128)(2,1)} %bitcast.29), calls=%async_computation | async-start | bytes 1048576 | tf_op jit(solution)/shard_map/all_to_all | solution.py:366
  29.3 0.6 pad_add_fusion.place
  29.9 0.0 copy-start.5
  29.9 17.9 %shard_map.94 = (bf16[2,8,16,256]{3,2,1,0:T(8,128)(2,1)}, bf16[2,8,16,256]{3,2,1,0:T(8,128)(2,1)}, bf16[2,8,16,256]{3,2,1,0:T(8,128)(2,1)}, bf16[2,8,16,256]{3,2,1,0:T(8,128)(2,1)}) custom-call(s32[3]{0:T(128)} %pad_add_fusion.place, bf16[2,8,32,256]{3,2,1,0:T(8,128)(2,1)} %bitcast.21, bf16[2,8,32,256]{3,2,1,0:T(8,128)(2,1)} %bitcast.17), custom_call_target="tpu_custom_call" | custom-call | flops 1600000000 | bytes 4000000 | tf_op jit(solution)/shard_map/pallas_call | solution.py:350
  47.8 1.0 collective-permute-start
  48.8 0.3 collective-permute-start.1
  49.2 1.4 %collective-permute-start.2 = (bf16[2,8,16,256]{3,2,1,0:T(8,128)(2,1)}, bf16[2,8,16,256]{3,2,1,0:T(8,128)(2,1)S(1)}, u32[]{:S(2)}, u32[]{:S(2)}) collective-permute-start(bf16[2,8,16,256]{3,2,1,0:T(8,128)(2,1)} %get-tuple-element.59), channel_id=1, source_target_pairs={{0,3},{1,2},{2,1},{3,0},{4,7},{5,6},{6,5},{7,4},{8,11},{9,10},{10,... | collective-permute-start | bytes 393224 | tf_op jit(solution)/shard_map/ppermute | solution.py:362
  50.6 0.6 copy-done.6
  51.2 3.2 %shard_map.93 = (f32[512,256]{1,0:T(8,128)S(1)}, f32[256,768]{1,0:T(8,128)S(1)}, f32[256,256]{1,0:T(8,128)S(1)}, f32[1,256]{1,0:T(1,128)S(1)}) custom-call(bf16[512,256]{1,0:T(8,128)(2,1)S(1)} %bitcast.22, bf16[512,256]{1,0:T(8,128)(2,1)S(1)} %bitcast.18, bf16[512,256]{1,0:T(8,128)(2,1)S(1)} %bitcast.19, f32[1,256]{1,0:T(1,128)S(1)} %bitcast.24, ...), custom_call_target="tpu_custom_call" | custom-call | flops 4000000000 | bytes 10000000 | tf_op jit(solution)/shard_map/pallas_call | solution.py:350
  54.4 0.0 copy-start.9
  54.4 0.9 copy-done.9
  55.3 0.0 all-to-all-done.pieces
  55.3 0.6 copy-done
  55.9 1.1 copy-done.10
  57.0 3.8 %shard_map.96 = (bf16[8,2,16,256]{3,2,1,0:T(8,128)(2,1)S(1)}, bf16[8,2,16,256]{3,2,1,0:T(8,128)(2,1)S(1)}, f32[256,768]{1,0:T(8,128)S(1)}, f32[1,256]{1,0:T(1,128)S(1)}) custom-call(s32[3]{0:T(128)S(1)} %copy-done, bf16[16,2,2,16,256]{4,3,2,1,0:T(8,128)(2,1)S(1)} %all-to-all-done.pieces, f32[1,256]{1,0:T(1,128)S(1)} %bitcast.25, ...), custom_call_target="tpu_custom_call" | custom-call | flops 4000000000 | bytes 10000000 | tf_op jit(solution)/shard_map/pallas_call | solution.py:350
  60.9 0.0 collective-permute-done.refs_1_
  60.9 0.0 collective-permute-done.1.refs_2_
  60.9 0.0 collective-permute-done.2.refs_3_
  61.0 3.9 %shard_map.97 = (bf16[8,16,256]{2,1,0:T(8,128)(2,1)S(1)}, bf16[8,16,256]{2,1,0:T(8,128)(2,1)S(1)}, bf16[8,16,256]{2,1,0:T(8,128)(2,1)S(1)}, bf16[8,16,256]{2,1,0...) custom-call(s32[3]{0:T(128)S(1)} %copy-done, bf16[2,8,16,256]{3,2,1,0:T(8,128)(2,1)S(1)} %copy-done.11, ...), custom_call_target="tpu_custom_call" | custom-call | flops 4000000000 | bytes 10000000 | tf_op jit(solution)/shard_map/pallas_call | solution.py:350
  64.9 0.2 collective-permute-start.3
  65.1 1.8 %collective-permute-start.4 = (bf16[8,2,16,256]{3,2,1,0:T(8,128)(2,1)S(1)}, bf16[8,2,16,256]{3,2,1,0:T(8,128)(2,1)S(1)}, u32[]{:S(2)}, u32[]{:S(2)}) collective-permute-start(bf16[8,2,16,256]{3,2,1,0:T(8,128)(2,1)S(1)} %get-tuple-element.68), channel_id=1, source_target_pairs={{0,8},{8,0},{16,24},{24,16},{32,40},{40,32},{48,56},{56,48},{1,9},... | collective-permute-start | bytes 393224 | tf_op jit(solution)/shard_map/ppermute | solution.py:362
  66.9 3.6 %collective-permute-done.4.refs_1_.rest_1_ = bf16[8,2,16,256]{3,2,1,0:T(8,128)(2,1)S(1)} collective-permute-done((bf16[8,2,16,256]{3,2,1,0:T(8,128)(2,1)S(1)}, bf16[8,2,16,256]{3,2,1,0:T(8,128)(2,1)S(1)}, u32[]{:S(2)}, u32[]{:S(2)}) %collective-permute-start.4) | collective-permute-done | bytes 131104 | tf_op jit(solution)/shard_map/ppermute | solution.py:362
  70.5 0.0 collective-permute-done.3.received
  70.5 0.8 shard_map.98
  71.3 6.8 %all-to-all-start.1 = ((bf16[16,5,16,128]{3,2,1,0:T(8,128)(2,1)}), bf16[16,5,16,128]{3,2,1,0:T(8,128)(2,1)S(1)}, u32[]{:S(2)}, u32[]{:S(2)}) async-start(bf16[16,5,16,128]{3,2,1,0:T(8,128)(2,1)} %shard_map.98), calls=%async_computation.1 | async-start | bytes 655360 | tf_op jit(solution)/shard_map/all_to_all | solution.py:366
  78.1 5.2 %collective-permute-start.5 = (bf16[8,2,16,256]{3,2,1,0:T(8,128)(2,1)S(1)}, bf16[8,2,16,256]{3,2,1,0:T(8,128)(2,1)S(1)}, u32[]{:S(2)}, u32[]{:S(2)}) collective-permute-start(bf16[8,2,16,256]{3,2,1,0:T(8,128)(2,1)S(1)} %shard_map.99), channel_id=1, source_target_pairs={{0,32},{8,40},{16,48},{24,56},{32,0},{40,8},{48,16},{56,24},{1,33}... | collective-permute-start | bytes 393224 | tf_op jit(solution)/shard_map/ppermute | solution.py:362
  83.3 1.6 %collective-permute-start.6 = (bf16[8,16,256]{2,1,0:T(8,128)(2,1)S(1)}, bf16[8,16,256]{2,1,0:T(8,128)(2,1)S(1)}, u32[]{:S(2)}, u32[]{:S(2)}) collective-permute-start(bf16[8,16,256]{2,1,0:T(8,128)(2,1)S(1)} %get-tuple-element.76), channel_id=1, source_target_pairs={{0,1},{1,0},{2,3},{3,2},{4,5},{5,4},{6,7},{7,6},{8,9},{9,8},{10,11... | collective-permute-start | bytes 196616 | tf_op jit(solution)/shard_map/ppermute | solution.py:362
  84.9 1.6 %collective-permute-start.7 = (bf16[8,16,256]{2,1,0:T(8,128)(2,1)S(1)}, bf16[8,16,256]{2,1,0:T(8,128)(2,1)S(1)}, u32[]{:S(2)}, u32[]{:S(2)}) collective-permute-start(bf16[8,16,256]{2,1,0:T(8,128)(2,1)S(1)} %get-tuple-element.77), channel_id=1, source_target_pairs={{0,2},{1,3},{2,0},{3,1},{4,6},{5,7},{6,4},{7,5},{8,10},{9,11},{10,... | collective-permute-start | bytes 196616 | tf_op jit(solution)/shard_map/ppermute | solution.py:362
  86.5 0.1 collective-permute-start.8
  86.5 0.0 collective-permute-done.6.rest_6_
  86.5 2.3 %collective-permute-done.7.rest_7_ = bf16[8,16,256]{2,1,0:T(8,128)(2,1)S(1)} collective-permute-done((bf16[8,16,256]{2,1,0:T(8,128)(2,1)S(1)}, bf16[8,16,256]{2,1,0:T(8,128)(2,1)S(1)}, u32[]{:S(2)}, u32[]{:S(2)}) %collective-permute-start.7) | collective-permute-done | bytes 65568 | tf_op jit(solution)/shard_map/ppermute | solution.py:362
  88.8 1.6 %collective-permute-done.8.rest_8_ = bf16[8,16,256]{2,1,0:T(8,128)(2,1)S(1)} collective-permute-done((bf16[8,16,256]{2,1,0:T(8,128)(2,1)S(1)}, bf16[8,16,256]{2,1,0:T(8,128)(2,1)S(1)}, u32[]{:S(2)}, u32[]{:S(2)}) %collective-permute-start.8) | collective-permute-done | bytes 65568 | tf_op jit(solution)/shard_map/ppermute | solution.py:362
  90.5 0.0 collective-permute-done.5.refs_2_.rest_2_
  90.5 0.7 shard_map.100
  91.2 4.6 %all-to-all-start.2 = ((bf16[8,5,16,128]{3,2,1,0:T(8,128)(2,1)}), bf16[8,5,16,128]{3,2,1,0:T(8,128)(2,1)S(1)}, u32[]{:S(2)}, u32[]{:S(2)}) async-start(bf16[8,5,16,128]{3,2,1,0:T(8,128)(2,1)} %shard_map.100), calls=%async_computation.2 | async-start | bytes 327680 | tf_op jit(solution)/shard_map/all_to_all | solution.py:366
  95.8 2.5 %collective-permute-start.9 = (bf16[8,2,16,256]{3,2,1,0:T(8,128)(2,1)S(1)}, bf16[8,2,16,256]{3,2,1,0:T(8,128)(2,1)S(1)}, u32[]{:S(2)}, u32[]{:S(2)}) collective-permute-start(bf16[8,2,16,256]{3,2,1,0:T(8,128)(2,1)S(1)} %shard_map.101), channel_id=1, source_target_pairs={{0,4},{4,0},{1,5},{5,1},{2,6},{6,2},{3,7},{7,3},{8,12},{12,8},{9,1... | collective-permute-start | bytes 393224 | tf_op jit(solution)/shard_map/ppermute | solution.py:362
  98.3 2.8 %collective-permute-done.9.refs_3_.rest_3_ = bf16[8,2,16,256]{3,2,1,0:T(8,128)(2,1)S(1)} collective-permute-done((bf16[8,2,16,256]{3,2,1,0:T(8,128)(2,1)S(1)}, bf16[8,2,16,256]{3,2,1,0:T(8,128)(2,1)S(1)}, u32[]{:S(2)}, u32[]{:S(2)}) %collective-permute-start.9) | collective-permute-done | bytes 131104 | tf_op jit(solution)/shard_map/ppermute | solution.py:362
  101.1 3.1 %all-to-all-done.2.received = bf16[8,5,16,128]{3,2,1,0:T(8,128)(2,1)S(1)} async-done(((bf16[8,5,16,128]{3,2,1,0:T(8,128)(2,1)}), bf16[8,5,16,128]{3,2,1,0:T(8,128)(2,1)S(1)}, u32[]{:S(2)}, u32[]{:S(2)}) %all-to-all-start.2) | async-done | bytes 163872 | tf_op jit(solution)/shard_map/all_to_all | solution.py:366
  104.2 0.7 shard_map.102
  105.0 6.4 %all-to-all-start.3 = ((bf16[16,4,16,128]{3,2,1,0:T(8,128)(2,1)}), bf16[16,4,16,128]{3,2,1,0:T(8,128)(2,1)S(1)}, u32[]{:S(2)}, u32[]{:S(2)}) async-start(bf16[16,4,16,128]{3,2,1,0:T(8,128)(2,1)} %get-tuple-element.91), calls=%async_computation.3 | async-start | bytes 524288 | tf_op jit(solution)/shard_map/all_to_all | solution.py:366
  111.4 0.1 collective-permute-start.10
  111.5 6.0 %collective-permute-done.10.rest_4_ = bf16[8,2,16,256]{3,2,1,0:T(8,128)(2,1)S(1)} collective-permute-done((bf16[8,2,16,256]{3,2,1,0:T(8,128)(2,1)S(1)}, bf16[8,2,16,256]{3,2,1,0:T(8,128)(2,1)S(1)}, u32[]{:S(2)}, u32[]{:S(2)}) %collective-permute-start.10) | collective-permute-done | bytes 131104 | tf_op jit(solution)/shard_map/ppermute | solution.py:362
  117.5 1.4 %all-to-all-done.3 = bf16[16,4,16,128]{3,2,1,0:T(8,128)(2,1)S(1)} async-done(((bf16[16,4,16,128]{3,2,1,0:T(8,128)(2,1)}), bf16[16,4,16,128]{3,2,1,0:T(8,128)(2,1)S(1)}, u32[]{:S(2)}, u32[]{:S(2)}) %all-to-all-start.3) | async-done | bytes 262176 | tf_op jit(solution)/shard_map/all_to_all | solution.py:366
  118.9 5.2 %collective-permute-start.11 = (bf16[64,16,128]{2,1,0:T(8,128)(2,1)S(1)}, bf16[64,16,128]{2,1,0:T(8,128)(2,1)S(1)}, u32[]{:S(2)}, u32[]{:S(2)}) collective-permute-start(bf16[64,16,128]{2,1,0:T(8,128)(2,1)S(1)} %bitcast.14), channel_id=1, source_target_pairs={{0,1},{1,0},{2,3},{3,2},{4,5},{5,4},{6,7},{7,6},{8,9},{9,8},{10,11... | collective-permute-start | bytes 786440 | tf_op jit(solution)/shard_map/ppermute | solution.py:362
  124.2 1.6 %shard_map.104 = bf16[2,8,32,256]{3,2,1,0:T(8,128)(2,1)} custom-call(s32[3]{0:T(128)S(1)} %copy-done, bf16[2,8,32,256]{3,2,1,0:T(8,128)(2,1)S(1)} %bitcast.23, f32[1,256]{1,0:T(1,128)S(1)} %bitcast.27, f32[2,8,32,256]{3,2,1,0:T(8,128)S(1)} %bitcast.28, bf16[8,2,16,256]{3,2,1,0:T(8,128)(2,1)S(1)} %get-tuple-element.93.refs_0_.rest_0_, ...), custom_call_target="tpu_custom_call" | custom-call | flops 1600000000 | bytes 4000000 | tf_op jit(solution)/shard_map/pallas_call | solution.py:350
  125.8 0.0 collective-permute-done.11.theirs
  125.8 1.6 %shard_map.105 = (f32[256,768]{1,0:T(8,128)}, f32[256,256]{1,0:T(8,128)}) custom-call(s32[3]{0:T(128)S(1)} %copy-done, bf16[64,16,128]{2,1,0:T(8,128)(2,1)S(1)} %bitcast.15, bf16[64,16,128]{2,1,0:T(8,128)(2,1)S(1)} %collective-permute-done.11.theirs), custom_call_target="tpu_custom_call" | custom-call | flops 800000000 | bytes 2000000 | tf_op jit(solution)/shard_map/pallas_call | solution.py:350
  (22 shorter events, 0.1 us)
Async XLA Ops:
  17.7 37.6 %all-to-all-start = ((bf16[16,2,2,16,256]{4,3,2,1,0:T(8,128)(2,1)}), bf16[16,2,2,16,256]{4,3,2,1,0:T(8,128)(2,1)S(1)}, u32[]{:S(2)}, u32[]{:S(2)}) async-start(bf16[16,2,2,16,256]{4,3,2,1,0:T(8,128)(2,1)} %bitcast.29), calls=%async_computation | async-start | bytes 1048576 | tf_op jit(solution)/shard_map/all_to_all | solution.py:366
  29.9 20.7 %copy-start.1 = (bf16[256,768]{1,0:T(8,128)(2,1)S(1)}, bf16[256,768]{1,0:T(8,128)(2,1)}, u32[]{:S(2)}) copy-start(bf16[256,768]{1,0:T(8,128)(2,1)} %refs_5_.1) | copy-start | bytes 1179652
  29.9 20.7 %copy-start.2 = (bf16[1,2,8,32,256]{4,3,2,1,0:T(8,128)(2,1)S(1)}, bf16[1,2,8,32,256]{4,3,2,1,0:T(8,128)(2,1)}, u32[]{:S(2)}) copy-start(bf16[1,2,8,32,256]{4,3,2,1,0:T(8,128)(2,1)} %param.8) | copy-start | bytes 786436
  29.9 20.7 %copy-start.3 = (bf16[1,2,8,32,256]{4,3,2,1,0:T(8,128)(2,1)S(1)}, bf16[1,2,8,32,256]{4,3,2,1,0:T(8,128)(2,1)}, u32[]{:S(2)}) copy-start(bf16[1,2,8,32,256]{4,3,2,1,0:T(8,128)(2,1)} %param.7) | copy-start | bytes 786436
  29.9 20.7 %copy-start.4 = (bf16[1,2,8,32,256]{4,3,2,1,0:T(8,128)(2,1)S(1)}, bf16[1,2,8,32,256]{4,3,2,1,0:T(8,128)(2,1)}, u32[]{:S(2)}) copy-start(bf16[1,2,8,32,256]{4,3,2,1,0:T(8,128)(2,1)} %param.6) | copy-start | bytes 786436
  29.9 20.7 %copy-start.5 = (bf16[256,256]{1,0:T(8,128)(2,1)S(1)}, bf16[256,256]{1,0:T(8,128)(2,1)}, u32[]{:S(2)}) copy-start(bf16[256,256]{1,0:T(8,128)(2,1)} %refs_6_.1) | copy-start | bytes 393220
  47.8 13.1 %collective-permute-start = (bf16[2,8,16,256]{3,2,1,0:T(8,128)(2,1)}, bf16[2,8,16,256]{3,2,1,0:T(8,128)(2,1)S(1)}, u32[]{:S(2)}, u32[]{:S(2)}) collective-permute-start(bf16[2,8,16,256]{3,2,1,0:T(8,128)(2,1)} %get-tuple-element.57), channel_id=1, source_target_pairs={{0,1},{1,0},{2,3},{3,2},{4,5},{5,4},{6,7},{7,6},{8,9},{9,8},{10,11... | collective-permute-start | bytes 393224 | tf_op jit(solution)/shard_map/ppermute | solution.py:362
  48.8 12.1 %collective-permute-start.1 = (bf16[2,8,16,256]{3,2,1,0:T(8,128)(2,1)}, bf16[2,8,16,256]{3,2,1,0:T(8,128)(2,1)S(1)}, u32[]{:S(2)}, u32[]{:S(2)}) collective-permute-start(bf16[2,8,16,256]{3,2,1,0:T(8,128)(2,1)} %get-tuple-element.58), channel_id=1, source_target_pairs={{0,2},{1,3},{2,0},{3,1},{4,6},{5,7},{6,4},{7,5},{8,10},{9,11},{10,... | collective-permute-start | bytes 393224 | tf_op jit(solution)/shard_map/ppermute | solution.py:362
  49.2 11.8 %collective-permute-start.2 = (bf16[2,8,16,256]{3,2,1,0:T(8,128)(2,1)}, bf16[2,8,16,256]{3,2,1,0:T(8,128)(2,1)S(1)}, u32[]{:S(2)}, u32[]{:S(2)}) collective-permute-start(bf16[2,8,16,256]{3,2,1,0:T(8,128)(2,1)} %get-tuple-element.59), channel_id=1, source_target_pairs={{0,3},{1,2},{2,1},{3,0},{4,7},{5,6},{6,5},{7,4},{8,11},{9,10},{10,... | collective-permute-start | bytes 393224 | tf_op jit(solution)/shard_map/ppermute | solution.py:362
  50.6 0.7 copy-start.6
  54.4 0.9 copy-start.9
  55.3 5.6 %copy-start.7 = (f32[512,256]{1,0:T(8,128)}, f32[512,256]{1,0:T(8,128)S(1)}, u32[]{:S(2)}) copy-start(f32[512,256]{1,0:T(8,128)S(1)} %get-tuple-element.55) | copy-start | bytes 1572868
  55.3 0.6 copy-start
  55.9 1.1 copy-start.10
  57.0 3.9 %copy-start.11 = (bf16[2,8,16,256]{3,2,1,0:T(8,128)(2,1)S(1)}, bf16[2,8,16,256]{3,2,1,0:T(8,128)(2,1)}, u32[]{:S(2)}) copy-start(bf16[2,8,16,256]{3,2,1,0:T(8,128)(2,1)} %get-tuple-element.56.refs_0_) | copy-start | bytes 393220
  64.9 5.6 %collective-permute-start.3 = (f32[65,16,128]{2,1,0:T(8,128)S(1)}, f32[65,16,128]{2,1,0:T(8,128)S(1)}, u32[]{:S(2)}, u32[]{:S(2)}) collective-permute-start(f32[65,16,128]{2,1,0:T(8,128)S(1)} %get-tuple-element.66), channel_id=1, source_target_pairs={{0,1},{1,0},{2,3},{3,2},{4,5},{5,4},{6,7},{7,6},{8,9},{9,8},{10,11... | collective-permute-start | bytes 1597448 | tf_op jit(solution)/shard_map/ppermute | solution.py:362
  65.1 5.4 %collective-permute-start.4 = (bf16[8,2,16,256]{3,2,1,0:T(8,128)(2,1)S(1)}, bf16[8,2,16,256]{3,2,1,0:T(8,128)(2,1)S(1)}, u32[]{:S(2)}, u32[]{:S(2)}) collective-permute-start(bf16[8,2,16,256]{3,2,1,0:T(8,128)(2,1)S(1)} %get-tuple-element.68), channel_id=1, source_target_pairs={{0,8},{8,0},{16,24},{24,16},{32,40},{40,32},{48,56},{56,48},{1,9},... | collective-permute-start | bytes 393224 | tf_op jit(solution)/shard_map/ppermute | solution.py:362
  71.3 19.1 %all-to-all-start.1 = ((bf16[16,5,16,128]{3,2,1,0:T(8,128)(2,1)}), bf16[16,5,16,128]{3,2,1,0:T(8,128)(2,1)S(1)}, u32[]{:S(2)}, u32[]{:S(2)}) async-start(bf16[16,5,16,128]{3,2,1,0:T(8,128)(2,1)} %shard_map.98), calls=%async_computation.1 | async-start | bytes 655360 | tf_op jit(solution)/shard_map/all_to_all | solution.py:366
  78.1 12.3 %collective-permute-start.5 = (bf16[8,2,16,256]{3,2,1,0:T(8,128)(2,1)S(1)}, bf16[8,2,16,256]{3,2,1,0:T(8,128)(2,1)S(1)}, u32[]{:S(2)}, u32[]{:S(2)}) collective-permute-start(bf16[8,2,16,256]{3,2,1,0:T(8,128)(2,1)S(1)} %shard_map.99), channel_id=1, source_target_pairs={{0,32},{8,40},{16,48},{24,56},{32,0},{40,8},{48,16},{56,24},{1,33}... | collective-permute-start | bytes 393224 | tf_op jit(solution)/shard_map/ppermute | solution.py:362
  83.3 3.2 %collective-permute-start.6 = (bf16[8,16,256]{2,1,0:T(8,128)(2,1)S(1)}, bf16[8,16,256]{2,1,0:T(8,128)(2,1)S(1)}, u32[]{:S(2)}, u32[]{:S(2)}) collective-permute-start(bf16[8,16,256]{2,1,0:T(8,128)(2,1)S(1)} %get-tuple-element.76), channel_id=1, source_target_pairs={{0,1},{1,0},{2,3},{3,2},{4,5},{5,4},{6,7},{7,6},{8,9},{9,8},{10,11... | collective-permute-start | bytes 196616 | tf_op jit(solution)/shard_map/ppermute | solution.py:362
  84.9 3.9 %collective-permute-start.7 = (bf16[8,16,256]{2,1,0:T(8,128)(2,1)S(1)}, bf16[8,16,256]{2,1,0:T(8,128)(2,1)S(1)}, u32[]{:S(2)}, u32[]{:S(2)}) collective-permute-start(bf16[8,16,256]{2,1,0:T(8,128)(2,1)S(1)} %get-tuple-element.77), channel_id=1, source_target_pairs={{0,2},{1,3},{2,0},{3,1},{4,6},{5,7},{6,4},{7,5},{8,10},{9,11},{10,... | collective-permute-start | bytes 196616 | tf_op jit(solution)/shard_map/ppermute | solution.py:362
  86.5 4.0 %collective-permute-start.8 = (bf16[8,16,256]{2,1,0:T(8,128)(2,1)S(1)}, bf16[8,16,256]{2,1,0:T(8,128)(2,1)S(1)}, u32[]{:S(2)}, u32[]{:S(2)}) collective-permute-start(bf16[8,16,256]{2,1,0:T(8,128)(2,1)S(1)} %get-tuple-element.78), channel_id=1, source_target_pairs={{0,3},{1,2},{2,1},{3,0},{4,7},{5,6},{6,5},{7,4},{8,11},{9,10},{10,... | collective-permute-start | bytes 196616 | tf_op jit(solution)/shard_map/ppermute | solution.py:362
  91.2 13.0 %all-to-all-start.2 = ((bf16[8,5,16,128]{3,2,1,0:T(8,128)(2,1)}), bf16[8,5,16,128]{3,2,1,0:T(8,128)(2,1)S(1)}, u32[]{:S(2)}, u32[]{:S(2)}) async-start(bf16[8,5,16,128]{3,2,1,0:T(8,128)(2,1)} %shard_map.100), calls=%async_computation.2 | async-start | bytes 327680 | tf_op jit(solution)/shard_map/all_to_all | solution.py:366
  95.8 5.3 %collective-permute-start.9 = (bf16[8,2,16,256]{3,2,1,0:T(8,128)(2,1)S(1)}, bf16[8,2,16,256]{3,2,1,0:T(8,128)(2,1)S(1)}, u32[]{:S(2)}, u32[]{:S(2)}) collective-permute-start(bf16[8,2,16,256]{3,2,1,0:T(8,128)(2,1)S(1)} %shard_map.101), channel_id=1, source_target_pairs={{0,4},{4,0},{1,5},{5,1},{2,6},{6,2},{3,7},{7,3},{8,12},{12,8},{9,1... | collective-permute-start | bytes 393224 | tf_op jit(solution)/shard_map/ppermute | solution.py:362
  104.9 19.2 %copy-start.8 = (f32[512,256]{1,0:T(8,128)S(1)}, f32[512,256]{1,0:T(8,128)}, u32[]{:S(2)}) copy-start(f32[512,256]{1,0:T(8,128)} %copy-done.7) | copy-start | bytes 1572868
  105.0 14.0 %all-to-all-start.3 = ((bf16[16,4,16,128]{3,2,1,0:T(8,128)(2,1)}), bf16[16,4,16,128]{3,2,1,0:T(8,128)(2,1)S(1)}, u32[]{:S(2)}, u32[]{:S(2)}) async-start(bf16[16,4,16,128]{3,2,1,0:T(8,128)(2,1)} %get-tuple-element.91), calls=%async_computation.3 | async-start | bytes 524288 | tf_op jit(solution)/shard_map/all_to_all | solution.py:366
  111.4 6.1 %collective-permute-start.10 = (bf16[8,2,16,256]{3,2,1,0:T(8,128)(2,1)S(1)}, bf16[8,2,16,256]{3,2,1,0:T(8,128)(2,1)S(1)}, u32[]{:S(2)}, u32[]{:S(2)}) collective-permute-start(bf16[8,2,16,256]{3,2,1,0:T(8,128)(2,1)S(1)} %shard_map.103), channel_id=1, source_target_pairs={{0,16},{8,24},{16,0},{24,8},{32,48},{40,56},{48,32},{56,40},{1,17}... | collective-permute-start | bytes 393224 | tf_op jit(solution)/shard_map/ppermute | solution.py:362
  118.9 6.9 %collective-permute-start.11 = (bf16[64,16,128]{2,1,0:T(8,128)(2,1)S(1)}, bf16[64,16,128]{2,1,0:T(8,128)(2,1)S(1)}, u32[]{:S(2)}, u32[]{:S(2)}) collective-permute-start(bf16[64,16,128]{2,1,0:T(8,128)(2,1)S(1)} %bitcast.14), channel_id=1, source_target_pairs={{0,1},{1,0},{2,3},{3,2},{4,5},{5,4},{6,7},{7,6},{8,9},{9,8},{10,11... | collective-permute-start | bytes 786440 | tf_op jit(solution)/shard_map/ppermute | solution.py:362

commit v4 on v3

--- a/solution.py
+++ b/solution.py
@@ -21,12 +21,12 @@
 PENCILS = 16
 ROWS = 16
 LANES = 128
+HALF = 32
 TILES = 64
 BF16 = jnp.bfloat16
 F32 = jnp.float32
 VMEM = pl.BlockSpec(memory_space=pltpu.VMEM)
 HBM = pl.BlockSpec(memory_space=pltpu.HBM)
-SMEM = pl.BlockSpec(memory_space=pltpu.SMEM)
 PLANE = ("y", "xh", "xl")
 FIRST = ("z", "xh")
 SECOND = ("xl", "c")
@@ -168,40 +168,43 @@
 ]
 
 
-def first_pieces_kernel(tokens, cotangent, pieces, sem):
-    copies = []
+def along_second():
+    return lax.axis_index("xl") * 2 + lax.axis_index("c")
+
+
+def along_first():
+    return lax.axis_index("z") * 2 + lax.axis_index("xh")
+
+
+def pieces_kernel(tokens, cotangent, to_first, *rest):
+    to_second, (held, sem) = rest[:4], rest[4:]
+    loads, firsts, seconds = [], [], []
     for kind, ref in enumerate((tokens, cotangent)):
+        at = kind * 9
+        loads.append(pltpu.make_async_copy(ref, held.at[kind], sem.at[at]))
         for x in range(2):
             for z in range(2):
-                copies.append(
-                    pltpu.make_async_copy(
-                        ref.at[x, :, pl.ds(z * ROWS, ROWS), :],
-                        pieces.at[:, z, kind, x],
-                        sem.at[len(copies)],
-                    )
+                source = held.at[kind, x, :, pl.ds(z * ROWS, ROWS), :]
+                target = to_first.at[:, z, kind, x]
+                firsts.append(
+                    (kind, pltpu.make_async_copy(source, target, sem.at[at + 1 + x * 2 + z]))
                 )
-    for copy in copies:
-        copy.start()
-    for copy in copies:
-        copy.wait()
-
-
-def second_pieces_kernel(place, tokens, cotangent, *rest):
-    pieces, sem = rest[:4], rest[4]
-    copies = []
-    for mask, out in enumerate(pieces):
-        peer = place[1] ^ mask
-        rows = pl.ds(pl.multiple_of((peer & 1) * ROWS, ROWS), ROWS)
-        for kind, ref in enumerate((tokens, cotangent)):
-            copies.append(
-                pltpu.make_async_copy(
-                    ref.at[peer >> 1, :, rows, :], out.at[kind], sem.at[len(copies)]
-                )
+        for mask, out in enumerate(to_second):
+            peer = along_second() ^ mask
+            rows = pl.ds(pl.multiple_of((peer & 1) * ROWS, ROWS), ROWS)
+            source = held.at[kind, peer >> 1, :, rows, :]
+            seconds.append(
+                (kind, pltpu.make_async_copy(source, out.at[kind], sem.at[at + 5 + mask]))
             )
-    for copy in copies:
-        copy.start()
-    for copy in copies:
-        copy.wait()
+    for load in loads:
+        load.start()
+    for now, load in enumerate(loads):
+        load.wait()
+        for kind, store in firsts + seconds:
+            if kind == now:
+                store.start()
+    for _, store in firsts + seconds:
+        store.wait()
 
 
 def third_kernel(
@@ -217,54 +220,57 @@
     out_out[...] = dot(attn[...], cot, 0, 0)
 
 
-def first_kernel(
-    place, pieces, gain, w_qkv, w_out, qkv_in, gain_in, stay, leave, qkv_out, gain_out, *scratch
-):
-    returned = scratch[-1]
-    tokens = pieces[:, 0].reshape(TOKENS, WIDTH)
-    cot = pieces[:, 1].reshape(TOKENS, WIDTH)
-    grad_normed, part_qkv, part_gain = axis_grads(
-        tokens, cot, gain[...], w_qkv[...], w_out[...], scratch[:-1], True
-    )
-    returned[...] = grad_normed.astype(BF16).reshape(returned.shape)
-    here = place[2]
-    for at, mask in enumerate(SPANS[3]):
-        stay[at] = returned[here ^ mask]
-        leave[at] = returned[here ^ mask ^ BITS[0]]
-    qkv_out[...] = qkv_in[...] + part_qkv
-    gain_out[...] = gain_in[...] + part_gain
-
-
-def second_kernel(place, *refs):
-    pieces, (gain, w_qkv, w_out, qkv_in, out_in, gain_in) = refs[:4], refs[4:10]
-    back, (own, other), scratch, halves = refs[10:14], refs[14:16], refs[16:-1], refs[-1]
-    tokens = jnp.concatenate([piece[0].reshape(-1, WIDTH) for piece in pieces], axis=0)
-    cot = jnp.concatenate([piece[1].reshape(-1, WIDTH) for piece in pieces], axis=0)
-    grad_normed, part_qkv, part_gain = axis_grads(
-        tokens, cot, gain[...], w_qkv[...], w_out[...], scratch, True
-    )
-    returned = grad_normed.astype(BF16)
-    rows = TOKENS // 4
-    for mask, out in enumerate(back):
-        out[...] = returned[mask * rows : (mask + 1) * rows].reshape(out.shape)
-    total = qkv_in[...] + part_qkv
+def pack(total, part_out, part_gain, halves, own, low, high):
     for at in range(2 * TILES):
         half, tile = divmod(at, TILES)
         if at < 96:
             row, col = divmod(at, 6)
             halves[half, tile] = total[row * 16 : row * 16 + 16, col * LANES : (col + 1) * LANES]
+        elif part_out is None:
+            halves[half, tile] = jnp.zeros((16, LANES), F32)
         else:
             row, col = divmod(at - 96, 2)
-            halves[half, tile] = out_in[row * 16 : row * 16 + 16, col * LANES : (col + 1) * LANES]
-    mine = place[0]
+            halves[half, tile] = part_out[row * 16 : row * 16 + 16, col * LANES : (col + 1) * LANES]
+    mine = lax.axis_index("c")
     own[0:TILES] = halves[mine]
-    other[0:TILES] = halves[1 - mine]
-    part_gain = gain_in[...] + part_gain
+    low[0:HALF] = halves[1 - mine, 0:HALF].astype(BF16)
+    high[0:HALF] = halves[1 - mine, HALF:TILES].astype(BF16)
     gains = jnp.concatenate(
         [part_gain[:, :LANES], part_gain[:, LANES:], jnp.zeros((14, LANES), F32)], axis=0
     )
     own[TILES] = gains
-    other[TILES] = gains
+    high[HALF] = gains.astype(BF16)
+
+
+def second_kernel(*refs):
+    pieces, (gain, w_qkv, w_out), parts = refs[:4], refs[4:7], refs[7:10]
+    back, packed, scratch, halves = refs[10:14], refs[14:17], refs[17:-1], refs[-1]
+    tokens = jnp.concatenate([piece[0].reshape(-1, WIDTH) for piece in pieces], axis=0)
+    cot = jnp.concatenate([piece[1].reshape(-1, WIDTH) for piece in pieces], axis=0)
+    grad_normed, part_qkv, part_gain = axis_grads(
+        tokens, cot, gain[...], w_qkv[...], w_out[...], scratch, True
+    )
+    returned = grad_normed.astype(BF16)
+    rows = TOKENS // 4
+    for mask, out in enumerate(back):
+        out[...] = returned[mask * rows : (mask + 1) * rows].reshape(out.shape)
+    third_qkv, part_out, third_gain = parts
+    pack(third_qkv[...] + part_qkv, part_out, third_gain[...] + part_gain, halves, *packed)
+
+
+def first_kernel(pieces, gain, w_qkv, w_out, *refs):
+    (stay, leave), packed, scratch, (returned, halves) = refs[:2], refs[2:5], refs[5:-2], refs[-2:]
+    tokens = pieces[:, 0].reshape(TOKENS, WIDTH)
+    cot = pieces[:, 1].reshape(TOKENS, WIDTH)
+    grad_normed, part_qkv, part_gain = axis_grads(
+        tokens, cot, gain[...], w_qkv[...], w_out[...], scratch, True
+    )
+    returned[...] = grad_normed.astype(BF16).reshape(returned.shape)
+    here = along_first()
+    for at, mask in enumerate(SPANS[3]):
+        stay[at] = returned[here ^ mask]
+        leave[at] = returned[here ^ mask ^ BITS[0]]
+    pack(part_qkv, None, part_gain, halves, *packed)
 
 
 def stage_kernel(*refs):
@@ -279,13 +285,26 @@
                 at += 1
 
 
-def pair_kernel(own, received, pieces):
+def pair_kernel(*refs):
+    sources, pieces = (refs[0:3], refs[3:6]), refs[6]
+
+    def summed(tiles):
+        half, at = divmod(tiles.start, HALF)
+        if tiles.start == TILES:
+            half, at = 1, HALF
+        total = None
+        for own, low, high in sources:
+            mine = own[tiles]
+            if tiles.start == TILES:
+                mine = mine.astype(BF16).astype(F32)
+            part = mine + (low, high)[half][at : at + tiles.stop - tiles.start].astype(F32)
+            total = part if total is None else total + part
+        return total.astype(BF16)
+
+    gains = summed(slice(TILES, TILES + 1))
     for peer in range(16):
-        tiles = slice(peer * 4, peer * 4 + 4)
-        pieces[peer, 0:4] = (own[tiles] + received[tiles]).astype(BF16)
-    gains = (own[TILES] + received[TILES]).astype(BF16)
-    for peer in range(16):
-        pieces[peer, 4] = gains
+        pieces[peer, 0:4] = summed(slice(peer * 4, peer * 4 + 4))
+        pieces[peer, 4:5] = gains
 
 
 def plane_kernel(received, pieces):
@@ -302,8 +321,8 @@
     gain_out[...] = jnp.concatenate([total[4, 0:1], total[4, 1:2]], axis=1)
 
 
-def assemble_kernel(place, mine, theirs, w_qkv_out, w_out_out, halves):
-    at_core = place[0]
+def assemble_kernel(mine, theirs, w_qkv_out, w_out_out, halves):
+    at_core = lax.axis_index("c")
     halves[at_core] = mine[...]
     halves[1 - at_core] = theirs[...]
     for at in range(2 * TILES):
@@ -317,17 +336,17 @@
             w_out_out[row * 16 : row * 16 + 16, col * LANES : (col + 1) * LANES] = rows
 
 
-def tokens_kernel(place, tokens, gain, third, *rest):
+def tokens_kernel(tokens, gain, third, *rest):
     groups, seconds = rest[:5], rest[5:9]
     out, from_first, from_second = rest[9:]
-    here = place[2]
+    here = along_first()
     from_first[here] = groups[0][0]
     for stage in range(4):
         span = 8 >> stage
         for at, mask in enumerate(sources_before(stage)):
             from_first[here ^ (mask ^ BITS[stage])] = groups[stage + 1][at * span]
     for mask, ref in enumerate(seconds):
-        from_second[place[1] ^ mask] = ref[...]
+        from_second[along_second() ^ mask] = ref[...]
     for x in range(2):
         for y in range(8):
             tokens_f = tokens[x, y].astype(F32)
@@ -335,10 +354,10 @@
             second = jnp.concatenate([from_second[x * 2, y], from_second[x * 2 + 1, y]], axis=0)
             grad_normed = third[x, y] + first.astype(F32) + second.astype(F32)
             square = jnp.mean(tokens_f * tokens_f, axis=-1, keepdims=True) + EPSILON
-            root = jnp.sqrt(square)
+            inverse = lax.rsqrt(square)
             gained = gain[...] * grad_normed
             inner = jnp.sum(gained * tokens_f, axis=-1, keepdims=True)
-            result = gained / root - tokens_f * (inner / (WIDTH * root * square))
+            result = gained * inverse - tokens_f * (inner * inverse / (WIDTH * square))
             out[x, y] = result.astype(BF16)
 
 
@@ -346,11 +365,11 @@
     return jax.ShapeDtypeStruct(dims, dtype)
 
 
-def kernel_call(body, outs, operands, us, scratch=(), scalars=0, space=VMEM):
+def kernel_call(body, outs, operands, us, scratch=(), space=VMEM):
     return pl.pallas_call(
         body,
         out_shape=outs,
-        in_specs=[SMEM] * scalars + [space] * (len(operands) - scalars),
+        in_specs=[space] * len(operands),
         out_specs=jax.tree.map(lambda _: space, outs),
         scratch_shapes=list(scratch),
         compiler_params=params(62 if space is HBM else 48),
@@ -367,35 +386,22 @@
 
 
 def on_device(count, tokens, attn, cotangent, gain, w_qkv, w_out):
-    core = lax.axis_index("c")
-    along_second = lax.axis_index("xl") * 2 + core
-    along_first = lax.axis_index("z") * 2 + lax.axis_index("xh")
-    place = jnp.stack([core, along_second, along_first]).astype(jnp.int32)
     gain_row = gain.reshape(1, WIDTH)
     local = tokens[0]
     upstream = cotangent[0]
     flat = (TOKENS, WIDTH)
     tile = (16, LANES)
-    to_first = kernel_call(
-        first_pieces_kernel,
-        shape((8, 2, 2, 2, ROWS, WIDTH), BF16),
+    to_first, *to_second = kernel_call(
+        pieces_kernel,
+        (shape((8, 2, 2, 2, ROWS, WIDTH), BF16),) + (shape((2, 8, ROWS, WIDTH), BF16),) * 4,
         (local, upstream),
         2,
-        [pltpu.SemaphoreType.DMA((8,))],
+        [pltpu.VMEM((2, *local.shape), BF16), pltpu.SemaphoreType.DMA((18,))],
         space=HBM,
     )
     at_first = exchange(to_first.reshape(16, 2, 2, ROWS, WIDTH), FIRST)
-    to_second = kernel_call(
-        second_pieces_kernel,
-        (shape((2, 8, ROWS, WIDTH), BF16),) * 4,
-        (place, local, upstream),
-        2,
-        [pltpu.SemaphoreType.DMA((8,))],
-        1,
-        HBM,
-    )
     at_second = [to_second[0]] + [swap(to_second[m], SECOND, m, 4) for m in (1, 2, 3)]
-    third, part_qkv, part_out, part_gain = kernel_call(
+    third, third_qkv, part_out, third_gain = kernel_call(
         third_kernel,
         (
             shape(flat, F32),
@@ -407,71 +413,61 @@
         5,
         SCRATCH,
     )
+    packed = (
+        shape((TILES + 1, *tile), F32),
+        shape((HALF, *tile), BF16),
+        shape((HALF + 1, *tile), BF16),
+    )
+    halves = pltpu.VMEM((2, TILES, *tile), F32)
+    *back, own, low, high = kernel_call(
+        second_kernel,
+        (shape((8, ROWS, WIDTH), BF16),) * 4 + packed,
+        (*at_second, gain_row, w_qkv, w_out, third_qkv, part_out, third_gain),
+        5,
+        SCRATCH + [halves],
+    )
+    from_second = [back[0]] + [swap(back[m], SECOND, m, 4) for m in (1, 2, 3)]
+    early = [own, swap(low, "c", 1, 2), swap(high, "c", 1, 2)]
     block = (2, ROWS, WIDTH)
-    stay, leave, part_qkv, part_gain = kernel_call(
+    stay, leave, own, low, high = kernel_call(
         first_kernel,
-        (
-            shape((8, *block), BF16),
-            shape((8, *block), BF16),
-            shape((WIDTH, TRIPLE), F32),
-            shape((1, WIDTH), F32),
-        ),
-        (place, at_first, gain_row, w_qkv, w_out, part_qkv, part_gain),
+        (shape((8, *block), BF16),) * 2 + packed,
+        (at_first, gain_row, w_qkv, w_out),
         5,
-        SCRATCH + [pltpu.VMEM((16, *block), BF16)],
-        1,
-    )
+        SCRATCH + [pltpu.VMEM((16, *block), BF16), halves],
+    )
+    low, high, early, from_second = lax.optimization_barrier((low, high, early, from_second))
+    late = [own, swap(low, "c", 1, 2), swap(high, "c", 1, 2)]
     groups = [stay, swap(leave, *SWAPS[0])]
-    *back, own, other = kernel_call(
-        second_kernel,
-        (shape((8, ROWS, WIDTH), BF16),) * 4 + (shape((TILES + 1, *tile), F32),) * 2,
-        (place, *at_second, gain_row, w_qkv, w_out, part_qkv, part_out, part_gain),
-        5,
-        SCRATCH + [pltpu.VMEM((2, TILES, *tile), F32)],
-        1,
-    )
-    received = swap(other, "c", 1, 2)
-    pieces = kernel_call(pair_kernel, shape((16, 5, *tile), BF16), (own, received), 1)
-    leave = kernel_call(stage_kernel, shape((8, *block), BF16), groups, 1)
-    pieces, leave, *back = lax.optimization_barrier((pieces, leave, *back))
+    for stage in (1, 2, 3):
+        leave = kernel_call(stage_kernel, shape((8, *block), BF16), groups, 20)
+        groups.append(swap(leave, *SWAPS[stage]))
+    pieces = kernel_call(pair_kernel, shape((16, 5, *tile), BF16), (*early, *late), 1)
     summed = exchange(pieces, PLANE)
-    from_second = [back[0]] + [swap(back[m], SECOND, m, 4) for m in (1, 2, 3)]
-    groups.append(swap(leave, *SWAPS[1]))
-    summed, groups, from_second = lax.optimization_barrier((summed, groups, from_second))
     pieces = kernel_call(plane_kernel, shape((8, 5, *tile), BF16), (summed,), 1)
-    leave = kernel_call(stage_kernel, shape((8, *block), BF16), groups, 1)
-    pieces, leave = lax.optimization_barrier((pieces, leave))
     summed = exchange(pieces, "z")
-    groups.append(swap(leave, *SWAPS[2]))
-    summed, groups = lax.optimization_barrier((summed, groups))
     pieces, d_gain = kernel_call(
         functools.partial(line_kernel, 1.0 / math.sqrt(count)),
         (shape((16, 4, *tile), BF16), shape((1, WIDTH), F32)),
         (summed,),
         1,
     )
-    leave = kernel_call(stage_kernel, shape((8, *block), BF16), groups, 1)
-    pieces, leave = lax.optimization_barrier((pieces, leave))
     mine = exchange(pieces, PLANE)
-    groups.append(swap(leave, *SWAPS[3]))
-    mine, groups = lax.optimization_barrier((mine, groups))
     mine = mine.reshape(TILES, *tile)
     theirs = swap(mine, "c", 1, 2)
     d_w_qkv, d_w_out = kernel_call(
         assemble_kernel,
         (shape((WIDTH, TRIPLE), F32), shape((WIDTH, WIDTH), F32)),
-        (place, mine, theirs),
+        (mine, theirs),
         1,
         [pltpu.VMEM((2, TILES, *tile), BF16)],
-        1,
     )
     d_tokens = kernel_call(
         tokens_kernel,
         shape(local.shape, BF16),
-        (place, local, gain_row, third.reshape(local.shape), *groups, *from_second),
+        (local, gain_row, third.reshape(local.shape), *groups, *from_second),
         2,
         [pltpu.VMEM((16, *block), BF16), pltpu.VMEM((4, 8, ROWS, WIDTH), BF16)],
-        1,
     )
     return (d_tokens[None], d_w_qkv, d_w_out, d_gain.reshape(WIDTH))
 

time: 128 us -> 92.7 us (0.72)
  Pallas kernels: 51.4 us -> 16.7 us
  waiting for transfers between devices: 20.9 us -> 22.3 us
    pallas_call x13 -> x12, Pallas kernels: 51.4 us -> 16.7 us  [kernel_call(): pl.pallas_call(body, out_shape=outs, in_specs=[space] * len(operands), ou...]
    all_to_all x4, waiting for transfers between devices: 4.5 us -> 16.8 us  [exchange(): return lax.all_to_all(pieces, axes, split_axis=0, concat_axis=0, tiled=True)]
    ppermute x12 -> x15, waiting for transfers between devices: 16.4 us -> 5.55 us  [swap(): return lax.ppermute(array, axis, [(i, i ^ mask) for i in range(size)])]
    unnamed x24 -> x18, local copies, waits for them, and re-layouts: 3.29 us -> 2.52 us
    ppermute x12 -> x15, starting transfers between devices: 21 us -> 20.7 us  [swap(): return lax.ppermute(array, axis, [(i, i ^ mask) for i in range(size)])]
  transfers between devices with their start and end apart: 16 -> 19, of which waited for: 7 -> 5; matrix products, arithmetic and copies ran while one was open for 0% -> 0% of each run, Pallas kernels for 21% -> 15%
where the time goes in v4:
time: 92.7 us; the launch traced here: 92.2 us
  starting transfers between devices  49.8 us (54%)
  waiting for transfers between devices  22.3 us (24%)
  Pallas kernels  16.7 us (18%)
  local copies, waits for them, and re-layouts  2.52 us (3%)
    all_to_all x4, starting transfers between devices, exchange(): return lax.all_to_all(pieces, axes, split_axis=0, concat_axis=0, tiled=True)  29.2 us
    ppermute x15, starting transfers between devices, swap(): return lax.ppermute(array, axis, [(i, i ^ mask) for i in range(size)])  20.7 us
    all_to_all x4, waiting for transfers between devices, exchange(): return lax.all_to_all(pieces, axes, split_axis=0, concat_axis=0, tiled=True)  16.8 us
    pallas_call x12, Pallas kernels, kernel_call(): pl.pallas_call(body, out_shape=outs, in_specs=[space] * len(operands), ou...  16.7 us
    ppermute x15, waiting for transfers between devices, swap(): return lax.ppermute(array, axis, [(i, i ^ mask) for i in range(size)])  5.55 us
    unnamed x18, local copies, waits for them, and re-layouts  2.52 us
  transfers between devices with their start and end apart: 19, of which 5 were waited for; matrix products, arithmetic and copies ran while one was open for 0% of the time, Pallas kernels for 15%

profile of v4, /device:TPU:1, one launch (start us, length us, event | category | flops | bytes accessed | tf_op | source)
XLA Modules:
  0.0 92.2 jit_solution(12047881337862288439)
XLA Ops:
  0.6 2.1 %shard_map.94 = (bf16[8,2,2,2,16,256]{5,4,3,2,1,0:T(8,128)(2,1)}, bf16[2,8,16,256]{3,2,1,0:T(8,128)(2,1)}, bf16[2,8,16,256]{3,2,1,0:T(8,128)(2,1)}, bf16[2,8,16,...) custom-call(bf16[2,8,32,256]{3,2,1,0:T(8,128)(2,1)} %bitcast.16, bf16[2,8,32,256]{3,2,1,0:T(8,128)(2,1)} %bitcast.13), custom_call_target="tpu_custom_call" | custom-call | flops 1600000000 | bytes 4000000 | tf_op jit(solution)/shard_map/pallas_call | solution.py:369
  2.8 0.0 copy-start
  2.8 0.0 copy-start.1
  2.8 0.0 copy-start.2
  2.8 0.0 copy-start.4
  2.8 11.7 %all-to-all-start = ((bf16[16,2,2,16,256]{4,3,2,1,0:T(8,128)(2,1)}), bf16[16,2,2,16,256]{4,3,2,1,0:T(8,128)(2,1)S(1)}, u32[]{:S(2)}, u32[]{:S(2)}) async-start(bf16[16,2,2,16,256]{4,3,2,1,0:T(8,128)(2,1)} %bitcast.24), calls=%async_computation | async-start | bytes 1048576 | tf_op jit(solution)/shard_map/all_to_all | solution.py:385
  14.5 1.0 %collective-permute-start.4 = (bf16[2,8,16,256]{3,2,1,0:T(8,128)(2,1)}, bf16[2,8,16,256]{3,2,1,0:T(8,128)(2,1)S(1)}, u32[]{:S(2)}, u32[]{:S(2)}) collective-permute-start(bf16[2,8,16,256]{3,2,1,0:T(8,128)(2,1)} %get-tuple-element.45), channel_id=1, source_target_pairs={{0,1},{1,0},{2,3},{3,2},{4,5},{5,4},{6,7},{7,6},{8,9},{9,8},{10,11... | collective-permute-start | bytes 393224 | tf_op jit(solution)/shard_map/ppermute | solution.py:381
  15.6 0.3 collective-permute-start.5
  15.9 1.4 %collective-permute-start.6 = (bf16[2,8,16,256]{3,2,1,0:T(8,128)(2,1)}, bf16[2,8,16,256]{3,2,1,0:T(8,128)(2,1)S(1)}, u32[]{:S(2)}, u32[]{:S(2)}) collective-permute-start(bf16[2,8,16,256]{3,2,1,0:T(8,128)(2,1)} %get-tuple-element.47), channel_id=1, source_target_pairs={{0,3},{1,2},{2,1},{3,0},{4,7},{5,6},{6,5},{7,4},{8,11},{9,10},{10,... | collective-permute-start | bytes 393224 | tf_op jit(solution)/shard_map/ppermute | solution.py:381
  17.3 0.6 copy-done.5
  18.0 3.2 %shard_map.93 = (f32[512,256]{1,0:T(8,128)S(1)}, f32[256,768]{1,0:T(8,128)S(1)}, f32[256,256]{1,0:T(8,128)S(1)}, f32[1,256]{1,0:T(1,128)S(1)}) custom-call(bf16[512,256]{1,0:T(8,128)(2,1)S(1)} %bitcast.17, bf16[512,256]{1,0:T(8,128)(2,1)S(1)} %bitcast.14, bf16[512,256]{1,0:T(8,128)(2,1)S(1)} %bitcast.15, f32[1,256]{1,0:T(1,128)S(1)} %bitcast.19, ...), custom_call_target="tpu_custom_call" | custom-call | flops 4000000000 | bytes 10000000 | tf_op jit(solution)/shard_map/pallas_call | solution.py:369
  21.2 0.0 collective-permute-done.4.refs_1_
  21.2 0.0 collective-permute-done.5.refs_2_
  21.2 5.4 %collective-permute-done.6.refs_3_ = bf16[2,8,16,256]{3,2,1,0:T(8,128)(2,1)S(1)} collective-permute-done((bf16[2,8,16,256]{3,2,1,0:T(8,128)(2,1)}, bf16[2,8,16,256]{3,2,1,0:T(8,128)(2,1)S(1)}, u32[]{:S(2)}, u32[]{:S(2)}) %collective-permute-start.6) | collective-permute-done | bytes 131104 | tf_op jit(solution)/shard_map/ppermute | solution.py:381
  26.6 3.5 %shard_map.99 = (bf16[8,16,256]{2,1,0:T(8,128)(2,1)S(1)}, bf16[8,16,256]{2,1,0:T(8,128)(2,1)S(1)}, bf16[8,16,256]{2,1,0:T(8,128)(2,1)S(1)}, bf16[8,16,256]{2,1,0...) custom-call(bf16[2,8,16,256]{3,2,1,0:T(8,128)(2,1)S(1)} %copy-done.8, ...), custom_call_target="tpu_custom_call" | custom-call | flops 4000000000 | bytes 10000000 | tf_op jit(solution)/shard_map/pallas_call | solution.py:369
  30.1 0.0 copy-start.6
  30.1 0.8 copy-done.6
  30.9 0.5 collective-permute-start.7
  31.4 0.0 collective-permute-start.10
  31.4 1.6 %collective-permute-start.11 = (bf16[8,16,256]{2,1,0:T(8,128)(2,1)S(1)}, bf16[8,16,256]{2,1,0:T(8,128)(2,1)S(1)}, u32[]{:S(2)}, u32[]{:S(2)}) collective-permute-start(bf16[8,16,256]{2,1,0:T(8,128)(2,1)S(1)} %get-tuple-element.57), channel_id=1, source_target_pairs={{0,3},{1,2},{2,1},{3,0},{4,7},{5,6},{6,5},{7,4},{8,11},{9,10},{10,... | collective-permute-start | bytes 196616 | tf_op jit(solution)/shard_map/ppermute | solution.py:381
  33.0 0.2 collective-permute-start.9
  33.3 3.4 %shard_map.95 = (bf16[8,2,16,256]{3,2,1,0:T(8,128)(2,1)S(1)}, bf16[8,2,16,256]{3,2,1,0:T(8,128)(2,1)S(1)}, f32[65,16,128]{2,1,0:T(8,128)S(1)}, bf16[32,16,128]{2,1,0:T(8,128)(2,1)S(1)}, bf16[33,16,128]{2,1,0:T(8,128)(2,1)S(1)}) custom-call(bf16[16,2,2,16,256]{4,3,2,1,0:T(8,128)(2,1)S(1)} %all-to-all-done.pieces, f32[1,256]{1,0:T(1,128)S(1)} %bitcast.21, ...), custom_call_target="tpu_custom_call" | custom-call | flops 4000000000 | bytes 10000000 | tf_op jit(solution)/shard_map/pallas_call | solution.py:369
  36.7 0.0 collective-permute-done.10.rest_7_
  36.7 0.0 collective-permute-done.11.rest_8_
  36.7 0.0 collective-permute-done.7.refs_1_
  36.8 0.0 collective-permute-done.8.refs_2_
  36.8 1.0 %collective-permute-start.13 = (bf16[33,16,128]{2,1,0:T(8,128)(2,1)S(1)}, bf16[33,16,128]{2,1,0:T(8,128)(2,1)S(1)}, u32[]{:S(2)}, u32[]{:S(2)}) collective-permute-start(bf16[33,16,128]{2,1,0:T(8,128)(2,1)S(1)} %get-tuple-element.67), channel_id=1, source_target_pairs={{0,1},{1,0},{2,3},{3,2},{4,5},{5,4},{6,7},{7,6},{8,9},{9,8},{10,11... | collective-permute-start | bytes 405512 | tf_op jit(solution)/shard_map/ppermute | solution.py:381
  37.7 0.1 collective-permute-start.12
  37.8 2.7 %collective-permute-start = (bf16[8,2,16,256]{3,2,1,0:T(8,128)(2,1)S(1)}, bf16[8,2,16,256]{3,2,1,0:T(8,128)(2,1)S(1)}, u32[]{:S(2)}, u32[]{:S(2)}) collective-permute-start(bf16[8,2,16,256]{3,2,1,0:T(8,128)(2,1)S(1)} %get-tuple-element.41), channel_id=1, source_target_pairs={{0,8},{8,0},{16,24},{24,16},{32,40},{40,32},{48,56},{56,48},{1,9},... | collective-permute-start | bytes 393224 | tf_op jit(solution)/shard_map/ppermute | solution.py:381
  40.5 1.0 %copy-done.7 = f32[65,16,128]{2,1,0:T(8,128)S(1)} copy-done((f32[65,16,128]{2,1,0:T(8,128)S(1)}, f32[65,16,128]{2,1,0:T(8,128)}, u32[]{:S(2)}) %copy-start.7) | copy-done | bytes 532504
  41.6 0.9 shard_map.101
  42.4 5.0 %all-to-all-start.1 = ((bf16[16,5,16,128]{3,2,1,0:T(8,128)(2,1)}), bf16[16,5,16,128]{3,2,1,0:T(8,128)(2,1)S(1)}, u32[]{:S(2)}, u32[]{:S(2)}) async-start(bf16[16,5,16,128]{3,2,1,0:T(8,128)(2,1)} %shard_map.101), calls=%async_computation.1 | async-start | bytes 655360 | tf_op jit(solution)/shard_map/all_to_all | solution.py:385
  47.5 7.6 %collective-permute-start.1 = (bf16[8,2,16,256]{3,2,1,0:T(8,128)(2,1)S(1)}, bf16[8,2,16,256]{3,2,1,0:T(8,128)(2,1)S(1)}, u32[]{:S(2)}, u32[]{:S(2)}) collective-permute-start(bf16[8,2,16,256]{3,2,1,0:T(8,128)(2,1)S(1)} %shard_map.96), channel_id=1, source_target_pairs={{0,32},{8,40},{16,48},{24,56},{32,0},{40,8},{48,16},{56,24},{1,33}... | collective-permute-start | bytes 393224 | tf_op jit(solution)/shard_map/ppermute | solution.py:381
  55.1 1.3 %all-to-all-done.1.received = bf16[16,5,16,128]{3,2,1,0:T(8,128)(2,1)S(1)} async-done(((bf16[16,5,16,128]{3,2,1,0:T(8,128)(2,1)}), bf16[16,5,16,128]{3,2,1,0:T(8,128)(2,1)S(1)}, u32[]{:S(2)}, u32[]{:S(2)}) %all-to-all-start.1) | async-done | bytes 327712 | tf_op jit(solution)/shard_map/all_to_all | solution.py:385
  56.4 0.7 shard_map.102
  57.1 8.9 %all-to-all-start.2 = ((bf16[8,5,16,128]{3,2,1,0:T(8,128)(2,1)}), bf16[8,5,16,128]{3,2,1,0:T(8,128)(2,1)S(1)}, u32[]{:S(2)}, u32[]{:S(2)}) async-start(bf16[8,5,16,128]{3,2,1,0:T(8,128)(2,1)} %shard_map.102), calls=%async_computation.2 | async-start | bytes 327680 | tf_op jit(solution)/shard_map/all_to_all | solution.py:385
  66.0 0.3 collective-permute-start.2
  66.4 8.0 %all-to-all-done.2.received = bf16[8,5,16,128]{3,2,1,0:T(8,128)(2,1)S(1)} async-done(((bf16[8,5,16,128]{3,2,1,0:T(8,128)(2,1)}), bf16[8,5,16,128]{3,2,1,0:T(8,128)(2,1)S(1)}, u32[]{:S(2)}, u32[]{:S(2)}) %all-to-all-start.2) | async-done | bytes 163872 | tf_op jit(solution)/shard_map/all_to_all | solution.py:385
  74.4 0.7 shard_map.103
  75.1 3.5 %all-to-all-start.3 = ((bf16[16,4,16,128]{3,2,1,0:T(8,128)(2,1)}), bf16[16,4,16,128]{3,2,1,0:T(8,128)(2,1)S(1)}, u32[]{:S(2)}, u32[]{:S(2)}) async-start(bf16[16,4,16,128]{3,2,1,0:T(8,128)(2,1)} %get-tuple-element.68), calls=%async_computation.3 | async-start | bytes 524288 | tf_op jit(solution)/shard_map/all_to_all | solution.py:385
  78.7 0.0 collective-permute-done.2.refs_3_.rest_3_
  78.7 0.1 collective-permute-start.3
  78.8 7.5 %all-to-all-done.3 = bf16[16,4,16,128]{3,2,1,0:T(8,128)(2,1)S(1)} async-done(((bf16[16,4,16,128]{3,2,1,0:T(8,128)(2,1)}), bf16[16,4,16,128]{3,2,1,0:T(8,128)(2,1)S(1)}, u32[]{:S(2)}, u32[]{:S(2)}) %all-to-all-start.3) | async-done | bytes 262176 | tf_op jit(solution)/shard_map/all_to_all | solution.py:385
  86.3 3.7 %collective-permute-start.14 = (bf16[64,16,128]{2,1,0:T(8,128)(2,1)S(1)}, bf16[64,16,128]{2,1,0:T(8,128)(2,1)S(1)}, u32[]{:S(2)}, u32[]{:S(2)}) collective-permute-start(bf16[64,16,128]{2,1,0:T(8,128)(2,1)S(1)} %bitcast.11), channel_id=1, source_target_pairs={{0,1},{1,0},{2,3},{3,2},{4,5},{5,4},{6,7},{7,6},{8,9},{9,8},{10,11... | collective-permute-start | bytes 786440 | tf_op jit(solution)/shard_map/ppermute | solution.py:381
  90.0 0.0 collective-permute-done.3.rest_4_
  90.0 1.0 %shard_map.100 = bf16[2,8,32,256]{3,2,1,0:T(8,128)(2,1)} custom-call(bf16[2,8,32,256]{3,2,1,0:T(8,128)(2,1)S(1)} %bitcast.18, f32[1,256]{1,0:T(1,128)S(1)} %bitcast.22, f32[2,8,32,256]{3,2,1,0:T(8,128)S(1)} %bitcast.23, bf16[8,2,16,256]{3,2,1,0:T(8,128)(2,1)S(1)} %get-tuple-element.40.refs_0_.rest_0_, ...), custom_call_target="tpu_custom_call" | custom-call | flops 1600000000 | bytes 4000000 | tf_op jit(solution)/shard_map/pallas_call | solution.py:369
  91.0 0.1 collective-permute-done.14.theirs
  91.1 1.1 %shard_map.104 = (f32[256,768]{1,0:T(8,128)}, f32[256,256]{1,0:T(8,128)}) custom-call(bf16[64,16,128]{2,1,0:T(8,128)(2,1)S(1)} %bitcast.12, bf16[64,16,128]{2,1,0:T(8,128)(2,1)S(1)} %collective-permute-done.14.theirs), custom_call_target="tpu_custom_call" | custom-call | flops 800000000 | bytes 2000000 | tf_op jit(solution)/shard_map/pallas_call | solution.py:369
  (20 shorter events, 0.1 us)
Async XLA Ops:
  0.6 16.7 %copy-start.3 = (bf16[1,2,8,32,256]{4,3,2,1,0:T(8,128)(2,1)S(1)}, bf16[1,2,8,32,256]{4,3,2,1,0:T(8,128)(2,1)}, u32[]{:S(2)}) copy-start(bf16[1,2,8,32,256]{4,3,2,1,0:T(8,128)(2,1)} %param.6) | copy-start | bytes 786436
  2.8 14.6 %copy-start = (bf16[256,768]{1,0:T(8,128)(2,1)S(1)}, bf16[256,768]{1,0:T(8,128)(2,1)}, u32[]{:S(2)}) copy-start(bf16[256,768]{1,0:T(8,128)(2,1)} %refs_5_.1) | copy-start | bytes 1179652
  2.8 14.6 %copy-start.1 = (bf16[1,2,8,32,256]{4,3,2,1,0:T(8,128)(2,1)S(1)}, bf16[1,2,8,32,256]{4,3,2,1,0:T(8,128)(2,1)}, u32[]{:S(2)}) copy-start(bf16[1,2,8,32,256]{4,3,2,1,0:T(8,128)(2,1)} %param.8) | copy-start | bytes 786436
  2.8 14.5 %copy-start.2 = (bf16[1,2,8,32,256]{4,3,2,1,0:T(8,128)(2,1)S(1)}, bf16[1,2,8,32,256]{4,3,2,1,0:T(8,128)(2,1)}, u32[]{:S(2)}) copy-start(bf16[1,2,8,32,256]{4,3,2,1,0:T(8,128)(2,1)} %param.7) | copy-start | bytes 786436
  2.8 14.5 %copy-start.4 = (bf16[256,256]{1,0:T(8,128)(2,1)S(1)}, bf16[256,256]{1,0:T(8,128)(2,1)}, u32[]{:S(2)}) copy-start(bf16[256,256]{1,0:T(8,128)(2,1)} %refs_6_.1) | copy-start | bytes 393220
  2.8 30.5 %all-to-all-start = ((bf16[16,2,2,16,256]{4,3,2,1,0:T(8,128)(2,1)}), bf16[16,2,2,16,256]{4,3,2,1,0:T(8,128)(2,1)S(1)}, u32[]{:S(2)}, u32[]{:S(2)}) async-start(bf16[16,2,2,16,256]{4,3,2,1,0:T(8,128)(2,1)} %bitcast.24), calls=%async_computation | async-start | bytes 1048576 | tf_op jit(solution)/shard_map/all_to_all | solution.py:385
  14.5 6.6 %collective-permute-start.4 = (bf16[2,8,16,256]{3,2,1,0:T(8,128)(2,1)}, bf16[2,8,16,256]{3,2,1,0:T(8,128)(2,1)S(1)}, u32[]{:S(2)}, u32[]{:S(2)}) collective-permute-start(bf16[2,8,16,256]{3,2,1,0:T(8,128)(2,1)} %get-tuple-element.45), channel_id=1, source_target_pairs={{0,1},{1,0},{2,3},{3,2},{4,5},{5,4},{6,7},{7,6},{8,9},{9,8},{10,11... | collective-permute-start | bytes 393224 | tf_op jit(solution)/shard_map/ppermute | solution.py:381
  15.6 5.6 %collective-permute-start.5 = (bf16[2,8,16,256]{3,2,1,0:T(8,128)(2,1)}, bf16[2,8,16,256]{3,2,1,0:T(8,128)(2,1)S(1)}, u32[]{:S(2)}, u32[]{:S(2)}) collective-permute-start(bf16[2,8,16,256]{3,2,1,0:T(8,128)(2,1)} %get-tuple-element.46), channel_id=1, source_target_pairs={{0,2},{1,3},{2,0},{3,1},{4,6},{5,7},{6,4},{7,5},{8,10},{9,11},{10,... | collective-permute-start | bytes 393224 | tf_op jit(solution)/shard_map/ppermute | solution.py:381
  15.9 10.7 %collective-permute-start.6 = (bf16[2,8,16,256]{3,2,1,0:T(8,128)(2,1)}, bf16[2,8,16,256]{3,2,1,0:T(8,128)(2,1)S(1)}, u32[]{:S(2)}, u32[]{:S(2)}) collective-permute-start(bf16[2,8,16,256]{3,2,1,0:T(8,128)(2,1)} %get-tuple-element.47), channel_id=1, source_target_pairs={{0,3},{1,2},{2,1},{3,0},{4,7},{5,6},{6,5},{7,4},{8,11},{9,10},{10,... | collective-permute-start | bytes 393224 | tf_op jit(solution)/shard_map/ppermute | solution.py:381
  17.3 0.7 copy-start.5
  18.0 8.6 %copy-start.8 = (bf16[2,8,16,256]{3,2,1,0:T(8,128)(2,1)S(1)}, bf16[2,8,16,256]{3,2,1,0:T(8,128)(2,1)}, u32[]{:S(2)}) copy-start(bf16[2,8,16,256]{3,2,1,0:T(8,128)(2,1)} %get-tuple-element.44.refs_0_) | copy-start | bytes 393220
  30.1 0.8 copy-start.6
  30.9 5.9 %collective-permute-start.8 = (bf16[33,16,128]{2,1,0:T(8,128)(2,1)S(1)}, bf16[33,16,128]{2,1,0:T(8,128)(2,1)S(1)}, u32[]{:S(2)}, u32[]{:S(2)}) collective-permute-start(bf16[33,16,128]{2,1,0:T(8,128)(2,1)S(1)} %get-tuple-element.53), channel_id=1, source_target_pairs={{0,1},{1,0},{2,3},{3,2},{4,5},{5,4},{6,7},{7,6},{8,9},{9,8},{10,11... | collective-permute-start | bytes 405512 | tf_op jit(solution)/shard_map/ppermute | solution.py:381
  30.9 5.9 %collective-permute-start.7 = (bf16[32,16,128]{2,1,0:T(8,128)(2,1)S(1)}, bf16[32,16,128]{2,1,0:T(8,128)(2,1)S(1)}, u32[]{:S(2)}, u32[]{:S(2)}) collective-permute-start(bf16[32,16,128]{2,1,0:T(8,128)(2,1)S(1)} %get-tuple-element.52), channel_id=1, source_target_pairs={{0,1},{1,0},{2,3},{3,2},{4,5},{5,4},{6,7},{7,6},{8,9},{9,8},{10,11... | collective-permute-start | bytes 393224 | tf_op jit(solution)/shard_map/ppermute | solution.py:381
  31.4 5.3 %collective-permute-start.10 = (bf16[8,16,256]{2,1,0:T(8,128)(2,1)S(1)}, bf16[8,16,256]{2,1,0:T(8,128)(2,1)S(1)}, u32[]{:S(2)}, u32[]{:S(2)}) collective-permute-start(bf16[8,16,256]{2,1,0:T(8,128)(2,1)S(1)} %get-tuple-element.56), channel_id=1, source_target_pairs={{0,2},{1,3},{2,0},{3,1},{4,6},{5,7},{6,4},{7,5},{8,10},{9,11},{10,... | collective-permute-start | bytes 196616 | tf_op jit(solution)/shard_map/ppermute | solution.py:381
  31.4 5.3 %collective-permute-start.11 = (bf16[8,16,256]{2,1,0:T(8,128)(2,1)S(1)}, bf16[8,16,256]{2,1,0:T(8,128)(2,1)S(1)}, u32[]{:S(2)}, u32[]{:S(2)}) collective-permute-start(bf16[8,16,256]{2,1,0:T(8,128)(2,1)S(1)} %get-tuple-element.57), channel_id=1, source_target_pairs={{0,3},{1,2},{2,1},{3,0},{4,7},{5,6},{6,5},{7,4},{8,11},{9,10},{10,... | collective-permute-start | bytes 196616 | tf_op jit(solution)/shard_map/ppermute | solution.py:381
  33.0 3.7 %collective-permute-start.9 = (bf16[8,16,256]{2,1,0:T(8,128)(2,1)S(1)}, bf16[8,16,256]{2,1,0:T(8,128)(2,1)S(1)}, u32[]{:S(2)}, u32[]{:S(2)}) collective-permute-start(bf16[8,16,256]{2,1,0:T(8,128)(2,1)S(1)} %get-tuple-element.55), channel_id=1, source_target_pairs={{0,1},{1,0},{2,3},{3,2},{4,5},{5,4},{6,7},{7,6},{8,9},{9,8},{10,11... | collective-permute-start | bytes 196616 | tf_op jit(solution)/shard_map/ppermute | solution.py:381
  36.8 3.8 %collective-permute-start.13 = (bf16[33,16,128]{2,1,0:T(8,128)(2,1)S(1)}, bf16[33,16,128]{2,1,0:T(8,128)(2,1)S(1)}, u32[]{:S(2)}, u32[]{:S(2)}) collective-permute-start(bf16[33,16,128]{2,1,0:T(8,128)(2,1)S(1)} %get-tuple-element.67), channel_id=1, source_target_pairs={{0,1},{1,0},{2,3},{3,2},{4,5},{5,4},{6,7},{7,6},{8,9},{9,8},{10,11... | collective-permute-start | bytes 405512 | tf_op jit(solution)/shard_map/ppermute | solution.py:381
  37.7 2.8 %collective-permute-start.12 = (bf16[32,16,128]{2,1,0:T(8,128)(2,1)S(1)}, bf16[32,16,128]{2,1,0:T(8,128)(2,1)S(1)}, u32[]{:S(2)}, u32[]{:S(2)}) collective-permute-start(bf16[32,16,128]{2,1,0:T(8,128)(2,1)S(1)} %get-tuple-element.66), channel_id=1, source_target_pairs={{0,1},{1,0},{2,3},{3,2},{4,5},{5,4},{6,7},{7,6},{8,9},{9,8},{10,11... | collective-permute-start | bytes 393224 | tf_op jit(solution)/shard_map/ppermute | solution.py:381
  37.8 9.6 %collective-permute-start = (bf16[8,2,16,256]{3,2,1,0:T(8,128)(2,1)S(1)}, bf16[8,2,16,256]{3,2,1,0:T(8,128)(2,1)S(1)}, u32[]{:S(2)}, u32[]{:S(2)}) collective-permute-start(bf16[8,2,16,256]{3,2,1,0:T(8,128)(2,1)S(1)} %get-tuple-element.41), channel_id=1, source_target_pairs={{0,8},{8,0},{16,24},{24,16},{32,40},{40,32},{48,56},{56,48},{1,9},... | collective-permute-start | bytes 393224 | tf_op jit(solution)/shard_map/ppermute | solution.py:381
  40.5 1.0 %copy-start.7 = (f32[65,16,128]{2,1,0:T(8,128)S(1)}, f32[65,16,128]{2,1,0:T(8,128)}, u32[]{:S(2)}) copy-start(f32[65,16,128]{2,1,0:T(8,128)} %copy-done.6) | copy-start | bytes 1597444
  42.4 14.0 %all-to-all-start.1 = ((bf16[16,5,16,128]{3,2,1,0:T(8,128)(2,1)}), bf16[16,5,16,128]{3,2,1,0:T(8,128)(2,1)S(1)}, u32[]{:S(2)}, u32[]{:S(2)}) async-start(bf16[16,5,16,128]{3,2,1,0:T(8,128)(2,1)} %shard_map.101), calls=%async_computation.1 | async-start | bytes 655360 | tf_op jit(solution)/shard_map/all_to_all | solution.py:385
  47.5 18.5 %collective-permute-start.1 = (bf16[8,2,16,256]{3,2,1,0:T(8,128)(2,1)S(1)}, bf16[8,2,16,256]{3,2,1,0:T(8,128)(2,1)S(1)}, u32[]{:S(2)}, u32[]{:S(2)}) collective-permute-start(bf16[8,2,16,256]{3,2,1,0:T(8,128)(2,1)S(1)} %shard_map.96), channel_id=1, source_target_pairs={{0,32},{8,40},{16,48},{24,56},{32,0},{40,8},{48,16},{56,24},{1,33}... | collective-permute-start | bytes 393224 | tf_op jit(solution)/shard_map/ppermute | solution.py:381
  57.1 17.3 %all-to-all-start.2 = ((bf16[8,5,16,128]{3,2,1,0:T(8,128)(2,1)}), bf16[8,5,16,128]{3,2,1,0:T(8,128)(2,1)S(1)}, u32[]{:S(2)}, u32[]{:S(2)}) async-start(bf16[8,5,16,128]{3,2,1,0:T(8,128)(2,1)} %shard_map.102), calls=%async_computation.2 | async-start | bytes 327680 | tf_op jit(solution)/shard_map/all_to_all | solution.py:385
  66.0 12.6 %collective-permute-start.2 = (bf16[8,2,16,256]{3,2,1,0:T(8,128)(2,1)S(1)}, bf16[8,2,16,256]{3,2,1,0:T(8,128)(2,1)S(1)}, u32[]{:S(2)}, u32[]{:S(2)}) collective-permute-start(bf16[8,2,16,256]{3,2,1,0:T(8,128)(2,1)S(1)} %shard_map.97), channel_id=1, source_target_pairs={{0,4},{4,0},{1,5},{5,1},{2,6},{6,2},{3,7},{7,3},{8,12},{12,8},{9,1... | collective-permute-start | bytes 393224 | tf_op jit(solution)/shard_map/ppermute | solution.py:381
  75.1 11.1 %all-to-all-start.3 = ((bf16[16,4,16,128]{3,2,1,0:T(8,128)(2,1)}), bf16[16,4,16,128]{3,2,1,0:T(8,128)(2,1)S(1)}, u32[]{:S(2)}, u32[]{:S(2)}) async-start(bf16[16,4,16,128]{3,2,1,0:T(8,128)(2,1)} %get-tuple-element.68), calls=%async_computation.3 | async-start | bytes 524288 | tf_op jit(solution)/shard_map/all_to_all | solution.py:385
  78.7 11.3 %collective-permute-start.3 = (bf16[8,2,16,256]{3,2,1,0:T(8,128)(2,1)S(1)}, bf16[8,2,16,256]{3,2,1,0:T(8,128)(2,1)S(1)}, u32[]{:S(2)}, u32[]{:S(2)}) collective-permute-start(bf16[8,2,16,256]{3,2,1,0:T(8,128)(2,1)S(1)} %shard_map.98), channel_id=1, source_target_pairs={{0,16},{8,24},{16,0},{24,8},{32,48},{40,56},{48,32},{56,40},{1,17}... | collective-permute-start | bytes 393224 | tf_op jit(solution)/shard_map/ppermute | solution.py:381
  86.3 4.9 %collective-permute-start.14 = (bf16[64,16,128]{2,1,0:T(8,128)(2,1)S(1)}, bf16[64,16,128]{2,1,0:T(8,128)(2,1)S(1)}, u32[]{:S(2)}, u32[]{:S(2)}) collective-permute-start(bf16[64,16,128]{2,1,0:T(8,128)(2,1)S(1)} %bitcast.11), channel_id=1, source_target_pairs={{0,1},{1,0},{2,3},{3,2},{4,5},{5,4},{6,7},{7,6},{8,9},{9,8},{10,11... | collective-permute-start | bytes 786440 | tf_op jit(solution)/shard_map/ppermute | solution.py:381

commit v5 on v4

--- a/solution.py
+++ b/solution.py
@@ -232,13 +232,13 @@
             row, col = divmod(at - 96, 2)
             halves[half, tile] = part_out[row * 16 : row * 16 + 16, col * LANES : (col + 1) * LANES]
     mine = lax.axis_index("c")
-    own[0:TILES] = halves[mine]
+    own[0:TILES] = halves[mine].astype(own.dtype)
     low[0:HALF] = halves[1 - mine, 0:HALF].astype(BF16)
     high[0:HALF] = halves[1 - mine, HALF:TILES].astype(BF16)
     gains = jnp.concatenate(
         [part_gain[:, :LANES], part_gain[:, LANES:], jnp.zeros((14, LANES), F32)], axis=0
     )
-    own[TILES] = gains
+    own[TILES] = gains.astype(own.dtype)
     high[HALF] = gains.astype(BF16)
 
 
@@ -258,8 +258,16 @@
     pack(third_qkv[...] + part_qkv, part_out, third_gain[...] + part_gain, halves, *packed)
 
 
-def first_kernel(pieces, gain, w_qkv, w_out, *refs):
-    (stay, leave), packed, scratch, (returned, halves) = refs[:2], refs[2:5], refs[5:-2], refs[-2:]
+def first_kernel(pieces, early_own, early_low, early_high, gain, w_qkv, w_out, *refs):
+    (stay, leave), packed, scratch, rest = refs[:2], refs[2:5], refs[5:-6], refs[-6:]
+    returned, halves, held_own, held_low, held_high, sem = rest
+    held = (held_own, held_low, held_high)
+    copies = [
+        pltpu.make_async_copy(source, target, sem.at[at])
+        for at, (source, target) in enumerate(zip((early_own, early_low, early_high), held))
+    ]
+    for copy in copies:
+        copy.start()
     tokens = pieces[:, 0].reshape(TOKENS, WIDTH)
     cot = pieces[:, 1].reshape(TOKENS, WIDTH)
     grad_normed, part_qkv, part_gain = axis_grads(
@@ -271,6 +279,16 @@
         stay[at] = returned[here ^ mask]
         leave[at] = returned[here ^ mask ^ BITS[0]]
     pack(part_qkv, None, part_gain, halves, *packed)
+    for copy in copies:
+        copy.wait()
+    own = packed[0]
+    own[0:HALF] += held_own[0:HALF].astype(F32) + held_low[...].astype(F32)
+    own[HALF:TILES] += held_own[HALF:TILES].astype(F32) + held_high[0:HALF].astype(F32)
+    own[TILES + 1] = both(held_own[TILES], held_high[HALF])
+
+
+def both(mine, theirs):
+    return mine.astype(BF16).astype(F32) + theirs.astype(F32)
 
 
 def stage_kernel(*refs):
@@ -285,26 +303,13 @@
                 at += 1
 
 
-def pair_kernel(*refs):
-    sources, pieces = (refs[0:3], refs[3:6]), refs[6]
-
-    def summed(tiles):
-        half, at = divmod(tiles.start, HALF)
-        if tiles.start == TILES:
-            half, at = 1, HALF
-        total = None
-        for own, low, high in sources:
-            mine = own[tiles]
-            if tiles.start == TILES:
-                mine = mine.astype(BF16).astype(F32)
-            part = mine + (low, high)[half][at : at + tiles.stop - tiles.start].astype(F32)
-            total = part if total is None else total + part
-        return total.astype(BF16)
-
-    gains = summed(slice(TILES, TILES + 1))
+def pair_kernel(own, low, high, pieces):
+    gains = (both(own[TILES], high[HALF]) + own[TILES + 1]).astype(BF16)
     for peer in range(16):
-        pieces[peer, 0:4] = summed(slice(peer * 4, peer * 4 + 4))
-        pieces[peer, 4:5] = gains
+        half, at = divmod(peer * 4, HALF)
+        received = (low, high)[half][at : at + 4].astype(F32)
+        pieces[peer, 0:4] = (own[peer * 4 : peer * 4 + 4] + received).astype(BF16)
+        pieces[peer, 4] = gains
 
 
 def plane_kernel(received, pieces):
@@ -365,11 +370,11 @@
     return jax.ShapeDtypeStruct(dims, dtype)
 
 
-def kernel_call(body, outs, operands, us, scratch=(), space=VMEM):
+def kernel_call(body, outs, operands, us, scratch=(), space=VMEM, spaces=None):
     return pl.pallas_call(
         body,
         out_shape=outs,
-        in_specs=[space] * len(operands),
+        in_specs=spaces or [space] * len(operands),
         out_specs=jax.tree.map(lambda _: space, outs),
         scratch_shapes=list(scratch),
         compiler_params=params(62 if space is HBM else 48),
@@ -410,11 +415,11 @@
             shape((1, WIDTH), F32),
         ),
         (local.reshape(flat), upstream.reshape(flat), attn.reshape(flat), gain_row, w_qkv, w_out),
-        5,
+        0.1,
         SCRATCH,
     )
     packed = (
-        shape((TILES + 1, *tile), F32),
+        shape((TILES + 1, *tile), BF16),
         shape((HALF, *tile), BF16),
         shape((HALF + 1, *tile), BF16),
     )
@@ -423,7 +428,7 @@
         second_kernel,
         (shape((8, ROWS, WIDTH), BF16),) * 4 + packed,
         (*at_second, gain_row, w_qkv, w_out, third_qkv, part_out, third_gain),
-        5,
+        50,
         SCRATCH + [halves],
     )
     from_second = [back[0]] + [swap(back[m], SECOND, m, 4) for m in (1, 2, 3)]
@@ -431,18 +436,30 @@
     block = (2, ROWS, WIDTH)
     stay, leave, own, low, high = kernel_call(
         first_kernel,
-        (shape((8, *block), BF16),) * 2 + packed,
-        (at_first, gain_row, w_qkv, w_out),
+        (
+            shape((8, *block), BF16),
+            shape((8, *block), BF16),
+            shape((TILES + 2, *tile), F32),
+            *packed[1:],
+        ),
+        (at_first, *early, gain_row, w_qkv, w_out),
         5,
-        SCRATCH + [pltpu.VMEM((16, *block), BF16), halves],
-    )
-    low, high, early, from_second = lax.optimization_barrier((low, high, early, from_second))
+        SCRATCH
+        + [
+            pltpu.VMEM((16, *block), BF16),
+            halves,
+            *[pltpu.VMEM(part.shape, part.dtype) for part in packed],
+            pltpu.SemaphoreType.DMA((3,)),
+        ],
+        spaces=[VMEM] + [HBM] * 3 + [VMEM] * 3,
+    )
+    low, high, from_second = lax.optimization_barrier((low, high, from_second))
     late = [own, swap(low, "c", 1, 2), swap(high, "c", 1, 2)]
     groups = [stay, swap(leave, *SWAPS[0])]
     for stage in (1, 2, 3):
         leave = kernel_call(stage_kernel, shape((8, *block), BF16), groups, 20)
         groups.append(swap(leave, *SWAPS[stage]))
-    pieces = kernel_call(pair_kernel, shape((16, 5, *tile), BF16), (*early, *late), 1)
+    pieces = kernel_call(pair_kernel, shape((16, 5, *tile), BF16), late, 1)
     summed = exchange(pieces, PLANE)
     pieces = kernel_call(plane_kernel, shape((8, 5, *tile), BF16), (summed,), 1)
     summed = exchange(pieces, "z")

time: 92.7 us -> 87.2 us (0.941)
  starting transfers between devices: 49.8 us -> 36 us
  waiting for transfers between devices: 22.3 us -> 32.1 us
  local copies, waits for them, and re-layouts: 2.52 us -> 0.65 us
    all_to_all x4, waiting for transfers between devices: 16.8 us -> 30.7 us  [exchange(): return lax.all_to_all(pieces, axes, split_axis=0, concat_axis=0, tiled=True)]
    all_to_all x4, starting transfers between devices: 29.2 us -> 20.4 us  [exchange(): return lax.all_to_all(pieces, axes, split_axis=0, concat_axis=0, tiled=True)]
    ppermute x15, starting transfers between devices: 20.7 us -> 15.6 us  [swap(): return lax.ppermute(array, axis, [(i, i ^ mask) for i in range(size)])]
    ppermute x15, waiting for transfers between devices: 5.55 us -> 1.39 us  [swap(): return lax.ppermute(array, axis, [(i, i ^ mask) for i in range(size)])]
    unnamed x18 -> x14, local copies, waits for them, and re-layouts: 2.52 us -> 0.65 us
  transfers between devices with their start and end apart: 19 -> 19, of which waited for: 5 -> 6; matrix products, arithmetic and copies ran while one was open for 0% -> 0% of each run, Pallas kernels for 15% -> 16%
where the time goes in v5:
time: 87.2 us; the launch traced here: 86.7 us
  starting transfers between devices  36 us (41%)
  waiting for transfers between devices  32.1 us (37%)
  Pallas kernels  17.1 us (20%)
    all_to_all x4, waiting for transfers between devices, exchange(): return lax.all_to_all(pieces, axes, split_axis=0, concat_axis=0, tiled=True)  30.7 us
    all_to_all x4, starting transfers between devices, exchange(): return lax.all_to_all(pieces, axes, split_axis=0, concat_axis=0, tiled=True)  20.4 us
    pallas_call x12, Pallas kernels, kernel_call(): pl.pallas_call(body, out_shape=outs, in_specs=spaces or [space] * len(ope...  17.1 us
    ppermute x15, starting transfers between devices, swap(): return lax.ppermute(array, axis, [(i, i ^ mask) for i in range(size)])  15.6 us
  transfers between devices with their start and end apart: 19, of which 6 were waited for; matrix products, arithmetic and copies ran while one was open for 0% of the time, Pallas kernels for 16%

profile of v5, /device:TPU:1, one launch (start us, length us, event | category | flops | bytes accessed | tf_op | source)
XLA Modules:
  0.0 86.7 jit_solution(17900820166378864980)
XLA Ops:
  0.6 2.1 %shard_map.94 = (bf16[8,2,2,2,16,256]{5,4,3,2,1,0:T(8,128)(2,1)}, bf16[2,8,16,256]{3,2,1,0:T(8,128)(2,1)}, bf16[2,8,16,256]{3,2,1,0:T(8,128)(2,1)}, bf16[2,8,16,...) custom-call(bf16[2,8,32,256]{3,2,1,0:T(8,128)(2,1)} %bitcast.16, bf16[2,8,32,256]{3,2,1,0:T(8,128)(2,1)} %bitcast.13), custom_call_target="tpu_custom_call" | custom-call | flops 1600000000 | bytes 4000000 | tf_op jit(solution)/shard_map/pallas_call | solution.py:374
  2.8 3.3 %collective-permute-start = (bf16[2,8,16,256]{3,2,1,0:T(8,128)(2,1)}, bf16[2,8,16,256]{3,2,1,0:T(8,128)(2,1)S(1)}, u32[]{:S(2)}, u32[]{:S(2)}) collective-permute-start(bf16[2,8,16,256]{3,2,1,0:T(8,128)(2,1)} %get-tuple-element.38), channel_id=1, source_target_pairs={{0,1},{1,0},{2,3},{3,2},{4,5},{5,4},{6,7},{7,6},{8,9},{9,8},{10,11... | collective-permute-start | bytes 393224 | tf_op jit(solution)/shard_map/ppermute | solution.py:386
  6.1 0.0 collective-permute-start.1
  6.1 1.7 %collective-permute-start.2 = (bf16[2,8,16,256]{3,2,1,0:T(8,128)(2,1)}, bf16[2,8,16,256]{3,2,1,0:T(8,128)(2,1)S(1)}, u32[]{:S(2)}, u32[]{:S(2)}) collective-permute-start(bf16[2,8,16,256]{3,2,1,0:T(8,128)(2,1)} %get-tuple-element.40), channel_id=1, source_target_pairs={{0,3},{1,2},{2,1},{3,0},{4,7},{5,6},{6,5},{7,4},{8,11},{9,10},{10,... | collective-permute-start | bytes 393224 | tf_op jit(solution)/shard_map/ppermute | solution.py:386
  7.8 9.2 %all-to-all-start = ((bf16[16,2,2,16,256]{4,3,2,1,0:T(8,128)(2,1)}), bf16[16,2,2,16,256]{4,3,2,1,0:T(8,128)(2,1)S(1)}, u32[]{:S(2)}, u32[]{:S(2)}) async-start(bf16[16,2,2,16,256]{4,3,2,1,0:T(8,128)(2,1)} %bitcast.24), calls=%async_computation | async-start | bytes 1048576 | tf_op jit(solution)/shard_map/all_to_all | solution.py:390
  17.0 0.0 copy-start.5
  17.1 0.6 copy-done.5
  17.7 3.2 %shard_map.93 = (f32[512,256]{1,0:T(8,128)S(1)}, f32[256,768]{1,0:T(8,128)S(1)}, f32[256,256]{1,0:T(8,128)S(1)}, f32[1,256]{1,0:T(1,128)S(1)}) custom-call(bf16[512,256]{1,0:T(8,128)(2,1)S(1)} %bitcast.17, bf16[512,256]{1,0:T(8,128)(2,1)S(1)} %bitcast.14, bf16[512,256]{1,0:T(8,128)(2,1)S(1)} %bitcast.15, f32[1,256]{1,0:T(1,128)S(1)} %bitcast.19, ...), custom_call_target="tpu_custom_call" | custom-call | flops 80000000 | bytes 200000 | tf_op jit(solution)/shard_map/pallas_call | solution.py:374
  20.9 0.0 collective-permute-done.refs_1_
  20.9 0.0 collective-permute-done.1.refs_2_
  20.9 0.0 collective-permute-done.2.refs_3_
  20.9 3.5 %shard_map.95 = (bf16[8,16,256]{2,1,0:T(8,128)(2,1)S(1)}, bf16[8,16,256]{2,1,0:T(8,128)(2,1)S(1)}, bf16[8,16,256]{2,1,0:T(8,128)(2,1)S(1)}, bf16[8,16,256]{2,1,0...) custom-call(bf16[2,8,16,256]{3,2,1,0:T(8,128)(2,1)S(1)} %copy-done.6, ...), custom_call_target="tpu_custom_call" | custom-call | flops 40000000000 | bytes 100000000 | tf_op jit(solution)/shard_map/pallas_call | solution.py:374
  24.4 0.5 collective-permute-start.4
  24.9 0.1 collective-permute-start.3
  25.1 0.4 collective-permute-start.9
  25.5 0.3 collective-permute-start.10
  25.8 1.4 %collective-permute-start.11 = (bf16[8,16,256]{2,1,0:T(8,128)(2,1)S(1)}, bf16[8,16,256]{2,1,0:T(8,128)(2,1)S(1)}, u32[]{:S(2)}, u32[]{:S(2)}) collective-permute-start(bf16[8,16,256]{2,1,0:T(8,128)(2,1)S(1)} %get-tuple-element.54), channel_id=1, source_target_pairs={{0,3},{1,2},{2,1},{3,0},{4,7},{5,6},{6,5},{7,4},{8,11},{9,10},{10,... | collective-permute-start | bytes 196616 | tf_op jit(solution)/shard_map/ppermute | solution.py:386
  27.2 0.0 collective-permute-done.3.early_low
  27.2 0.0 collective-permute-done.4.early_high
  27.2 7.5 %all-to-all-done.pieces = bf16[16,2,2,16,256]{4,3,2,1,0:T(8,128)(2,1)S(1)} async-done(((bf16[16,2,2,16,256]{4,3,2,1,0:T(8,128)(2,1)}), bf16[16,2,2,16,256]{4,3,2,1,0:T(8,128)(2,1)S(1)}, u32[]{:S(2)}, u32[]{:S(2)}) %all-to-all-start) | async-done | bytes 524320 | tf_op jit(solution)/shard_map/all_to_all | solution.py:390
  34.7 3.9 %shard_map.96 = (bf16[8,2,16,256]{3,2,1,0:T(8,128)(2,1)S(1)}, bf16[8,2,16,256]{3,2,1,0:T(8,128)(2,1)S(1)}, f32[66,16,128]{2,1,0:T(8,128)S(1)}, bf16[32,16,128]{2,1,0:T(8,128)(2,1)S(1)}, bf16[33,16,128]{2,1,0:T(8,128)(2,1)S(1)}) custom-call(bf16[16,2,2,16,256]{4,3,2,1,0:T(8,128)(2,1)S(1)} %all-to-all-done.pieces, ...), custom_call_target="tpu_custom_call" | custom-call | flops 4000000000 | bytes 10000000 | tf_op jit(solution)/shard_map/pallas_call | solution.py:374
  38.7 0.0 collective-permute-done.9.rest_6_
  38.7 0.0 collective-permute-done.10.rest_7_
  38.7 0.0 collective-permute-done.11.rest_8_
  38.7 2.6 %collective-permute-start.13 = (bf16[33,16,128]{2,1,0:T(8,128)(2,1)S(1)}, bf16[33,16,128]{2,1,0:T(8,128)(2,1)S(1)}, u32[]{:S(2)}, u32[]{:S(2)}) collective-permute-start(bf16[33,16,128]{2,1,0:T(8,128)(2,1)S(1)} %get-tuple-element.61), channel_id=1, source_target_pairs={{0,1},{1,0},{2,3},{3,2},{4,5},{5,4},{6,7},{7,6},{8,9},{9,8},{10,11... | collective-permute-start | bytes 405512 | tf_op jit(solution)/shard_map/ppermute | solution.py:386
  41.3 0.1 collective-permute-start.12
  41.4 0.0 collective-permute-start.5
  41.4 1.2 %collective-permute-done.12.low = bf16[32,16,128]{2,1,0:T(8,128)(2,1)S(1)} collective-permute-done((bf16[32,16,128]{2,1,0:T(8,128)(2,1)S(1)}, bf16[32,16,128]{2,1,0:T(8,128)(2,1)S(1)}, u32[]{:S(2)}, u32[]{:S(2)}) %collective-permute-start.12) | collective-permute-done | bytes 131104 | tf_op jit(solution)/shard_map/ppermute | solution.py:386
  42.6 0.0 collective-permute-done.13.high
  42.6 0.8 shard_map.101
  43.4 4.4 %all-to-all-start.1 = ((bf16[16,5,16,128]{3,2,1,0:T(8,128)(2,1)}), bf16[16,5,16,128]{3,2,1,0:T(8,128)(2,1)S(1)}, u32[]{:S(2)}, u32[]{:S(2)}) async-start(bf16[16,5,16,128]{3,2,1,0:T(8,128)(2,1)} %shard_map.101), calls=%async_computation.1 | async-start | bytes 655360 | tf_op jit(solution)/shard_map/all_to_all | solution.py:390
  47.8 0.0 collective-permute-done.5.refs_1_.rest_1_
  47.8 0.9 %collective-permute-start.6 = (bf16[8,2,16,256]{3,2,1,0:T(8,128)(2,1)S(1)}, bf16[8,2,16,256]{3,2,1,0:T(8,128)(2,1)S(1)}, u32[]{:S(2)}, u32[]{:S(2)}) collective-permute-start(bf16[8,2,16,256]{3,2,1,0:T(8,128)(2,1)S(1)} %shard_map.97), channel_id=1, source_target_pairs={{0,32},{8,40},{16,48},{24,56},{32,0},{40,8},{48,16},{56,24},{1,33}... | collective-permute-start | bytes 393224 | tf_op jit(solution)/shard_map/ppermute | solution.py:386
  48.7 8.1 %all-to-all-done.1.received = bf16[16,5,16,128]{3,2,1,0:T(8,128)(2,1)S(1)} async-done(((bf16[16,5,16,128]{3,2,1,0:T(8,128)(2,1)}), bf16[16,5,16,128]{3,2,1,0:T(8,128)(2,1)S(1)}, u32[]{:S(2)}, u32[]{:S(2)}) %all-to-all-start.1) | async-done | bytes 327712 | tf_op jit(solution)/shard_map/all_to_all | solution.py:390
  56.8 0.7 shard_map.102
  57.5 3.4 %all-to-all-start.2 = ((bf16[8,5,16,128]{3,2,1,0:T(8,128)(2,1)}), bf16[8,5,16,128]{3,2,1,0:T(8,128)(2,1)S(1)}, u32[]{:S(2)}, u32[]{:S(2)}) async-start(bf16[8,5,16,128]{3,2,1,0:T(8,128)(2,1)} %shard_map.102), calls=%async_computation.2 | async-start | bytes 327680 | tf_op jit(solution)/shard_map/all_to_all | solution.py:390
  60.9 0.0 collective-permute-done.6.refs_2_.rest_2_
  60.9 0.3 collective-permute-start.7
  61.3 7.6 %all-to-all-done.2.received = bf16[8,5,16,128]{3,2,1,0:T(8,128)(2,1)S(1)} async-done(((bf16[8,5,16,128]{3,2,1,0:T(8,128)(2,1)}), bf16[8,5,16,128]{3,2,1,0:T(8,128)(2,1)S(1)}, u32[]{:S(2)}, u32[]{:S(2)}) %all-to-all-start.2) | async-done | bytes 163872 | tf_op jit(solution)/shard_map/all_to_all | solution.py:390
  68.9 0.7 shard_map.103
  69.6 3.5 %all-to-all-start.3 = ((bf16[16,4,16,128]{3,2,1,0:T(8,128)(2,1)}), bf16[16,4,16,128]{3,2,1,0:T(8,128)(2,1)S(1)}, u32[]{:S(2)}, u32[]{:S(2)}) async-start(bf16[16,4,16,128]{3,2,1,0:T(8,128)(2,1)} %get-tuple-element.62), calls=%async_computation.3 | async-start | bytes 524288 | tf_op jit(solution)/shard_map/all_to_all | solution.py:390
  73.1 0.0 collective-permute-done.7.refs_3_.rest_3_
  73.2 0.1 collective-permute-start.8
  73.3 7.5 %all-to-all-done.3 = bf16[16,4,16,128]{3,2,1,0:T(8,128)(2,1)S(1)} async-done(((bf16[16,4,16,128]{3,2,1,0:T(8,128)(2,1)}), bf16[16,4,16,128]{3,2,1,0:T(8,128)(2,1)S(1)}, u32[]{:S(2)}, u32[]{:S(2)}) %all-to-all-start.3) | async-done | bytes 262176 | tf_op jit(solution)/shard_map/all_to_all | solution.py:390
  80.8 3.7 %collective-permute-start.14 = (bf16[64,16,128]{2,1,0:T(8,128)(2,1)S(1)}, bf16[64,16,128]{2,1,0:T(8,128)(2,1)S(1)}, u32[]{:S(2)}, u32[]{:S(2)}) collective-permute-start(bf16[64,16,128]{2,1,0:T(8,128)(2,1)S(1)} %bitcast.11), channel_id=1, source_target_pairs={{0,1},{1,0},{2,3},{3,2},{4,5},{5,4},{6,7},{7,6},{8,9},{9,8},{10,11... | collective-permute-start | bytes 786440 | tf_op jit(solution)/shard_map/ppermute | solution.py:386
  84.5 1.0 %shard_map.100 = bf16[2,8,32,256]{3,2,1,0:T(8,128)(2,1)} custom-call(bf16[2,8,32,256]{3,2,1,0:T(8,128)(2,1)S(1)} %bitcast.18, f32[1,256]{1,0:T(1,128)S(1)} %bitcast.22, f32[2,8,32,256]{3,2,1,0:T(8,128)S(1)} %bitcast.23, bf16[8,2,16,256]{3,2,1,0:T(8,128)(2,1)S(1)} %get-tuple-element.47.refs_0_.rest_0_, ...), custom_call_target="tpu_custom_call" | custom-call | flops 1600000000 | bytes 4000000 | tf_op jit(solution)/shard_map/pallas_call | solution.py:374
  85.6 0.1 collective-permute-done.14.theirs
  85.7 1.1 %shard_map.104 = (f32[256,768]{1,0:T(8,128)}, f32[256,256]{1,0:T(8,128)}) custom-call(bf16[64,16,128]{2,1,0:T(8,128)(2,1)S(1)} %bitcast.12, bf16[64,16,128]{2,1,0:T(8,128)(2,1)S(1)} %collective-permute-done.14.theirs), custom_call_target="tpu_custom_call" | custom-call | flops 800000000 | bytes 2000000 | tf_op jit(solution)/shard_map/pallas_call | solution.py:374
  (16 shorter events, 0.1 us)
Async XLA Ops:
  0.6 16.4 %copy-start.3 = (bf16[1,2,8,32,256]{4,3,2,1,0:T(8,128)(2,1)S(1)}, bf16[1,2,8,32,256]{4,3,2,1,0:T(8,128)(2,1)}, u32[]{:S(2)}) copy-start(bf16[1,2,8,32,256]{4,3,2,1,0:T(8,128)(2,1)} %param.6) | copy-start | bytes 786436
  2.8 18.1 %collective-permute-start = (bf16[2,8,16,256]{3,2,1,0:T(8,128)(2,1)}, bf16[2,8,16,256]{3,2,1,0:T(8,128)(2,1)S(1)}, u32[]{:S(2)}, u32[]{:S(2)}) collective-permute-start(bf16[2,8,16,256]{3,2,1,0:T(8,128)(2,1)} %get-tuple-element.38), channel_id=1, source_target_pairs={{0,1},{1,0},{2,3},{3,2},{4,5},{5,4},{6,7},{7,6},{8,9},{9,8},{10,11... | collective-permute-start | bytes 393224 | tf_op jit(solution)/shard_map/ppermute | solution.py:386
  6.1 14.8 %collective-permute-start.1 = (bf16[2,8,16,256]{3,2,1,0:T(8,128)(2,1)}, bf16[2,8,16,256]{3,2,1,0:T(8,128)(2,1)S(1)}, u32[]{:S(2)}, u32[]{:S(2)}) collective-permute-start(bf16[2,8,16,256]{3,2,1,0:T(8,128)(2,1)} %get-tuple-element.39), channel_id=1, source_target_pairs={{0,2},{1,3},{2,0},{3,1},{4,6},{5,7},{6,4},{7,5},{8,10},{9,11},{10,... | collective-permute-start | bytes 393224 | tf_op jit(solution)/shard_map/ppermute | solution.py:386
  6.1 14.8 %collective-permute-start.2 = (bf16[2,8,16,256]{3,2,1,0:T(8,128)(2,1)}, bf16[2,8,16,256]{3,2,1,0:T(8,128)(2,1)S(1)}, u32[]{:S(2)}, u32[]{:S(2)}) collective-permute-start(bf16[2,8,16,256]{3,2,1,0:T(8,128)(2,1)} %get-tuple-element.40), channel_id=1, source_target_pairs={{0,3},{1,2},{2,1},{3,0},{4,7},{5,6},{6,5},{7,4},{8,11},{9,10},{10,... | collective-permute-start | bytes 393224 | tf_op jit(solution)/shard_map/ppermute | solution.py:386
  7.8 9.2 %copy-start = (bf16[256,768]{1,0:T(8,128)(2,1)S(1)}, bf16[256,768]{1,0:T(8,128)(2,1)}, u32[]{:S(2)}) copy-start(bf16[256,768]{1,0:T(8,128)(2,1)} %w_qkv.3) | copy-start | bytes 1179652
  7.8 9.2 %copy-start.1 = (bf16[1,2,8,32,256]{4,3,2,1,0:T(8,128)(2,1)S(1)}, bf16[1,2,8,32,256]{4,3,2,1,0:T(8,128)(2,1)}, u32[]{:S(2)}) copy-start(bf16[1,2,8,32,256]{4,3,2,1,0:T(8,128)(2,1)} %param.8) | copy-start | bytes 786436
  7.8 9.2 %copy-start.2 = (bf16[1,2,8,32,256]{4,3,2,1,0:T(8,128)(2,1)S(1)}, bf16[1,2,8,32,256]{4,3,2,1,0:T(8,128)(2,1)}, u32[]{:S(2)}) copy-start(bf16[1,2,8,32,256]{4,3,2,1,0:T(8,128)(2,1)} %param.7) | copy-start | bytes 786436
  7.8 9.2 %copy-start.4 = (bf16[256,256]{1,0:T(8,128)(2,1)S(1)}, bf16[256,256]{1,0:T(8,128)(2,1)}, u32[]{:S(2)}) copy-start(bf16[256,256]{1,0:T(8,128)(2,1)} %w_out.3) | copy-start | bytes 393220
  7.8 26.9 %all-to-all-start = ((bf16[16,2,2,16,256]{4,3,2,1,0:T(8,128)(2,1)}), bf16[16,2,2,16,256]{4,3,2,1,0:T(8,128)(2,1)S(1)}, u32[]{:S(2)}, u32[]{:S(2)}) async-start(bf16[16,2,2,16,256]{4,3,2,1,0:T(8,128)(2,1)} %bitcast.24), calls=%async_computation | async-start | bytes 1048576 | tf_op jit(solution)/shard_map/all_to_all | solution.py:390
  17.0 0.7 copy-start.5
  17.7 3.2 %copy-start.6 = (bf16[2,8,16,256]{3,2,1,0:T(8,128)(2,1)S(1)}, bf16[2,8,16,256]{3,2,1,0:T(8,128)(2,1)}, u32[]{:S(2)}) copy-start(bf16[2,8,16,256]{3,2,1,0:T(8,128)(2,1)} %get-tuple-element.37.refs_0_) | copy-start | bytes 393220
  24.4 2.8 %collective-permute-start.4 = (bf16[33,16,128]{2,1,0:T(8,128)(2,1)S(1)}, bf16[33,16,128]{2,1,0:T(8,128)(2,1)S(1)}, u32[]{:S(2)}, u32[]{:S(2)}) collective-permute-start(bf16[33,16,128]{2,1,0:T(8,128)(2,1)S(1)} %get-tuple-element.46), channel_id=1, source_target_pairs={{0,1},{1,0},{2,3},{3,2},{4,5},{5,4},{6,7},{7,6},{8,9},{9,8},{10,11... | collective-permute-start | bytes 405512 | tf_op jit(solution)/shard_map/ppermute | solution.py:386
  24.9 2.2 %collective-permute-start.3 = (bf16[32,16,128]{2,1,0:T(8,128)(2,1)S(1)}, bf16[32,16,128]{2,1,0:T(8,128)(2,1)S(1)}, u32[]{:S(2)}, u32[]{:S(2)}) collective-permute-start(bf16[32,16,128]{2,1,0:T(8,128)(2,1)S(1)} %get-tuple-element.45), channel_id=1, source_target_pairs={{0,1},{1,0},{2,3},{3,2},{4,5},{5,4},{6,7},{7,6},{8,9},{9,8},{10,11... | collective-permute-start | bytes 393224 | tf_op jit(solution)/shard_map/ppermute | solution.py:386
  25.1 13.6 %collective-permute-start.9 = (bf16[8,16,256]{2,1,0:T(8,128)(2,1)S(1)}, bf16[8,16,256]{2,1,0:T(8,128)(2,1)S(1)}, u32[]{:S(2)}, u32[]{:S(2)}) collective-permute-start(bf16[8,16,256]{2,1,0:T(8,128)(2,1)S(1)} %get-tuple-element.52), channel_id=1, source_target_pairs={{0,1},{1,0},{2,3},{3,2},{4,5},{5,4},{6,7},{7,6},{8,9},{9,8},{10,11... | collective-permute-start | bytes 196616 | tf_op jit(solution)/shard_map/ppermute | solution.py:386
  25.5 13.2 %collective-permute-start.10 = (bf16[8,16,256]{2,1,0:T(8,128)(2,1)S(1)}, bf16[8,16,256]{2,1,0:T(8,128)(2,1)S(1)}, u32[]{:S(2)}, u32[]{:S(2)}) collective-permute-start(bf16[8,16,256]{2,1,0:T(8,128)(2,1)S(1)} %get-tuple-element.53), channel_id=1, source_target_pairs={{0,2},{1,3},{2,0},{3,1},{4,6},{5,7},{6,4},{7,5},{8,10},{9,11},{10,... | collective-permute-start | bytes 196616 | tf_op jit(solution)/shard_map/ppermute | solution.py:386
  25.8 12.9 %collective-permute-start.11 = (bf16[8,16,256]{2,1,0:T(8,128)(2,1)S(1)}, bf16[8,16,256]{2,1,0:T(8,128)(2,1)S(1)}, u32[]{:S(2)}, u32[]{:S(2)}) collective-permute-start(bf16[8,16,256]{2,1,0:T(8,128)(2,1)S(1)} %get-tuple-element.54), channel_id=1, source_target_pairs={{0,3},{1,2},{2,1},{3,0},{4,7},{5,6},{6,5},{7,4},{8,11},{9,10},{10,... | collective-permute-start | bytes 196616 | tf_op jit(solution)/shard_map/ppermute | solution.py:386
  38.7 3.9 %collective-permute-start.13 = (bf16[33,16,128]{2,1,0:T(8,128)(2,1)S(1)}, bf16[33,16,128]{2,1,0:T(8,128)(2,1)S(1)}, u32[]{:S(2)}, u32[]{:S(2)}) collective-permute-start(bf16[33,16,128]{2,1,0:T(8,128)(2,1)S(1)} %get-tuple-element.61), channel_id=1, source_target_pairs={{0,1},{1,0},{2,3},{3,2},{4,5},{5,4},{6,7},{7,6},{8,9},{9,8},{10,11... | collective-permute-start | bytes 405512 | tf_op jit(solution)/shard_map/ppermute | solution.py:386
  41.3 1.3 %collective-permute-start.12 = (bf16[32,16,128]{2,1,0:T(8,128)(2,1)S(1)}, bf16[32,16,128]{2,1,0:T(8,128)(2,1)S(1)}, u32[]{:S(2)}, u32[]{:S(2)}) collective-permute-start(bf16[32,16,128]{2,1,0:T(8,128)(2,1)S(1)} %get-tuple-element.60), channel_id=1, source_target_pairs={{0,1},{1,0},{2,3},{3,2},{4,5},{5,4},{6,7},{7,6},{8,9},{9,8},{10,11... | collective-permute-start | bytes 393224 | tf_op jit(solution)/shard_map/ppermute | solution.py:386
  41.4 6.4 %collective-permute-start.5 = (bf16[8,2,16,256]{3,2,1,0:T(8,128)(2,1)S(1)}, bf16[8,2,16,256]{3,2,1,0:T(8,128)(2,1)S(1)}, u32[]{:S(2)}, u32[]{:S(2)}) collective-permute-start(bf16[8,2,16,256]{3,2,1,0:T(8,128)(2,1)S(1)} %get-tuple-element.48), channel_id=1, source_target_pairs={{0,8},{8,0},{16,24},{24,16},{32,40},{40,32},{48,56},{56,48},{1,9},... | collective-permute-start | bytes 393224 | tf_op jit(solution)/shard_map/ppermute | solution.py:386
  43.4 13.4 %all-to-all-start.1 = ((bf16[16,5,16,128]{3,2,1,0:T(8,128)(2,1)}), bf16[16,5,16,128]{3,2,1,0:T(8,128)(2,1)S(1)}, u32[]{:S(2)}, u32[]{:S(2)}) async-start(bf16[16,5,16,128]{3,2,1,0:T(8,128)(2,1)} %shard_map.101), calls=%async_computation.1 | async-start | bytes 655360 | tf_op jit(solution)/shard_map/all_to_all | solution.py:390
  47.8 13.1 %collective-permute-start.6 = (bf16[8,2,16,256]{3,2,1,0:T(8,128)(2,1)S(1)}, bf16[8,2,16,256]{3,2,1,0:T(8,128)(2,1)S(1)}, u32[]{:S(2)}, u32[]{:S(2)}) collective-permute-start(bf16[8,2,16,256]{3,2,1,0:T(8,128)(2,1)S(1)} %shard_map.97), channel_id=1, source_target_pairs={{0,32},{8,40},{16,48},{24,56},{32,0},{40,8},{48,16},{56,24},{1,33}... | collective-permute-start | bytes 393224 | tf_op jit(solution)/shard_map/ppermute | solution.py:386
  57.5 11.4 %all-to-all-start.2 = ((bf16[8,5,16,128]{3,2,1,0:T(8,128)(2,1)}), bf16[8,5,16,128]{3,2,1,0:T(8,128)(2,1)S(1)}, u32[]{:S(2)}, u32[]{:S(2)}) async-start(bf16[8,5,16,128]{3,2,1,0:T(8,128)(2,1)} %shard_map.102), calls=%async_computation.2 | async-start | bytes 327680 | tf_op jit(solution)/shard_map/all_to_all | solution.py:390
  60.9 12.2 %collective-permute-start.7 = (bf16[8,2,16,256]{3,2,1,0:T(8,128)(2,1)S(1)}, bf16[8,2,16,256]{3,2,1,0:T(8,128)(2,1)S(1)}, u32[]{:S(2)}, u32[]{:S(2)}) collective-permute-start(bf16[8,2,16,256]{3,2,1,0:T(8,128)(2,1)S(1)} %shard_map.98), channel_id=1, source_target_pairs={{0,4},{4,0},{1,5},{5,1},{2,6},{6,2},{3,7},{7,3},{8,12},{12,8},{9,1... | collective-permute-start | bytes 393224 | tf_op jit(solution)/shard_map/ppermute | solution.py:386
  69.6 11.2 %all-to-all-start.3 = ((bf16[16,4,16,128]{3,2,1,0:T(8,128)(2,1)}), bf16[16,4,16,128]{3,2,1,0:T(8,128)(2,1)S(1)}, u32[]{:S(2)}, u32[]{:S(2)}) async-start(bf16[16,4,16,128]{3,2,1,0:T(8,128)(2,1)} %get-tuple-element.62), calls=%async_computation.3 | async-start | bytes 524288 | tf_op jit(solution)/shard_map/all_to_all | solution.py:390
  73.2 11.3 %collective-permute-start.8 = (bf16[8,2,16,256]{3,2,1,0:T(8,128)(2,1)S(1)}, bf16[8,2,16,256]{3,2,1,0:T(8,128)(2,1)S(1)}, u32[]{:S(2)}, u32[]{:S(2)}) collective-permute-start(bf16[8,2,16,256]{3,2,1,0:T(8,128)(2,1)S(1)} %shard_map.99), channel_id=1, source_target_pairs={{0,16},{8,24},{16,0},{24,8},{32,48},{40,56},{48,32},{56,40},{1,17}... | collective-permute-start | bytes 393224 | tf_op jit(solution)/shard_map/ppermute | solution.py:386
  80.8 4.9 %collective-permute-start.14 = (bf16[64,16,128]{2,1,0:T(8,128)(2,1)S(1)}, bf16[64,16,128]{2,1,0:T(8,128)(2,1)S(1)}, u32[]{:S(2)}, u32[]{:S(2)}) collective-permute-start(bf16[64,16,128]{2,1,0:T(8,128)(2,1)S(1)} %bitcast.11), channel_id=1, source_target_pairs={{0,1},{1,0},{2,3},{3,2},{4,5},{5,4},{6,7},{7,6},{8,9},{9,8},{10,11... | collective-permute-start | bytes 786440 | tf_op jit(solution)/shard_map/ppermute | solution.py:386

commit v6 on v5

--- a/solution.py
+++ b/solution.py
@@ -176,35 +176,43 @@
     return lax.axis_index("z") * 2 + lax.axis_index("xh")
 
 
-def pieces_kernel(tokens, cotangent, to_first, *rest):
-    to_second, (held, sem) = rest[:4], rest[4:]
-    loads, firsts, seconds = [], [], []
+def pieces_kernel(tokens, cotangent, to_first, near, mate, far, held, sem):
+    core, chip = lax.axis_index("c"), lax.axis_index("xl")
+    loads, stores = [], []
     for kind, ref in enumerate((tokens, cotangent)):
-        at = kind * 9
-        loads.append(pltpu.make_async_copy(ref, held.at[kind], sem.at[at]))
         for x in range(2):
-            for z in range(2):
-                source = held.at[kind, x, :, pl.ds(z * ROWS, ROWS), :]
-                target = to_first.at[:, z, kind, x]
-                firsts.append(
-                    (kind, pltpu.make_async_copy(source, target, sem.at[at + 1 + x * 2 + z]))
+            at = len(loads) * 5
+            source = held.at[kind, x]
+            loads.append(pltpu.make_async_copy(ref.at[x], source, sem.at[at]))
+            targets = [(z, to_first.at[:, z, kind, x]) for z in range(2)]
+            copies = [
+                pltpu.make_async_copy(
+                    source.at[:, pl.ds(z * ROWS, ROWS), :], target, sem.at[at + 1 + z]
                 )
-        for mask, out in enumerate(to_second):
-            peer = along_second() ^ mask
-            rows = pl.ds(pl.multiple_of((peer & 1) * ROWS, ROWS), ROWS)
-            source = held.at[kind, peer >> 1, :, rows, :]
-            seconds.append(
-                (kind, pltpu.make_async_copy(source, out.at[kind], sem.at[at + 5 + mask]))
-            )
+                for z, target in targets
+            ]
+            stores.append(copies)
     for load in loads:
         load.start()
-    for now, load in enumerate(loads):
+    for load, copies in zip(loads, stores):
         load.wait()
-        for kind, store in firsts + seconds:
-            if kind == now:
-                store.start()
-    for _, store in firsts + seconds:
-        store.wait()
+        for copy in copies:
+            copy.start()
+    late = []
+    for kind in range(2):
+        for other in range(2):
+            z = core ^ other
+            rows = pl.ds(pl.multiple_of(z * ROWS, ROWS), ROWS)
+            for target, x in (((near, mate)[other].at[kind], chip), (far.at[other, kind], 1 - chip)):
+                late.append(
+                    pltpu.make_async_copy(
+                        held.at[kind, x, :, rows, :], target, sem.at[20 + len(late)]
+                    )
+                )
+                late[-1].start()
+    for copies in stores + [late]:
+        for copy in copies:
+            copy.wait()
 
 
 def third_kernel(
@@ -245,6 +253,8 @@
 def second_kernel(*refs):
     pieces, (gain, w_qkv, w_out), parts = refs[:4], refs[4:7], refs[7:10]
     back, packed, scratch, halves = refs[10:14], refs[14:17], refs[17:-1], refs[-1]
+    near, mate, far, passed = pieces
+    pieces = (near, mate, far.at[0], passed.at[1])
     tokens = jnp.concatenate([piece[0].reshape(-1, WIDTH) for piece in pieces], axis=0)
     cot = jnp.concatenate([piece[1].reshape(-1, WIDTH) for piece in pieces], axis=0)
     grad_normed, part_qkv, part_gain = axis_grads(
@@ -396,16 +406,23 @@
     upstream = cotangent[0]
     flat = (TOKENS, WIDTH)
     tile = (16, LANES)
-    to_first, *to_second = kernel_call(
+    quarter = (2, 8, ROWS, WIDTH)
+    to_first, near, mate, far = kernel_call(
         pieces_kernel,
-        (shape((8, 2, 2, 2, ROWS, WIDTH), BF16),) + (shape((2, 8, ROWS, WIDTH), BF16),) * 4,
+        (
+            shape((8, 2, 2, 2, ROWS, WIDTH), BF16),
+            shape(quarter, BF16),
+            shape(quarter, BF16),
+            shape((2, *quarter), BF16),
+        ),
         (local, upstream),
         2,
-        [pltpu.VMEM((2, *local.shape), BF16), pltpu.SemaphoreType.DMA((18,))],
+        [pltpu.VMEM((2, *local.shape), BF16), pltpu.SemaphoreType.DMA((28,))],
         space=HBM,
     )
     at_first = exchange(to_first.reshape(16, 2, 2, ROWS, WIDTH), FIRST)
-    at_second = [to_second[0]] + [swap(to_second[m], SECOND, m, 4) for m in (1, 2, 3)]
+    far = swap(far, "xl", 1, 2)
+    at_second = [near, swap(mate, "c", 1, 2), far, swap(far, "c", 1, 2)]
     third, third_qkv, part_out, third_gain = kernel_call(
         third_kernel,
         (
@@ -415,7 +432,7 @@
             shape((1, WIDTH), F32),
         ),
         (local.reshape(flat), upstream.reshape(flat), attn.reshape(flat), gain_row, w_qkv, w_out),
-        0.1,
+        5,
         SCRATCH,
     )
     packed = (
@@ -428,7 +445,7 @@
         second_kernel,
         (shape((8, ROWS, WIDTH), BF16),) * 4 + packed,
         (*at_second, gain_row, w_qkv, w_out, third_qkv, part_out, third_gain),
-        50,
+        5,
         SCRATCH + [halves],
     )
     from_second = [back[0]] + [swap(back[m], SECOND, m, 4) for m in (1, 2, 3)]

time: 87.2 us -> 85.2 us (0.977)
  waiting for transfers between devices: 32.1 us -> 29.6 us
    all_to_all x4, waiting for transfers between devices: 30.7 us -> 28.2 us  [exchange(): return lax.all_to_all(pieces, axes, split_axis=0, concat_axis=0, tiled=True)]
    all_to_all x4, starting transfers between devices: 20.4 us -> 21.8 us  [exchange(): return lax.all_to_all(pieces, axes, split_axis=0, concat_axis=0, tiled=True)]
    ppermute x15, starting transfers between devices: 15.6 us -> 14.6 us  [swap(): return lax.ppermute(array, axis, [(i, i ^ mask) for i in range(size)])]
where the time goes in v6:
time: 85.2 us; the launch traced here: 84.7 us
  starting transfers between devices  36.5 us (43%)
  waiting for transfers between devices  29.6 us (35%)
  Pallas kernels  17.2 us (20%)
    all_to_all x4, waiting for transfers between devices, exchange(): return lax.all_to_all(pieces, axes, split_axis=0, concat_axis=0, tiled=True)  28.2 us
    all_to_all x4, starting transfers between devices, exchange(): return lax.all_to_all(pieces, axes, split_axis=0, concat_axis=0, tiled=True)  21.8 us
    pallas_call x12, Pallas kernels, kernel_call(): pl.pallas_call(body, out_shape=outs, in_specs=spaces or [space] * len(ope...  17.2 us
    ppermute x15, starting transfers between devices, swap(): return lax.ppermute(array, axis, [(i, i ^ mask) for i in range(size)])  14.6 us
  transfers between devices with their start and end apart: 19, of which 6 were waited for; matrix products, arithmetic and copies ran while one was open for 0% of the time, Pallas kernels for 16%

profile of v6, /device:TPU:1, one launch (start us, length us, event | category | flops | bytes accessed | tf_op | source)
XLA Modules:
  0.0 84.7 jit_solution(1222345409292748898)
XLA Ops:
  0.6 2.2 %shard_map.94 = (bf16[8,2,2,2,16,256]{5,4,3,2,1,0:T(8,128)(2,1)}, bf16[2,8,16,256]{3,2,1,0:T(8,128)(2,1)}, bf16[2,8,16,256]{3,2,1,0:T(8,128)(2,1)}, bf16[2,2,8,16,256]{4,3,2,1,0:T(8,128)(2,1)}) custom-call(bf16[2,8,32,256]{3,2,1,0:T(8,128)(2,1)} %bitcast.16, bf16[2,8,32,256]{3,2,1,0:T(8,128)(2,1)} %bitcast.13), custom_call_target="tpu_custom_call" | custom-call | flops 1600000000 | bytes 4000000 | tf_op jit(solution)/shard_map/pallas_call | solution.py:384
  2.9 2.1 %collective-permute-start.1 = (bf16[2,2,8,16,256]{4,3,2,1,0:T(8,128)(2,1)}, bf16[2,2,8,16,256]{4,3,2,1,0:T(8,128)(2,1)S(1)}, u32[]{:S(2)}, u32[]{:S(2)}) collective-permute-start(bf16[2,2,8,16,256]{4,3,2,1,0:T(8,128)(2,1)} %get-tuple-element.38), channel_id=1, source_target_pairs={{0,2},{2,0},{1,3},{3,1},{4,6},{6,4},{5,7},{7,5},{8,10},{10,8},{9,1... | collective-permute-start | bytes 786440 | tf_op jit(solution)/shard_map/ppermute | solution.py:396
  5.0 10.6 %all-to-all-start = ((bf16[16,2,2,16,256]{4,3,2,1,0:T(8,128)(2,1)}), bf16[16,2,2,16,256]{4,3,2,1,0:T(8,128)(2,1)S(1)}, u32[]{:S(2)}, u32[]{:S(2)}) async-start(bf16[16,2,2,16,256]{4,3,2,1,0:T(8,128)(2,1)} %bitcast.24), calls=%async_computation | async-start | bytes 1048576 | tf_op jit(solution)/shard_map/all_to_all | solution.py:400
  15.6 1.3 %collective-permute-start = (bf16[2,8,16,256]{3,2,1,0:T(8,128)(2,1)}, bf16[2,8,16,256]{3,2,1,0:T(8,128)(2,1)S(1)}, u32[]{:S(2)}, u32[]{:S(2)}) collective-permute-start(bf16[2,8,16,256]{3,2,1,0:T(8,128)(2,1)} %get-tuple-element.37), channel_id=1, source_target_pairs={{0,1},{1,0},{2,3},{3,2},{4,5},{5,4},{6,7},{7,6},{8,9},{9,8},{10,11... | collective-permute-start | bytes 393224 | tf_op jit(solution)/shard_map/ppermute | solution.py:396
  16.9 0.0 collective-permute-done.1.refs_2_
  16.9 0.1 collective-permute-start.2
  17.1 0.6 copy-done.5
  17.7 3.2 %shard_map.93 = (f32[512,256]{1,0:T(8,128)S(1)}, f32[256,768]{1,0:T(8,128)S(1)}, f32[256,256]{1,0:T(8,128)S(1)}, f32[1,256]{1,0:T(1,128)S(1)}) custom-call(bf16[512,256]{1,0:T(8,128)(2,1)S(1)} %bitcast.17, bf16[512,256]{1,0:T(8,128)(2,1)S(1)} %bitcast.14, bf16[512,256]{1,0:T(8,128)(2,1)S(1)} %bitcast.15, f32[1,256]{1,0:T(1,128)S(1)} %bitcast.19, ...), custom_call_target="tpu_custom_call" | custom-call | flops 4000000000 | bytes 10000000 | tf_op jit(solution)/shard_map/pallas_call | solution.py:384
  20.9 0.0 collective-permute-done.refs_1_
  20.9 0.0 collective-permute-done.2.refs_3_
  20.9 3.5 %shard_map.95 = (bf16[8,16,256]{2,1,0:T(8,128)(2,1)S(1)}, bf16[8,16,256]{2,1,0:T(8,128)(2,1)S(1)}, bf16[8,16,256]{2,1,0:T(8,128)(2,1)S(1)}, bf16[8,16,256]{2,1,0...) custom-call(bf16[2,8,16,256]{3,2,1,0:T(8,128)(2,1)S(1)} %copy-done.6, ...), custom_call_target="tpu_custom_call" | custom-call | flops 4000000000 | bytes 10000000 | tf_op jit(solution)/shard_map/pallas_call | solution.py:384
  24.4 0.5 collective-permute-start.4
  24.9 0.1 collective-permute-start.3
  25.0 0.4 collective-permute-start.9
  25.4 0.0 collective-permute-start.10
  25.5 1.7 %collective-permute-start.11 = (bf16[8,16,256]{2,1,0:T(8,128)(2,1)S(1)}, bf16[8,16,256]{2,1,0:T(8,128)(2,1)S(1)}, u32[]{:S(2)}, u32[]{:S(2)}) collective-permute-start(bf16[8,16,256]{2,1,0:T(8,128)(2,1)S(1)} %get-tuple-element.52), channel_id=1, source_target_pairs={{0,3},{1,2},{2,1},{3,0},{4,7},{5,6},{6,5},{7,4},{8,11},{9,10},{10,... | collective-permute-start | bytes 196616 | tf_op jit(solution)/shard_map/ppermute | solution.py:396
  27.2 0.0 collective-permute-done.3.early_low
  27.2 0.0 collective-permute-done.4.early_high
  27.2 5.7 %all-to-all-done.pieces = bf16[16,2,2,16,256]{4,3,2,1,0:T(8,128)(2,1)S(1)} async-done(((bf16[16,2,2,16,256]{4,3,2,1,0:T(8,128)(2,1)}), bf16[16,2,2,16,256]{4,3,2,1,0:T(8,128)(2,1)S(1)}, u32[]{:S(2)}, u32[]{:S(2)}) %all-to-all-start) | async-done | bytes 524320 | tf_op jit(solution)/shard_map/all_to_all | solution.py:400
  32.8 3.9 %shard_map.96 = (bf16[8,2,16,256]{3,2,1,0:T(8,128)(2,1)S(1)}, bf16[8,2,16,256]{3,2,1,0:T(8,128)(2,1)S(1)}, f32[66,16,128]{2,1,0:T(8,128)S(1)}, bf16[32,16,128]{2,1,0:T(8,128)(2,1)S(1)}, bf16[33,16,128]{2,1,0:T(8,128)(2,1)S(1)}) custom-call(bf16[16,2,2,16,256]{4,3,2,1,0:T(8,128)(2,1)S(1)} %all-to-all-done.pieces, ...), custom_call_target="tpu_custom_call" | custom-call | flops 4000000000 | bytes 10000000 | tf_op jit(solution)/shard_map/pallas_call | solution.py:384
  36.8 0.0 collective-permute-done.9.rest_6_
  36.8 0.0 collective-permute-done.10.rest_7_
  36.8 0.0 collective-permute-done.11.rest_8_
  36.8 2.5 %collective-permute-start.13 = (bf16[33,16,128]{2,1,0:T(8,128)(2,1)S(1)}, bf16[33,16,128]{2,1,0:T(8,128)(2,1)S(1)}, u32[]{:S(2)}, u32[]{:S(2)}) collective-permute-start(bf16[33,16,128]{2,1,0:T(8,128)(2,1)S(1)} %get-tuple-element.59), channel_id=1, source_target_pairs={{0,1},{1,0},{2,3},{3,2},{4,5},{5,4},{6,7},{7,6},{8,9},{9,8},{10,11... | collective-permute-start | bytes 405512 | tf_op jit(solution)/shard_map/ppermute | solution.py:396
  39.3 0.1 collective-permute-start.12
  39.4 0.0 collective-permute-start.5
  39.4 1.2 %collective-permute-done.12.low = bf16[32,16,128]{2,1,0:T(8,128)(2,1)S(1)} collective-permute-done((bf16[32,16,128]{2,1,0:T(8,128)(2,1)S(1)}, bf16[32,16,128]{2,1,0:T(8,128)(2,1)S(1)}, u32[]{:S(2)}, u32[]{:S(2)}) %collective-permute-start.12) | collective-permute-done | bytes 131104 | tf_op jit(solution)/shard_map/ppermute | solution.py:396
  40.7 0.0 collective-permute-done.13.high
  40.7 0.8 shard_map.101
  41.4 4.3 %all-to-all-start.1 = ((bf16[16,5,16,128]{3,2,1,0:T(8,128)(2,1)}), bf16[16,5,16,128]{3,2,1,0:T(8,128)(2,1)S(1)}, u32[]{:S(2)}, u32[]{:S(2)}) async-start(bf16[16,5,16,128]{3,2,1,0:T(8,128)(2,1)} %shard_map.101), calls=%async_computation.1 | async-start | bytes 655360 | tf_op jit(solution)/shard_map/all_to_all | solution.py:400
  45.8 0.0 collective-permute-done.5.refs_1_.rest_1_
  45.8 1.6 %collective-permute-start.6 = (bf16[8,2,16,256]{3,2,1,0:T(8,128)(2,1)S(1)}, bf16[8,2,16,256]{3,2,1,0:T(8,128)(2,1)S(1)}, u32[]{:S(2)}, u32[]{:S(2)}) collective-permute-start(bf16[8,2,16,256]{3,2,1,0:T(8,128)(2,1)S(1)} %shard_map.97), channel_id=1, source_target_pairs={{0,32},{8,40},{16,48},{24,56},{32,0},{40,8},{48,16},{56,24},{1,33}... | collective-permute-start | bytes 393224 | tf_op jit(solution)/shard_map/ppermute | solution.py:396
  47.4 7.4 %all-to-all-done.1.received = bf16[16,5,16,128]{3,2,1,0:T(8,128)(2,1)S(1)} async-done(((bf16[16,5,16,128]{3,2,1,0:T(8,128)(2,1)}), bf16[16,5,16,128]{3,2,1,0:T(8,128)(2,1)S(1)}, u32[]{:S(2)}, u32[]{:S(2)}) %all-to-all-start.1) | async-done | bytes 327712 | tf_op jit(solution)/shard_map/all_to_all | solution.py:400
  54.8 0.7 shard_map.102
  55.5 3.4 %all-to-all-start.2 = ((bf16[8,5,16,128]{3,2,1,0:T(8,128)(2,1)}), bf16[8,5,16,128]{3,2,1,0:T(8,128)(2,1)S(1)}, u32[]{:S(2)}, u32[]{:S(2)}) async-start(bf16[8,5,16,128]{3,2,1,0:T(8,128)(2,1)} %shard_map.102), calls=%async_computation.2 | async-start | bytes 327680 | tf_op jit(solution)/shard_map/all_to_all | solution.py:400
  58.9 0.0 collective-permute-done.6.refs_2_.rest_2_
  58.9 0.3 collective-permute-start.7
  59.3 7.6 %all-to-all-done.2.received = bf16[8,5,16,128]{3,2,1,0:T(8,128)(2,1)S(1)} async-done(((bf16[8,5,16,128]{3,2,1,0:T(8,128)(2,1)}), bf16[8,5,16,128]{3,2,1,0:T(8,128)(2,1)S(1)}, u32[]{:S(2)}, u32[]{:S(2)}) %all-to-all-start.2) | async-done | bytes 163872 | tf_op jit(solution)/shard_map/all_to_all | solution.py:400
  66.8 0.7 shard_map.103
  67.6 3.5 %all-to-all-start.3 = ((bf16[16,4,16,128]{3,2,1,0:T(8,128)(2,1)}), bf16[16,4,16,128]{3,2,1,0:T(8,128)(2,1)S(1)}, u32[]{:S(2)}, u32[]{:S(2)}) async-start(bf16[16,4,16,128]{3,2,1,0:T(8,128)(2,1)} %get-tuple-element.60), calls=%async_computation.3 | async-start | bytes 524288 | tf_op jit(solution)/shard_map/all_to_all | solution.py:400
  71.1 0.0 collective-permute-done.7.refs_3_.rest_3_
  71.2 0.1 collective-permute-start.8
  71.3 7.5 %all-to-all-done.3 = bf16[16,4,16,128]{3,2,1,0:T(8,128)(2,1)S(1)} async-done(((bf16[16,4,16,128]{3,2,1,0:T(8,128)(2,1)}), bf16[16,4,16,128]{3,2,1,0:T(8,128)(2,1)S(1)}, u32[]{:S(2)}, u32[]{:S(2)}) %all-to-all-start.3) | async-done | bytes 262176 | tf_op jit(solution)/shard_map/all_to_all | solution.py:400
  78.8 3.7 %collective-permute-start.14 = (bf16[64,16,128]{2,1,0:T(8,128)(2,1)S(1)}, bf16[64,16,128]{2,1,0:T(8,128)(2,1)S(1)}, u32[]{:S(2)}, u32[]{:S(2)}) collective-permute-start(bf16[64,16,128]{2,1,0:T(8,128)(2,1)S(1)} %bitcast.11), channel_id=1, source_target_pairs={{0,1},{1,0},{2,3},{3,2},{4,5},{5,4},{6,7},{7,6},{8,9},{9,8},{10,11... | collective-permute-start | bytes 786440 | tf_op jit(solution)/shard_map/ppermute | solution.py:396
  82.5 0.0 collective-permute-done.8.rest_4_
  82.5 1.0 %shard_map.100 = bf16[2,8,32,256]{3,2,1,0:T(8,128)(2,1)} custom-call(bf16[2,8,32,256]{3,2,1,0:T(8,128)(2,1)S(1)} %bitcast.18, f32[1,256]{1,0:T(1,128)S(1)} %bitcast.22, f32[2,8,32,256]{3,2,1,0:T(8,128)S(1)} %bitcast.23, bf16[8,2,16,256]{3,2,1,0:T(8,128)(2,1)S(1)} %get-tuple-element.45.refs_0_.rest_0_, ...), custom_call_target="tpu_custom_call" | custom-call | flops 1600000000 | bytes 4000000 | tf_op jit(solution)/shard_map/pallas_call | solution.py:384
  83.5 0.1 collective-permute-done.14.theirs
  83.6 1.1 %shard_map.104 = (f32[256,768]{1,0:T(8,128)}, f32[256,256]{1,0:T(8,128)}) custom-call(bf16[64,16,128]{2,1,0:T(8,128)(2,1)S(1)} %bitcast.12, bf16[64,16,128]{2,1,0:T(8,128)(2,1)S(1)} %collective-permute-done.14.theirs), custom_call_target="tpu_custom_call" | custom-call | flops 800000000 | bytes 2000000 | tf_op jit(solution)/shard_map/pallas_call | solution.py:384
  (16 shorter events, 0.1 us)
Async XLA Ops:
  0.6 16.4 %copy-start.3 = (bf16[1,2,8,32,256]{4,3,2,1,0:T(8,128)(2,1)S(1)}, bf16[1,2,8,32,256]{4,3,2,1,0:T(8,128)(2,1)}, u32[]{:S(2)}) copy-start(bf16[1,2,8,32,256]{4,3,2,1,0:T(8,128)(2,1)} %param.6) | copy-start | bytes 786436
  2.9 14.1 %collective-permute-start.1 = (bf16[2,2,8,16,256]{4,3,2,1,0:T(8,128)(2,1)}, bf16[2,2,8,16,256]{4,3,2,1,0:T(8,128)(2,1)S(1)}, u32[]{:S(2)}, u32[]{:S(2)}) collective-permute-start(bf16[2,2,8,16,256]{4,3,2,1,0:T(8,128)(2,1)} %get-tuple-element.38), channel_id=1, source_target_pairs={{0,2},{2,0},{1,3},{3,1},{4,6},{6,4},{5,7},{7,5},{8,10},{10,8},{9,1... | collective-permute-start | bytes 786440 | tf_op jit(solution)/shard_map/ppermute | solution.py:396
  5.0 12.1 %copy-start = (bf16[256,768]{1,0:T(8,128)(2,1)S(1)}, bf16[256,768]{1,0:T(8,128)(2,1)}, u32[]{:S(2)}) copy-start(bf16[256,768]{1,0:T(8,128)(2,1)} %w_qkv.3) | copy-start | bytes 1179652
  5.0 12.1 %copy-start.1 = (bf16[1,2,8,32,256]{4,3,2,1,0:T(8,128)(2,1)S(1)}, bf16[1,2,8,32,256]{4,3,2,1,0:T(8,128)(2,1)}, u32[]{:S(2)}) copy-start(bf16[1,2,8,32,256]{4,3,2,1,0:T(8,128)(2,1)} %param.8) | copy-start | bytes 786436
  5.0 12.1 %copy-start.2 = (bf16[1,2,8,32,256]{4,3,2,1,0:T(8,128)(2,1)S(1)}, bf16[1,2,8,32,256]{4,3,2,1,0:T(8,128)(2,1)}, u32[]{:S(2)}) copy-start(bf16[1,2,8,32,256]{4,3,2,1,0:T(8,128)(2,1)} %param.7) | copy-start | bytes 786436
  5.0 12.1 %copy-start.4 = (bf16[256,256]{1,0:T(8,128)(2,1)S(1)}, bf16[256,256]{1,0:T(8,128)(2,1)}, u32[]{:S(2)}) copy-start(bf16[256,256]{1,0:T(8,128)(2,1)} %w_out.3) | copy-start | bytes 393220
  5.0 27.8 %all-to-all-start = ((bf16[16,2,2,16,256]{4,3,2,1,0:T(8,128)(2,1)}), bf16[16,2,2,16,256]{4,3,2,1,0:T(8,128)(2,1)S(1)}, u32[]{:S(2)}, u32[]{:S(2)}) async-start(bf16[16,2,2,16,256]{4,3,2,1,0:T(8,128)(2,1)} %bitcast.24), calls=%async_computation | async-start | bytes 1048576 | tf_op jit(solution)/shard_map/all_to_all | solution.py:400
  15.6 5.3 %collective-permute-start = (bf16[2,8,16,256]{3,2,1,0:T(8,128)(2,1)}, bf16[2,8,16,256]{3,2,1,0:T(8,128)(2,1)S(1)}, u32[]{:S(2)}, u32[]{:S(2)}) collective-permute-start(bf16[2,8,16,256]{3,2,1,0:T(8,128)(2,1)} %get-tuple-element.37), channel_id=1, source_target_pairs={{0,1},{1,0},{2,3},{3,2},{4,5},{5,4},{6,7},{7,6},{8,9},{9,8},{10,11... | collective-permute-start | bytes 393224 | tf_op jit(solution)/shard_map/ppermute | solution.py:396
  16.9 4.0 %collective-permute-start.2 = (bf16[2,2,8,16,256]{4,3,2,1,0:T(8,128)(2,1)S(1)}, bf16[2,2,8,16,256]{4,3,2,1,0:T(8,128)(2,1)S(1)}, u32[]{:S(2)}, u32[]{:S(2)}) collective-permute-start(bf16[2,2,8,16,256]{4,3,2,1,0:T(8,128)(2,1)S(1)} %collective-permute-done.1.refs_2_), channel_id=1, source_target_pairs={{0,1},{1,0},{2,3},{3,2},{4,5},{5,4},{6,7},{7,6},{8,9},{9,8},{10,11... | collective-permute-start | bytes 786440 | tf_op jit(solution)/shard_map/ppermute | solution.py:396
  17.0 0.7 copy-start.5
  17.7 3.2 %copy-start.6 = (bf16[2,8,16,256]{3,2,1,0:T(8,128)(2,1)S(1)}, bf16[2,8,16,256]{3,2,1,0:T(8,128)(2,1)}, u32[]{:S(2)}) copy-start(bf16[2,8,16,256]{3,2,1,0:T(8,128)(2,1)} %get-tuple-element.36.refs_0_) | copy-start | bytes 393220
  24.4 2.7 %collective-permute-start.4 = (bf16[33,16,128]{2,1,0:T(8,128)(2,1)S(1)}, bf16[33,16,128]{2,1,0:T(8,128)(2,1)S(1)}, u32[]{:S(2)}, u32[]{:S(2)}) collective-permute-start(bf16[33,16,128]{2,1,0:T(8,128)(2,1)S(1)} %get-tuple-element.44), channel_id=1, source_target_pairs={{0,1},{1,0},{2,3},{3,2},{4,5},{5,4},{6,7},{7,6},{8,9},{9,8},{10,11... | collective-permute-start | bytes 405512 | tf_op jit(solution)/shard_map/ppermute | solution.py:396
  24.9 2.2 %collective-permute-start.3 = (bf16[32,16,128]{2,1,0:T(8,128)(2,1)S(1)}, bf16[32,16,128]{2,1,0:T(8,128)(2,1)S(1)}, u32[]{:S(2)}, u32[]{:S(2)}) collective-permute-start(bf16[32,16,128]{2,1,0:T(8,128)(2,1)S(1)} %get-tuple-element.43), channel_id=1, source_target_pairs={{0,1},{1,0},{2,3},{3,2},{4,5},{5,4},{6,7},{7,6},{8,9},{9,8},{10,11... | collective-permute-start | bytes 393224 | tf_op jit(solution)/shard_map/ppermute | solution.py:396
  25.0 11.7 %collective-permute-start.9 = (bf16[8,16,256]{2,1,0:T(8,128)(2,1)S(1)}, bf16[8,16,256]{2,1,0:T(8,128)(2,1)S(1)}, u32[]{:S(2)}, u32[]{:S(2)}) collective-permute-start(bf16[8,16,256]{2,1,0:T(8,128)(2,1)S(1)} %get-tuple-element.50), channel_id=1, source_target_pairs={{0,1},{1,0},{2,3},{3,2},{4,5},{5,4},{6,7},{7,6},{8,9},{9,8},{10,11... | collective-permute-start | bytes 196616 | tf_op jit(solution)/shard_map/ppermute | solution.py:396
  25.4 11.3 %collective-permute-start.10 = (bf16[8,16,256]{2,1,0:T(8,128)(2,1)S(1)}, bf16[8,16,256]{2,1,0:T(8,128)(2,1)S(1)}, u32[]{:S(2)}, u32[]{:S(2)}) collective-permute-start(bf16[8,16,256]{2,1,0:T(8,128)(2,1)S(1)} %get-tuple-element.51), channel_id=1, source_target_pairs={{0,2},{1,3},{2,0},{3,1},{4,6},{5,7},{6,4},{7,5},{8,10},{9,11},{10,... | collective-permute-start | bytes 196616 | tf_op jit(solution)/shard_map/ppermute | solution.py:396
  25.5 11.3 %collective-permute-start.11 = (bf16[8,16,256]{2,1,0:T(8,128)(2,1)S(1)}, bf16[8,16,256]{2,1,0:T(8,128)(2,1)S(1)}, u32[]{:S(2)}, u32[]{:S(2)}) collective-permute-start(bf16[8,16,256]{2,1,0:T(8,128)(2,1)S(1)} %get-tuple-element.52), channel_id=1, source_target_pairs={{0,3},{1,2},{2,1},{3,0},{4,7},{5,6},{6,5},{7,4},{8,11},{9,10},{10,... | collective-permute-start | bytes 196616 | tf_op jit(solution)/shard_map/ppermute | solution.py:396
  36.8 3.9 %collective-permute-start.13 = (bf16[33,16,128]{2,1,0:T(8,128)(2,1)S(1)}, bf16[33,16,128]{2,1,0:T(8,128)(2,1)S(1)}, u32[]{:S(2)}, u32[]{:S(2)}) collective-permute-start(bf16[33,16,128]{2,1,0:T(8,128)(2,1)S(1)} %get-tuple-element.59), channel_id=1, source_target_pairs={{0,1},{1,0},{2,3},{3,2},{4,5},{5,4},{6,7},{7,6},{8,9},{9,8},{10,11... | collective-permute-start | bytes 405512 | tf_op jit(solution)/shard_map/ppermute | solution.py:396
  39.3 1.3 %collective-permute-start.12 = (bf16[32,16,128]{2,1,0:T(8,128)(2,1)S(1)}, bf16[32,16,128]{2,1,0:T(8,128)(2,1)S(1)}, u32[]{:S(2)}, u32[]{:S(2)}) collective-permute-start(bf16[32,16,128]{2,1,0:T(8,128)(2,1)S(1)} %get-tuple-element.58), channel_id=1, source_target_pairs={{0,1},{1,0},{2,3},{3,2},{4,5},{5,4},{6,7},{7,6},{8,9},{9,8},{10,11... | collective-permute-start | bytes 393224 | tf_op jit(solution)/shard_map/ppermute | solution.py:396
  39.4 6.4 %collective-permute-start.5 = (bf16[8,2,16,256]{3,2,1,0:T(8,128)(2,1)S(1)}, bf16[8,2,16,256]{3,2,1,0:T(8,128)(2,1)S(1)}, u32[]{:S(2)}, u32[]{:S(2)}) collective-permute-start(bf16[8,2,16,256]{3,2,1,0:T(8,128)(2,1)S(1)} %get-tuple-element.46), channel_id=1, source_target_pairs={{0,8},{8,0},{16,24},{24,16},{32,40},{40,32},{48,56},{56,48},{1,9},... | collective-permute-start | bytes 393224 | tf_op jit(solution)/shard_map/ppermute | solution.py:396
  41.4 13.3 %all-to-all-start.1 = ((bf16[16,5,16,128]{3,2,1,0:T(8,128)(2,1)}), bf16[16,5,16,128]{3,2,1,0:T(8,128)(2,1)S(1)}, u32[]{:S(2)}, u32[]{:S(2)}) async-start(bf16[16,5,16,128]{3,2,1,0:T(8,128)(2,1)} %shard_map.101), calls=%async_computation.1 | async-start | bytes 655360 | tf_op jit(solution)/shard_map/all_to_all | solution.py:400
  45.8 13.1 %collective-permute-start.6 = (bf16[8,2,16,256]{3,2,1,0:T(8,128)(2,1)S(1)}, bf16[8,2,16,256]{3,2,1,0:T(8,128)(2,1)S(1)}, u32[]{:S(2)}, u32[]{:S(2)}) collective-permute-start(bf16[8,2,16,256]{3,2,1,0:T(8,128)(2,1)S(1)} %shard_map.97), channel_id=1, source_target_pairs={{0,32},{8,40},{16,48},{24,56},{32,0},{40,8},{48,16},{56,24},{1,33}... | collective-permute-start | bytes 393224 | tf_op jit(solution)/shard_map/ppermute | solution.py:396
  55.5 11.4 %all-to-all-start.2 = ((bf16[8,5,16,128]{3,2,1,0:T(8,128)(2,1)}), bf16[8,5,16,128]{3,2,1,0:T(8,128)(2,1)S(1)}, u32[]{:S(2)}, u32[]{:S(2)}) async-start(bf16[8,5,16,128]{3,2,1,0:T(8,128)(2,1)} %shard_map.102), calls=%async_computation.2 | async-start | bytes 327680 | tf_op jit(solution)/shard_map/all_to_all | solution.py:400
  58.9 12.2 %collective-permute-start.7 = (bf16[8,2,16,256]{3,2,1,0:T(8,128)(2,1)S(1)}, bf16[8,2,16,256]{3,2,1,0:T(8,128)(2,1)S(1)}, u32[]{:S(2)}, u32[]{:S(2)}) collective-permute-start(bf16[8,2,16,256]{3,2,1,0:T(8,128)(2,1)S(1)} %shard_map.98), channel_id=1, source_target_pairs={{0,4},{4,0},{1,5},{5,1},{2,6},{6,2},{3,7},{7,3},{8,12},{12,8},{9,1... | collective-permute-start | bytes 393224 | tf_op jit(solution)/shard_map/ppermute | solution.py:396
  67.6 11.2 %all-to-all-start.3 = ((bf16[16,4,16,128]{3,2,1,0:T(8,128)(2,1)}), bf16[16,4,16,128]{3,2,1,0:T(8,128)(2,1)S(1)}, u32[]{:S(2)}, u32[]{:S(2)}) async-start(bf16[16,4,16,128]{3,2,1,0:T(8,128)(2,1)} %get-tuple-element.60), calls=%async_computation.3 | async-start | bytes 524288 | tf_op jit(solution)/shard_map/all_to_all | solution.py:400
  71.2 11.3 %collective-permute-start.8 = (bf16[8,2,16,256]{3,2,1,0:T(8,128)(2,1)S(1)}, bf16[8,2,16,256]{3,2,1,0:T(8,128)(2,1)S(1)}, u32[]{:S(2)}, u32[]{:S(2)}) collective-permute-start(bf16[8,2,16,256]{3,2,1,0:T(8,128)(2,1)S(1)} %shard_map.99), channel_id=1, source_target_pairs={{0,16},{8,24},{16,0},{24,8},{32,48},{40,56},{48,32},{56,40},{1,17}... | collective-permute-start | bytes 393224 | tf_op jit(solution)/shard_map/ppermute | solution.py:396
  78.8 4.9 %collective-permute-start.14 = (bf16[64,16,128]{2,1,0:T(8,128)(2,1)S(1)}, bf16[64,16,128]{2,1,0:T(8,128)(2,1)S(1)}, u32[]{:S(2)}, u32[]{:S(2)}) collective-permute-start(bf16[64,16,128]{2,1,0:T(8,128)(2,1)S(1)} %bitcast.11), channel_id=1, source_target_pairs={{0,1},{1,0},{2,3},{3,2},{4,5},{5,4},{6,7},{7,6},{8,9},{9,8},{10,11... | collective-permute-start | bytes 786440 | tf_op jit(solution)/shard_map/ppermute | solution.py:396

commit v7 on v6

--- a/solution.py
+++ b/solution.py
@@ -102,7 +102,6 @@
     )
     block = block.astype(F32).astype(BF16)
     lane = lax.broadcasted_iota(jnp.int32, (LENGTH, LANES), 1)
-    part_gain = jnp.zeros((1, WIDTH), F32)
     for base in range(0, PENCILS, GROUP):
         group = slice(base * LENGTH, (base + GROUP) * LENGTH)
         if strided:
@@ -122,20 +121,18 @@
             tokens_f = tokens[group].astype(F32)
             cot = cotangent[group]
         square = jnp.mean(tokens_f * tokens_f, axis=-1, keepdims=True) + EPSILON
-        unit = tokens_f * lax.rsqrt(square)
-        normed = (unit * gain).astype(BF16)
+        normed = (tokens_f * lax.rsqrt(square) * gain).astype(BF16)
         normed_rows[group] = normed
         qkv = dot(normed, w_qkv, 1, 0).astype(BF16)
         grad_attn = dot(cot, w_out, 1, 1).astype(BF16)
         joined = attention(qkv, grad_attn, block, lane, GROUP)
         joined_rows[group] = joined
         grad_normed = dot(joined, w_qkv, 1, 1)
-        part_gain = part_gain + jnp.sum(grad_normed * unit, axis=0, keepdims=True)
         for i, rows in enumerate(rows_of):
             for col in range(2):
                 grad_cols[col, rows, :] = grad_normed[spans_of(i), col * LANES : (col + 1) * LANES]
     part_qkv = dot(normed_rows[...], joined_rows[...], 0, 0)
-    return jnp.concatenate([grad_cols[0], grad_cols[1]], axis=1), part_qkv, part_gain
+    return jnp.concatenate([grad_cols[0], grad_cols[1]], axis=1), part_qkv
 
 
 def spans_of(i):
@@ -176,22 +173,24 @@
     return lax.axis_index("z") * 2 + lax.axis_index("xh")
 
 
-def pieces_kernel(tokens, cotangent, to_first, near, mate, far, held, sem):
+def pieces_kernel(tokens, cotangent, to_first, far, held, sem):
     core, chip = lax.axis_index("c"), lax.axis_index("xl")
     loads, stores = [], []
     for kind, ref in enumerate((tokens, cotangent)):
         for x in range(2):
-            at = len(loads) * 5
+            at = len(loads) * 3
             source = held.at[kind, x]
             loads.append(pltpu.make_async_copy(ref.at[x], source, sem.at[at]))
-            targets = [(z, to_first.at[:, z, kind, x]) for z in range(2)]
-            copies = [
-                pltpu.make_async_copy(
-                    source.at[:, pl.ds(z * ROWS, ROWS), :], target, sem.at[at + 1 + z]
-                )
-                for z, target in targets
-            ]
-            stores.append(copies)
+            stores.append(
+                [
+                    pltpu.make_async_copy(
+                        source.at[:, pl.ds(z * ROWS, ROWS), :],
+                        to_first.at[:, z, kind, x],
+                        sem.at[at + 1 + z],
+                    )
+                    for z in range(2)
+                ]
+            )
     for load in loads:
         load.start()
     for load, copies in zip(loads, stores):
@@ -201,34 +200,39 @@
     late = []
     for kind in range(2):
         for other in range(2):
-            z = core ^ other
-            rows = pl.ds(pl.multiple_of(z * ROWS, ROWS), ROWS)
-            for target, x in (((near, mate)[other].at[kind], chip), (far.at[other, kind], 1 - chip)):
-                late.append(
-                    pltpu.make_async_copy(
-                        held.at[kind, x, :, rows, :], target, sem.at[20 + len(late)]
-                    )
+            rows = pl.ds(pl.multiple_of((core ^ other) * ROWS, ROWS), ROWS)
+            late.append(
+                pltpu.make_async_copy(
+                    held.at[kind, 1 - chip, :, rows, :], far.at[other, kind], sem.at[12 + len(late)]
                 )
-                late[-1].start()
+            )
+            late[-1].start()
     for copies in stores + [late]:
         for copy in copies:
             copy.wait()
 
 
+def chip_pieces_kernel(tokens, cotangent, near, mate):
+    core, chip = lax.axis_index("c"), lax.axis_index("xl")
+    for other, out in enumerate((near, mate)):
+        rows = pl.ds(pl.multiple_of((core ^ other) * ROWS, ROWS), ROWS)
+        for kind, ref in enumerate((tokens, cotangent)):
+            out[kind] = ref[chip, :, rows, :]
+
+
 def third_kernel(
-    tokens, cotangent, attn, gain, w_qkv, w_out, normed_out, qkv_out, out_out, gain_out, *scratch
+    tokens, cotangent, attn, gain, w_qkv, w_out, normed_out, qkv_out, out_out, *scratch
 ):
     cot = cotangent[...]
-    grad_normed, part_qkv, part_gain = axis_grads(
+    grad_normed, part_qkv = axis_grads(
         tokens[...], cot, gain[...], w_qkv[...], w_out[...], scratch, False
     )
     normed_out[...] = grad_normed
     qkv_out[...] = part_qkv
-    gain_out[...] = part_gain
     out_out[...] = dot(attn[...], cot, 0, 0)
 
 
-def pack(total, part_out, part_gain, halves, own, low, high):
+def pack(total, part_out, halves, own, low, high):
     for at in range(2 * TILES):
         half, tile = divmod(at, TILES)
         if at < 96:
@@ -243,29 +247,24 @@
     own[0:TILES] = halves[mine].astype(own.dtype)
     low[0:HALF] = halves[1 - mine, 0:HALF].astype(BF16)
     high[0:HALF] = halves[1 - mine, HALF:TILES].astype(BF16)
-    gains = jnp.concatenate(
-        [part_gain[:, :LANES], part_gain[:, LANES:], jnp.zeros((14, LANES), F32)], axis=0
-    )
-    own[TILES] = gains.astype(own.dtype)
-    high[HALF] = gains.astype(BF16)
 
 
 def second_kernel(*refs):
-    pieces, (gain, w_qkv, w_out), parts = refs[:4], refs[4:7], refs[7:10]
-    back, packed, scratch, halves = refs[10:14], refs[14:17], refs[17:-1], refs[-1]
+    pieces, (gain, w_qkv, w_out), parts = refs[:4], refs[4:7], refs[7:9]
+    back, packed, scratch, halves = refs[9:13], refs[13:16], refs[16:-1], refs[-1]
     near, mate, far, passed = pieces
     pieces = (near, mate, far.at[0], passed.at[1])
     tokens = jnp.concatenate([piece[0].reshape(-1, WIDTH) for piece in pieces], axis=0)
     cot = jnp.concatenate([piece[1].reshape(-1, WIDTH) for piece in pieces], axis=0)
-    grad_normed, part_qkv, part_gain = axis_grads(
+    grad_normed, part_qkv = axis_grads(
         tokens, cot, gain[...], w_qkv[...], w_out[...], scratch, True
     )
     returned = grad_normed.astype(BF16)
     rows = TOKENS // 4
     for mask, out in enumerate(back):
         out[...] = returned[mask * rows : (mask + 1) * rows].reshape(out.shape)
-    third_qkv, part_out, third_gain = parts
-    pack(third_qkv[...] + part_qkv, part_out, third_gain[...] + part_gain, halves, *packed)
+    third_qkv, part_out = parts
+    pack(third_qkv[...] + part_qkv, part_out, halves, *packed)
 
 
 def first_kernel(pieces, early_own, early_low, early_high, gain, w_qkv, w_out, *refs):
@@ -280,7 +279,7 @@
         copy.start()
     tokens = pieces[:, 0].reshape(TOKENS, WIDTH)
     cot = pieces[:, 1].reshape(TOKENS, WIDTH)
-    grad_normed, part_qkv, part_gain = axis_grads(
+    grad_normed, part_qkv = axis_grads(
         tokens, cot, gain[...], w_qkv[...], w_out[...], scratch, True
     )
     returned[...] = grad_normed.astype(BF16).reshape(returned.shape)
@@ -288,17 +287,12 @@
     for at, mask in enumerate(SPANS[3]):
         stay[at] = returned[here ^ mask]
         leave[at] = returned[here ^ mask ^ BITS[0]]
-    pack(part_qkv, None, part_gain, halves, *packed)
+    pack(part_qkv, None, halves, *packed)
     for copy in copies:
         copy.wait()
     own = packed[0]
     own[0:HALF] += held_own[0:HALF].astype(F32) + held_low[...].astype(F32)
-    own[HALF:TILES] += held_own[HALF:TILES].astype(F32) + held_high[0:HALF].astype(F32)
-    own[TILES + 1] = both(held_own[TILES], held_high[HALF])
-
-
-def both(mine, theirs):
-    return mine.astype(BF16).astype(F32) + theirs.astype(F32)
+    own[HALF:TILES] += held_own[HALF:TILES].astype(F32) + held_high[...].astype(F32)
 
 
 def stage_kernel(*refs):
@@ -314,12 +308,10 @@
 
 
 def pair_kernel(own, low, high, pieces):
-    gains = (both(own[TILES], high[HALF]) + own[TILES + 1]).astype(BF16)
     for peer in range(16):
         half, at = divmod(peer * 4, HALF)
         received = (low, high)[half][at : at + 4].astype(F32)
-        pieces[peer, 0:4] = (own[peer * 4 : peer * 4 + 4] + received).astype(BF16)
-        pieces[peer, 4] = gains
+        pieces[peer] = (own[peer * 4 : peer * 4 + 4] + received).astype(BF16)
 
 
 def plane_kernel(received, pieces):
@@ -328,15 +320,13 @@
         pieces[peer] = total
 
 
-def line_kernel(scale, received, pieces, gain_out):
-    total = jnp.sum(received[...].astype(F32), axis=0) * scale
-    low = total[0:4].astype(BF16)
+def line_kernel(scale, received, pieces):
+    total = (jnp.sum(received[...].astype(F32), axis=0) * scale).astype(BF16)
     for peer in range(16):
-        pieces[peer] = low
-    gain_out[...] = jnp.concatenate([total[4, 0:1], total[4, 1:2]], axis=1)
-
-
-def assemble_kernel(mine, theirs, w_qkv_out, w_out_out, halves):
+        pieces[peer] = total
+
+
+def assemble_kernel(mine, theirs, gain, w_qkv, w_qkv_out, w_out_out, gain_out, halves):
     at_core = lax.axis_index("c")
     halves[at_core] = mine[...]
     halves[1 - at_core] = theirs[...]
@@ -349,6 +339,15 @@
         else:
             row, col = divmod(at - 96, 2)
             w_out_out[row * 16 : row * 16 + 16, col * LANES : (col + 1) * LANES] = rows
+    products = jnp.zeros((WIDTH, LANES), F32)
+    for col in range(6):
+        cols = slice(col * LANES, (col + 1) * LANES)
+        products = products + w_qkv_out[:, cols] * w_qkv[:, cols].astype(F32)
+    ones = jnp.ones((8, LANES), BF16)
+    high = products.astype(BF16)
+    low = (products - high.astype(F32)).astype(BF16)
+    total = dot(ones, high, 1, 1) + dot(ones, low, 1, 1)
+    gain_out[...] = total[0:1] / gain[...]
 
 
 def tokens_kernel(tokens, gain, third, *rest):
@@ -407,44 +406,37 @@
     flat = (TOKENS, WIDTH)
     tile = (16, LANES)
     quarter = (2, 8, ROWS, WIDTH)
-    to_first, near, mate, far = kernel_call(
+    to_first, far = kernel_call(
         pieces_kernel,
-        (
-            shape((8, 2, 2, 2, ROWS, WIDTH), BF16),
-            shape(quarter, BF16),
-            shape(quarter, BF16),
-            shape((2, *quarter), BF16),
-        ),
+        (shape((8, 2, 2, 2, ROWS, WIDTH), BF16), shape((2, *quarter), BF16)),
         (local, upstream),
         2,
-        [pltpu.VMEM((2, *local.shape), BF16), pltpu.SemaphoreType.DMA((28,))],
+        [pltpu.VMEM((2, *local.shape), BF16), pltpu.SemaphoreType.DMA((16,))],
         space=HBM,
     )
     at_first = exchange(to_first.reshape(16, 2, 2, ROWS, WIDTH), FIRST)
     far = swap(far, "xl", 1, 2)
+    near, mate = kernel_call(
+        chip_pieces_kernel, (shape(quarter, BF16),) * 2, (local, upstream), 1
+    )
     at_second = [near, swap(mate, "c", 1, 2), far, swap(far, "c", 1, 2)]
-    third, third_qkv, part_out, third_gain = kernel_call(
+    third, third_qkv, part_out = kernel_call(
         third_kernel,
-        (
-            shape(flat, F32),
-            shape((WIDTH, TRIPLE), F32),
-            shape((WIDTH, WIDTH), F32),
-            shape((1, WIDTH), F32),
-        ),
+        (shape(flat, F32), shape((WIDTH, TRIPLE), F32), shape((WIDTH, WIDTH), F32)),
         (local.reshape(flat), upstream.reshape(flat), attn.reshape(flat), gain_row, w_qkv, w_out),
         5,
         SCRATCH,
     )
     packed = (
-        shape((TILES + 1, *tile), BF16),
+        shape((TILES, *tile), BF16),
         shape((HALF, *tile), BF16),
-        shape((HALF + 1, *tile), BF16),
+        shape((HALF, *tile), BF16),
     )
     halves = pltpu.VMEM((2, TILES, *tile), F32)
     *back, own, low, high = kernel_call(
         second_kernel,
         (shape((8, ROWS, WIDTH), BF16),) * 4 + packed,
-        (*at_second, gain_row, w_qkv, w_out, third_qkv, part_out, third_gain),
+        (*at_second, gain_row, w_qkv, w_out, third_qkv, part_out),
         5,
         SCRATCH + [halves],
     )
@@ -456,7 +448,7 @@
         (
             shape((8, *block), BF16),
             shape((8, *block), BF16),
-            shape((TILES + 2, *tile), F32),
+            shape((TILES, *tile), F32),
             *packed[1:],
         ),
         (at_first, *early, gain_row, w_qkv, w_out),
@@ -476,23 +468,27 @@
     for stage in (1, 2, 3):
         leave = kernel_call(stage_kernel, shape((8, *block), BF16), groups, 20)
         groups.append(swap(leave, *SWAPS[stage]))
-    pieces = kernel_call(pair_kernel, shape((16, 5, *tile), BF16), late, 1)
+    pieces = kernel_call(pair_kernel, shape((16, 4, *tile), BF16), late, 1)
     summed = exchange(pieces, PLANE)
-    pieces = kernel_call(plane_kernel, shape((8, 5, *tile), BF16), (summed,), 1)
+    pieces = kernel_call(plane_kernel, shape((8, 4, *tile), BF16), (summed,), 1)
     summed = exchange(pieces, "z")
-    pieces, d_gain = kernel_call(
+    pieces = kernel_call(
         functools.partial(line_kernel, 1.0 / math.sqrt(count)),
-        (shape((16, 4, *tile), BF16), shape((1, WIDTH), F32)),
+        shape((16, 4, *tile), BF16),
         (summed,),
         1,
     )
     mine = exchange(pieces, PLANE)
     mine = mine.reshape(TILES, *tile)
     theirs = swap(mine, "c", 1, 2)
-    d_w_qkv, d_w_out = kernel_call(
+    d_w_qkv, d_w_out, d_gain = kernel_call(
         assemble_kernel,
-        (shape((WIDTH, TRIPLE), F32), shape((WIDTH, WIDTH), F32)),
-        (mine, theirs),
+        (
+            shape((WIDTH, TRIPLE), F32),
+            shape((WIDTH, WIDTH), F32),
+            shape((1, WIDTH), F32),
+        ),
+        (mine, theirs, gain_row, w_qkv),
         1,
         [pltpu.VMEM((2, TILES, *tile), BF16)],
     )

time: 85.2 us -> 83.9 us (0.985)
  waiting for transfers between devices: 29.6 us -> 28.7 us
    all_to_all x4, waiting for transfers between devices: 28.2 us -> 27.3 us  [exchange(): return lax.all_to_all(pieces, axes, split_axis=0, concat_axis=0, tiled=True)]
    pallas_call x12 -> x13, Pallas kernels: 17.2 us -> 17 us  [kernel_call(): pl.pallas_call(body, out_shape=outs, in_specs=spaces or [space] * len(ope...]
  transfers between devices with their start and end apart: 19 -> 19, of which waited for: 6 -> 7; matrix products, arithmetic and copies ran while one was open for 0% -> 0% of each run, Pallas kernels for 16% -> 17%
where the time goes in v7:
time: 83.9 us; the launch traced here: 83.4 us
  starting transfers between devices  36.2 us (43%)
  waiting for transfers between devices  28.7 us (34%)
  Pallas kernels  17 us (20%)
  between operations  0.85 us (1%)
    all_to_all x4, waiting for transfers between devices, exchange(): return lax.all_to_all(pieces, axes, split_axis=0, concat_axis=0, tiled=True)  27.3 us
    all_to_all x4, starting transfers between devices, exchange(): return lax.all_to_all(pieces, axes, split_axis=0, concat_axis=0, tiled=True)  21.8 us
    pallas_call x13, Pallas kernels, kernel_call(): pl.pallas_call(body, out_shape=outs, in_specs=spaces or [space] * len(ope...  17 us
    ppermute x15, starting transfers between devices, swap(): return lax.ppermute(array, axis, [(i, i ^ mask) for i in range(size)])  14.4 us
  transfers between devices with their start and end apart: 19, of which 7 were waited for; matrix products, arithmetic and copies ran while one was open for 0% of the time, Pallas kernels for 17%

profile of v7, /device:TPU:1, one launch (start us, length us, event | category | flops | bytes accessed | tf_op | source)
XLA Modules:
  0.0 83.4 jit_solution(1868127983217401977)
XLA Ops:
  0.6 2.0 %shard_map.94 = (bf16[8,2,2,2,16,256]{5,4,3,2,1,0:T(8,128)(2,1)}, bf16[2,2,8,16,256]{4,3,2,1,0:T(8,128)(2,1)}) custom-call(bf16[2,8,32,256]{3,2,1,0:T(8,128)(2,1)} %bitcast.17, bf16[2,8,32,256]{3,2,1,0:T(8,128)(2,1)} %bitcast.13), custom_call_target="tpu_custom_call" | custom-call | flops 1600000000 | bytes 4000000 | tf_op jit(solution)/shard_map/pallas_call | solution.py:383
  2.6 2.1 %collective-permute-start.1 = (bf16[2,2,8,16,256]{4,3,2,1,0:T(8,128)(2,1)}, bf16[2,2,8,16,256]{4,3,2,1,0:T(8,128)(2,1)S(1)}, u32[]{:S(2)}, u32[]{:S(2)}) collective-permute-start(bf16[2,2,8,16,256]{4,3,2,1,0:T(8,128)(2,1)} %get-tuple-element.36), channel_id=1, source_target_pairs={{0,2},{2,0},{1,3},{3,1},{4,6},{6,4},{5,7},{7,5},{8,10},{10,8},{9,1... | collective-permute-start | bytes 786440 | tf_op jit(solution)/shard_map/ppermute | solution.py:395
  4.7 10.6 %all-to-all-start = ((bf16[16,2,2,16,256]{4,3,2,1,0:T(8,128)(2,1)}), bf16[16,2,2,16,256]{4,3,2,1,0:T(8,128)(2,1)S(1)}, u32[]{:S(2)}, u32[]{:S(2)}) async-start(bf16[16,2,2,16,256]{4,3,2,1,0:T(8,128)(2,1)} %bitcast.27), calls=%async_computation | async-start | bytes 1048576 | tf_op jit(solution)/shard_map/all_to_all | solution.py:399
  15.4 0.0 copy-start
  15.4 0.0 copy-start.2
  15.4 0.0 copy-start.4
  15.4 1.3 %collective-permute-start = (bf16[2,8,16,256]{3,2,1,0:T(8,128)(2,1)S(1)}, bf16[2,8,16,256]{3,2,1,0:T(8,128)(2,1)S(1)}, u32[]{:S(2)}, u32[]{:S(2)}) collective-permute-start(bf16[2,8,16,256]{3,2,1,0:T(8,128)(2,1)S(1)} %get-tuple-element.35), channel_id=1, source_target_pairs={{0,1},{1,0},{2,3},{3,2},{4,5},{5,4},{6,7},{7,6},{8,9},{9,8},{10,11... | collective-permute-start | bytes 393224 | tf_op jit(solution)/shard_map/ppermute | solution.py:395
  16.8 0.0 collective-permute-done.1.refs_2_
  16.8 0.1 collective-permute-start.2
  16.9 0.7 copy-done.5
  17.5 3.2 %shard_map.93 = (f32[512,256]{1,0:T(8,128)S(1)}, f32[256,768]{1,0:T(8,128)S(1)}, f32[256,256]{1,0:T(8,128)S(1)}) custom-call(bf16[512,256]{1,0:T(8,128)(2,1)S(1)} %bitcast.19, bf16[512,256]{1,0:T(8,128)(2,1)S(1)} %bitcast.15, bf16[512,256]{1,0:T(8,128)(2,1)S(1)} %bitcast.16, f32[1,256]{1,0:T(1,128)S(1)} %bitcast.21, bf16[256,768]{1,0:T(8,128)(2,1)S(1)} %copy-done, ...), custom_call_target="tpu_custom_call" | custom-call | flops 4000000000 | bytes 10000000 | tf_op jit(solution)/shard_map/pallas_call | solution.py:383
  20.7 0.0 collective-permute-done.refs_1_
  20.7 0.0 collective-permute-done.2.refs_3_
  20.8 3.5 %shard_map.96 = (bf16[8,16,256]{2,1,0:T(8,128)(2,1)S(1)}, bf16[8,16,256]{2,1,0:T(8,128)(2,1)S(1)}, bf16[8,16,256]{2,1,0:T(8,128)(2,1)S(1)}, bf16[8,16,256]{2,1,0...) custom-call(bf16[2,8,16,256]{3,2,1,0:T(8,128)(2,1)S(1)} %get-tuple-e, ...), custom_call_target="tpu_custom_call" | custom-call | flops 4000000000 | bytes 10000000 | tf_op jit(solution)/shard_map/pallas_call | solution.py:383
  24.2 0.5 collective-permute-start.3
  24.8 0.1 collective-permute-start.4
  24.9 0.4 collective-permute-start.9
  25.3 0.0 collective-permute-start.10
  25.3 1.7 %collective-permute-start.11 = (bf16[8,16,256]{2,1,0:T(8,128)(2,1)S(1)}, bf16[8,16,256]{2,1,0:T(8,128)(2,1)S(1)}, u32[]{:S(2)}, u32[]{:S(2)}) collective-permute-start(bf16[8,16,256]{2,1,0:T(8,128)(2,1)S(1)} %get-tuple-element.49), channel_id=1, source_target_pairs={{0,3},{1,2},{2,1},{3,0},{4,7},{5,6},{6,5},{7,4},{8,11},{9,10},{10,... | collective-permute-start | bytes 196616 | tf_op jit(solution)/shard_map/ppermute | solution.py:395
  27.0 0.0 collective-permute-done.3.early_low
  27.0 0.0 collective-permute-done.4.early_high
  27.0 5.6 %all-to-all-done.pieces = bf16[16,2,2,16,256]{4,3,2,1,0:T(8,128)(2,1)S(1)} async-done(((bf16[16,2,2,16,256]{4,3,2,1,0:T(8,128)(2,1)}), bf16[16,2,2,16,256]{4,3,2,1,0:T(8,128)(2,1)S(1)}, u32[]{:S(2)}, u32[]{:S(2)}) %all-to-all-start) | async-done | bytes 524320 | tf_op jit(solution)/shard_map/all_to_all | solution.py:399
  32.6 3.9 %shard_map.97 = (bf16[8,2,16,256]{3,2,1,0:T(8,128)(2,1)S(1)}, bf16[8,2,16,256]{3,2,1,0:T(8,128)(2,1)S(1)}, f32[64,16,128]{2,1,0:T(8,128)S(1)}, bf16[32,16,128]{2,1,0:T(8,128)(2,1)S(1)}, bf16[32,16,128]{2,1,0:T(8,128)(2,1)S(1)}) custom-call(bf16[16,2,2,16,256]{4,3,2,1,0:T(8,128)(2,1)S(1)} %all-to-all-done.pieces, ...), custom_call_target="tpu_custom_call" | custom-call | flops 4000000000 | bytes 10000000 | tf_op jit(solution)/shard_map/pallas_call | solution.py:383
  36.5 0.0 collective-permute-done.9.rest_6_
  36.5 0.0 collective-permute-done.10.rest_7_
  36.5 0.0 collective-permute-done.11.rest_8_
  36.5 2.5 %collective-permute-start.12 = (bf16[32,16,128]{2,1,0:T(8,128)(2,1)S(1)}, bf16[32,16,128]{2,1,0:T(8,128)(2,1)S(1)}, u32[]{:S(2)}, u32[]{:S(2)}) collective-permute-start(bf16[32,16,128]{2,1,0:T(8,128)(2,1)S(1)} %get-tuple-element.55), channel_id=1, source_target_pairs={{0,1},{1,0},{2,3},{3,2},{4,5},{5,4},{6,7},{7,6},{8,9},{9,8},{10,11... | collective-permute-start | bytes 393224 | tf_op jit(solution)/shard_map/ppermute | solution.py:395
  39.0 0.1 collective-permute-start.13
  39.1 0.9 %collective-permute-done.12.low = bf16[32,16,128]{2,1,0:T(8,128)(2,1)S(1)} collective-permute-done((bf16[32,16,128]{2,1,0:T(8,128)(2,1)S(1)}, bf16[32,16,128]{2,1,0:T(8,128)(2,1)S(1)}, u32[]{:S(2)}, u32[]{:S(2)}) %collective-permute-start.12) | collective-permute-done | bytes 131104 | tf_op jit(solution)/shard_map/ppermute | solution.py:395
  40.0 0.4 collective-permute-done.13.high
  40.4 0.7 shard_map.102
  41.1 4.3 %all-to-all-start.1 = ((bf16[16,4,16,128]{3,2,1,0:T(8,128)(2,1)}), bf16[16,4,16,128]{3,2,1,0:T(8,128)(2,1)S(1)}, u32[]{:S(2)}, u32[]{:S(2)}) async-start(bf16[16,4,16,128]{3,2,1,0:T(8,128)(2,1)} %shard_map.102), calls=%async_computation.1 | async-start | bytes 524288 | tf_op jit(solution)/shard_map/all_to_all | solution.py:399
  45.4 0.0 collective-permute-done.5.refs_1_.rest_1_
  45.5 1.6 %collective-permute-start.6 = (bf16[8,2,16,256]{3,2,1,0:T(8,128)(2,1)S(1)}, bf16[8,2,16,256]{3,2,1,0:T(8,128)(2,1)S(1)}, u32[]{:S(2)}, u32[]{:S(2)}) collective-permute-start(bf16[8,2,16,256]{3,2,1,0:T(8,128)(2,1)S(1)} %shard_map.98), channel_id=1, source_target_pairs={{0,32},{8,40},{16,48},{24,56},{32,0},{40,8},{48,16},{56,24},{1,33}... | collective-permute-start | bytes 393224 | tf_op jit(solution)/shard_map/ppermute | solution.py:395
  47.1 6.7 %all-to-all-done.1.received = bf16[16,4,16,128]{3,2,1,0:T(8,128)(2,1)S(1)} async-done(((bf16[16,4,16,128]{3,2,1,0:T(8,128)(2,1)}), bf16[16,4,16,128]{3,2,1,0:T(8,128)(2,1)S(1)}, u32[]{:S(2)}, u32[]{:S(2)}) %all-to-all-start.1) | async-done | bytes 262176 | tf_op jit(solution)/shard_map/all_to_all | solution.py:399
  53.8 0.7 shard_map.103
  54.5 3.4 %all-to-all-start.2 = ((bf16[8,4,16,128]{3,2,1,0:T(8,128)(2,1)}), bf16[8,4,16,128]{3,2,1,0:T(8,128)(2,1)S(1)}, u32[]{:S(2)}, u32[]{:S(2)}) async-start(bf16[8,4,16,128]{3,2,1,0:T(8,128)(2,1)} %shard_map.103), calls=%async_computation.2 | async-start | bytes 262144 | tf_op jit(solution)/shard_map/all_to_all | solution.py:399
  57.8 0.0 collective-permute-done.6.refs_2_.rest_2_
  57.9 0.3 collective-permute-start.7
  58.1 7.7 %all-to-all-done.2.received = bf16[8,4,16,128]{3,2,1,0:T(8,128)(2,1)S(1)} async-done(((bf16[8,4,16,128]{3,2,1,0:T(8,128)(2,1)}), bf16[8,4,16,128]{3,2,1,0:T(8,128)(2,1)S(1)}, u32[]{:S(2)}, u32[]{:S(2)}) %all-to-all-start.2) | async-done | bytes 131104 | tf_op jit(solution)/shard_map/all_to_all | solution.py:399
  65.8 0.7 shard_map.104
  66.5 3.5 %all-to-all-start.3 = ((bf16[16,4,16,128]{3,2,1,0:T(8,128)(2,1)}), bf16[16,4,16,128]{3,2,1,0:T(8,128)(2,1)S(1)}, u32[]{:S(2)}, u32[]{:S(2)}) async-start(bf16[16,4,16,128]{3,2,1,0:T(8,128)(2,1)} %shard_map.104), calls=%async_computation.3 | async-start | bytes 524288 | tf_op jit(solution)/shard_map/all_to_all | solution.py:399
  70.1 0.1 collective-permute-start.8
  70.2 7.4 %all-to-all-done.3 = bf16[16,4,16,128]{3,2,1,0:T(8,128)(2,1)S(1)} async-done(((bf16[16,4,16,128]{3,2,1,0:T(8,128)(2,1)}), bf16[16,4,16,128]{3,2,1,0:T(8,128)(2,1)S(1)}, u32[]{:S(2)}, u32[]{:S(2)}) %all-to-all-start.3) | async-done | bytes 262176 | tf_op jit(solution)/shard_map/all_to_all | solution.py:399
  77.6 3.5 %collective-permute-start.14 = (bf16[64,16,128]{2,1,0:T(8,128)(2,1)S(1)}, bf16[64,16,128]{2,1,0:T(8,128)(2,1)S(1)}, u32[]{:S(2)}, u32[]{:S(2)}) collective-permute-start(bf16[64,16,128]{2,1,0:T(8,128)(2,1)S(1)} %bitcast.11), channel_id=1, source_target_pairs={{0,1},{1,0},{2,3},{3,2},{4,5},{5,4},{6,7},{7,6},{8,9},{9,8},{10,11... | collective-permute-start | bytes 786440 | tf_op jit(solution)/shard_map/ppermute | solution.py:395
  81.1 1.0 %shard_map.101 = bf16[2,8,32,256]{3,2,1,0:T(8,128)(2,1)} custom-call(bf16[2,8,32,256]{3,2,1,0:T(8,128)(2,1)S(1)} %bitcast.20, f32[1,256]{1,0:T(1,128)S(1)} %bitcast.24, f32[2,8,32,256]{3,2,1,0:T(8,128)S(1)} %bitcast.26, bf16[8,2,16,256]{3,2,1,0:T(8,128)(2,1)S(1)} %get-tuple-element.42.refs_0_.rest_0_, ...), custom_call_target="tpu_custom_call" | custom-call | flops 1600000000 | bytes 4000000 | tf_op jit(solution)/shard_map/pallas_call | solution.py:383
  82.1 0.1 collective-permute-done.14.theirs
  82.3 1.1 %shard_map.105 = (f32[256,768]{1,0:T(8,128)}, f32[256,256]{1,0:T(8,128)}, f32[1,256]{1,0:T(1,128)}) custom-call(bf16[64,16,128]{2,1,0:T(8,128)(2,1)S(1)} %bitcast.12, bf16[64,16,128]{2,1,0:T(8,128)(2,1)S(1)} %collective-permute-done.14.theirs, f32[1,256]{1,0:T(1,128)S(1)} %bitcast.25, bf16[256,768]{1,0:T(8,128)(2,1)S(1)} %copy-done), custom_call_target="tpu_custom_call" | custom-call | flops 800000000 | bytes 2000000 | tf_op jit(solution)/shard_map/pallas_call | solution.py:383
  (15 shorter events, 0.1 us)
Async XLA Ops:
  2.6 14.1 %collective-permute-start.1 = (bf16[2,2,8,16,256]{4,3,2,1,0:T(8,128)(2,1)}, bf16[2,2,8,16,256]{4,3,2,1,0:T(8,128)(2,1)S(1)}, u32[]{:S(2)}, u32[]{:S(2)}) collective-permute-start(bf16[2,2,8,16,256]{4,3,2,1,0:T(8,128)(2,1)} %get-tuple-element.36), channel_id=1, source_target_pairs={{0,2},{2,0},{1,3},{3,1},{4,6},{6,4},{5,7},{7,5},{8,10},{10,8},{9,1... | collective-permute-start | bytes 786440 | tf_op jit(solution)/shard_map/ppermute | solution.py:395
  4.7 10.6 %copy-start.1 = (bf16[1,2,8,32,256]{4,3,2,1,0:T(8,128)(2,1)S(1)}, bf16[1,2,8,32,256]{4,3,2,1,0:T(8,128)(2,1)}, u32[]{:S(2)}) copy-start(bf16[1,2,8,32,256]{4,3,2,1,0:T(8,128)(2,1)} %param.8) | copy-start | bytes 786436
  4.7 10.6 %copy-start.3 = (bf16[1,2,8,32,256]{4,3,2,1,0:T(8,128)(2,1)S(1)}, bf16[1,2,8,32,256]{4,3,2,1,0:T(8,128)(2,1)}, u32[]{:S(2)}) copy-start(bf16[1,2,8,32,256]{4,3,2,1,0:T(8,128)(2,1)} %param.6) | copy-start | bytes 786436
  4.7 27.8 %all-to-all-start = ((bf16[16,2,2,16,256]{4,3,2,1,0:T(8,128)(2,1)}), bf16[16,2,2,16,256]{4,3,2,1,0:T(8,128)(2,1)S(1)}, u32[]{:S(2)}, u32[]{:S(2)}) async-start(bf16[16,2,2,16,256]{4,3,2,1,0:T(8,128)(2,1)} %bitcast.27), calls=%async_computation | async-start | bytes 1048576 | tf_op jit(solution)/shard_map/all_to_all | solution.py:399
  15.4 1.5 %copy-start = (bf16[256,768]{1,0:T(8,128)(2,1)S(1)}, bf16[256,768]{1,0:T(8,128)(2,1)}, u32[]{:S(2)}) copy-start(bf16[256,768]{1,0:T(8,128)(2,1)} %w_qkv.5) | copy-start | bytes 1179652
  15.4 1.5 %copy-start.2 = (bf16[1,2,8,32,256]{4,3,2,1,0:T(8,128)(2,1)S(1)}, bf16[1,2,8,32,256]{4,3,2,1,0:T(8,128)(2,1)}, u32[]{:S(2)}) copy-start(bf16[1,2,8,32,256]{4,3,2,1,0:T(8,128)(2,1)} %param.7) | copy-start | bytes 786436
  15.4 1.5 %copy-start.4 = (bf16[256,256]{1,0:T(8,128)(2,1)S(1)}, bf16[256,256]{1,0:T(8,128)(2,1)}, u32[]{:S(2)}) copy-start(bf16[256,256]{1,0:T(8,128)(2,1)} %w_out.3) | copy-start | bytes 393220
  15.4 5.3 %collective-permute-start = (bf16[2,8,16,256]{3,2,1,0:T(8,128)(2,1)S(1)}, bf16[2,8,16,256]{3,2,1,0:T(8,128)(2,1)S(1)}, u32[]{:S(2)}, u32[]{:S(2)}) collective-permute-start(bf16[2,8,16,256]{3,2,1,0:T(8,128)(2,1)S(1)} %get-tuple-element.35), channel_id=1, source_target_pairs={{0,1},{1,0},{2,3},{3,2},{4,5},{5,4},{6,7},{7,6},{8,9},{9,8},{10,11... | collective-permute-start | bytes 393224 | tf_op jit(solution)/shard_map/ppermute | solution.py:395
  16.8 4.0 %collective-permute-start.2 = (bf16[2,2,8,16,256]{4,3,2,1,0:T(8,128)(2,1)S(1)}, bf16[2,2,8,16,256]{4,3,2,1,0:T(8,128)(2,1)S(1)}, u32[]{:S(2)}, u32[]{:S(2)}) collective-permute-start(bf16[2,2,8,16,256]{4,3,2,1,0:T(8,128)(2,1)S(1)} %collective-permute-done.1.refs_2_), channel_id=1, source_target_pairs={{0,1},{1,0},{2,3},{3,2},{4,5},{5,4},{6,7},{7,6},{8,9},{9,8},{10,11... | collective-permute-start | bytes 786440 | tf_op jit(solution)/shard_map/ppermute | solution.py:395
  16.9 0.7 copy-start.5
  24.2 2.8 %collective-permute-start.3 = (bf16[32,16,128]{2,1,0:T(8,128)(2,1)S(1)}, bf16[32,16,128]{2,1,0:T(8,128)(2,1)S(1)}, u32[]{:S(2)}, u32[]{:S(2)}) collective-permute-start(bf16[32,16,128]{2,1,0:T(8,128)(2,1)S(1)} %get-tuple-element.40), channel_id=1, source_target_pairs={{0,1},{1,0},{2,3},{3,2},{4,5},{5,4},{6,7},{7,6},{8,9},{9,8},{10,11... | collective-permute-start | bytes 393224 | tf_op jit(solution)/shard_map/ppermute | solution.py:395
  24.8 2.2 %collective-permute-start.4 = (bf16[32,16,128]{2,1,0:T(8,128)(2,1)S(1)}, bf16[32,16,128]{2,1,0:T(8,128)(2,1)S(1)}, u32[]{:S(2)}, u32[]{:S(2)}) collective-permute-start(bf16[32,16,128]{2,1,0:T(8,128)(2,1)S(1)} %get-tuple-element.41), channel_id=1, source_target_pairs={{0,1},{1,0},{2,3},{3,2},{4,5},{5,4},{6,7},{7,6},{8,9},{9,8},{10,11... | collective-permute-start | bytes 393224 | tf_op jit(solution)/shard_map/ppermute | solution.py:395
  24.9 11.6 %collective-permute-start.9 = (bf16[8,16,256]{2,1,0:T(8,128)(2,1)S(1)}, bf16[8,16,256]{2,1,0:T(8,128)(2,1)S(1)}, u32[]{:S(2)}, u32[]{:S(2)}) collective-permute-start(bf16[8,16,256]{2,1,0:T(8,128)(2,1)S(1)} %get-tuple-element.47), channel_id=1, source_target_pairs={{0,1},{1,0},{2,3},{3,2},{4,5},{5,4},{6,7},{7,6},{8,9},{9,8},{10,11... | collective-permute-start | bytes 196616 | tf_op jit(solution)/shard_map/ppermute | solution.py:395
  25.3 11.2 %collective-permute-start.10 = (bf16[8,16,256]{2,1,0:T(8,128)(2,1)S(1)}, bf16[8,16,256]{2,1,0:T(8,128)(2,1)S(1)}, u32[]{:S(2)}, u32[]{:S(2)}) collective-permute-start(bf16[8,16,256]{2,1,0:T(8,128)(2,1)S(1)} %get-tuple-element.48), channel_id=1, source_target_pairs={{0,2},{1,3},{2,0},{3,1},{4,6},{5,7},{6,4},{7,5},{8,10},{9,11},{10,... | collective-permute-start | bytes 196616 | tf_op jit(solution)/shard_map/ppermute | solution.py:395
  25.3 11.2 %collective-permute-start.11 = (bf16[8,16,256]{2,1,0:T(8,128)(2,1)S(1)}, bf16[8,16,256]{2,1,0:T(8,128)(2,1)S(1)}, u32[]{:S(2)}, u32[]{:S(2)}) collective-permute-start(bf16[8,16,256]{2,1,0:T(8,128)(2,1)S(1)} %get-tuple-element.49), channel_id=1, source_target_pairs={{0,3},{1,2},{2,1},{3,0},{4,7},{5,6},{6,5},{7,4},{8,11},{9,10},{10,... | collective-permute-start | bytes 196616 | tf_op jit(solution)/shard_map/ppermute | solution.py:395
  36.5 3.5 %collective-permute-start.12 = (bf16[32,16,128]{2,1,0:T(8,128)(2,1)S(1)}, bf16[32,16,128]{2,1,0:T(8,128)(2,1)S(1)}, u32[]{:S(2)}, u32[]{:S(2)}) collective-permute-start(bf16[32,16,128]{2,1,0:T(8,128)(2,1)S(1)} %get-tuple-element.55), channel_id=1, source_target_pairs={{0,1},{1,0},{2,3},{3,2},{4,5},{5,4},{6,7},{7,6},{8,9},{9,8},{10,11... | collective-permute-start | bytes 393224 | tf_op jit(solution)/shard_map/ppermute | solution.py:395
  39.0 1.3 %collective-permute-start.13 = (bf16[32,16,128]{2,1,0:T(8,128)(2,1)S(1)}, bf16[32,16,128]{2,1,0:T(8,128)(2,1)S(1)}, u32[]{:S(2)}, u32[]{:S(2)}) collective-permute-start(bf16[32,16,128]{2,1,0:T(8,128)(2,1)S(1)} %get-tuple-element.56), channel_id=1, source_target_pairs={{0,1},{1,0},{2,3},{3,2},{4,5},{5,4},{6,7},{7,6},{8,9},{9,8},{10,11... | collective-permute-start | bytes 393224 | tf_op jit(solution)/shard_map/ppermute | solution.py:395
  39.1 6.3 %collective-permute-start.5 = (bf16[8,2,16,256]{3,2,1,0:T(8,128)(2,1)S(1)}, bf16[8,2,16,256]{3,2,1,0:T(8,128)(2,1)S(1)}, u32[]{:S(2)}, u32[]{:S(2)}) collective-permute-start(bf16[8,2,16,256]{3,2,1,0:T(8,128)(2,1)S(1)} %get-tuple-element.43), channel_id=1, source_target_pairs={{0,8},{8,0},{16,24},{24,16},{32,40},{40,32},{48,56},{56,48},{1,9},... | collective-permute-start | bytes 393224 | tf_op jit(solution)/shard_map/ppermute | solution.py:395
  41.1 12.6 %all-to-all-start.1 = ((bf16[16,4,16,128]{3,2,1,0:T(8,128)(2,1)}), bf16[16,4,16,128]{3,2,1,0:T(8,128)(2,1)S(1)}, u32[]{:S(2)}, u32[]{:S(2)}) async-start(bf16[16,4,16,128]{3,2,1,0:T(8,128)(2,1)} %shard_map.102), calls=%async_computation.1 | async-start | bytes 524288 | tf_op jit(solution)/shard_map/all_to_all | solution.py:399
  45.5 12.4 %collective-permute-start.6 = (bf16[8,2,16,256]{3,2,1,0:T(8,128)(2,1)S(1)}, bf16[8,2,16,256]{3,2,1,0:T(8,128)(2,1)S(1)}, u32[]{:S(2)}, u32[]{:S(2)}) collective-permute-start(bf16[8,2,16,256]{3,2,1,0:T(8,128)(2,1)S(1)} %shard_map.98), channel_id=1, source_target_pairs={{0,32},{8,40},{16,48},{24,56},{32,0},{40,8},{48,16},{56,24},{1,33}... | collective-permute-start | bytes 393224 | tf_op jit(solution)/shard_map/ppermute | solution.py:395
  54.5 11.3 %all-to-all-start.2 = ((bf16[8,4,16,128]{3,2,1,0:T(8,128)(2,1)}), bf16[8,4,16,128]{3,2,1,0:T(8,128)(2,1)S(1)}, u32[]{:S(2)}, u32[]{:S(2)}) async-start(bf16[8,4,16,128]{3,2,1,0:T(8,128)(2,1)} %shard_map.103), calls=%async_computation.2 | async-start | bytes 262144 | tf_op jit(solution)/shard_map/all_to_all | solution.py:399
  57.9 12.2 %collective-permute-start.7 = (bf16[8,2,16,256]{3,2,1,0:T(8,128)(2,1)S(1)}, bf16[8,2,16,256]{3,2,1,0:T(8,128)(2,1)S(1)}, u32[]{:S(2)}, u32[]{:S(2)}) collective-permute-start(bf16[8,2,16,256]{3,2,1,0:T(8,128)(2,1)S(1)} %shard_map.99), channel_id=1, source_target_pairs={{0,4},{4,0},{1,5},{5,1},{2,6},{6,2},{3,7},{7,3},{8,12},{12,8},{9,1... | collective-permute-start | bytes 393224 | tf_op jit(solution)/shard_map/ppermute | solution.py:395
  66.5 11.0 %all-to-all-start.3 = ((bf16[16,4,16,128]{3,2,1,0:T(8,128)(2,1)}), bf16[16,4,16,128]{3,2,1,0:T(8,128)(2,1)S(1)}, u32[]{:S(2)}, u32[]{:S(2)}) async-start(bf16[16,4,16,128]{3,2,1,0:T(8,128)(2,1)} %shard_map.104), calls=%async_computation.3 | async-start | bytes 524288 | tf_op jit(solution)/shard_map/all_to_all | solution.py:399
  70.1 11.0 %collective-permute-start.8 = (bf16[8,2,16,256]{3,2,1,0:T(8,128)(2,1)S(1)}, bf16[8,2,16,256]{3,2,1,0:T(8,128)(2,1)S(1)}, u32[]{:S(2)}, u32[]{:S(2)}) collective-permute-start(bf16[8,2,16,256]{3,2,1,0:T(8,128)(2,1)S(1)} %shard_map.100), channel_id=1, source_target_pairs={{0,16},{8,24},{16,0},{24,8},{32,48},{40,56},{48,32},{56,40},{1,17}... | collective-permute-start | bytes 393224 | tf_op jit(solution)/shard_map/ppermute | solution.py:395
  77.6 4.7 %collective-permute-start.14 = (bf16[64,16,128]{2,1,0:T(8,128)(2,1)S(1)}, bf16[64,16,128]{2,1,0:T(8,128)(2,1)S(1)}, u32[]{:S(2)}, u32[]{:S(2)}) collective-permute-start(bf16[64,16,128]{2,1,0:T(8,128)(2,1)S(1)} %bitcast.11), channel_id=1, source_target_pairs={{0,1},{1,0},{2,3},{3,2},{4,5},{5,4},{6,7},{7,6},{8,9},{9,8},{10,11... | collective-permute-start | bytes 786440 | tf_op jit(solution)/shard_map/ppermute | solution.py:395

commit v8 on v7

--- a/solution.py
+++ b/solution.py
@@ -27,8 +27,8 @@
 F32 = jnp.float32
 VMEM = pl.BlockSpec(memory_space=pltpu.VMEM)
 HBM = pl.BlockSpec(memory_space=pltpu.HBM)
-PLANE = ("y", "xh", "xl")
-FIRST = ("z", "xh")
+PLANE = ("xh", "xl", "y")
+FIRST = ("xh", "z")
 SECOND = ("xl", "c")
 
 
@@ -139,7 +139,7 @@
     return slice(i * LENGTH, (i + 1) * LENGTH)
 
 
-BITS = (2, 8, 1, 4)
+BITS = (1, 4, 8, 2)
 SWAPS = (("z", 1, 8), ("z", 4, 8), ("xh", 1, 2), ("z", 2, 8))
 
 
@@ -170,46 +170,25 @@
 
 
 def along_first():
-    return lax.axis_index("z") * 2 + lax.axis_index("xh")
+    return lax.axis_index("xh") * 8 + lax.axis_index("z")
 
 
 def pieces_kernel(tokens, cotangent, to_first, far, held, sem):
     core, chip = lax.axis_index("c"), lax.axis_index("xl")
-    loads, stores = [], []
-    for kind, ref in enumerate((tokens, cotangent)):
-        for x in range(2):
-            at = len(loads) * 3
-            source = held.at[kind, x]
-            loads.append(pltpu.make_async_copy(ref.at[x], source, sem.at[at]))
-            stores.append(
-                [
-                    pltpu.make_async_copy(
-                        source.at[:, pl.ds(z * ROWS, ROWS), :],
-                        to_first.at[:, z, kind, x],
-                        sem.at[at + 1 + z],
-                    )
-                    for z in range(2)
-                ]
-            )
+    loads = [
+        pltpu.make_async_copy(ref, held.at[kind], sem.at[kind])
+        for kind, ref in enumerate((tokens, cotangent))
+    ]
     for load in loads:
         load.start()
-    for load, copies in zip(loads, stores):
+    for kind, load in enumerate(loads):
         load.wait()
-        for copy in copies:
-            copy.start()
-    late = []
-    for kind in range(2):
+        for x in range(2):
+            for z in range(2):
+                to_first[:, z, kind, x] = held[kind, x, :, z * ROWS : (z + 1) * ROWS, :]
         for other in range(2):
             rows = pl.ds(pl.multiple_of((core ^ other) * ROWS, ROWS), ROWS)
-            late.append(
-                pltpu.make_async_copy(
-                    held.at[kind, 1 - chip, :, rows, :], far.at[other, kind], sem.at[12 + len(late)]
-                )
-            )
-            late[-1].start()
-    for copies in stores + [late]:
-        for copy in copies:
-            copy.wait()
+            far[other, kind] = held[kind, 1 - chip, :, rows, :]
 
 
 def chip_pieces_kernel(tokens, cotangent, near, mate):
@@ -379,12 +358,12 @@
     return jax.ShapeDtypeStruct(dims, dtype)
 
 
-def kernel_call(body, outs, operands, us, scratch=(), space=VMEM, spaces=None):
+def kernel_call(body, outs, operands, us, scratch=(), space=VMEM, spaces=None, out_spaces=None):
     return pl.pallas_call(
         body,
         out_shape=outs,
         in_specs=spaces or [space] * len(operands),
-        out_specs=jax.tree.map(lambda _: space, outs),
+        out_specs=out_spaces or jax.tree.map(lambda _: space, outs),
         scratch_shapes=list(scratch),
         compiler_params=params(62 if space is HBM else 48),
         cost_estimate=cost(us),
@@ -411,8 +390,9 @@
         (shape((8, 2, 2, 2, ROWS, WIDTH), BF16), shape((2, *quarter), BF16)),
         (local, upstream),
         2,
-        [pltpu.VMEM((2, *local.shape), BF16), pltpu.SemaphoreType.DMA((16,))],
+        [pltpu.VMEM((2, *local.shape), BF16), pltpu.SemaphoreType.DMA((2,))],
         space=HBM,
+        out_spaces=(VMEM, VMEM),
     )
     at_first = exchange(to_first.reshape(16, 2, 2, ROWS, WIDTH), FIRST)
     far = swap(far, "xl", 1, 2)
@@ -504,7 +484,7 @@
 
 def solution(mesh):
     fine = Mesh(mesh.devices.reshape(4, 8, 2, 2, 2), ("y", "z", "xh", "xl", "c"))
-    split = P("y", FIRST, SECOND, None, None)
+    split = P("y", ("z", "xh"), SECOND, None, None)
     count = 4 * 32 * 32 * 32
     return jax.shard_map(
         functools.partial(on_device, count),

time: 83.9 us -> 83.3 us (level)
  waiting for transfers between devices: 28.7 us -> 22.2 us
  starting transfers between devices: 36.2 us -> 42.1 us
    all_to_all x4, waiting for transfers between devices: 27.3 us -> 22 us  [exchange(): return lax.all_to_all(pieces, axes, split_axis=0, concat_axis=0, tiled=True)]
    ppermute x15, starting transfers between devices: 14.4 us -> 18.6 us  [swap(): return lax.ppermute(array, axis, [(i, i ^ mask) for i in range(size)])]
    all_to_all x4, starting transfers between devices: 21.8 us -> 23.4 us  [exchange(): return lax.all_to_all(pieces, axes, split_axis=0, concat_axis=0, tiled=True)]
    ppermute x15, waiting for transfers between devices: 1.39 us -> 0.18 us  [swap(): return lax.ppermute(array, axis, [(i, i ^ mask) for i in range(size)])]
  transfers between devices with their start and end apart: 19 -> 19, of which waited for: 7 -> 5; matrix products, arithmetic and copies ran while one was open for 0% -> 0% of each run, Pallas kernels for 17% -> 17%
where the time goes in v8:
time: 83.3 us; the launch traced here: 82.7 us
  starting transfers between devices  42.1 us (51%)
  waiting for transfers between devices  22.2 us (27%)
  Pallas kernels  16.9 us (20%)
  between operations  0.84 us (1%)
    all_to_all x4, starting transfers between devices, exchange(): return lax.all_to_all(pieces, axes, split_axis=0, concat_axis=0, tiled=True)  23.4 us
    all_to_all x4, waiting for transfers between devices, exchange(): return lax.all_to_all(pieces, axes, split_axis=0, concat_axis=0, tiled=True)  22 us
    ppermute x15, starting transfers between devices, swap(): return lax.ppermute(array, axis, [(i, i ^ mask) for i in range(size)])  18.6 us
    pallas_call x13, Pallas kernels, kernel_call(): pl.pallas_call(body, out_shape=outs, in_specs=spaces or [space] * len(ope...  16.9 us
  transfers between devices with their start and end apart: 19, of which 5 were waited for; matrix products, arithmetic and copies ran while one was open for 0% of the time, Pallas kernels for 17%

profile of v8, /device:TPU:1, one launch (start us, length us, event | category | flops | bytes accessed | tf_op | source)
XLA Modules:
  0.0 82.7 jit_solution(10334951466930591514)
XLA Ops:
  0.6 1.9 %shard_map.94 = (bf16[8,2,2,2,16,256]{5,4,3,2,1,0:T(8,128)(2,1)}, bf16[2,2,8,16,256]{4,3,2,1,0:T(8,128)(2,1)}) custom-call(bf16[2,8,32,256]{3,2,1,0:T(8,128)(2,1)} %bitcast.17, bf16[2,8,32,256]{3,2,1,0:T(8,128)(2,1)} %bitcast.13), custom_call_target="tpu_custom_call" | custom-call | flops 1600000000 | bytes 4000000 | tf_op jit(solution)/shard_map/pallas_call | solution.py:362
  2.6 2.1 %collective-permute-start.1 = (bf16[2,2,8,16,256]{4,3,2,1,0:T(8,128)(2,1)}, bf16[2,2,8,16,256]{4,3,2,1,0:T(8,128)(2,1)S(1)}, u32[]{:S(2)}, u32[]{:S(2)}) collective-permute-start(bf16[2,2,8,16,256]{4,3,2,1,0:T(8,128)(2,1)} %get-tuple-element.36), channel_id=1, source_target_pairs={{0,2},{2,0},{1,3},{3,1},{4,6},{6,4},{5,7},{7,5},{8,10},{10,8},{9,1... | collective-permute-start | bytes 786440 | tf_op jit(solution)/shard_map/ppermute | solution.py:374
  4.7 10.6 %all-to-all-start = ((bf16[16,2,2,16,256]{4,3,2,1,0:T(8,128)(2,1)}), bf16[16,2,2,16,256]{4,3,2,1,0:T(8,128)(2,1)S(1)}, u32[]{:S(2)}, u32[]{:S(2)}) async-start(bf16[16,2,2,16,256]{4,3,2,1,0:T(8,128)(2,1)} %bitcast.27), calls=%async_computation | async-start | bytes 1048576 | tf_op jit(solution)/shard_map/all_to_all | solution.py:378
  15.3 0.0 copy-start
  15.3 0.0 copy-start.2
  15.4 0.0 copy-start.4
  15.4 1.3 %collective-permute-start = (bf16[2,8,16,256]{3,2,1,0:T(8,128)(2,1)S(1)}, bf16[2,8,16,256]{3,2,1,0:T(8,128)(2,1)S(1)}, u32[]{:S(2)}, u32[]{:S(2)}) collective-permute-start(bf16[2,8,16,256]{3,2,1,0:T(8,128)(2,1)S(1)} %get-tuple-element.35), channel_id=1, source_target_pairs={{0,1},{1,0},{2,3},{3,2},{4,5},{5,4},{6,7},{7,6},{8,9},{9,8},{10,11... | collective-permute-start | bytes 393224 | tf_op jit(solution)/shard_map/ppermute | solution.py:374
  16.7 0.0 collective-permute-done.1.refs_2_
  16.7 0.1 collective-permute-start.2
  16.9 0.7 copy-done.5
  17.5 3.2 %shard_map.93 = (f32[512,256]{1,0:T(8,128)S(1)}, f32[256,768]{1,0:T(8,128)S(1)}, f32[256,256]{1,0:T(8,128)S(1)}) custom-call(bf16[512,256]{1,0:T(8,128)(2,1)S(1)} %bitcast.19, bf16[512,256]{1,0:T(8,128)(2,1)S(1)} %bitcast.15, bf16[512,256]{1,0:T(8,128)(2,1)S(1)} %bitcast.16, f32[1,256]{1,0:T(1,128)S(1)} %bitcast.21, bf16[256,768]{1,0:T(8,128)(2,1)S(1)} %copy-done, ...), custom_call_target="tpu_custom_call" | custom-call | flops 4000000000 | bytes 10000000 | tf_op jit(solution)/shard_map/pallas_call | solution.py:362
  20.7 0.0 collective-permute-done.refs_1_
  20.7 0.0 collective-permute-done.2.refs_3_
  20.7 3.5 %shard_map.96 = (bf16[8,16,256]{2,1,0:T(8,128)(2,1)S(1)}, bf16[8,16,256]{2,1,0:T(8,128)(2,1)S(1)}, bf16[8,16,256]{2,1,0:T(8,128)(2,1)S(1)}, bf16[8,16,256]{2,1,0...) custom-call(bf16[2,8,16,256]{3,2,1,0:T(8,128)(2,1)S(1)} %get-tuple-e, ...), custom_call_target="tpu_custom_call" | custom-call | flops 4000000000 | bytes 10000000 | tf_op jit(solution)/shard_map/pallas_call | solution.py:362
  24.2 0.6 collective-permute-start.3
  24.8 0.1 collective-permute-start.4
  24.9 0.4 collective-permute-start.9
  25.3 1.7 %collective-permute-start.11 = (bf16[8,16,256]{2,1,0:T(8,128)(2,1)S(1)}, bf16[8,16,256]{2,1,0:T(8,128)(2,1)S(1)}, u32[]{:S(2)}, u32[]{:S(2)}) collective-permute-start(bf16[8,16,256]{2,1,0:T(8,128)(2,1)S(1)} %get-tuple-element.49), channel_id=1, source_target_pairs={{0,3},{1,2},{2,1},{3,0},{4,7},{5,6},{6,5},{7,4},{8,11},{9,10},{10,... | collective-permute-start | bytes 196616 | tf_op jit(solution)/shard_map/ppermute | solution.py:374
  27.0 0.0 collective-permute-done.3.early_low
  27.0 0.0 collective-permute-done.4.early_high
  27.0 2.6 %all-to-all-done.pieces = bf16[16,2,2,16,256]{4,3,2,1,0:T(8,128)(2,1)S(1)} async-done(((bf16[16,2,2,16,256]{4,3,2,1,0:T(8,128)(2,1)}), bf16[16,2,2,16,256]{4,3,2,1,0:T(8,128)(2,1)S(1)}, u32[]{:S(2)}, u32[]{:S(2)}) %all-to-all-start) | async-done | bytes 524320 | tf_op jit(solution)/shard_map/all_to_all | solution.py:378
  29.6 3.9 %shard_map.97 = (bf16[8,2,16,256]{3,2,1,0:T(8,128)(2,1)S(1)}, bf16[8,2,16,256]{3,2,1,0:T(8,128)(2,1)S(1)}, f32[64,16,128]{2,1,0:T(8,128)S(1)}, bf16[32,16,128]{2,1,0:T(8,128)(2,1)S(1)}, bf16[32,16,128]{2,1,0:T(8,128)(2,1)S(1)}) custom-call(bf16[16,2,2,16,256]{4,3,2,1,0:T(8,128)(2,1)S(1)} %all-to-all-done.pieces, ...), custom_call_target="tpu_custom_call" | custom-call | flops 4000000000 | bytes 10000000 | tf_op jit(solution)/shard_map/pallas_call | solution.py:362
  33.5 0.0 collective-permute-done.10.rest_7_
  33.5 0.0 collective-permute-done.11.rest_8_
  33.5 3.7 %collective-permute-start.12 = (bf16[32,16,128]{2,1,0:T(8,128)(2,1)S(1)}, bf16[32,16,128]{2,1,0:T(8,128)(2,1)S(1)}, u32[]{:S(2)}, u32[]{:S(2)}) collective-permute-start(bf16[32,16,128]{2,1,0:T(8,128)(2,1)S(1)} %get-tuple-element.55), channel_id=1, source_target_pairs={{0,1},{1,0},{2,3},{3,2},{4,5},{5,4},{6,7},{7,6},{8,9},{9,8},{10,11... | collective-permute-start | bytes 393224 | tf_op jit(solution)/shard_map/ppermute | solution.py:374
  37.2 0.1 collective-permute-start.13
  37.3 1.2 %collective-permute-start.5 = (bf16[8,2,16,256]{3,2,1,0:T(8,128)(2,1)S(1)}, bf16[8,2,16,256]{3,2,1,0:T(8,128)(2,1)S(1)}, u32[]{:S(2)}, u32[]{:S(2)}) collective-permute-start(bf16[8,2,16,256]{3,2,1,0:T(8,128)(2,1)S(1)} %get-tuple-element.43), channel_id=1, source_target_pairs={{0,8},{8,0},{16,24},{24,16},{32,40},{40,32},{48,56},{56,48},{1,9},... | collective-permute-start | bytes 393224 | tf_op jit(solution)/shard_map/ppermute | solution.py:374
  38.5 0.0 collective-permute-done.12.low
  38.5 0.0 collective-permute-done.13.high
  38.6 0.7 shard_map.102
  39.3 5.6 %all-to-all-start.1 = ((bf16[16,4,16,128]{3,2,1,0:T(8,128)(2,1)}), bf16[16,4,16,128]{3,2,1,0:T(8,128)(2,1)S(1)}, u32[]{:S(2)}, u32[]{:S(2)}) async-start(bf16[16,4,16,128]{3,2,1,0:T(8,128)(2,1)} %shard_map.102), calls=%async_computation.1 | async-start | bytes 524288 | tf_op jit(solution)/shard_map/all_to_all | solution.py:378
  44.9 0.0 collective-permute-done.5.refs_1_.rest_1_
  44.9 2.0 %collective-permute-start.6 = (bf16[8,2,16,256]{3,2,1,0:T(8,128)(2,1)S(1)}, bf16[8,2,16,256]{3,2,1,0:T(8,128)(2,1)S(1)}, u32[]{:S(2)}, u32[]{:S(2)}) collective-permute-start(bf16[8,2,16,256]{3,2,1,0:T(8,128)(2,1)S(1)} %shard_map.98), channel_id=1, source_target_pairs={{0,32},{8,40},{16,48},{24,56},{32,0},{40,8},{48,16},{56,24},{1,33}... | collective-permute-start | bytes 393224 | tf_op jit(solution)/shard_map/ppermute | solution.py:374
  46.9 5.4 %all-to-all-done.1.received = bf16[16,4,16,128]{3,2,1,0:T(8,128)(2,1)S(1)} async-done(((bf16[16,4,16,128]{3,2,1,0:T(8,128)(2,1)}), bf16[16,4,16,128]{3,2,1,0:T(8,128)(2,1)S(1)}, u32[]{:S(2)}, u32[]{:S(2)}) %all-to-all-start.1) | async-done | bytes 262176 | tf_op jit(solution)/shard_map/all_to_all | solution.py:378
  52.4 0.7 shard_map.103
  53.0 3.5 %all-to-all-start.2 = ((bf16[8,4,16,128]{3,2,1,0:T(8,128)(2,1)}), bf16[8,4,16,128]{3,2,1,0:T(8,128)(2,1)S(1)}, u32[]{:S(2)}, u32[]{:S(2)}) async-start(bf16[8,4,16,128]{3,2,1,0:T(8,128)(2,1)} %shard_map.103), calls=%async_computation.2 | async-start | bytes 262144 | tf_op jit(solution)/shard_map/all_to_all | solution.py:378
  56.6 0.0 collective-permute-done.6.refs_2_.rest_2_
  56.6 1.2 %collective-permute-start.7 = (bf16[8,2,16,256]{3,2,1,0:T(8,128)(2,1)S(1)}, bf16[8,2,16,256]{3,2,1,0:T(8,128)(2,1)S(1)}, u32[]{:S(2)}, u32[]{:S(2)}) collective-permute-start(bf16[8,2,16,256]{3,2,1,0:T(8,128)(2,1)S(1)} %shard_map.99), channel_id=1, source_target_pairs={{0,4},{4,0},{1,5},{5,1},{2,6},{6,2},{3,7},{7,3},{8,12},{12,8},{9,1... | collective-permute-start | bytes 393224 | tf_op jit(solution)/shard_map/ppermute | solution.py:374
  57.8 6.8 %all-to-all-done.2.received = bf16[8,4,16,128]{3,2,1,0:T(8,128)(2,1)S(1)} async-done(((bf16[8,4,16,128]{3,2,1,0:T(8,128)(2,1)}), bf16[8,4,16,128]{3,2,1,0:T(8,128)(2,1)S(1)}, u32[]{:S(2)}, u32[]{:S(2)}) %all-to-all-start.2) | async-done | bytes 131104 | tf_op jit(solution)/shard_map/all_to_all | solution.py:378
  64.6 0.7 shard_map.104
  65.3 3.7 %all-to-all-start.3 = ((bf16[16,4,16,128]{3,2,1,0:T(8,128)(2,1)}), bf16[16,4,16,128]{3,2,1,0:T(8,128)(2,1)S(1)}, u32[]{:S(2)}, u32[]{:S(2)}) async-start(bf16[16,4,16,128]{3,2,1,0:T(8,128)(2,1)} %shard_map.104), calls=%async_computation.3 | async-start | bytes 524288 | tf_op jit(solution)/shard_map/all_to_all | solution.py:378
  69.1 0.0 collective-permute-done.7.refs_3_.rest_3_
  69.1 0.1 collective-permute-start.8
  69.2 7.2 %all-to-all-done.3 = bf16[16,4,16,128]{3,2,1,0:T(8,128)(2,1)S(1)} async-done(((bf16[16,4,16,128]{3,2,1,0:T(8,128)(2,1)}), bf16[16,4,16,128]{3,2,1,0:T(8,128)(2,1)S(1)}, u32[]{:S(2)}, u32[]{:S(2)}) %all-to-all-start.3) | async-done | bytes 262176 | tf_op jit(solution)/shard_map/all_to_all | solution.py:378
  76.4 4.1 %collective-permute-start.14 = (bf16[64,16,128]{2,1,0:T(8,128)(2,1)S(1)}, bf16[64,16,128]{2,1,0:T(8,128)(2,1)S(1)}, u32[]{:S(2)}, u32[]{:S(2)}) collective-permute-start(bf16[64,16,128]{2,1,0:T(8,128)(2,1)S(1)} %bitcast.11), channel_id=1, source_target_pairs={{0,1},{1,0},{2,3},{3,2},{4,5},{5,4},{6,7},{7,6},{8,9},{9,8},{10,11... | collective-permute-start | bytes 786440 | tf_op jit(solution)/shard_map/ppermute | solution.py:374
  80.5 1.0 %shard_map.101 = bf16[2,8,32,256]{3,2,1,0:T(8,128)(2,1)} custom-call(bf16[2,8,32,256]{3,2,1,0:T(8,128)(2,1)S(1)} %bitcast.20, f32[1,256]{1,0:T(1,128)S(1)} %bitcast.24, f32[2,8,32,256]{3,2,1,0:T(8,128)S(1)} %bitcast.26, bf16[8,2,16,256]{3,2,1,0:T(8,128)(2,1)S(1)} %get-tuple-element.42.refs_0_.rest_0_, ...), custom_call_target="tpu_custom_call" | custom-call | flops 1600000000 | bytes 4000000 | tf_op jit(solution)/shard_map/pallas_call | solution.py:362
  81.5 0.1 collective-permute-done.14.theirs
  81.6 1.1 %shard_map.105 = (f32[256,768]{1,0:T(8,128)}, f32[256,256]{1,0:T(8,128)}, f32[1,256]{1,0:T(1,128)}) custom-call(bf16[64,16,128]{2,1,0:T(8,128)(2,1)S(1)} %bitcast.12, bf16[64,16,128]{2,1,0:T(8,128)(2,1)S(1)} %collective-permute-done.14.theirs, f32[1,256]{1,0:T(1,128)S(1)} %bitcast.25, bf16[256,768]{1,0:T(8,128)(2,1)S(1)} %copy-done), custom_call_target="tpu_custom_call" | custom-call | flops 800000000 | bytes 2000000 | tf_op jit(solution)/shard_map/pallas_call | solution.py:362
  (15 shorter events, 0.1 us)
Async XLA Ops:
  2.6 14.1 %collective-permute-start.1 = (bf16[2,2,8,16,256]{4,3,2,1,0:T(8,128)(2,1)}, bf16[2,2,8,16,256]{4,3,2,1,0:T(8,128)(2,1)S(1)}, u32[]{:S(2)}, u32[]{:S(2)}) collective-permute-start(bf16[2,2,8,16,256]{4,3,2,1,0:T(8,128)(2,1)} %get-tuple-element.36), channel_id=1, source_target_pairs={{0,2},{2,0},{1,3},{3,1},{4,6},{6,4},{5,7},{7,5},{8,10},{10,8},{9,1... | collective-permute-start | bytes 786440 | tf_op jit(solution)/shard_map/ppermute | solution.py:374
  4.7 10.6 %copy-start.1 = (bf16[1,2,8,32,256]{4,3,2,1,0:T(8,128)(2,1)S(1)}, bf16[1,2,8,32,256]{4,3,2,1,0:T(8,128)(2,1)}, u32[]{:S(2)}) copy-start(bf16[1,2,8,32,256]{4,3,2,1,0:T(8,128)(2,1)} %param.8) | copy-start | bytes 786436
  4.7 10.6 %copy-start.3 = (bf16[1,2,8,32,256]{4,3,2,1,0:T(8,128)(2,1)S(1)}, bf16[1,2,8,32,256]{4,3,2,1,0:T(8,128)(2,1)}, u32[]{:S(2)}) copy-start(bf16[1,2,8,32,256]{4,3,2,1,0:T(8,128)(2,1)} %param.6) | copy-start | bytes 786436
  4.7 24.9 %all-to-all-start = ((bf16[16,2,2,16,256]{4,3,2,1,0:T(8,128)(2,1)}), bf16[16,2,2,16,256]{4,3,2,1,0:T(8,128)(2,1)S(1)}, u32[]{:S(2)}, u32[]{:S(2)}) async-start(bf16[16,2,2,16,256]{4,3,2,1,0:T(8,128)(2,1)} %bitcast.27), calls=%async_computation | async-start | bytes 1048576 | tf_op jit(solution)/shard_map/all_to_all | solution.py:378
  15.3 1.5 %copy-start = (bf16[256,768]{1,0:T(8,128)(2,1)S(1)}, bf16[256,768]{1,0:T(8,128)(2,1)}, u32[]{:S(2)}) copy-start(bf16[256,768]{1,0:T(8,128)(2,1)} %w_qkv.5) | copy-start | bytes 1179652
  15.3 1.5 %copy-start.2 = (bf16[1,2,8,32,256]{4,3,2,1,0:T(8,128)(2,1)S(1)}, bf16[1,2,8,32,256]{4,3,2,1,0:T(8,128)(2,1)}, u32[]{:S(2)}) copy-start(bf16[1,2,8,32,256]{4,3,2,1,0:T(8,128)(2,1)} %param.7) | copy-start | bytes 786436
  15.4 1.5 %copy-start.4 = (bf16[256,256]{1,0:T(8,128)(2,1)S(1)}, bf16[256,256]{1,0:T(8,128)(2,1)}, u32[]{:S(2)}) copy-start(bf16[256,256]{1,0:T(8,128)(2,1)} %w_out.3) | copy-start | bytes 393220
  15.4 5.3 %collective-permute-start = (bf16[2,8,16,256]{3,2,1,0:T(8,128)(2,1)S(1)}, bf16[2,8,16,256]{3,2,1,0:T(8,128)(2,1)S(1)}, u32[]{:S(2)}, u32[]{:S(2)}) collective-permute-start(bf16[2,8,16,256]{3,2,1,0:T(8,128)(2,1)S(1)} %get-tuple-element.35), channel_id=1, source_target_pairs={{0,1},{1,0},{2,3},{3,2},{4,5},{5,4},{6,7},{7,6},{8,9},{9,8},{10,11... | collective-permute-start | bytes 393224 | tf_op jit(solution)/shard_map/ppermute | solution.py:374
  16.7 4.0 %collective-permute-start.2 = (bf16[2,2,8,16,256]{4,3,2,1,0:T(8,128)(2,1)S(1)}, bf16[2,2,8,16,256]{4,3,2,1,0:T(8,128)(2,1)S(1)}, u32[]{:S(2)}, u32[]{:S(2)}) collective-permute-start(bf16[2,2,8,16,256]{4,3,2,1,0:T(8,128)(2,1)S(1)} %collective-permute-done.1.refs_2_), channel_id=1, source_target_pairs={{0,1},{1,0},{2,3},{3,2},{4,5},{5,4},{6,7},{7,6},{8,9},{9,8},{10,11... | collective-permute-start | bytes 786440 | tf_op jit(solution)/shard_map/ppermute | solution.py:374
  16.8 0.7 copy-start.5
  24.2 2.8 %collective-permute-start.3 = (bf16[32,16,128]{2,1,0:T(8,128)(2,1)S(1)}, bf16[32,16,128]{2,1,0:T(8,128)(2,1)S(1)}, u32[]{:S(2)}, u32[]{:S(2)}) collective-permute-start(bf16[32,16,128]{2,1,0:T(8,128)(2,1)S(1)} %get-tuple-element.40), channel_id=1, source_target_pairs={{0,1},{1,0},{2,3},{3,2},{4,5},{5,4},{6,7},{7,6},{8,9},{9,8},{10,11... | collective-permute-start | bytes 393224 | tf_op jit(solution)/shard_map/ppermute | solution.py:374
  24.8 2.2 %collective-permute-start.4 = (bf16[32,16,128]{2,1,0:T(8,128)(2,1)S(1)}, bf16[32,16,128]{2,1,0:T(8,128)(2,1)S(1)}, u32[]{:S(2)}, u32[]{:S(2)}) collective-permute-start(bf16[32,16,128]{2,1,0:T(8,128)(2,1)S(1)} %get-tuple-element.41), channel_id=1, source_target_pairs={{0,1},{1,0},{2,3},{3,2},{4,5},{5,4},{6,7},{7,6},{8,9},{9,8},{10,11... | collective-permute-start | bytes 393224 | tf_op jit(solution)/shard_map/ppermute | solution.py:374
  24.9 8.7 %collective-permute-start.9 = (bf16[8,16,256]{2,1,0:T(8,128)(2,1)S(1)}, bf16[8,16,256]{2,1,0:T(8,128)(2,1)S(1)}, u32[]{:S(2)}, u32[]{:S(2)}) collective-permute-start(bf16[8,16,256]{2,1,0:T(8,128)(2,1)S(1)} %get-tuple-element.47), channel_id=1, source_target_pairs={{0,1},{1,0},{2,3},{3,2},{4,5},{5,4},{6,7},{7,6},{8,9},{9,8},{10,11... | collective-permute-start | bytes 196616 | tf_op jit(solution)/shard_map/ppermute | solution.py:374
  25.3 8.3 %collective-permute-start.10 = (bf16[8,16,256]{2,1,0:T(8,128)(2,1)S(1)}, bf16[8,16,256]{2,1,0:T(8,128)(2,1)S(1)}, u32[]{:S(2)}, u32[]{:S(2)}) collective-permute-start(bf16[8,16,256]{2,1,0:T(8,128)(2,1)S(1)} %get-tuple-element.48), channel_id=1, source_target_pairs={{0,2},{1,3},{2,0},{3,1},{4,6},{5,7},{6,4},{7,5},{8,10},{9,11},{10,... | collective-permute-start | bytes 196616 | tf_op jit(solution)/shard_map/ppermute | solution.py:374
  25.3 8.3 %collective-permute-start.11 = (bf16[8,16,256]{2,1,0:T(8,128)(2,1)S(1)}, bf16[8,16,256]{2,1,0:T(8,128)(2,1)S(1)}, u32[]{:S(2)}, u32[]{:S(2)}) collective-permute-start(bf16[8,16,256]{2,1,0:T(8,128)(2,1)S(1)} %get-tuple-element.49), channel_id=1, source_target_pairs={{0,3},{1,2},{2,1},{3,0},{4,7},{5,6},{6,5},{7,4},{8,11},{9,10},{10,... | collective-permute-start | bytes 196616 | tf_op jit(solution)/shard_map/ppermute | solution.py:374
  33.5 5.0 %collective-permute-start.12 = (bf16[32,16,128]{2,1,0:T(8,128)(2,1)S(1)}, bf16[32,16,128]{2,1,0:T(8,128)(2,1)S(1)}, u32[]{:S(2)}, u32[]{:S(2)}) collective-permute-start(bf16[32,16,128]{2,1,0:T(8,128)(2,1)S(1)} %get-tuple-element.55), channel_id=1, source_target_pairs={{0,1},{1,0},{2,3},{3,2},{4,5},{5,4},{6,7},{7,6},{8,9},{9,8},{10,11... | collective-permute-start | bytes 393224 | tf_op jit(solution)/shard_map/ppermute | solution.py:374
  37.2 1.3 %collective-permute-start.13 = (bf16[32,16,128]{2,1,0:T(8,128)(2,1)S(1)}, bf16[32,16,128]{2,1,0:T(8,128)(2,1)S(1)}, u32[]{:S(2)}, u32[]{:S(2)}) collective-permute-start(bf16[32,16,128]{2,1,0:T(8,128)(2,1)S(1)} %get-tuple-element.56), channel_id=1, source_target_pairs={{0,1},{1,0},{2,3},{3,2},{4,5},{5,4},{6,7},{7,6},{8,9},{9,8},{10,11... | collective-permute-start | bytes 393224 | tf_op jit(solution)/shard_map/ppermute | solution.py:374
  37.3 7.6 %collective-permute-start.5 = (bf16[8,2,16,256]{3,2,1,0:T(8,128)(2,1)S(1)}, bf16[8,2,16,256]{3,2,1,0:T(8,128)(2,1)S(1)}, u32[]{:S(2)}, u32[]{:S(2)}) collective-permute-start(bf16[8,2,16,256]{3,2,1,0:T(8,128)(2,1)S(1)} %get-tuple-element.43), channel_id=1, source_target_pairs={{0,8},{8,0},{16,24},{24,16},{32,40},{40,32},{48,56},{56,48},{1,9},... | collective-permute-start | bytes 393224 | tf_op jit(solution)/shard_map/ppermute | solution.py:374
  39.3 13.0 %all-to-all-start.1 = ((bf16[16,4,16,128]{3,2,1,0:T(8,128)(2,1)}), bf16[16,4,16,128]{3,2,1,0:T(8,128)(2,1)S(1)}, u32[]{:S(2)}, u32[]{:S(2)}) async-start(bf16[16,4,16,128]{3,2,1,0:T(8,128)(2,1)} %shard_map.102), calls=%async_computation.1 | async-start | bytes 524288 | tf_op jit(solution)/shard_map/all_to_all | solution.py:378
  44.9 11.6 %collective-permute-start.6 = (bf16[8,2,16,256]{3,2,1,0:T(8,128)(2,1)S(1)}, bf16[8,2,16,256]{3,2,1,0:T(8,128)(2,1)S(1)}, u32[]{:S(2)}, u32[]{:S(2)}) collective-permute-start(bf16[8,2,16,256]{3,2,1,0:T(8,128)(2,1)S(1)} %shard_map.98), channel_id=1, source_target_pairs={{0,32},{8,40},{16,48},{24,56},{32,0},{40,8},{48,16},{56,24},{1,33}... | collective-permute-start | bytes 393224 | tf_op jit(solution)/shard_map/ppermute | solution.py:374
  53.0 11.5 %all-to-all-start.2 = ((bf16[8,4,16,128]{3,2,1,0:T(8,128)(2,1)}), bf16[8,4,16,128]{3,2,1,0:T(8,128)(2,1)S(1)}, u32[]{:S(2)}, u32[]{:S(2)}) async-start(bf16[8,4,16,128]{3,2,1,0:T(8,128)(2,1)} %shard_map.103), calls=%async_computation.2 | async-start | bytes 262144 | tf_op jit(solution)/shard_map/all_to_all | solution.py:378
  56.6 12.5 %collective-permute-start.7 = (bf16[8,2,16,256]{3,2,1,0:T(8,128)(2,1)S(1)}, bf16[8,2,16,256]{3,2,1,0:T(8,128)(2,1)S(1)}, u32[]{:S(2)}, u32[]{:S(2)}) collective-permute-start(bf16[8,2,16,256]{3,2,1,0:T(8,128)(2,1)S(1)} %shard_map.99), channel_id=1, source_target_pairs={{0,4},{4,0},{1,5},{5,1},{2,6},{6,2},{3,7},{7,3},{8,12},{12,8},{9,1... | collective-permute-start | bytes 393224 | tf_op jit(solution)/shard_map/ppermute | solution.py:374
  65.3 11.1 %all-to-all-start.3 = ((bf16[16,4,16,128]{3,2,1,0:T(8,128)(2,1)}), bf16[16,4,16,128]{3,2,1,0:T(8,128)(2,1)S(1)}, u32[]{:S(2)}, u32[]{:S(2)}) async-start(bf16[16,4,16,128]{3,2,1,0:T(8,128)(2,1)} %shard_map.104), calls=%async_computation.3 | async-start | bytes 524288 | tf_op jit(solution)/shard_map/all_to_all | solution.py:378
  69.1 11.4 %collective-permute-start.8 = (bf16[8,2,16,256]{3,2,1,0:T(8,128)(2,1)S(1)}, bf16[8,2,16,256]{3,2,1,0:T(8,128)(2,1)S(1)}, u32[]{:S(2)}, u32[]{:S(2)}) collective-permute-start(bf16[8,2,16,256]{3,2,1,0:T(8,128)(2,1)S(1)} %shard_map.100), channel_id=1, source_target_pairs={{0,16},{8,24},{16,0},{24,8},{32,48},{40,56},{48,32},{56,40},{1,17}... | collective-permute-start | bytes 393224 | tf_op jit(solution)/shard_map/ppermute | solution.py:374
  76.4 5.2 %collective-permute-start.14 = (bf16[64,16,128]{2,1,0:T(8,128)(2,1)S(1)}, bf16[64,16,128]{2,1,0:T(8,128)(2,1)S(1)}, u32[]{:S(2)}, u32[]{:S(2)}) collective-permute-start(bf16[64,16,128]{2,1,0:T(8,128)(2,1)S(1)} %bitcast.11), channel_id=1, source_target_pairs={{0,1},{1,0},{2,3},{3,2},{4,5},{5,4},{6,7},{7,6},{8,9},{9,8},{10,11... | collective-permute-start | bytes 786440 | tf_op jit(solution)/shard_map/ppermute | solution.py:374

commit v9 on v8

--- a/solution.py
+++ b/solution.py
@@ -21,7 +21,6 @@
 PENCILS = 16
 ROWS = 16
 LANES = 128
-HALF = 32
 TILES = 64
 BF16 = jnp.bfloat16
 F32 = jnp.float32
@@ -211,7 +210,7 @@
     out_out[...] = dot(attn[...], cot, 0, 0)
 
 
-def pack(total, part_out, halves, own, low, high):
+def pack(total, part_out, halves, own, other):
     for at in range(2 * TILES):
         half, tile = divmod(at, TILES)
         if at < 96:
@@ -224,13 +223,12 @@
             halves[half, tile] = part_out[row * 16 : row * 16 + 16, col * LANES : (col + 1) * LANES]
     mine = lax.axis_index("c")
     own[0:TILES] = halves[mine].astype(own.dtype)
-    low[0:HALF] = halves[1 - mine, 0:HALF].astype(BF16)
-    high[0:HALF] = halves[1 - mine, HALF:TILES].astype(BF16)
+    other[...] = halves[1 - mine].astype(BF16)
 
 
 def second_kernel(*refs):
     pieces, (gain, w_qkv, w_out), parts = refs[:4], refs[4:7], refs[7:9]
-    back, packed, scratch, halves = refs[9:13], refs[13:16], refs[16:-1], refs[-1]
+    back, packed, scratch, halves = refs[9:13], refs[13:15], refs[15:-1], refs[-1]
     near, mate, far, passed = pieces
     pieces = (near, mate, far.at[0], passed.at[1])
     tokens = jnp.concatenate([piece[0].reshape(-1, WIDTH) for piece in pieces], axis=0)
@@ -246,13 +244,13 @@
     pack(third_qkv[...] + part_qkv, part_out, halves, *packed)
 
 
-def first_kernel(pieces, early_own, early_low, early_high, gain, w_qkv, w_out, *refs):
-    (stay, leave), packed, scratch, rest = refs[:2], refs[2:5], refs[5:-6], refs[-6:]
-    returned, halves, held_own, held_low, held_high, sem = rest
-    held = (held_own, held_low, held_high)
+def first_kernel(pieces, early_own, early_other, gain, w_qkv, w_out, *refs):
+    (stay, leave), packed, scratch, rest = refs[:2], refs[2:4], refs[4:-5], refs[-5:]
+    returned, halves, held_own, held_other, sem = rest
+    held = (held_own, held_other)
     copies = [
         pltpu.make_async_copy(source, target, sem.at[at])
-        for at, (source, target) in enumerate(zip((early_own, early_low, early_high), held))
+        for at, (source, target) in enumerate(zip((early_own, early_other), held))
     ]
     for copy in copies:
         copy.start()
@@ -270,8 +268,7 @@
     for copy in copies:
         copy.wait()
     own = packed[0]
-    own[0:HALF] += held_own[0:HALF].astype(F32) + held_low[...].astype(F32)
-    own[HALF:TILES] += held_own[HALF:TILES].astype(F32) + held_high[...].astype(F32)
+    own[...] += held_own[...].astype(F32) + held_other[...].astype(F32)
 
 
 def stage_kernel(*refs):
@@ -286,11 +283,10 @@
                 at += 1
 
 
-def pair_kernel(own, low, high, pieces):
+def pair_kernel(own, received, pieces):
     for peer in range(16):
-        half, at = divmod(peer * 4, HALF)
-        received = (low, high)[half][at : at + 4].astype(F32)
-        pieces[peer] = (own[peer * 4 : peer * 4 + 4] + received).astype(BF16)
+        tiles = slice(peer * 4, peer * 4 + 4)
+        pieces[peer] = (own[tiles] + received[tiles].astype(F32)).astype(BF16)
 
 
 def plane_kernel(received, pieces):
@@ -399,6 +395,7 @@
     near, mate = kernel_call(
         chip_pieces_kernel, (shape(quarter, BF16),) * 2, (local, upstream), 1
     )
+    far, mate = lax.optimization_barrier((far, mate))
     at_second = [near, swap(mate, "c", 1, 2), far, swap(far, "c", 1, 2)]
     third, third_qkv, part_out = kernel_call(
         third_kernel,
@@ -409,11 +406,10 @@
     )
     packed = (
         shape((TILES, *tile), BF16),
-        shape((HALF, *tile), BF16),
-        shape((HALF, *tile), BF16),
+        shape((TILES, *tile), BF16),
     )
     halves = pltpu.VMEM((2, TILES, *tile), F32)
-    *back, own, low, high = kernel_call(
+    *back, own, other = kernel_call(
         second_kernel,
         (shape((8, ROWS, WIDTH), BF16),) * 4 + packed,
         (*at_second, gain_row, w_qkv, w_out, third_qkv, part_out),
@@ -421,9 +417,9 @@
         SCRATCH + [halves],
     )
     from_second = [back[0]] + [swap(back[m], SECOND, m, 4) for m in (1, 2, 3)]
-    early = [own, swap(low, "c", 1, 2), swap(high, "c", 1, 2)]
+    early = [own, swap(other, "c", 1, 2)]
     block = (2, ROWS, WIDTH)
-    stay, leave, own, low, high = kernel_call(
+    stay, leave, own, other = kernel_call(
         first_kernel,
         (
             shape((8, *block), BF16),
@@ -438,12 +434,12 @@
             pltpu.VMEM((16, *block), BF16),
             halves,
             *[pltpu.VMEM(part.shape, part.dtype) for part in packed],
-            pltpu.SemaphoreType.DMA((3,)),
+            pltpu.SemaphoreType.DMA((2,)),
         ],
-        spaces=[VMEM] + [HBM] * 3 + [VMEM] * 3,
-    )
-    low, high, from_second = lax.optimization_barrier((low, high, from_second))
-    late = [own, swap(low, "c", 1, 2), swap(high, "c", 1, 2)]
+        spaces=[VMEM] + [HBM] * 2 + [VMEM] * 3,
+    )
+    other, from_second = lax.optimization_barrier((other, from_second))
+    late = [own, swap(other, "c", 1, 2)]
     groups = [stay, swap(leave, *SWAPS[0])]
     for stage in (1, 2, 3):
         leave = kernel_call(stage_kernel, shape((8, *block), BF16), groups, 20)

time: 83.3 us -> 82.8 us (level)
    ppermute x15 -> x13, starting transfers between devices: 18.6 us -> 18.4 us  [swap(): return lax.ppermute(array, axis, [(i, i ^ mask) for i in range(size)])]
  transfers between devices with their start and end apart: 19 -> 17, of which waited for: 5 -> 5; matrix products, arithmetic and copies ran while one was open for 0% -> 0% of each run, Pallas kernels for 17% -> 16%
where the time goes in v9:
time: 82.8 us; the launch traced here: 82.2 us
  starting transfers between devices  41.7 us (50%)
  waiting for transfers between devices  22.4 us (27%)
  Pallas kernels  16.6 us (20%)
  between operations  0.85 us (1%)
    all_to_all x4, starting transfers between devices, exchange(): return lax.all_to_all(pieces, axes, split_axis=0, concat_axis=0, tiled=True)  23.3 us
    all_to_all x4, waiting for transfers between devices, exchange(): return lax.all_to_all(pieces, axes, split_axis=0, concat_axis=0, tiled=True)  22.2 us
    ppermute x13, starting transfers between devices, swap(): return lax.ppermute(array, axis, [(i, i ^ mask) for i in range(size)])  18.4 us
    pallas_call x13, Pallas kernels, kernel_call(): pl.pallas_call(body, out_shape=outs, in_specs=spaces or [space] * len(ope...  16.6 us
  transfers between devices with their start and end apart: 17, of which 5 were waited for; matrix products, arithmetic and copies ran while one was open for 0% of the time, Pallas kernels for 16%

profile of v9, /device:TPU:1, one launch (start us, length us, event | category | flops | bytes accessed | tf_op | source)
XLA Modules:
  0.0 82.2 jit_solution(1260662992364424478)
XLA Ops:
  0.6 1.9 %shard_map.94 = (bf16[8,2,2,2,16,256]{5,4,3,2,1,0:T(8,128)(2,1)}, bf16[2,2,8,16,256]{4,3,2,1,0:T(8,128)(2,1)}) custom-call(bf16[2,8,32,256]{3,2,1,0:T(8,128)(2,1)} %bitcast.17, bf16[2,8,32,256]{3,2,1,0:T(8,128)(2,1)} %bitcast.13), custom_call_target="tpu_custom_call" | custom-call | flops 1600000000 | bytes 4000000 | tf_op jit(solution)/shard_map/pallas_call | solution.py:358
  2.6 2.1 %collective-permute-start = (bf16[2,2,8,16,256]{4,3,2,1,0:T(8,128)(2,1)}, bf16[2,2,8,16,256]{4,3,2,1,0:T(8,128)(2,1)S(1)}, u32[]{:S(2)}, u32[]{:S(2)}) collective-permute-start(bf16[2,2,8,16,256]{4,3,2,1,0:T(8,128)(2,1)} %get-tuple-element.34), channel_id=1, source_target_pairs={{0,2},{2,0},{1,3},{3,1},{4,6},{6,4},{5,7},{7,5},{8,10},{10,8},{9,1... | collective-permute-start | bytes 786440 | tf_op jit(solution)/shard_map/ppermute | solution.py:370
  4.7 10.6 %all-to-all-start = ((bf16[16,2,2,16,256]{4,3,2,1,0:T(8,128)(2,1)}), bf16[16,2,2,16,256]{4,3,2,1,0:T(8,128)(2,1)S(1)}, u32[]{:S(2)}, u32[]{:S(2)}) async-start(bf16[16,2,2,16,256]{4,3,2,1,0:T(8,128)(2,1)} %bitcast.27), calls=%async_computation | async-start | bytes 1048576 | tf_op jit(solution)/shard_map/all_to_all | solution.py:374
  15.3 0.0 copy-done.1
  15.3 0.0 copy-start
  15.3 0.0 copy-start.2
  15.4 0.0 copy-start.4
  15.4 0.0 collective-permute-done.refs_2_
  15.4 1.3 %collective-permute-start.1 = (bf16[2,8,16,256]{3,2,1,0:T(8,128)(2,1)S(1)}, bf16[2,8,16,256]{3,2,1,0:T(8,128)(2,1)S(1)}, u32[]{:S(2)}, u32[]{:S(2)}) collective-permute-start(bf16[2,8,16,256]{3,2,1,0:T(8,128)(2,1)S(1)} %get-tuple-element.36), channel_id=1, source_target_pairs={{0,1},{1,0},{2,3},{3,2},{4,5},{5,4},{6,7},{7,6},{8,9},{9,8},{10,11... | collective-permute-start | bytes 393224 | tf_op jit(solution)/shard_map/ppermute | solution.py:370
  16.7 0.1 collective-permute-start.2
  16.9 0.7 copy-done.5
  17.5 3.2 %shard_map.93 = (f32[512,256]{1,0:T(8,128)S(1)}, f32[256,768]{1,0:T(8,128)S(1)}, f32[256,256]{1,0:T(8,128)S(1)}) custom-call(bf16[512,256]{1,0:T(8,128)(2,1)S(1)} %bitcast.19, bf16[512,256]{1,0:T(8,128)(2,1)S(1)} %bitcast.15, bf16[512,256]{1,0:T(8,128)(2,1)S(1)} %bitcast.16, f32[1,256]{1,0:T(1,128)S(1)} %bitcast.21, bf16[256,768]{1,0:T(8,128)(2,1)S(1)} %copy-done, ...), custom_call_target="tpu_custom_call" | custom-call | flops 4000000000 | bytes 10000000 | tf_op jit(solution)/shard_map/pallas_call | solution.py:358
  20.7 0.0 collective-permute-done.1.refs_1_
  20.7 0.0 collective-permute-done.2.refs_3_
  20.7 3.5 %shard_map.96 = (bf16[8,16,256]{2,1,0:T(8,128)(2,1)S(1)}, bf16[8,16,256]{2,1,0:T(8,128)(2,1)S(1)}, bf16[8,16,256]{2,1,0:T(8,128)(2,1)S(1)}, bf16[8,16,256]{2,1,0...) custom-call(bf16[2,8,16,256]{3,2,1,0:T(8,128)(2,1)S(1)} %get-tuple-element.33.refs_0_, ...), custom_call_target="tpu_custom_call" | custom-call | flops 4000000000 | bytes 10000000 | tf_op jit(solution)/shard_map/pallas_call | solution.py:358
  24.2 0.6 collective-permute-start.3
  24.8 0.1 collective-permute-start.8
  24.9 0.0 collective-permute-start.9
  24.9 2.0 %collective-permute-start.10 = (bf16[8,16,256]{2,1,0:T(8,128)(2,1)S(1)}, bf16[8,16,256]{2,1,0:T(8,128)(2,1)S(1)}, u32[]{:S(2)}, u32[]{:S(2)}) collective-permute-start(bf16[8,16,256]{2,1,0:T(8,128)(2,1)S(1)} %get-tuple-element.48), channel_id=1, source_target_pairs={{0,3},{1,2},{2,1},{3,0},{4,7},{5,6},{6,5},{7,4},{8,11},{9,10},{10,... | collective-permute-start | bytes 196616 | tf_op jit(solution)/shard_map/ppermute | solution.py:370
  26.9 0.0 collective-permute-done.3.early_other
  26.9 2.7 %all-to-all-done.pieces = bf16[16,2,2,16,256]{4,3,2,1,0:T(8,128)(2,1)S(1)} async-done(((bf16[16,2,2,16,256]{4,3,2,1,0:T(8,128)(2,1)}), bf16[16,2,2,16,256]{4,3,2,1,0:T(8,128)(2,1)S(1)}, u32[]{:S(2)}, u32[]{:S(2)}) %all-to-all-start) | async-done | bytes 524320 | tf_op jit(solution)/shard_map/all_to_all | solution.py:374
  29.6 3.6 %shard_map.97 = (bf16[8,2,16,256]{3,2,1,0:T(8,128)(2,1)S(1)}, bf16[8,2,16,256]{3,2,1,0:T(8,128)(2,1)S(1)}, f32[64,16,128]{2,1,0:T(8,128)S(1)}, bf16[64,16,128]{2,1,0:T(8,128)(2,1)S(1)}) custom-call(bf16[16,2,2,16,256]{4,3,2,1,0:T(8,128)(2,1)S(1)} %all-to-all-done.pieces, bf16[64,16,128]{2,1,0:T(8,128)(2,1)S(1)} %get-tuple-element.40.early_own, ...), custom_call_target="tpu_custom_call" | custom-call | flops 4000000000 | bytes 10000000 | tf_op jit(solution)/shard_map/pallas_call | solution.py:358
  33.2 0.0 collective-permute-done.8.rest_6_
  33.2 0.0 collective-permute-done.9.rest_7_
  33.2 0.0 collective-permute-done.10.rest_8_
  33.2 3.7 %collective-permute-start.11 = (bf16[64,16,128]{2,1,0:T(8,128)(2,1)S(1)}, bf16[64,16,128]{2,1,0:T(8,128)(2,1)S(1)}, u32[]{:S(2)}, u32[]{:S(2)}) collective-permute-start(bf16[64,16,128]{2,1,0:T(8,128)(2,1)S(1)} %get-tuple-element.54), channel_id=1, source_target_pairs={{0,1},{1,0},{2,3},{3,2},{4,5},{5,4},{6,7},{7,6},{8,9},{9,8},{10,11... | collective-permute-start | bytes 786440 | tf_op jit(solution)/shard_map/ppermute | solution.py:370
  36.9 1.2 %collective-permute-start.4 = (bf16[8,2,16,256]{3,2,1,0:T(8,128)(2,1)S(1)}, bf16[8,2,16,256]{3,2,1,0:T(8,128)(2,1)S(1)}, u32[]{:S(2)}, u32[]{:S(2)}) collective-permute-start(bf16[8,2,16,256]{3,2,1,0:T(8,128)(2,1)S(1)} %get-tuple-element.43), channel_id=1, source_target_pairs={{0,8},{8,0},{16,24},{24,16},{32,40},{40,32},{48,56},{56,48},{1,9},... | collective-permute-start | bytes 393224 | tf_op jit(solution)/shard_map/ppermute | solution.py:370
  38.1 0.0 collective-permute-done.11.received
  38.1 0.7 shard_map.102
  38.9 5.6 %all-to-all-start.1 = ((bf16[16,4,16,128]{3,2,1,0:T(8,128)(2,1)}), bf16[16,4,16,128]{3,2,1,0:T(8,128)(2,1)S(1)}, u32[]{:S(2)}, u32[]{:S(2)}) async-start(bf16[16,4,16,128]{3,2,1,0:T(8,128)(2,1)} %shard_map.102), calls=%async_computation.1 | async-start | bytes 524288 | tf_op jit(solution)/shard_map/all_to_all | solution.py:374
  44.5 0.0 collective-permute-done.4.refs_1_.rest_1_
  44.5 1.9 %collective-permute-start.5 = (bf16[8,2,16,256]{3,2,1,0:T(8,128)(2,1)S(1)}, bf16[8,2,16,256]{3,2,1,0:T(8,128)(2,1)S(1)}, u32[]{:S(2)}, u32[]{:S(2)}) collective-permute-start(bf16[8,2,16,256]{3,2,1,0:T(8,128)(2,1)S(1)} %shard_map.98), channel_id=1, source_target_pairs={{0,32},{8,40},{16,48},{24,56},{32,0},{40,8},{48,16},{56,24},{1,33}... | collective-permute-start | bytes 393224 | tf_op jit(solution)/shard_map/ppermute | solution.py:370
  46.4 5.7 %all-to-all-done.1.received = bf16[16,4,16,128]{3,2,1,0:T(8,128)(2,1)S(1)} async-done(((bf16[16,4,16,128]{3,2,1,0:T(8,128)(2,1)}), bf16[16,4,16,128]{3,2,1,0:T(8,128)(2,1)S(1)}, u32[]{:S(2)}, u32[]{:S(2)}) %all-to-all-start.1) | async-done | bytes 262176 | tf_op jit(solution)/shard_map/all_to_all | solution.py:374
  52.1 0.7 shard_map.103
  52.8 3.4 %all-to-all-start.2 = ((bf16[8,4,16,128]{3,2,1,0:T(8,128)(2,1)}), bf16[8,4,16,128]{3,2,1,0:T(8,128)(2,1)S(1)}, u32[]{:S(2)}, u32[]{:S(2)}) async-start(bf16[8,4,16,128]{3,2,1,0:T(8,128)(2,1)} %shard_map.103), calls=%async_computation.2 | async-start | bytes 262144 | tf_op jit(solution)/shard_map/all_to_all | solution.py:374
  56.1 0.0 collective-permute-done.5.refs_2_.rest_2_
  56.2 1.2 %collective-permute-start.6 = (bf16[8,2,16,256]{3,2,1,0:T(8,128)(2,1)S(1)}, bf16[8,2,16,256]{3,2,1,0:T(8,128)(2,1)S(1)}, u32[]{:S(2)}, u32[]{:S(2)}) collective-permute-start(bf16[8,2,16,256]{3,2,1,0:T(8,128)(2,1)S(1)} %shard_map.99), channel_id=1, source_target_pairs={{0,4},{4,0},{1,5},{5,1},{2,6},{6,2},{3,7},{7,3},{8,12},{12,8},{9,1... | collective-permute-start | bytes 393224 | tf_op jit(solution)/shard_map/ppermute | solution.py:370
  57.4 6.7 %all-to-all-done.2.received = bf16[8,4,16,128]{3,2,1,0:T(8,128)(2,1)S(1)} async-done(((bf16[8,4,16,128]{3,2,1,0:T(8,128)(2,1)}), bf16[8,4,16,128]{3,2,1,0:T(8,128)(2,1)S(1)}, u32[]{:S(2)}, u32[]{:S(2)}) %all-to-all-start.2) | async-done | bytes 131104 | tf_op jit(solution)/shard_map/all_to_all | solution.py:374
  64.1 0.7 shard_map.104
  64.8 3.7 %all-to-all-start.3 = ((bf16[16,4,16,128]{3,2,1,0:T(8,128)(2,1)}), bf16[16,4,16,128]{3,2,1,0:T(8,128)(2,1)S(1)}, u32[]{:S(2)}, u32[]{:S(2)}) async-start(bf16[16,4,16,128]{3,2,1,0:T(8,128)(2,1)} %shard_map.104), calls=%async_computation.3 | async-start | bytes 524288 | tf_op jit(solution)/shard_map/all_to_all | solution.py:374
  68.6 0.0 collective-permute-done.6.refs_3_.rest_3_
  68.6 0.1 collective-permute-start.7
  68.7 7.2 %all-to-all-done.3 = bf16[16,4,16,128]{3,2,1,0:T(8,128)(2,1)S(1)} async-done(((bf16[16,4,16,128]{3,2,1,0:T(8,128)(2,1)}), bf16[16,4,16,128]{3,2,1,0:T(8,128)(2,1)S(1)}, u32[]{:S(2)}, u32[]{:S(2)}) %all-to-all-start.3) | async-done | bytes 262176 | tf_op jit(solution)/shard_map/all_to_all | solution.py:374
  75.9 4.0 %collective-permute-start.12 = (bf16[64,16,128]{2,1,0:T(8,128)(2,1)S(1)}, bf16[64,16,128]{2,1,0:T(8,128)(2,1)S(1)}, u32[]{:S(2)}, u32[]{:S(2)}) collective-permute-start(bf16[64,16,128]{2,1,0:T(8,128)(2,1)S(1)} %bitcast.11), channel_id=1, source_target_pairs={{0,1},{1,0},{2,3},{3,2},{4,5},{5,4},{6,7},{7,6},{8,9},{9,8},{10,11... | collective-permute-start | bytes 786440 | tf_op jit(solution)/shard_map/ppermute | solution.py:370
  79.9 0.0 collective-permute-done.7.rest_4_
  79.9 1.0 %shard_map.101 = bf16[2,8,32,256]{3,2,1,0:T(8,128)(2,1)} custom-call(bf16[2,8,32,256]{3,2,1,0:T(8,128)(2,1)S(1)} %bitcast.20, f32[1,256]{1,0:T(1,128)S(1)} %bitcast.24, f32[2,8,32,256]{3,2,1,0:T(8,128)S(1)} %bitcast.26, bf16[8,2,16,256]{3,2,1,0:T(8,128)(2,1)S(1)} %get-tuple-element.42.refs_0_.rest_0_, ...), custom_call_target="tpu_custom_call" | custom-call | flops 1600000000 | bytes 4000000 | tf_op jit(solution)/shard_map/pallas_call | solution.py:358
  81.0 0.1 collective-permute-done.12.theirs
  81.1 1.1 %shard_map.105 = (f32[256,768]{1,0:T(8,128)}, f32[256,256]{1,0:T(8,128)}, f32[1,256]{1,0:T(1,128)}) custom-call(bf16[64,16,128]{2,1,0:T(8,128)(2,1)S(1)} %bitcast.12, bf16[64,16,128]{2,1,0:T(8,128)(2,1)S(1)} %collective-permute-done.12.theirs, f32[1,256]{1,0:T(1,128)S(1)} %bitcast.25, bf16[256,768]{1,0:T(8,128)(2,1)S(1)} %copy-done), custom_call_target="tpu_custom_call" | custom-call | flops 800000000 | bytes 2000000 | tf_op jit(solution)/shard_map/pallas_call | solution.py:358
  (11 shorter events, 0.1 us)
Async XLA Ops:
  2.6 12.8 %collective-permute-start = (bf16[2,2,8,16,256]{4,3,2,1,0:T(8,128)(2,1)}, bf16[2,2,8,16,256]{4,3,2,1,0:T(8,128)(2,1)S(1)}, u32[]{:S(2)}, u32[]{:S(2)}) collective-permute-start(bf16[2,2,8,16,256]{4,3,2,1,0:T(8,128)(2,1)} %get-tuple-element.34), channel_id=1, source_target_pairs={{0,2},{2,0},{1,3},{3,1},{4,6},{6,4},{5,7},{7,5},{8,10},{10,8},{9,1... | collective-permute-start | bytes 786440 | tf_op jit(solution)/shard_map/ppermute | solution.py:370
  4.7 10.6 %copy-start.1 = (bf16[1,2,8,32,256]{4,3,2,1,0:T(8,128)(2,1)S(1)}, bf16[1,2,8,32,256]{4,3,2,1,0:T(8,128)(2,1)}, u32[]{:S(2)}) copy-start(bf16[1,2,8,32,256]{4,3,2,1,0:T(8,128)(2,1)} %param.8) | copy-start | bytes 786436
  4.7 10.6 %copy-start.3 = (bf16[1,2,8,32,256]{4,3,2,1,0:T(8,128)(2,1)S(1)}, bf16[1,2,8,32,256]{4,3,2,1,0:T(8,128)(2,1)}, u32[]{:S(2)}) copy-start(bf16[1,2,8,32,256]{4,3,2,1,0:T(8,128)(2,1)} %param.6) | copy-start | bytes 786436
  4.7 24.9 %all-to-all-start = ((bf16[16,2,2,16,256]{4,3,2,1,0:T(8,128)(2,1)}), bf16[16,2,2,16,256]{4,3,2,1,0:T(8,128)(2,1)S(1)}, u32[]{:S(2)}, u32[]{:S(2)}) async-start(bf16[16,2,2,16,256]{4,3,2,1,0:T(8,128)(2,1)} %bitcast.27), calls=%async_computation | async-start | bytes 1048576 | tf_op jit(solution)/shard_map/all_to_all | solution.py:374
  15.3 1.5 %copy-start = (bf16[256,768]{1,0:T(8,128)(2,1)S(1)}, bf16[256,768]{1,0:T(8,128)(2,1)}, u32[]{:S(2)}) copy-start(bf16[256,768]{1,0:T(8,128)(2,1)} %w_qkv.5) | copy-start | bytes 1179652
  15.3 1.5 %copy-start.2 = (bf16[1,2,8,32,256]{4,3,2,1,0:T(8,128)(2,1)S(1)}, bf16[1,2,8,32,256]{4,3,2,1,0:T(8,128)(2,1)}, u32[]{:S(2)}) copy-start(bf16[1,2,8,32,256]{4,3,2,1,0:T(8,128)(2,1)} %param.7) | copy-start | bytes 786436
  15.4 1.5 %copy-start.4 = (bf16[256,256]{1,0:T(8,128)(2,1)S(1)}, bf16[256,256]{1,0:T(8,128)(2,1)}, u32[]{:S(2)}) copy-start(bf16[256,256]{1,0:T(8,128)(2,1)} %w_out.3) | copy-start | bytes 393220
  15.4 5.3 %collective-permute-start.1 = (bf16[2,8,16,256]{3,2,1,0:T(8,128)(2,1)S(1)}, bf16[2,8,16,256]{3,2,1,0:T(8,128)(2,1)S(1)}, u32[]{:S(2)}, u32[]{:S(2)}) collective-permute-start(bf16[2,8,16,256]{3,2,1,0:T(8,128)(2,1)S(1)} %get-tuple-element.36), channel_id=1, source_target_pairs={{0,1},{1,0},{2,3},{3,2},{4,5},{5,4},{6,7},{7,6},{8,9},{9,8},{10,11... | collective-permute-start | bytes 393224 | tf_op jit(solution)/shard_map/ppermute | solution.py:370
  16.7 4.0 %collective-permute-start.2 = (bf16[2,2,8,16,256]{4,3,2,1,0:T(8,128)(2,1)S(1)}, bf16[2,2,8,16,256]{4,3,2,1,0:T(8,128)(2,1)S(1)}, u32[]{:S(2)}, u32[]{:S(2)}) collective-permute-start(bf16[2,2,8,16,256]{4,3,2,1,0:T(8,128)(2,1)S(1)} %collective-permute-done.refs_2_), channel_id=1, source_target_pairs={{0,1},{1,0},{2,3},{3,2},{4,5},{5,4},{6,7},{7,6},{8,9},{9,8},{10,11... | collective-permute-start | bytes 786440 | tf_op jit(solution)/shard_map/ppermute | solution.py:370
  16.8 0.7 copy-start.5
  24.2 2.7 %collective-permute-start.3 = (bf16[64,16,128]{2,1,0:T(8,128)(2,1)S(1)}, bf16[64,16,128]{2,1,0:T(8,128)(2,1)S(1)}, u32[]{:S(2)}, u32[]{:S(2)}) collective-permute-start(bf16[64,16,128]{2,1,0:T(8,128)(2,1)S(1)} %get-tuple-element.41), channel_id=1, source_target_pairs={{0,1},{1,0},{2,3},{3,2},{4,5},{5,4},{6,7},{7,6},{8,9},{9,8},{10,11... | collective-permute-start | bytes 786440 | tf_op jit(solution)/shard_map/ppermute | solution.py:370
  24.8 8.4 %collective-permute-start.8 = (bf16[8,16,256]{2,1,0:T(8,128)(2,1)S(1)}, bf16[8,16,256]{2,1,0:T(8,128)(2,1)S(1)}, u32[]{:S(2)}, u32[]{:S(2)}) collective-permute-start(bf16[8,16,256]{2,1,0:T(8,128)(2,1)S(1)} %get-tuple-element.46), channel_id=1, source_target_pairs={{0,1},{1,0},{2,3},{3,2},{4,5},{5,4},{6,7},{7,6},{8,9},{9,8},{10,11... | collective-permute-start | bytes 196616 | tf_op jit(solution)/shard_map/ppermute | solution.py:370
  24.9 8.3 %collective-permute-start.9 = (bf16[8,16,256]{2,1,0:T(8,128)(2,1)S(1)}, bf16[8,16,256]{2,1,0:T(8,128)(2,1)S(1)}, u32[]{:S(2)}, u32[]{:S(2)}) collective-permute-start(bf16[8,16,256]{2,1,0:T(8,128)(2,1)S(1)} %get-tuple-element.47), channel_id=1, source_target_pairs={{0,2},{1,3},{2,0},{3,1},{4,6},{5,7},{6,4},{7,5},{8,10},{9,11},{10,... | collective-permute-start | bytes 196616 | tf_op jit(solution)/shard_map/ppermute | solution.py:370
  24.9 8.3 %collective-permute-start.10 = (bf16[8,16,256]{2,1,0:T(8,128)(2,1)S(1)}, bf16[8,16,256]{2,1,0:T(8,128)(2,1)S(1)}, u32[]{:S(2)}, u32[]{:S(2)}) collective-permute-start(bf16[8,16,256]{2,1,0:T(8,128)(2,1)S(1)} %get-tuple-element.48), channel_id=1, source_target_pairs={{0,3},{1,2},{2,1},{3,0},{4,7},{5,6},{6,5},{7,4},{8,11},{9,10},{10,... | collective-permute-start | bytes 196616 | tf_op jit(solution)/shard_map/ppermute | solution.py:370
  33.2 4.9 %collective-permute-start.11 = (bf16[64,16,128]{2,1,0:T(8,128)(2,1)S(1)}, bf16[64,16,128]{2,1,0:T(8,128)(2,1)S(1)}, u32[]{:S(2)}, u32[]{:S(2)}) collective-permute-start(bf16[64,16,128]{2,1,0:T(8,128)(2,1)S(1)} %get-tuple-element.54), channel_id=1, source_target_pairs={{0,1},{1,0},{2,3},{3,2},{4,5},{5,4},{6,7},{7,6},{8,9},{9,8},{10,11... | collective-permute-start | bytes 786440 | tf_op jit(solution)/shard_map/ppermute | solution.py:370
  36.9 7.6 %collective-permute-start.4 = (bf16[8,2,16,256]{3,2,1,0:T(8,128)(2,1)S(1)}, bf16[8,2,16,256]{3,2,1,0:T(8,128)(2,1)S(1)}, u32[]{:S(2)}, u32[]{:S(2)}) collective-permute-start(bf16[8,2,16,256]{3,2,1,0:T(8,128)(2,1)S(1)} %get-tuple-element.43), channel_id=1, source_target_pairs={{0,8},{8,0},{16,24},{24,16},{32,40},{40,32},{48,56},{56,48},{1,9},... | collective-permute-start | bytes 393224 | tf_op jit(solution)/shard_map/ppermute | solution.py:370
  38.9 13.2 %all-to-all-start.1 = ((bf16[16,4,16,128]{3,2,1,0:T(8,128)(2,1)}), bf16[16,4,16,128]{3,2,1,0:T(8,128)(2,1)S(1)}, u32[]{:S(2)}, u32[]{:S(2)}) async-start(bf16[16,4,16,128]{3,2,1,0:T(8,128)(2,1)} %shard_map.102), calls=%async_computation.1 | async-start | bytes 524288 | tf_op jit(solution)/shard_map/all_to_all | solution.py:374
  44.5 11.6 %collective-permute-start.5 = (bf16[8,2,16,256]{3,2,1,0:T(8,128)(2,1)S(1)}, bf16[8,2,16,256]{3,2,1,0:T(8,128)(2,1)S(1)}, u32[]{:S(2)}, u32[]{:S(2)}) collective-permute-start(bf16[8,2,16,256]{3,2,1,0:T(8,128)(2,1)S(1)} %shard_map.98), channel_id=1, source_target_pairs={{0,32},{8,40},{16,48},{24,56},{32,0},{40,8},{48,16},{56,24},{1,33}... | collective-permute-start | bytes 393224 | tf_op jit(solution)/shard_map/ppermute | solution.py:370
  52.8 11.3 %all-to-all-start.2 = ((bf16[8,4,16,128]{3,2,1,0:T(8,128)(2,1)}), bf16[8,4,16,128]{3,2,1,0:T(8,128)(2,1)S(1)}, u32[]{:S(2)}, u32[]{:S(2)}) async-start(bf16[8,4,16,128]{3,2,1,0:T(8,128)(2,1)} %shard_map.103), calls=%async_computation.2 | async-start | bytes 262144 | tf_op jit(solution)/shard_map/all_to_all | solution.py:374
  56.2 12.4 %collective-permute-start.6 = (bf16[8,2,16,256]{3,2,1,0:T(8,128)(2,1)S(1)}, bf16[8,2,16,256]{3,2,1,0:T(8,128)(2,1)S(1)}, u32[]{:S(2)}, u32[]{:S(2)}) collective-permute-start(bf16[8,2,16,256]{3,2,1,0:T(8,128)(2,1)S(1)} %shard_map.99), channel_id=1, source_target_pairs={{0,4},{4,0},{1,5},{5,1},{2,6},{6,2},{3,7},{7,3},{8,12},{12,8},{9,1... | collective-permute-start | bytes 393224 | tf_op jit(solution)/shard_map/ppermute | solution.py:370
  64.8 11.1 %all-to-all-start.3 = ((bf16[16,4,16,128]{3,2,1,0:T(8,128)(2,1)}), bf16[16,4,16,128]{3,2,1,0:T(8,128)(2,1)S(1)}, u32[]{:S(2)}, u32[]{:S(2)}) async-start(bf16[16,4,16,128]{3,2,1,0:T(8,128)(2,1)} %shard_map.104), calls=%async_computation.3 | async-start | bytes 524288 | tf_op jit(solution)/shard_map/all_to_all | solution.py:374
  68.6 11.3 %collective-permute-start.7 = (bf16[8,2,16,256]{3,2,1,0:T(8,128)(2,1)S(1)}, bf16[8,2,16,256]{3,2,1,0:T(8,128)(2,1)S(1)}, u32[]{:S(2)}, u32[]{:S(2)}) collective-permute-start(bf16[8,2,16,256]{3,2,1,0:T(8,128)(2,1)S(1)} %shard_map.100), channel_id=1, source_target_pairs={{0,16},{8,24},{16,0},{24,8},{32,48},{40,56},{48,32},{56,40},{1,17}... | collective-permute-start | bytes 393224 | tf_op jit(solution)/shard_map/ppermute | solution.py:370
  75.9 5.2 %collective-permute-start.12 = (bf16[64,16,128]{2,1,0:T(8,128)(2,1)S(1)}, bf16[64,16,128]{2,1,0:T(8,128)(2,1)S(1)}, u32[]{:S(2)}, u32[]{:S(2)}) collective-permute-start(bf16[64,16,128]{2,1,0:T(8,128)(2,1)S(1)} %bitcast.11), channel_id=1, source_target_pairs={{0,1},{1,0},{2,3},{3,2},{4,5},{5,4},{6,7},{7,6},{8,9},{9,8},{10,11... | collective-permute-start | bytes 786440 | tf_op jit(solution)/shard_map/ppermute | solution.py:370

commit v10 on v9

--- a/solution.py
+++ b/solution.py
@@ -26,7 +26,7 @@
 F32 = jnp.float32
 VMEM = pl.BlockSpec(memory_space=pltpu.VMEM)
 HBM = pl.BlockSpec(memory_space=pltpu.HBM)
-PLANE = ("xh", "xl", "y")
+PLANE = ("xl", "y", "xh")
 FIRST = ("xh", "z")
 SECOND = ("xl", "c")
 
@@ -244,16 +244,15 @@
     pack(third_qkv[...] + part_qkv, part_out, halves, *packed)
 
 
-def first_kernel(pieces, early_own, early_other, gain, w_qkv, w_out, *refs):
-    (stay, leave), packed, scratch, rest = refs[:2], refs[2:4], refs[4:-5], refs[-5:]
-    returned, halves, held_own, held_other, sem = rest
-    held = (held_own, held_other)
-    copies = [
-        pltpu.make_async_copy(source, target, sem.at[at])
-        for at, (source, target) in enumerate(zip((early_own, early_other), held))
-    ]
-    for copy in copies:
-        copy.start()
+def early_kernel(own, received, total):
+    total[...] = (own[...].astype(F32) + received[...].astype(F32)).astype(BF16)
+
+
+def first_kernel(pieces, early, gain, w_qkv, w_out, *refs):
+    (stay, leave), packed, scratch, rest = refs[:2], refs[2:4], refs[4:-4], refs[-4:]
+    returned, halves, held, sem = rest
+    load = pltpu.make_async_copy(early, held, sem.at[0])
+    load.start()
     tokens = pieces[:, 0].reshape(TOKENS, WIDTH)
     cot = pieces[:, 1].reshape(TOKENS, WIDTH)
     grad_normed, part_qkv = axis_grads(
@@ -265,10 +264,9 @@
         stay[at] = returned[here ^ mask]
         leave[at] = returned[here ^ mask ^ BITS[0]]
     pack(part_qkv, None, halves, *packed)
-    for copy in copies:
-        copy.wait()
+    load.wait()
     own = packed[0]
-    own[...] += held_own[...].astype(F32) + held_other[...].astype(F32)
+    own[...] += held[...].astype(F32)
 
 
 def stage_kernel(*refs):
@@ -417,7 +415,9 @@
         SCRATCH + [halves],
     )
     from_second = [back[0]] + [swap(back[m], SECOND, m, 4) for m in (1, 2, 3)]
-    early = [own, swap(other, "c", 1, 2)]
+    early = kernel_call(
+        early_kernel, shape((TILES, *tile), BF16), (own, swap(other, "c", 1, 2)), 1
+    )
     block = (2, ROWS, WIDTH)
     stay, leave, own, other = kernel_call(
         first_kernel,
@@ -427,16 +427,16 @@
             shape((TILES, *tile), F32),
             *packed[1:],
         ),
-        (at_first, *early, gain_row, w_qkv, w_out),
+        (at_first, early, gain_row, w_qkv, w_out),
         5,
         SCRATCH
         + [
             pltpu.VMEM((16, *block), BF16),
             halves,
-            *[pltpu.VMEM(part.shape, part.dtype) for part in packed],
-            pltpu.SemaphoreType.DMA((2,)),
+            pltpu.VMEM((TILES, *tile), BF16),
+            pltpu.SemaphoreType.DMA((1,)),
         ],
-        spaces=[VMEM] + [HBM] * 2 + [VMEM] * 3,
+        spaces=[VMEM, HBM] + [VMEM] * 3,
     )
     other, from_second = lax.optimization_barrier((other, from_second))
     late = [own, swap(other, "c", 1, 2)]

time: 82.8 us -> 82.8 us (level)
    pallas_call x13 -> x14, Pallas kernels: 16.6 us -> 16.6 us  [kernel_call(): pl.pallas_call(body, out_shape=outs, in_specs=spaces or [space] * len(ope...]
where the time goes in v10:
time: 82.8 us; the launch traced here: 82.2 us
  starting transfers between devices  41.7 us (50%)
  waiting for transfers between devices  22.4 us (27%)
  Pallas kernels  16.6 us (20%)
  between operations  0.86 us (1%)
    all_to_all x4, starting transfers between devices, exchange(): return lax.all_to_all(pieces, axes, split_axis=0, concat_axis=0, tiled=True)  23.1 us
    all_to_all x4, waiting for transfers between devices, exchange(): return lax.all_to_all(pieces, axes, split_axis=0, concat_axis=0, tiled=True)  22.2 us
    ppermute x13, starting transfers between devices, swap(): return lax.ppermute(array, axis, [(i, i ^ mask) for i in range(size)])  18.6 us
    pallas_call x14, Pallas kernels, kernel_call(): pl.pallas_call(body, out_shape=outs, in_specs=spaces or [space] * len(ope...  16.6 us
  transfers between devices with their start and end apart: 17, of which 5 were waited for; matrix products, arithmetic and copies ran while one was open for 0% of the time, Pallas kernels for 16%

profile of v10, /device:TPU:1, one launch (start us, length us, event | category | flops | bytes accessed | tf_op | source)
XLA Modules:
  0.0 82.2 jit_solution(12730973160654503282)
XLA Ops:
  0.6 1.9 %shard_map.94 = (bf16[8,2,2,2,16,256]{5,4,3,2,1,0:T(8,128)(2,1)}, bf16[2,2,8,16,256]{4,3,2,1,0:T(8,128)(2,1)}) custom-call(bf16[2,8,32,256]{3,2,1,0:T(8,128)(2,1)} %bitcast.17, bf16[2,8,32,256]{3,2,1,0:T(8,128)(2,1)} %bitcast.13), custom_call_target="tpu_custom_call" | custom-call | flops 1600000000 | bytes 4000000 | tf_op jit(solution)/shard_map/pallas_call | solution.py:356
  2.6 2.1 %collective-permute-start = (bf16[2,2,8,16,256]{4,3,2,1,0:T(8,128)(2,1)}, bf16[2,2,8,16,256]{4,3,2,1,0:T(8,128)(2,1)S(1)}, u32[]{:S(2)}, u32[]{:S(2)}) collective-permute-start(bf16[2,2,8,16,256]{4,3,2,1,0:T(8,128)(2,1)} %get-tuple-element.34), channel_id=1, source_target_pairs={{0,2},{2,0},{1,3},{3,1},{4,6},{6,4},{5,7},{7,5},{8,10},{10,8},{9,1... | collective-permute-start | bytes 786440 | tf_op jit(solution)/shard_map/ppermute | solution.py:368
  4.7 10.6 %all-to-all-start = ((bf16[16,2,2,16,256]{4,3,2,1,0:T(8,128)(2,1)}), bf16[16,2,2,16,256]{4,3,2,1,0:T(8,128)(2,1)S(1)}, u32[]{:S(2)}, u32[]{:S(2)}) async-start(bf16[16,2,2,16,256]{4,3,2,1,0:T(8,128)(2,1)} %bitcast.27), calls=%async_computation | async-start | bytes 1048576 | tf_op jit(solution)/shard_map/all_to_all | solution.py:372
  15.3 0.0 copy-start
  15.3 0.0 copy-start.2
  15.4 0.0 copy-start.4
  15.4 0.0 collective-permute-done.refs_2_
  15.4 1.3 %collective-permute-start.1 = (bf16[2,8,16,256]{3,2,1,0:T(8,128)(2,1)S(1)}, bf16[2,8,16,256]{3,2,1,0:T(8,128)(2,1)S(1)}, u32[]{:S(2)}, u32[]{:S(2)}) collective-permute-start(bf16[2,8,16,256]{3,2,1,0:T(8,128)(2,1)S(1)} %get-tuple-element.36), channel_id=1, source_target_pairs={{0,1},{1,0},{2,3},{3,2},{4,5},{5,4},{6,7},{7,6},{8,9},{9,8},{10,11... | collective-permute-start | bytes 393224 | tf_op jit(solution)/shard_map/ppermute | solution.py:368
  16.7 0.1 collective-permute-start.2
  16.9 0.7 copy-done.5
  17.5 3.2 %shard_map.93 = (f32[512,256]{1,0:T(8,128)S(1)}, f32[256,768]{1,0:T(8,128)S(1)}, f32[256,256]{1,0:T(8,128)S(1)}) custom-call(bf16[512,256]{1,0:T(8,128)(2,1)S(1)} %bitcast.19, bf16[512,256]{1,0:T(8,128)(2,1)S(1)} %bitcast.15, bf16[512,256]{1,0:T(8,128)(2,1)S(1)} %bitcast.16, f32[1,256]{1,0:T(1,128)S(1)} %bitcast.21, bf16[256,768]{1,0:T(8,128)(2,1)S(1)} %copy-done, ...), custom_call_target="tpu_custom_call" | custom-call | flops 4000000000 | bytes 10000000 | tf_op jit(solution)/shard_map/pallas_call | solution.py:356
  20.7 0.0 collective-permute-done.1.refs_1_
  20.7 0.0 collective-permute-done.2.refs_3_
  20.7 3.5 %shard_map.96 = (bf16[8,16,256]{2,1,0:T(8,128)(2,1)S(1)}, bf16[8,16,256]{2,1,0:T(8,128)(2,1)S(1)}, bf16[8,16,256]{2,1,0:T(8,128)(2,1)S(1)}, bf16[8,16,256]{2,1,0...) custom-call(bf16[2,8,16,256]{3,2,1,0:T(8,128)(2,1)S(1)} %get-tuple-element.33.refs_0_, ...), custom_call_target="tpu_custom_call" | custom-call | flops 4000000000 | bytes 10000000 | tf_op jit(solution)/shard_map/pallas_call | solution.py:356
  24.2 0.6 collective-permute-start.3
  24.8 0.1 collective-permute-start.8
  24.9 0.0 collective-permute-start.9
  24.9 2.0 %collective-permute-start.10 = (bf16[8,16,256]{2,1,0:T(8,128)(2,1)S(1)}, bf16[8,16,256]{2,1,0:T(8,128)(2,1)S(1)}, u32[]{:S(2)}, u32[]{:S(2)}) collective-permute-start(bf16[8,16,256]{2,1,0:T(8,128)(2,1)S(1)} %get-tuple-element.48), channel_id=1, source_target_pairs={{0,3},{1,2},{2,1},{3,0},{4,7},{5,6},{6,5},{7,4},{8,11},{9,10},{10,... | collective-permute-start | bytes 196616 | tf_op jit(solution)/shard_map/ppermute | solution.py:368
  26.9 0.0 collective-permute-done.3.received
  26.9 0.1 shard_map.97.early
  27.0 2.6 %all-to-all-done.pieces = bf16[16,2,2,16,256]{4,3,2,1,0:T(8,128)(2,1)S(1)} async-done(((bf16[16,2,2,16,256]{4,3,2,1,0:T(8,128)(2,1)}), bf16[16,2,2,16,256]{4,3,2,1,0:T(8,128)(2,1)S(1)}, u32[]{:S(2)}, u32[]{:S(2)}) %all-to-all-start) | async-done | bytes 524320 | tf_op jit(solution)/shard_map/all_to_all | solution.py:372
  29.6 3.5 %shard_map.98 = (bf16[8,2,16,256]{3,2,1,0:T(8,128)(2,1)S(1)}, bf16[8,2,16,256]{3,2,1,0:T(8,128)(2,1)S(1)}, f32[64,16,128]{2,1,0:T(8,128)S(1)}, bf16[64,16,128]{2,1,0:T(8,128)(2,1)S(1)}) custom-call(bf16[16,2,2,16,256]{4,3,2,1,0:T(8,128)(2,1)S(1)} %all-to-all-done.pieces, bf16[64,16,128]{2,1,0:T(8,128)(2,1)S(1)} %shard_map.97.early, f32[1,256]{1,0:T(1,128)S(1)} %bitcast.23, ...), custom_call_target="tpu_custom_call" | custom-call | flops 4000000000 | bytes 10000000 | tf_op jit(solution)/shard_map/pallas_call | solution.py:356
  33.1 0.0 collective-permute-done.8.rest_6_
  33.1 0.0 collective-permute-done.9.rest_7_
  33.1 0.0 collective-permute-done.10.rest_8_
  33.1 3.7 %collective-permute-start.11 = (bf16[64,16,128]{2,1,0:T(8,128)(2,1)S(1)}, bf16[64,16,128]{2,1,0:T(8,128)(2,1)S(1)}, u32[]{:S(2)}, u32[]{:S(2)}) collective-permute-start(bf16[64,16,128]{2,1,0:T(8,128)(2,1)S(1)} %get-tuple-element.54), channel_id=1, source_target_pairs={{0,1},{1,0},{2,3},{3,2},{4,5},{5,4},{6,7},{7,6},{8,9},{9,8},{10,11... | collective-permute-start | bytes 786440 | tf_op jit(solution)/shard_map/ppermute | solution.py:368
  36.8 1.2 %collective-permute-start.4 = (bf16[8,2,16,256]{3,2,1,0:T(8,128)(2,1)S(1)}, bf16[8,2,16,256]{3,2,1,0:T(8,128)(2,1)S(1)}, u32[]{:S(2)}, u32[]{:S(2)}) collective-permute-start(bf16[8,2,16,256]{3,2,1,0:T(8,128)(2,1)S(1)} %get-tuple-element.43), channel_id=1, source_target_pairs={{0,8},{8,0},{16,24},{24,16},{32,40},{40,32},{48,56},{56,48},{1,9},... | collective-permute-start | bytes 393224 | tf_op jit(solution)/shard_map/ppermute | solution.py:368
  38.0 0.0 collective-permute-done.11.received
  38.1 0.7 shard_map.103
  38.8 5.6 %all-to-all-start.1 = ((bf16[16,4,16,128]{3,2,1,0:T(8,128)(2,1)}), bf16[16,4,16,128]{3,2,1,0:T(8,128)(2,1)S(1)}, u32[]{:S(2)}, u32[]{:S(2)}) async-start(bf16[16,4,16,128]{3,2,1,0:T(8,128)(2,1)} %shard_map.103), calls=%async_computation.1 | async-start | bytes 524288 | tf_op jit(solution)/shard_map/all_to_all | solution.py:372
  44.4 0.0 collective-permute-done.4.refs_1_.rest_1_
  44.5 1.9 %collective-permute-start.5 = (bf16[8,2,16,256]{3,2,1,0:T(8,128)(2,1)S(1)}, bf16[8,2,16,256]{3,2,1,0:T(8,128)(2,1)S(1)}, u32[]{:S(2)}, u32[]{:S(2)}) collective-permute-start(bf16[8,2,16,256]{3,2,1,0:T(8,128)(2,1)S(1)} %shard_map.99), channel_id=1, source_target_pairs={{0,32},{8,40},{16,48},{24,56},{32,0},{40,8},{48,16},{56,24},{1,33}... | collective-permute-start | bytes 393224 | tf_op jit(solution)/shard_map/ppermute | solution.py:368
  46.3 5.8 %all-to-all-done.1.received = bf16[16,4,16,128]{3,2,1,0:T(8,128)(2,1)S(1)} async-done(((bf16[16,4,16,128]{3,2,1,0:T(8,128)(2,1)}), bf16[16,4,16,128]{3,2,1,0:T(8,128)(2,1)S(1)}, u32[]{:S(2)}, u32[]{:S(2)}) %all-to-all-start.1) | async-done | bytes 262176 | tf_op jit(solution)/shard_map/all_to_all | solution.py:372
  52.2 0.7 shard_map.104
  52.9 3.4 %all-to-all-start.2 = ((bf16[8,4,16,128]{3,2,1,0:T(8,128)(2,1)}), bf16[8,4,16,128]{3,2,1,0:T(8,128)(2,1)S(1)}, u32[]{:S(2)}, u32[]{:S(2)}) async-start(bf16[8,4,16,128]{3,2,1,0:T(8,128)(2,1)} %shard_map.104), calls=%async_computation.2 | async-start | bytes 262144 | tf_op jit(solution)/shard_map/all_to_all | solution.py:372
  56.2 0.0 collective-permute-done.5.refs_2_.rest_2_
  56.3 1.4 %collective-permute-start.6 = (bf16[8,2,16,256]{3,2,1,0:T(8,128)(2,1)S(1)}, bf16[8,2,16,256]{3,2,1,0:T(8,128)(2,1)S(1)}, u32[]{:S(2)}, u32[]{:S(2)}) collective-permute-start(bf16[8,2,16,256]{3,2,1,0:T(8,128)(2,1)S(1)} %shard_map.100), channel_id=1, source_target_pairs={{0,4},{4,0},{1,5},{5,1},{2,6},{6,2},{3,7},{7,3},{8,12},{12,8},{9,1... | collective-permute-start | bytes 393224 | tf_op jit(solution)/shard_map/ppermute | solution.py:368
  57.6 6.5 %all-to-all-done.2.received = bf16[8,4,16,128]{3,2,1,0:T(8,128)(2,1)S(1)} async-done(((bf16[8,4,16,128]{3,2,1,0:T(8,128)(2,1)}), bf16[8,4,16,128]{3,2,1,0:T(8,128)(2,1)S(1)}, u32[]{:S(2)}, u32[]{:S(2)}) %all-to-all-start.2) | async-done | bytes 131104 | tf_op jit(solution)/shard_map/all_to_all | solution.py:372
  64.1 0.7 shard_map.105
  64.9 3.5 %all-to-all-start.3 = ((bf16[16,4,16,128]{3,2,1,0:T(8,128)(2,1)}), bf16[16,4,16,128]{3,2,1,0:T(8,128)(2,1)S(1)}, u32[]{:S(2)}, u32[]{:S(2)}) async-start(bf16[16,4,16,128]{3,2,1,0:T(8,128)(2,1)} %shard_map.105), calls=%async_computation.3 | async-start | bytes 524288 | tf_op jit(solution)/shard_map/all_to_all | solution.py:372
  68.4 0.0 collective-permute-done.6.refs_3_.rest_3_
  68.4 0.1 collective-permute-start.7
  68.5 7.3 %all-to-all-done.3 = bf16[16,4,16,128]{3,2,1,0:T(8,128)(2,1)S(1)} async-done(((bf16[16,4,16,128]{3,2,1,0:T(8,128)(2,1)}), bf16[16,4,16,128]{3,2,1,0:T(8,128)(2,1)S(1)}, u32[]{:S(2)}, u32[]{:S(2)}) %all-to-all-start.3) | async-done | bytes 262176 | tf_op jit(solution)/shard_map/all_to_all | solution.py:372
  75.9 4.1 %collective-permute-start.12 = (bf16[64,16,128]{2,1,0:T(8,128)(2,1)S(1)}, bf16[64,16,128]{2,1,0:T(8,128)(2,1)S(1)}, u32[]{:S(2)}, u32[]{:S(2)}) collective-permute-start(bf16[64,16,128]{2,1,0:T(8,128)(2,1)S(1)} %bitcast.11), channel_id=1, source_target_pairs={{0,1},{1,0},{2,3},{3,2},{4,5},{5,4},{6,7},{7,6},{8,9},{9,8},{10,11... | collective-permute-start | bytes 786440 | tf_op jit(solution)/shard_map/ppermute | solution.py:368
  80.0 0.0 collective-permute-done.7.rest_4_
  80.0 1.0 %shard_map.102 = bf16[2,8,32,256]{3,2,1,0:T(8,128)(2,1)} custom-call(bf16[2,8,32,256]{3,2,1,0:T(8,128)(2,1)S(1)} %bitcast.20, f32[1,256]{1,0:T(1,128)S(1)} %bitcast.24, f32[2,8,32,256]{3,2,1,0:T(8,128)S(1)} %bitcast.26, bf16[8,2,16,256]{3,2,1,0:T(8,128)(2,1)S(1)} %get-tuple-element.42.refs_0_.rest_0_, ...), custom_call_target="tpu_custom_call" | custom-call | flops 1600000000 | bytes 4000000 | tf_op jit(solution)/shard_map/pallas_call | solution.py:356
  81.0 0.1 collective-permute-done.12.theirs
  81.1 1.1 %shard_map.106 = (f32[256,768]{1,0:T(8,128)}, f32[256,256]{1,0:T(8,128)}, f32[1,256]{1,0:T(1,128)}) custom-call(bf16[64,16,128]{2,1,0:T(8,128)(2,1)S(1)} %bitcast.12, bf16[64,16,128]{2,1,0:T(8,128)(2,1)S(1)} %collective-permute-done.12.theirs, f32[1,256]{1,0:T(1,128)S(1)} %bitcast.25, bf16[256,768]{1,0:T(8,128)(2,1)S(1)} %copy-done), custom_call_target="tpu_custom_call" | custom-call | flops 800000000 | bytes 2000000 | tf_op jit(solution)/shard_map/pallas_call | solution.py:356
  (12 shorter events, 0.1 us)
Async XLA Ops:
  2.6 12.8 %collective-permute-start = (bf16[2,2,8,16,256]{4,3,2,1,0:T(8,128)(2,1)}, bf16[2,2,8,16,256]{4,3,2,1,0:T(8,128)(2,1)S(1)}, u32[]{:S(2)}, u32[]{:S(2)}) collective-permute-start(bf16[2,2,8,16,256]{4,3,2,1,0:T(8,128)(2,1)} %get-tuple-element.34), channel_id=1, source_target_pairs={{0,2},{2,0},{1,3},{3,1},{4,6},{6,4},{5,7},{7,5},{8,10},{10,8},{9,1... | collective-permute-start | bytes 786440 | tf_op jit(solution)/shard_map/ppermute | solution.py:368
  4.7 10.6 %copy-start.1 = (bf16[1,2,8,32,256]{4,3,2,1,0:T(8,128)(2,1)S(1)}, bf16[1,2,8,32,256]{4,3,2,1,0:T(8,128)(2,1)}, u32[]{:S(2)}) copy-start(bf16[1,2,8,32,256]{4,3,2,1,0:T(8,128)(2,1)} %param.8) | copy-start | bytes 786436
  4.7 10.6 %copy-start.3 = (bf16[1,2,8,32,256]{4,3,2,1,0:T(8,128)(2,1)S(1)}, bf16[1,2,8,32,256]{4,3,2,1,0:T(8,128)(2,1)}, u32[]{:S(2)}) copy-start(bf16[1,2,8,32,256]{4,3,2,1,0:T(8,128)(2,1)} %param.6) | copy-start | bytes 786436
  4.7 24.9 %all-to-all-start = ((bf16[16,2,2,16,256]{4,3,2,1,0:T(8,128)(2,1)}), bf16[16,2,2,16,256]{4,3,2,1,0:T(8,128)(2,1)S(1)}, u32[]{:S(2)}, u32[]{:S(2)}) async-start(bf16[16,2,2,16,256]{4,3,2,1,0:T(8,128)(2,1)} %bitcast.27), calls=%async_computation | async-start | bytes 1048576 | tf_op jit(solution)/shard_map/all_to_all | solution.py:372
  15.3 1.5 %copy-start = (bf16[256,768]{1,0:T(8,128)(2,1)S(1)}, bf16[256,768]{1,0:T(8,128)(2,1)}, u32[]{:S(2)}) copy-start(bf16[256,768]{1,0:T(8,128)(2,1)} %w_qkv.5) | copy-start | bytes 1179652
  15.3 1.5 %copy-start.2 = (bf16[1,2,8,32,256]{4,3,2,1,0:T(8,128)(2,1)S(1)}, bf16[1,2,8,32,256]{4,3,2,1,0:T(8,128)(2,1)}, u32[]{:S(2)}) copy-start(bf16[1,2,8,32,256]{4,3,2,1,0:T(8,128)(2,1)} %param.7) | copy-start | bytes 786436
  15.4 1.5 %copy-start.4 = (bf16[256,256]{1,0:T(8,128)(2,1)S(1)}, bf16[256,256]{1,0:T(8,128)(2,1)}, u32[]{:S(2)}) copy-start(bf16[256,256]{1,0:T(8,128)(2,1)} %w_out.3) | copy-start | bytes 393220
  15.4 5.3 %collective-permute-start.1 = (bf16[2,8,16,256]{3,2,1,0:T(8,128)(2,1)S(1)}, bf16[2,8,16,256]{3,2,1,0:T(8,128)(2,1)S(1)}, u32[]{:S(2)}, u32[]{:S(2)}) collective-permute-start(bf16[2,8,16,256]{3,2,1,0:T(8,128)(2,1)S(1)} %get-tuple-element.36), channel_id=1, source_target_pairs={{0,1},{1,0},{2,3},{3,2},{4,5},{5,4},{6,7},{7,6},{8,9},{9,8},{10,11... | collective-permute-start | bytes 393224 | tf_op jit(solution)/shard_map/ppermute | solution.py:368
  16.7 4.0 %collective-permute-start.2 = (bf16[2,2,8,16,256]{4,3,2,1,0:T(8,128)(2,1)S(1)}, bf16[2,2,8,16,256]{4,3,2,1,0:T(8,128)(2,1)S(1)}, u32[]{:S(2)}, u32[]{:S(2)}) collective-permute-start(bf16[2,2,8,16,256]{4,3,2,1,0:T(8,128)(2,1)S(1)} %collective-permute-done.refs_2_), channel_id=1, source_target_pairs={{0,1},{1,0},{2,3},{3,2},{4,5},{5,4},{6,7},{7,6},{8,9},{9,8},{10,11... | collective-permute-start | bytes 786440 | tf_op jit(solution)/shard_map/ppermute | solution.py:368
  16.8 0.7 copy-start.5
  24.2 2.7 %collective-permute-start.3 = (bf16[64,16,128]{2,1,0:T(8,128)(2,1)S(1)}, bf16[64,16,128]{2,1,0:T(8,128)(2,1)S(1)}, u32[]{:S(2)}, u32[]{:S(2)}) collective-permute-start(bf16[64,16,128]{2,1,0:T(8,128)(2,1)S(1)} %get-tuple-element.41), channel_id=1, source_target_pairs={{0,1},{1,0},{2,3},{3,2},{4,5},{5,4},{6,7},{7,6},{8,9},{9,8},{10,11... | collective-permute-start | bytes 786440 | tf_op jit(solution)/shard_map/ppermute | solution.py:368
  24.8 8.4 %collective-permute-start.8 = (bf16[8,16,256]{2,1,0:T(8,128)(2,1)S(1)}, bf16[8,16,256]{2,1,0:T(8,128)(2,1)S(1)}, u32[]{:S(2)}, u32[]{:S(2)}) collective-permute-start(bf16[8,16,256]{2,1,0:T(8,128)(2,1)S(1)} %get-tuple-element.46), channel_id=1, source_target_pairs={{0,1},{1,0},{2,3},{3,2},{4,5},{5,4},{6,7},{7,6},{8,9},{9,8},{10,11... | collective-permute-start | bytes 196616 | tf_op jit(solution)/shard_map/ppermute | solution.py:368
  24.9 8.3 %collective-permute-start.9 = (bf16[8,16,256]{2,1,0:T(8,128)(2,1)S(1)}, bf16[8,16,256]{2,1,0:T(8,128)(2,1)S(1)}, u32[]{:S(2)}, u32[]{:S(2)}) collective-permute-start(bf16[8,16,256]{2,1,0:T(8,128)(2,1)S(1)} %get-tuple-element.47), channel_id=1, source_target_pairs={{0,2},{1,3},{2,0},{3,1},{4,6},{5,7},{6,4},{7,5},{8,10},{9,11},{10,... | collective-permute-start | bytes 196616 | tf_op jit(solution)/shard_map/ppermute | solution.py:368
  24.9 8.3 %collective-permute-start.10 = (bf16[8,16,256]{2,1,0:T(8,128)(2,1)S(1)}, bf16[8,16,256]{2,1,0:T(8,128)(2,1)S(1)}, u32[]{:S(2)}, u32[]{:S(2)}) collective-permute-start(bf16[8,16,256]{2,1,0:T(8,128)(2,1)S(1)} %get-tuple-element.48), channel_id=1, source_target_pairs={{0,3},{1,2},{2,1},{3,0},{4,7},{5,6},{6,5},{7,4},{8,11},{9,10},{10,... | collective-permute-start | bytes 196616 | tf_op jit(solution)/shard_map/ppermute | solution.py:368
  33.1 4.9 %collective-permute-start.11 = (bf16[64,16,128]{2,1,0:T(8,128)(2,1)S(1)}, bf16[64,16,128]{2,1,0:T(8,128)(2,1)S(1)}, u32[]{:S(2)}, u32[]{:S(2)}) collective-permute-start(bf16[64,16,128]{2,1,0:T(8,128)(2,1)S(1)} %get-tuple-element.54), channel_id=1, source_target_pairs={{0,1},{1,0},{2,3},{3,2},{4,5},{5,4},{6,7},{7,6},{8,9},{9,8},{10,11... | collective-permute-start | bytes 786440 | tf_op jit(solution)/shard_map/ppermute | solution.py:368
  36.8 7.6 %collective-permute-start.4 = (bf16[8,2,16,256]{3,2,1,0:T(8,128)(2,1)S(1)}, bf16[8,2,16,256]{3,2,1,0:T(8,128)(2,1)S(1)}, u32[]{:S(2)}, u32[]{:S(2)}) collective-permute-start(bf16[8,2,16,256]{3,2,1,0:T(8,128)(2,1)S(1)} %get-tuple-element.43), channel_id=1, source_target_pairs={{0,8},{8,0},{16,24},{24,16},{32,40},{40,32},{48,56},{56,48},{1,9},... | collective-permute-start | bytes 393224 | tf_op jit(solution)/shard_map/ppermute | solution.py:368
  38.8 13.4 %all-to-all-start.1 = ((bf16[16,4,16,128]{3,2,1,0:T(8,128)(2,1)}), bf16[16,4,16,128]{3,2,1,0:T(8,128)(2,1)S(1)}, u32[]{:S(2)}, u32[]{:S(2)}) async-start(bf16[16,4,16,128]{3,2,1,0:T(8,128)(2,1)} %shard_map.103), calls=%async_computation.1 | async-start | bytes 524288 | tf_op jit(solution)/shard_map/all_to_all | solution.py:372
  44.5 11.8 %collective-permute-start.5 = (bf16[8,2,16,256]{3,2,1,0:T(8,128)(2,1)S(1)}, bf16[8,2,16,256]{3,2,1,0:T(8,128)(2,1)S(1)}, u32[]{:S(2)}, u32[]{:S(2)}) collective-permute-start(bf16[8,2,16,256]{3,2,1,0:T(8,128)(2,1)S(1)} %shard_map.99), channel_id=1, source_target_pairs={{0,32},{8,40},{16,48},{24,56},{32,0},{40,8},{48,16},{56,24},{1,33}... | collective-permute-start | bytes 393224 | tf_op jit(solution)/shard_map/ppermute | solution.py:368
  52.9 11.3 %all-to-all-start.2 = ((bf16[8,4,16,128]{3,2,1,0:T(8,128)(2,1)}), bf16[8,4,16,128]{3,2,1,0:T(8,128)(2,1)S(1)}, u32[]{:S(2)}, u32[]{:S(2)}) async-start(bf16[8,4,16,128]{3,2,1,0:T(8,128)(2,1)} %shard_map.104), calls=%async_computation.2 | async-start | bytes 262144 | tf_op jit(solution)/shard_map/all_to_all | solution.py:372
  56.3 12.1 %collective-permute-start.6 = (bf16[8,2,16,256]{3,2,1,0:T(8,128)(2,1)S(1)}, bf16[8,2,16,256]{3,2,1,0:T(8,128)(2,1)S(1)}, u32[]{:S(2)}, u32[]{:S(2)}) collective-permute-start(bf16[8,2,16,256]{3,2,1,0:T(8,128)(2,1)S(1)} %shard_map.100), channel_id=1, source_target_pairs={{0,4},{4,0},{1,5},{5,1},{2,6},{6,2},{3,7},{7,3},{8,12},{12,8},{9,1... | collective-permute-start | bytes 393224 | tf_op jit(solution)/shard_map/ppermute | solution.py:368
  64.9 11.0 %all-to-all-start.3 = ((bf16[16,4,16,128]{3,2,1,0:T(8,128)(2,1)}), bf16[16,4,16,128]{3,2,1,0:T(8,128)(2,1)S(1)}, u32[]{:S(2)}, u32[]{:S(2)}) async-start(bf16[16,4,16,128]{3,2,1,0:T(8,128)(2,1)} %shard_map.105), calls=%async_computation.3 | async-start | bytes 524288 | tf_op jit(solution)/shard_map/all_to_all | solution.py:372
  68.4 11.5 %collective-permute-start.7 = (bf16[8,2,16,256]{3,2,1,0:T(8,128)(2,1)S(1)}, bf16[8,2,16,256]{3,2,1,0:T(8,128)(2,1)S(1)}, u32[]{:S(2)}, u32[]{:S(2)}) collective-permute-start(bf16[8,2,16,256]{3,2,1,0:T(8,128)(2,1)S(1)} %shard_map.101), channel_id=1, source_target_pairs={{0,16},{8,24},{16,0},{24,8},{32,48},{40,56},{48,32},{56,40},{1,17}... | collective-permute-start | bytes 393224 | tf_op jit(solution)/shard_map/ppermute | solution.py:368
  75.9 5.2 %collective-permute-start.12 = (bf16[64,16,128]{2,1,0:T(8,128)(2,1)S(1)}, bf16[64,16,128]{2,1,0:T(8,128)(2,1)S(1)}, u32[]{:S(2)}, u32[]{:S(2)}) collective-permute-start(bf16[64,16,128]{2,1,0:T(8,128)(2,1)S(1)} %bitcast.11), channel_id=1, source_target_pairs={{0,1},{1,0},{2,3},{3,2},{4,5},{5,4},{6,7},{7,6},{8,9},{9,8},{10,11... | collective-permute-start | bytes 786440 | tf_op jit(solution)/shard_map/ppermute | solution.py:368

commit v11 on v10

--- a/solution.py
+++ b/solution.py
@@ -21,6 +21,7 @@
 PENCILS = 16
 ROWS = 16
 LANES = 128
+QKV_TILES = 48
 TILES = 64
 BF16 = jnp.bfloat16
 F32 = jnp.float32
@@ -210,20 +211,28 @@
     out_out[...] = dot(attn[...], cot, 0, 0)
 
 
+def place_of(at):
+    if at < 96:
+        return divmod(at, QKV_TILES)
+    half, tile = divmod(at - 96, TILES - QKV_TILES)
+    return half, QKV_TILES + tile
+
+
 def pack(total, part_out, halves, own, other):
     for at in range(2 * TILES):
-        half, tile = divmod(at, TILES)
+        half, tile = place_of(at)
         if at < 96:
             row, col = divmod(at, 6)
             halves[half, tile] = total[row * 16 : row * 16 + 16, col * LANES : (col + 1) * LANES]
         elif part_out is None:
-            halves[half, tile] = jnp.zeros((16, LANES), F32)
+            continue
         else:
             row, col = divmod(at - 96, 2)
             halves[half, tile] = part_out[row * 16 : row * 16 + 16, col * LANES : (col + 1) * LANES]
     mine = lax.axis_index("c")
-    own[0:TILES] = halves[mine].astype(own.dtype)
-    other[...] = halves[1 - mine].astype(BF16)
+    count = other.shape[0]
+    own[0:count] = halves[mine, 0:count].astype(own.dtype)
+    other[...] = halves[1 - mine, 0:count].astype(BF16)
 
 
 def second_kernel(*refs):
@@ -266,7 +275,8 @@
     pack(part_qkv, None, halves, *packed)
     load.wait()
     own = packed[0]
-    own[...] += held[...].astype(F32)
+    own[0:QKV_TILES] += held[0:QKV_TILES].astype(F32)
+    own[QKV_TILES:TILES] = held[QKV_TILES:TILES].astype(F32)
 
 
 def stage_kernel(*refs):
@@ -284,7 +294,10 @@
 def pair_kernel(own, received, pieces):
     for peer in range(16):
         tiles = slice(peer * 4, peer * 4 + 4)
-        pieces[peer] = (own[tiles] + received[tiles].astype(F32)).astype(BF16)
+        total = own[tiles]
+        if tiles.stop <= QKV_TILES:
+            total = total + received[tiles].astype(F32)
+        pieces[peer] = total.astype(BF16)
 
 
 def plane_kernel(received, pieces):
@@ -304,7 +317,7 @@
     halves[at_core] = mine[...]
     halves[1 - at_core] = theirs[...]
     for at in range(2 * TILES):
-        half, tile = divmod(at, TILES)
+        half, tile = place_of(at)
         rows = halves[half, tile].astype(F32)
         if at < 96:
             row, col = divmod(at, 6)
@@ -425,7 +438,7 @@
             shape((8, *block), BF16),
             shape((8, *block), BF16),
             shape((TILES, *tile), F32),
-            *packed[1:],
+            shape((QKV_TILES, *tile), BF16),
         ),
         (at_first, early, gain_row, w_qkv, w_out),
         5,

time: 82.8 us -> 82.7 us (level)
  no operation moved by 1% of the time
where the time goes in v11:
time: 82.7 us; the launch traced here: 82.1 us
  starting transfers between devices  41.6 us (50%)
  waiting for transfers between devices  22.4 us (27%)
  Pallas kernels  16.6 us (20%)
  between operations  0.86 us (1%)
    all_to_all x4, starting transfers between devices, exchange(): return lax.all_to_all(pieces, axes, split_axis=0, concat_axis=0, tiled=True)  23.1 us
    all_to_all x4, waiting for transfers between devices, exchange(): return lax.all_to_all(pieces, axes, split_axis=0, concat_axis=0, tiled=True)  22.3 us
    ppermute x13, starting transfers between devices, swap(): return lax.ppermute(array, axis, [(i, i ^ mask) for i in range(size)])  18.5 us
    pallas_call x14, Pallas kernels, kernel_call(): pl.pallas_call(body, out_shape=outs, in_specs=spaces or [space] * len(ope...  16.6 us
  transfers between devices with their start and end apart: 17, of which 5 were waited for; matrix products, arithmetic and copies ran while one was open for 0% of the time, Pallas kernels for 16%

profile of v11, /device:TPU:1, one launch (start us, length us, event | category | flops | bytes accessed | tf_op | source)
XLA Modules:
  0.0 82.1 jit_solution(12981858144323214673)
XLA Ops:
  0.6 1.9 %shard_map.94 = (bf16[8,2,2,2,16,256]{5,4,3,2,1,0:T(8,128)(2,1)}, bf16[2,2,8,16,256]{4,3,2,1,0:T(8,128)(2,1)}) custom-call(bf16[2,8,32,256]{3,2,1,0:T(8,128)(2,1)} %bitcast.17, bf16[2,8,32,256]{3,2,1,0:T(8,128)(2,1)} %bitcast.13), custom_call_target="tpu_custom_call" | custom-call | flops 1600000000 | bytes 4000000 | tf_op jit(solution)/shard_map/pallas_call | solution.py:369
  2.6 2.1 %collective-permute-start = (bf16[2,2,8,16,256]{4,3,2,1,0:T(8,128)(2,1)}, bf16[2,2,8,16,256]{4,3,2,1,0:T(8,128)(2,1)S(1)}, u32[]{:S(2)}, u32[]{:S(2)}) collective-permute-start(bf16[2,2,8,16,256]{4,3,2,1,0:T(8,128)(2,1)} %get-tuple-element.34), channel_id=1, source_target_pairs={{0,2},{2,0},{1,3},{3,1},{4,6},{6,4},{5,7},{7,5},{8,10},{10,8},{9,1... | collective-permute-start | bytes 786440 | tf_op jit(solution)/shard_map/ppermute | solution.py:381
  4.7 10.6 %all-to-all-start = ((bf16[16,2,2,16,256]{4,3,2,1,0:T(8,128)(2,1)}), bf16[16,2,2,16,256]{4,3,2,1,0:T(8,128)(2,1)S(1)}, u32[]{:S(2)}, u32[]{:S(2)}) async-start(bf16[16,2,2,16,256]{4,3,2,1,0:T(8,128)(2,1)} %bitcast.27), calls=%async_computation | async-start | bytes 1048576 | tf_op jit(solution)/shard_map/all_to_all | solution.py:385
  15.3 0.0 copy-start
  15.3 0.0 copy-start.2
  15.4 0.0 copy-start.4
  15.4 0.0 collective-permute-done.refs_2_
  15.4 1.3 %collective-permute-start.1 = (bf16[2,8,16,256]{3,2,1,0:T(8,128)(2,1)S(1)}, bf16[2,8,16,256]{3,2,1,0:T(8,128)(2,1)S(1)}, u32[]{:S(2)}, u32[]{:S(2)}) collective-permute-start(bf16[2,8,16,256]{3,2,1,0:T(8,128)(2,1)S(1)} %get-tuple-element.36), channel_id=1, source_target_pairs={{0,1},{1,0},{2,3},{3,2},{4,5},{5,4},{6,7},{7,6},{8,9},{9,8},{10,11... | collective-permute-start | bytes 393224 | tf_op jit(solution)/shard_map/ppermute | solution.py:381
  16.7 0.1 collective-permute-start.2
  16.9 0.7 copy-done.5
  17.5 3.2 %shard_map.93 = (f32[512,256]{1,0:T(8,128)S(1)}, f32[256,768]{1,0:T(8,128)S(1)}, f32[256,256]{1,0:T(8,128)S(1)}) custom-call(bf16[512,256]{1,0:T(8,128)(2,1)S(1)} %bitcast.19, bf16[512,256]{1,0:T(8,128)(2,1)S(1)} %bitcast.15, bf16[512,256]{1,0:T(8,128)(2,1)S(1)} %bitcast.16, f32[1,256]{1,0:T(1,128)S(1)} %bitcast.21, bf16[256,768]{1,0:T(8,128)(2,1)S(1)} %copy-done, ...), custom_call_target="tpu_custom_call" | custom-call | flops 4000000000 | bytes 10000000 | tf_op jit(solution)/shard_map/pallas_call | solution.py:369
  20.7 0.0 collective-permute-done.1.refs_1_
  20.7 0.0 collective-permute-done.2.refs_3_
  20.7 3.5 %shard_map.96 = (bf16[8,16,256]{2,1,0:T(8,128)(2,1)S(1)}, bf16[8,16,256]{2,1,0:T(8,128)(2,1)S(1)}, bf16[8,16,256]{2,1,0:T(8,128)(2,1)S(1)}, bf16[8,16,256]{2,1,0...) custom-call(bf16[2,8,16,256]{3,2,1,0:T(8,128)(2,1)S(1)} %get-tuple-element.33.refs_0_, ...), custom_call_target="tpu_custom_call" | custom-call | flops 4000000000 | bytes 10000000 | tf_op jit(solution)/shard_map/pallas_call | solution.py:369
  24.2 0.6 collective-permute-start.3
  24.8 0.1 collective-permute-start.8
  24.9 0.0 collective-permute-start.9
  24.9 2.0 %collective-permute-start.10 = (bf16[8,16,256]{2,1,0:T(8,128)(2,1)S(1)}, bf16[8,16,256]{2,1,0:T(8,128)(2,1)S(1)}, u32[]{:S(2)}, u32[]{:S(2)}) collective-permute-start(bf16[8,16,256]{2,1,0:T(8,128)(2,1)S(1)} %get-tuple-element.48), channel_id=1, source_target_pairs={{0,3},{1,2},{2,1},{3,0},{4,7},{5,6},{6,5},{7,4},{8,11},{9,10},{10,... | collective-permute-start | bytes 196616 | tf_op jit(solution)/shard_map/ppermute | solution.py:381
  26.9 0.0 collective-permute-done.3.received
  26.9 0.1 shard_map.97.early
  27.0 2.6 %all-to-all-done.pieces = bf16[16,2,2,16,256]{4,3,2,1,0:T(8,128)(2,1)S(1)} async-done(((bf16[16,2,2,16,256]{4,3,2,1,0:T(8,128)(2,1)}), bf16[16,2,2,16,256]{4,3,2,1,0:T(8,128)(2,1)S(1)}, u32[]{:S(2)}, u32[]{:S(2)}) %all-to-all-start) | async-done | bytes 524320 | tf_op jit(solution)/shard_map/all_to_all | solution.py:385
  29.6 3.5 %shard_map.98 = (bf16[8,2,16,256]{3,2,1,0:T(8,128)(2,1)S(1)}, bf16[8,2,16,256]{3,2,1,0:T(8,128)(2,1)S(1)}, f32[64,16,128]{2,1,0:T(8,128)S(1)}, bf16[48,16,128]{2,1,0:T(8,128)(2,1)S(1)}) custom-call(bf16[16,2,2,16,256]{4,3,2,1,0:T(8,128)(2,1)S(1)} %all-to-all-done.pieces, bf16[64,16,128]{2,1,0:T(8,128)(2,1)S(1)} %shard_map.97.early, f32[1,256]{1,0:T(1,128)S(1)} %bitcast.23, ...), custom_call_target="tpu_custom_call" | custom-call | flops 4000000000 | bytes 10000000 | tf_op jit(solution)/shard_map/pallas_call | solution.py:369
  33.1 0.0 collective-permute-done.8.rest_6_
  33.1 0.0 collective-permute-done.9.rest_7_
  33.1 0.0 collective-permute-done.10.rest_8_
  33.1 3.7 %collective-permute-start.11 = (bf16[48,16,128]{2,1,0:T(8,128)(2,1)S(1)}, bf16[48,16,128]{2,1,0:T(8,128)(2,1)S(1)}, u32[]{:S(2)}, u32[]{:S(2)}) collective-permute-start(bf16[48,16,128]{2,1,0:T(8,128)(2,1)S(1)} %get-tuple-element.54), channel_id=1, source_target_pairs={{0,1},{1,0},{2,3},{3,2},{4,5},{5,4},{6,7},{7,6},{8,9},{9,8},{10,11... | collective-permute-start | bytes 589832 | tf_op jit(solution)/shard_map/ppermute | solution.py:381
  36.8 1.2 %collective-permute-start.4 = (bf16[8,2,16,256]{3,2,1,0:T(8,128)(2,1)S(1)}, bf16[8,2,16,256]{3,2,1,0:T(8,128)(2,1)S(1)}, u32[]{:S(2)}, u32[]{:S(2)}) collective-permute-start(bf16[8,2,16,256]{3,2,1,0:T(8,128)(2,1)S(1)} %get-tuple-element.43), channel_id=1, source_target_pairs={{0,8},{8,0},{16,24},{24,16},{32,40},{40,32},{48,56},{56,48},{1,9},... | collective-permute-start | bytes 393224 | tf_op jit(solution)/shard_map/ppermute | solution.py:381
  38.0 0.0 collective-permute-done.11.received
  38.0 0.7 shard_map.103
  38.8 5.6 %all-to-all-start.1 = ((bf16[16,4,16,128]{3,2,1,0:T(8,128)(2,1)}), bf16[16,4,16,128]{3,2,1,0:T(8,128)(2,1)S(1)}, u32[]{:S(2)}, u32[]{:S(2)}) async-start(bf16[16,4,16,128]{3,2,1,0:T(8,128)(2,1)} %shard_map.103), calls=%async_computation.1 | async-start | bytes 524288 | tf_op jit(solution)/shard_map/all_to_all | solution.py:385
  44.4 0.0 collective-permute-done.4.refs_1_.rest_1_
  44.4 1.8 %collective-permute-start.5 = (bf16[8,2,16,256]{3,2,1,0:T(8,128)(2,1)S(1)}, bf16[8,2,16,256]{3,2,1,0:T(8,128)(2,1)S(1)}, u32[]{:S(2)}, u32[]{:S(2)}) collective-permute-start(bf16[8,2,16,256]{3,2,1,0:T(8,128)(2,1)S(1)} %shard_map.99), channel_id=1, source_target_pairs={{0,32},{8,40},{16,48},{24,56},{32,0},{40,8},{48,16},{56,24},{1,33}... | collective-permute-start | bytes 393224 | tf_op jit(solution)/shard_map/ppermute | solution.py:381
  46.2 5.9 %all-to-all-done.1.received = bf16[16,4,16,128]{3,2,1,0:T(8,128)(2,1)S(1)} async-done(((bf16[16,4,16,128]{3,2,1,0:T(8,128)(2,1)}), bf16[16,4,16,128]{3,2,1,0:T(8,128)(2,1)S(1)}, u32[]{:S(2)}, u32[]{:S(2)}) %all-to-all-start.1) | async-done | bytes 262176 | tf_op jit(solution)/shard_map/all_to_all | solution.py:385
  52.1 0.7 shard_map.104
  52.8 3.4 %all-to-all-start.2 = ((bf16[8,4,16,128]{3,2,1,0:T(8,128)(2,1)}), bf16[8,4,16,128]{3,2,1,0:T(8,128)(2,1)S(1)}, u32[]{:S(2)}, u32[]{:S(2)}) async-start(bf16[8,4,16,128]{3,2,1,0:T(8,128)(2,1)} %shard_map.104), calls=%async_computation.2 | async-start | bytes 262144 | tf_op jit(solution)/shard_map/all_to_all | solution.py:385
  56.2 0.0 collective-permute-done.5.refs_2_.rest_2_
  56.2 1.4 %collective-permute-start.6 = (bf16[8,2,16,256]{3,2,1,0:T(8,128)(2,1)S(1)}, bf16[8,2,16,256]{3,2,1,0:T(8,128)(2,1)S(1)}, u32[]{:S(2)}, u32[]{:S(2)}) collective-permute-start(bf16[8,2,16,256]{3,2,1,0:T(8,128)(2,1)S(1)} %shard_map.100), channel_id=1, source_target_pairs={{0,4},{4,0},{1,5},{5,1},{2,6},{6,2},{3,7},{7,3},{8,12},{12,8},{9,1... | collective-permute-start | bytes 393224 | tf_op jit(solution)/shard_map/ppermute | solution.py:381
  57.6 6.4 %all-to-all-done.2.received = bf16[8,4,16,128]{3,2,1,0:T(8,128)(2,1)S(1)} async-done(((bf16[8,4,16,128]{3,2,1,0:T(8,128)(2,1)}), bf16[8,4,16,128]{3,2,1,0:T(8,128)(2,1)S(1)}, u32[]{:S(2)}, u32[]{:S(2)}) %all-to-all-start.2) | async-done | bytes 131104 | tf_op jit(solution)/shard_map/all_to_all | solution.py:385
  64.0 0.7 shard_map.105
  64.8 3.5 %all-to-all-start.3 = ((bf16[16,4,16,128]{3,2,1,0:T(8,128)(2,1)}), bf16[16,4,16,128]{3,2,1,0:T(8,128)(2,1)S(1)}, u32[]{:S(2)}, u32[]{:S(2)}) async-start(bf16[16,4,16,128]{3,2,1,0:T(8,128)(2,1)} %shard_map.105), calls=%async_computation.3 | async-start | bytes 524288 | tf_op jit(solution)/shard_map/all_to_all | solution.py:385
  68.3 0.0 collective-permute-done.6.refs_3_.rest_3_
  68.4 0.1 collective-permute-start.7
  68.5 7.3 %all-to-all-done.3 = bf16[16,4,16,128]{3,2,1,0:T(8,128)(2,1)S(1)} async-done(((bf16[16,4,16,128]{3,2,1,0:T(8,128)(2,1)}), bf16[16,4,16,128]{3,2,1,0:T(8,128)(2,1)S(1)}, u32[]{:S(2)}, u32[]{:S(2)}) %all-to-all-start.3) | async-done | bytes 262176 | tf_op jit(solution)/shard_map/all_to_all | solution.py:385
  75.8 4.1 %collective-permute-start.12 = (bf16[64,16,128]{2,1,0:T(8,128)(2,1)S(1)}, bf16[64,16,128]{2,1,0:T(8,128)(2,1)S(1)}, u32[]{:S(2)}, u32[]{:S(2)}) collective-permute-start(bf16[64,16,128]{2,1,0:T(8,128)(2,1)S(1)} %bitcast.11), channel_id=1, source_target_pairs={{0,1},{1,0},{2,3},{3,2},{4,5},{5,4},{6,7},{7,6},{8,9},{9,8},{10,11... | collective-permute-start | bytes 786440 | tf_op jit(solution)/shard_map/ppermute | solution.py:381
  79.8 0.0 collective-permute-done.7.rest_4_
  79.9 1.0 %shard_map.102 = bf16[2,8,32,256]{3,2,1,0:T(8,128)(2,1)} custom-call(bf16[2,8,32,256]{3,2,1,0:T(8,128)(2,1)S(1)} %bitcast.20, f32[1,256]{1,0:T(1,128)S(1)} %bitcast.24, f32[2,8,32,256]{3,2,1,0:T(8,128)S(1)} %bitcast.26, bf16[8,2,16,256]{3,2,1,0:T(8,128)(2,1)S(1)} %get-tuple-element.42.refs_0_.rest_0_, ...), custom_call_target="tpu_custom_call" | custom-call | flops 1600000000 | bytes 4000000 | tf_op jit(solution)/shard_map/pallas_call | solution.py:369
  80.9 0.1 collective-permute-done.12.theirs
  81.0 1.1 %shard_map.106 = (f32[256,768]{1,0:T(8,128)}, f32[256,256]{1,0:T(8,128)}, f32[1,256]{1,0:T(1,128)}) custom-call(bf16[64,16,128]{2,1,0:T(8,128)(2,1)S(1)} %bitcast.12, bf16[64,16,128]{2,1,0:T(8,128)(2,1)S(1)} %collective-permute-done.12.theirs, f32[1,256]{1,0:T(1,128)S(1)} %bitcast.25, bf16[256,768]{1,0:T(8,128)(2,1)S(1)} %copy-done), custom_call_target="tpu_custom_call" | custom-call | flops 800000000 | bytes 2000000 | tf_op jit(solution)/shard_map/pallas_call | solution.py:369
  (12 shorter events, 0.1 us)
Async XLA Ops:
  2.6 12.8 %collective-permute-start = (bf16[2,2,8,16,256]{4,3,2,1,0:T(8,128)(2,1)}, bf16[2,2,8,16,256]{4,3,2,1,0:T(8,128)(2,1)S(1)}, u32[]{:S(2)}, u32[]{:S(2)}) collective-permute-start(bf16[2,2,8,16,256]{4,3,2,1,0:T(8,128)(2,1)} %get-tuple-element.34), channel_id=1, source_target_pairs={{0,2},{2,0},{1,3},{3,1},{4,6},{6,4},{5,7},{7,5},{8,10},{10,8},{9,1... | collective-permute-start | bytes 786440 | tf_op jit(solution)/shard_map/ppermute | solution.py:381
  4.7 10.6 %copy-start.1 = (bf16[1,2,8,32,256]{4,3,2,1,0:T(8,128)(2,1)S(1)}, bf16[1,2,8,32,256]{4,3,2,1,0:T(8,128)(2,1)}, u32[]{:S(2)}) copy-start(bf16[1,2,8,32,256]{4,3,2,1,0:T(8,128)(2,1)} %param.8) | copy-start | bytes 786436
  4.7 10.6 %copy-start.3 = (bf16[1,2,8,32,256]{4,3,2,1,0:T(8,128)(2,1)S(1)}, bf16[1,2,8,32,256]{4,3,2,1,0:T(8,128)(2,1)}, u32[]{:S(2)}) copy-start(bf16[1,2,8,32,256]{4,3,2,1,0:T(8,128)(2,1)} %param.6) | copy-start | bytes 786436
  4.7 24.9 %all-to-all-start = ((bf16[16,2,2,16,256]{4,3,2,1,0:T(8,128)(2,1)}), bf16[16,2,2,16,256]{4,3,2,1,0:T(8,128)(2,1)S(1)}, u32[]{:S(2)}, u32[]{:S(2)}) async-start(bf16[16,2,2,16,256]{4,3,2,1,0:T(8,128)(2,1)} %bitcast.27), calls=%async_computation | async-start | bytes 1048576 | tf_op jit(solution)/shard_map/all_to_all | solution.py:385
  15.3 1.5 %copy-start = (bf16[256,768]{1,0:T(8,128)(2,1)S(1)}, bf16[256,768]{1,0:T(8,128)(2,1)}, u32[]{:S(2)}) copy-start(bf16[256,768]{1,0:T(8,128)(2,1)} %w_qkv.5) | copy-start | bytes 1179652
  15.3 1.5 %copy-start.2 = (bf16[1,2,8,32,256]{4,3,2,1,0:T(8,128)(2,1)S(1)}, bf16[1,2,8,32,256]{4,3,2,1,0:T(8,128)(2,1)}, u32[]{:S(2)}) copy-start(bf16[1,2,8,32,256]{4,3,2,1,0:T(8,128)(2,1)} %param.7) | copy-start | bytes 786436
  15.4 1.5 %copy-start.4 = (bf16[256,256]{1,0:T(8,128)(2,1)S(1)}, bf16[256,256]{1,0:T(8,128)(2,1)}, u32[]{:S(2)}) copy-start(bf16[256,256]{1,0:T(8,128)(2,1)} %w_out.3) | copy-start | bytes 393220
  15.4 5.3 %collective-permute-start.1 = (bf16[2,8,16,256]{3,2,1,0:T(8,128)(2,1)S(1)}, bf16[2,8,16,256]{3,2,1,0:T(8,128)(2,1)S(1)}, u32[]{:S(2)}, u32[]{:S(2)}) collective-permute-start(bf16[2,8,16,256]{3,2,1,0:T(8,128)(2,1)S(1)} %get-tuple-element.36), channel_id=1, source_target_pairs={{0,1},{1,0},{2,3},{3,2},{4,5},{5,4},{6,7},{7,6},{8,9},{9,8},{10,11... | collective-permute-start | bytes 393224 | tf_op jit(solution)/shard_map/ppermute | solution.py:381
  16.7 4.0 %collective-permute-start.2 = (bf16[2,2,8,16,256]{4,3,2,1,0:T(8,128)(2,1)S(1)}, bf16[2,2,8,16,256]{4,3,2,1,0:T(8,128)(2,1)S(1)}, u32[]{:S(2)}, u32[]{:S(2)}) collective-permute-start(bf16[2,2,8,16,256]{4,3,2,1,0:T(8,128)(2,1)S(1)} %collective-permute-done.refs_2_), channel_id=1, source_target_pairs={{0,1},{1,0},{2,3},{3,2},{4,5},{5,4},{6,7},{7,6},{8,9},{9,8},{10,11... | collective-permute-start | bytes 786440 | tf_op jit(solution)/shard_map/ppermute | solution.py:381
  16.8 0.7 copy-start.5
  24.2 2.7 %collective-permute-start.3 = (bf16[64,16,128]{2,1,0:T(8,128)(2,1)S(1)}, bf16[64,16,128]{2,1,0:T(8,128)(2,1)S(1)}, u32[]{:S(2)}, u32[]{:S(2)}) collective-permute-start(bf16[64,16,128]{2,1,0:T(8,128)(2,1)S(1)} %get-tuple-element.41), channel_id=1, source_target_pairs={{0,1},{1,0},{2,3},{3,2},{4,5},{5,4},{6,7},{7,6},{8,9},{9,8},{10,11... | collective-permute-start | bytes 786440 | tf_op jit(solution)/shard_map/ppermute | solution.py:381
  24.8 8.3 %collective-permute-start.8 = (bf16[8,16,256]{2,1,0:T(8,128)(2,1)S(1)}, bf16[8,16,256]{2,1,0:T(8,128)(2,1)S(1)}, u32[]{:S(2)}, u32[]{:S(2)}) collective-permute-start(bf16[8,16,256]{2,1,0:T(8,128)(2,1)S(1)} %get-tuple-element.46), channel_id=1, source_target_pairs={{0,1},{1,0},{2,3},{3,2},{4,5},{5,4},{6,7},{7,6},{8,9},{9,8},{10,11... | collective-permute-start | bytes 196616 | tf_op jit(solution)/shard_map/ppermute | solution.py:381
  24.9 8.3 %collective-permute-start.9 = (bf16[8,16,256]{2,1,0:T(8,128)(2,1)S(1)}, bf16[8,16,256]{2,1,0:T(8,128)(2,1)S(1)}, u32[]{:S(2)}, u32[]{:S(2)}) collective-permute-start(bf16[8,16,256]{2,1,0:T(8,128)(2,1)S(1)} %get-tuple-element.47), channel_id=1, source_target_pairs={{0,2},{1,3},{2,0},{3,1},{4,6},{5,7},{6,4},{7,5},{8,10},{9,11},{10,... | collective-permute-start | bytes 196616 | tf_op jit(solution)/shard_map/ppermute | solution.py:381
  24.9 8.3 %collective-permute-start.10 = (bf16[8,16,256]{2,1,0:T(8,128)(2,1)S(1)}, bf16[8,16,256]{2,1,0:T(8,128)(2,1)S(1)}, u32[]{:S(2)}, u32[]{:S(2)}) collective-permute-start(bf16[8,16,256]{2,1,0:T(8,128)(2,1)S(1)} %get-tuple-element.48), channel_id=1, source_target_pairs={{0,3},{1,2},{2,1},{3,0},{4,7},{5,6},{6,5},{7,4},{8,11},{9,10},{10,... | collective-permute-start | bytes 196616 | tf_op jit(solution)/shard_map/ppermute | solution.py:381
  33.1 4.9 %collective-permute-start.11 = (bf16[48,16,128]{2,1,0:T(8,128)(2,1)S(1)}, bf16[48,16,128]{2,1,0:T(8,128)(2,1)S(1)}, u32[]{:S(2)}, u32[]{:S(2)}) collective-permute-start(bf16[48,16,128]{2,1,0:T(8,128)(2,1)S(1)} %get-tuple-element.54), channel_id=1, source_target_pairs={{0,1},{1,0},{2,3},{3,2},{4,5},{5,4},{6,7},{7,6},{8,9},{9,8},{10,11... | collective-permute-start | bytes 589832 | tf_op jit(solution)/shard_map/ppermute | solution.py:381
  36.8 7.6 %collective-permute-start.4 = (bf16[8,2,16,256]{3,2,1,0:T(8,128)(2,1)S(1)}, bf16[8,2,16,256]{3,2,1,0:T(8,128)(2,1)S(1)}, u32[]{:S(2)}, u32[]{:S(2)}) collective-permute-start(bf16[8,2,16,256]{3,2,1,0:T(8,128)(2,1)S(1)} %get-tuple-element.43), channel_id=1, source_target_pairs={{0,8},{8,0},{16,24},{24,16},{32,40},{40,32},{48,56},{56,48},{1,9},... | collective-permute-start | bytes 393224 | tf_op jit(solution)/shard_map/ppermute | solution.py:381
  38.8 13.4 %all-to-all-start.1 = ((bf16[16,4,16,128]{3,2,1,0:T(8,128)(2,1)}), bf16[16,4,16,128]{3,2,1,0:T(8,128)(2,1)S(1)}, u32[]{:S(2)}, u32[]{:S(2)}) async-start(bf16[16,4,16,128]{3,2,1,0:T(8,128)(2,1)} %shard_map.103), calls=%async_computation.1 | async-start | bytes 524288 | tf_op jit(solution)/shard_map/all_to_all | solution.py:385
  44.4 11.8 %collective-permute-start.5 = (bf16[8,2,16,256]{3,2,1,0:T(8,128)(2,1)S(1)}, bf16[8,2,16,256]{3,2,1,0:T(8,128)(2,1)S(1)}, u32[]{:S(2)}, u32[]{:S(2)}) collective-permute-start(bf16[8,2,16,256]{3,2,1,0:T(8,128)(2,1)S(1)} %shard_map.99), channel_id=1, source_target_pairs={{0,32},{8,40},{16,48},{24,56},{32,0},{40,8},{48,16},{56,24},{1,33}... | collective-permute-start | bytes 393224 | tf_op jit(solution)/shard_map/ppermute | solution.py:381
  52.8 11.2 %all-to-all-start.2 = ((bf16[8,4,16,128]{3,2,1,0:T(8,128)(2,1)}), bf16[8,4,16,128]{3,2,1,0:T(8,128)(2,1)S(1)}, u32[]{:S(2)}, u32[]{:S(2)}) async-start(bf16[8,4,16,128]{3,2,1,0:T(8,128)(2,1)} %shard_map.104), calls=%async_computation.2 | async-start | bytes 262144 | tf_op jit(solution)/shard_map/all_to_all | solution.py:385
  56.2 12.1 %collective-permute-start.6 = (bf16[8,2,16,256]{3,2,1,0:T(8,128)(2,1)S(1)}, bf16[8,2,16,256]{3,2,1,0:T(8,128)(2,1)S(1)}, u32[]{:S(2)}, u32[]{:S(2)}) collective-permute-start(bf16[8,2,16,256]{3,2,1,0:T(8,128)(2,1)S(1)} %shard_map.100), channel_id=1, source_target_pairs={{0,4},{4,0},{1,5},{5,1},{2,6},{6,2},{3,7},{7,3},{8,12},{12,8},{9,1... | collective-permute-start | bytes 393224 | tf_op jit(solution)/shard_map/ppermute | solution.py:381
  64.8 11.0 %all-to-all-start.3 = ((bf16[16,4,16,128]{3,2,1,0:T(8,128)(2,1)}), bf16[16,4,16,128]{3,2,1,0:T(8,128)(2,1)S(1)}, u32[]{:S(2)}, u32[]{:S(2)}) async-start(bf16[16,4,16,128]{3,2,1,0:T(8,128)(2,1)} %shard_map.105), calls=%async_computation.3 | async-start | bytes 524288 | tf_op jit(solution)/shard_map/all_to_all | solution.py:385
  68.4 11.5 %collective-permute-start.7 = (bf16[8,2,16,256]{3,2,1,0:T(8,128)(2,1)S(1)}, bf16[8,2,16,256]{3,2,1,0:T(8,128)(2,1)S(1)}, u32[]{:S(2)}, u32[]{:S(2)}) collective-permute-start(bf16[8,2,16,256]{3,2,1,0:T(8,128)(2,1)S(1)} %shard_map.101), channel_id=1, source_target_pairs={{0,16},{8,24},{16,0},{24,8},{32,48},{40,56},{48,32},{56,40},{1,17}... | collective-permute-start | bytes 393224 | tf_op jit(solution)/shard_map/ppermute | solution.py:381
  75.8 5.2 %collective-permute-start.12 = (bf16[64,16,128]{2,1,0:T(8,128)(2,1)S(1)}, bf16[64,16,128]{2,1,0:T(8,128)(2,1)S(1)}, u32[]{:S(2)}, u32[]{:S(2)}) collective-permute-start(bf16[64,16,128]{2,1,0:T(8,128)(2,1)S(1)} %bitcast.11), channel_id=1, source_target_pairs={{0,1},{1,0},{2,3},{3,2},{4,5},{5,4},{6,7},{7,6},{8,9},{9,8},{10,11... | collective-permute-start | bytes 786440 | tf_op jit(solution)/shard_map/ppermute | solution.py:381
